TPU v7x, 32 devices: a whole 2x2x4 slice. The times are simulated.
32 devices in a mesh: pair: 4 (over y, x), aux: 8 (over z, core).
Axes of the slice: x: 2, y: 2, z: 4, core: 2. Of those that a mesh axis runs over, the one named last changes fastest.
Arguments:
- integrals: bfloat16 [128, 49152], P('pair', 'aux'), may hold values from -6 to 6
- block_mask: int32 [2, 768], P(None, 'aux'), may hold values 0 or 1
- block_atom: int32 [2], replicated, may hold values from 0 to 15
- green_occ: bfloat16 [2, 16, 64, 64], replicated, may hold values from -0.75 to 0.75
- green_virt: bfloat16 [2, 16, 64, 64], replicated, may hold values from -0.75 to 0.75
- time_weights: float32 [2], replicated, may hold values from 0.3 to 3
Outputs:
- polarizability: float32 [2, 768, 768], P(None, 'aux', 'pair')
- energy: float32 [], replicated
All inputs are finite; a program needn't handle non-finite values. No bound on the sum of `block_mask` on one device may be relied on, other than what follows from the above.
Results may differ from a plain program's by a relative error of at most 0.004.
Values may be sent and summed in bfloat16 or wider, within the bound.
No kernel may reach another device: no remote copies, remote signals or barrier semaphores. Data moves between devices by JAX's collectives and lax.ppermute only.
A program may use at most 192 MiB of HBM per device.

v0:
```python
import jax
import jax.numpy as jnp
from jax import lax
from jax.sharding import PartitionSpec as P

BLK = 64


def per_device(integrals, block_mask, block_atom, green_occ, green_virt, time_weights):
    rows = integrals.shape[0]
    aux_here = integrals.shape[1] // BLK
    pair_count = lax.axis_size("pair")
    aux_total = aux_here * lax.axis_size("aux")
    first_row = lax.axis_index("pair") * rows
    row_block = (first_row + jnp.arange(rows, dtype=jnp.int32)) // BLK
    row_mask = block_mask[row_block]
    three = integrals.reshape(rows, aux_here, BLK)
    masked = jnp.where(row_mask[:, :, None] > 0, three, jnp.zeros_like(three))
    row_atom = block_atom[row_block]
    occ_rows = green_occ[:, row_atom]
    virt_rows = green_virt[:, row_atom]
    scale = 1.0 / jnp.sqrt(jnp.float32(rows * pair_count * BLK))
    occ_half = jnp.einsum(
        "rpn,trnl->trpl", masked, occ_rows, preferred_element_type=jnp.float32
    ).astype(jnp.bfloat16)
    masked_flat = masked.reshape(rows, aux_here * BLK)
    piece = lax.all_gather(masked_flat, "aux", axis=1, tiled=True)
    count = piece.shape[1] // BLK
    partner = piece.reshape(rows, count, BLK)
    partner_half = jnp.einsum(
        "rqn,trnl->trql", partner, virt_rows, preferred_element_type=jnp.float32
    ).astype(jnp.bfloat16)
    part = jnp.einsum("trpl,trql->tpq", occ_half, partner_half, preferred_element_type=jnp.float32)
    chi_tile = lax.psum_scatter(part * scale, "pair", scatter_dimension=2, tiled=True)
    local_sum = jnp.sum(time_weights[:, None, None] * chi_tile * chi_tile)
    summed = lax.psum(local_sum, ("pair", "aux"))
    energy = -summed / jnp.float32(aux_total * aux_total)
    return (chi_tile, energy)


def solution(mesh):
    placed = (P("pair", "aux"), P(None, "aux"), P(), P(), P(), P())
    return jax.shard_map(
        per_device,
        mesh=mesh,
        in_specs=placed,
        out_specs=(P(None, "aux", "pair"), P()),
        check_vma=False,
    )
```

profile of v0, /device:TPU:0, one launch (start us, length us, event | category | flops | bytes accessed | tf_op | source)
XLA Modules:
  0.0 146.9 jit_solution(12446607883005672119)
XLA Ops:
  7.2 0.0 copy-start
  7.2 0.0 copy-start.1
  7.2 0.0 all-gather.2.cloned.1.call-start
  7.2 1.3 fusion.32
  8.6 1.3 fusion.29
  9.9 1.3 gather_fusion.1
  11.2 0.6 broadcast_in_dim.21
  11.7 0.7 broadcast_in_dim.23
  12.4 1.8 %broadcast_select_fusion = bf16[32,6144]{1,0:T(8,128)(2,1)} fusion(pred[32,6144]{1,0:T(8,128)(4,1)S(1)} %broadcast_in_dim.23, bf16[32,6144]{1,0:T(8,128)(2,1)} %param.6), kind=kLoop, calls=%fused_computation.20 | loop fusion | flops 196608 | bytes 983040 | tf_op jit(solution)/shard_map/jit(_where)/select_n | solution.py:18
  14.2 0.0 all-gather.2.cloned.1.call-update
  14.3 0.0 reduce-scatter.4.cloned.1.call-start
  14.3 2.6 %reshape.91 = bf16[32,96,64]{2,1,0:T(8,128)(2,1)} reshape(bf16[32,6144]{1,0:T(8,128)(2,1)} %param.6) | data formatting | bytes 786432 | tf_op jit(solution)/shard_map/reshape | solution.py:17
  17.0 0.0 copy-done
  17.0 0.7 gather_fusion
  17.7 0.0 copy-done.1
  17.7 0.7 gather_fusion.2
  18.5 3.2 %fusion.9 = bf16[2,32,96,64]{2,3,1,0:T(8,128)(2,1)} fusion(bf16[32,96,64]{2,1,0:T(8,128)(2,1)} %reshape.91, pred[32,96]{1,0:T(8,128)(4,1)S(1)} %broadcast_compare_fusion, bf16[32,2,64,64]{3,2,1,0:T(8,128)(2,1)S(1)} %gather_fusion), kind=kOutput, calls=%fused_computation.9 | convolution fusion | flops 50921472 | bytes 1707008 | tf_op jit(solution)/shard_map/rpn,trnl->trpl/dot_general | solution.py:23
  21.7 0.0 copy-start.2
  21.7 33.7 %all-gather.2.cloned.1.call-done = bf16[32,49152]{1,0:T(8,128)(2,1)} async-done(((bf16[32,6144]{1,0:T(8,128)(2,1)}), bf16[32,49152]{1,0:T(8,128)(2,1)}) %all-gather.2.cloned.1.call-update) | async-done | bytes 3145744 | tf_op jit(solution)/shard_map/all_gather | solution.py:27
  55.4 8.4 %reshape.92 = bf16[32,768,64]{2,1,0:T(8,128)(2,1)} reshape(bf16[32,49152]{1,0:T(8,128)(2,1)} %all-gather.2.cloned.1.call-done) | data formatting | bytes 6291456 | tf_op jit(solution)/shard_map/reshape | solution.py:29
  63.8 0.0 copy-done.2
  63.9 0.0 copy-start.4
  63.9 5.9 %fusion.15 = f32[2,96,768]{2,1,0:T(8,128)S(1)} fusion(bf16[2,32,96,64]{2,3,1,0:T(8,128)(2,1)S(1)} %copy-done.2, bf16[32,768,64]{2,1,0:T(8,128)(2,1)} %reshape.92, bf16[32,2,64,64]{3,2,1,0:T(8,128)(2,1)S(1)} %gather_fusion.2), kind=kOutput, calls=%fused_computation.11 | convolution fusion | flops 1009926144 | bytes 5046272 | tf_op jit(solution)/shard_map/trpl,trql->tpq/dot_general | solution.py:33
  69.8 0.5 copy.21
  70.3 1.4 reshape.129
  71.6 0.0 reduce-scatter.4.cloned.1.call-update
  71.7 25.1 %reduce-scatter.4.cloned.1.call-done = f32[192,192]{1,0:T(8,128)} async-done(((f32[768,192]{1,0:T(8,128)}), f32[192,192]{1,0:T(8,128)}) %reduce-scatter.4.cloned.1.call-update) | async-done | bytes 147472
  96.8 1.1 reshape.130
  97.9 0.1 copy.22
  98.0 0.0 copy-done.4
  98.0 0.0 copy-start.3
  98.0 0.7 fusion.27
  98.7 39.5 %psum.7 = f32[]{:T(128)} all-reduce(f32[]{:T(128)} %fusion.27), channel_id=1, replica_groups=mesh['pair'=4,'aux'=8] {'pair','aux'}, use_global_device_ids=true, to_apply=%region_2.3 | all-reduce | flops 1 | bytes 8 | tf_op jit(solution)/shard_map/psum | solution.py:36
  138.9 0.0 copy-done.3
  (3 shorter events, 0.0 us)
Async XLA Ops:
  7.2 9.8 %copy-start = (bf16[2,16,64,64]{3,2,1,0:T(8,128)(2,1)S(1)}, bf16[2,16,64,64]{3,2,1,0:T(8,128)(2,1)}, u32[]{:S(2)}) copy-start(bf16[2,16,64,64]{3,2,1,0:T(8,128)(2,1)} %param.9) | copy-start | bytes 786436
  7.2 10.6 %copy-start.1 = (bf16[2,16,64,64]{3,2,1,0:T(8,128)(2,1)S(1)}, bf16[2,16,64,64]{3,2,1,0:T(8,128)(2,1)}, u32[]{:S(2)}) copy-start(bf16[2,16,64,64]{3,2,1,0:T(8,128)(2,1)} %param.10) | copy-start | bytes 786436
  7.2 48.2 %all-gather.2.cloned.1.call-start = ((), (), s32[]{:S(2)}) async-start(), calls=%async_computation.1 | async-start | bytes 3538944 | tf_op jit(solution)/shard_map/all_gather | solution.py:27
  14.3 82.5 %reduce-scatter.4.cloned.1.call-start = ((), (), s32[]{:S(2)}) async-start(), calls=%async_computation.2 | async-start | bytes 983040
  21.7 42.1 %copy-start.2 = (bf16[2,32,96,64]{2,3,1,0:T(8,128)(2,1)S(1)}, bf16[2,32,96,64]{2,3,1,0:T(8,128)(2,1)}, u32[]{:S(2)}) copy-start(bf16[2,32,96,64]{2,3,1,0:T(8,128)(2,1)} %fusion.9) | copy-start | bytes 2359300
  63.9 34.1 %copy-start.4 = (f32[2]{0:T(128)S(1)}, f32[2]{0:T(128)}, u32[]{:S(2)}) copy-start(f32[2]{0:T(128)} %param.11) | copy-start | bytes 28
  98.0 40.9 %copy-start.3 = (f32[2,96,192]{2,1,0:T(8,128)}, f32[2,96,192]{2,1,0:T(8,128)S(1)}, u32[]{:S(2)}) copy-start(f32[2,96,192]{2,1,0:T(8,128)S(1)} %copy.22) | copy-start | bytes 442372
Sparse Core Ops, SparseCore 0:
  14.4 40.9 all-gather.1
  71.8 24.9 reduce-scatter.3
where the time goes:
time: 147 us
  waiting for transfers between devices  58.8 us (40%)
  blocking collectives  39.5 us (27%)
  local copies, waits for them, and re-layouts  19.5 us (13%)
  between operations  16 us (11%)
  matrix products  9.13 us (6%)
  other arithmetic  3.84 us (3%)
    psum x1, blocking collectives, per_device(): summed = lax.psum(local_sum, ('pair', 'aux'))  39.5 us
    all_gather x1, waiting for transfers between devices, per_device(): piece = lax.all_gather(masked_flat, 'aux', axis=1, tiled=True)  33.7 us
    unnamed x3, waiting for transfers between devices  25.1 us
    reshape x1, local copies, waits for them, and re-layouts, per_device(): partner = piece.reshape(rows, count, BLK)  8.45 us
    dot_general x1, matrix products, per_device(): jnp.einsum('trpl,trql->tpq', occ_half, partner_half, preferred_element_ty...  5.92 us
    dot_general x1, matrix products, per_device(): jnp.einsum('rpn,trnl->trpl', masked, occ_rows, preferred_element_type=jnp...  3.22 us
    unnamed x14, local copies, waits for them, and re-layouts  3.1 us
  transfers between devices with their start and end apart: 2, of which 2 were waited for; matrix products, arithmetic and copies ran while one was open for 5% of the time, Pallas kernels for 0%

commit v1 on v0

v1 whole, which is shorter than its diff:
```python
import functools
import jax
import jax.numpy as jnp
from jax import lax
from jax.experimental import pallas as pl
from jax.experimental.pallas import tpu as pltpu
from jax.sharding import PartitionSpec as P

BLK = 64
VMEM = pl.BlockSpec(memory_space=pltpu.VMEM)
SMEM = pl.BlockSpec(memory_space=pltpu.SMEM)
PARAMS = pltpu.CompilerParams(vmem_limit_bytes=40 * 1024 * 1024)
NT_DIMS = (((1,), (1,)), ((), ()))


def arrange_kernel(rows, aux, x_ref, mask_ref, y_ref, wide):
    groups = rows // 8
    block = lax.axis_index("pair") * rows // BLK
    low = lax.broadcasted_iota(jnp.int32, (8, 128), 1) < BLK
    for i in range(aux // 2):
        tile = x_ref[:, i * 128:(i + 1) * 128].astype(jnp.float32)
        keep0 = mask_ref[block, 2 * i] > 0
        keep1 = mask_ref[block, 2 * i + 1] > 0
        for g in range(0, groups, 2):
            first = tile[8 * g:8 * g + 8]
            second = tile[8 * g + 8:8 * g + 16]
            even = jnp.where(low, first, pltpu.roll(second, BLK, 1))
            odd = jnp.where(low, pltpu.roll(first, BLK, 1), second)
            even = jnp.where(keep0, even, 0.0)
            odd = jnp.where(keep1, odd, 0.0)
            half = g // 2
            wide[half, pl.ds(2 * i, 8, stride=aux), :] = even
            wide[half, pl.ds(2 * i + 1, 8, stride=aux), :] = odd
    for s in range(8):
        for half in range(groups // 2):
            y_ref[s, :, half * 128:(half + 1) * 128] = wide[half, s * aux:(s + 1) * aux, :].astype(y_ref.dtype)


def arrange(integrals, block_mask):
    rows, width = integrals.shape
    aux = width // BLK
    return pl.pallas_call(
        functools.partial(arrange_kernel, rows, aux),
        out_shape=jax.ShapeDtypeStruct((8, aux, rows // 8 * BLK), jnp.bfloat16),
        in_specs=[VMEM, SMEM],
        out_specs=VMEM,
        scratch_shapes=[pltpu.VMEM((rows // 16, 8 * aux, 128), jnp.float32)],
        compiler_params=PARAMS,
        name="arrange",
    )(integrals, block_mask)


def transform_kernel(nt, atom_ref, y_ref, occ_ref, virt_ref, z_ref):
    steps, aux, wide = y_ref.shape
    copies = wide // BLK
    same = (
        lax.broadcasted_iota(jnp.int32, (wide, wide), 0) // BLK
        == lax.broadcasted_iota(jnp.int32, (wide, wide), 1) // BLK
    )
    y = y_ref[...].reshape(steps * aux, wide)
    for t in range(nt):
        occ = jnp.concatenate([occ_ref[t, 0]] * copies, axis=0)
        virt = jnp.concatenate([virt_ref[t, 0]] * copies, axis=0)
        both = lax.dot_general(occ, virt, NT_DIMS, preferred_element_type=jnp.float32)
        both = jnp.where(same, both, 0.0)
        high = both.astype(jnp.bfloat16)
        rest = (both - high.astype(jnp.float32)).astype(jnp.bfloat16)
        z = jnp.dot(y, high, preferred_element_type=jnp.float32)
        z += jnp.dot(y, rest, preferred_element_type=jnp.float32)
        z = z.astype(jnp.bfloat16)
        for s in range(steps):
            z_ref[s, t * aux:(t + 1) * aux, :] = z[s * aux:(s + 1) * aux]


def transform(atom, y, green_occ, green_virt):
    nt = green_occ.shape[0]
    steps, aux, wide = y.shape
    green = pl.BlockSpec((nt, 1, BLK, BLK), lambda i, atom: (0, atom[0], 0, 0))
    return pl.pallas_call(
        functools.partial(transform_kernel, nt),
        out_shape=jax.ShapeDtypeStruct((steps, nt * aux, wide), jnp.bfloat16),
        grid_spec=pltpu.PrefetchScalarGridSpec(
            num_scalar_prefetch=1,
            grid=(1,),
            in_specs=[pl.BlockSpec((steps, aux, wide), lambda i, atom: (0, 0, 0)), green, green],
            out_specs=pl.BlockSpec((steps, nt * aux, wide), lambda i, atom: (0, 0, 0)),
        ),
        compiler_params=PARAMS,
        name="transform",
    )(atom, y, green_occ, green_virt)


def products(z_ref, first_ref, second_ref):
    total = None
    for s in range(z_ref.shape[0]):
        partner = jnp.concatenate([first_ref[s], second_ref[s]], axis=0)
        term = lax.dot_general(z_ref[s], partner, NT_DIMS, preferred_element_type=jnp.float32)
        total = term if total is None else total + term
    return total


def chunk_kernel(z_ref, mine_ref, other_ref, out_ref):
    odd = lax.rem(lax.axis_index("aux"), 2)

    @pl.when(odd == 0)
    def _():
        out_ref[...] = products(z_ref, mine_ref, other_ref)

    @pl.when(odd == 1)
    def _():
        out_ref[...] = products(z_ref, other_ref, mine_ref)


def chunk(z, mine, other):
    return pl.pallas_call(
        chunk_kernel,
        out_shape=jax.ShapeDtypeStruct((z.shape[1], 2 * mine.shape[1]), jnp.float32),
        in_specs=[VMEM] * 3,
        out_specs=VMEM,
        compiler_params=PARAMS,
        name="chunk",
    )(z, mine, other)


def finish_kernel(scale, count, nt, weight_ref, *refs):
    parts, (chi_ref, sum_ref) = refs[:count], refs[count:]
    aux = chi_ref.shape[1]
    total = parts[0][...]
    for part in parts[1:]:
        total += part[...].astype(jnp.float32)
    total *= scale
    local = jnp.zeros((1, 1), jnp.float32)
    for t in range(nt):
        chi = total[t * aux:(t + 1) * aux]
        chi_ref[t] = chi
        local += weight_ref[t] * jnp.sum(chi * chi, keepdims=True)
    sum_ref[...] = jnp.broadcast_to(local, sum_ref.shape)


def finish(scale, time_weights, parts, replicas):
    nt = time_weights.shape[0]
    height, width = parts[0].shape
    return pl.pallas_call(
        functools.partial(finish_kernel, scale, len(parts), nt),
        out_shape=(
            jax.ShapeDtypeStruct((nt, height // nt, width), jnp.float32),
            jax.ShapeDtypeStruct((replicas, 128), jnp.float32),
        ),
        in_specs=[SMEM] + [VMEM] * len(parts),
        out_specs=(VMEM, VMEM),
        compiler_params=PARAMS,
        name="finish",
    )(time_weights, *parts)


def per_device(integrals, block_mask, block_atom, green_occ, green_virt, time_weights):
    rows = integrals.shape[0]
    aux_here = integrals.shape[1] // BLK
    pairs, auxes = lax.axis_size("pair"), lax.axis_size("aux")
    pair, aux = lax.axis_index("pair"), lax.axis_index("aux")
    chips = auxes // 2
    aux_total = aux_here * auxes
    columns = aux_total // pairs
    nt = green_occ.shape[0]

    sibling = [(i, i ^ 1) for i in range(auxes)]
    onward = [(i, (i + 2) % auxes) for i in range(auxes)]
    y = arrange(integrals, block_mask)
    atom = lax.dynamic_slice(block_atom, (pair * rows // BLK,), (1,))
    z = transform(atom, y, green_occ, green_virt)
    mine = y
    chunks = []
    for step in range(chips):
        other = lax.ppermute(mine, "aux", sibling)
        following = lax.ppermute(mine, "aux", onward) if step < chips - 1 else None
        chunks.append(chunk(z, mine, other))
        mine = following
    stacked = jnp.stack(chunks)
    order = (aux // 2 - jnp.arange(chips)) % chips
    whole = stacked[order]
    whole = whole.transpose(1, 0, 2).reshape(nt * aux_here, aux_total)
    parts = [lax.dynamic_slice(whole, (0, pair * columns), (nt * aux_here, columns))]
    for j in range(1, pairs):
        towards = [(i, (i + j) % pairs) for i in range(pairs)]
        target = (pair + j) % pairs
        piece = lax.dynamic_slice(whole, (0, target * columns), (nt * aux_here, columns))
        parts.append(lax.ppermute(piece.astype(jnp.bfloat16), "pair", towards))
    scale = float((rows * pairs * BLK) ** -0.5)
    chi, sums = finish(scale, time_weights, parts, pairs * auxes)
    everyone = lax.all_to_all(sums, ("pair", "aux"), 0, 0, tiled=True)
    energy = -jnp.sum(everyone[:, 0]) / jnp.float32(aux_total * aux_total)
    return chi, energy


def solution(mesh):
    placed = (P("pair", "aux"), P(None, "aux"), P(), P(), P(), P())
    return jax.shard_map(
        per_device,
        mesh=mesh,
        in_specs=placed,
        out_specs=(P(None, "aux", "pair"), P()),
        check_vma=False,
    )
```

time: 147 us -> 70.7 us (0.48)
  blocking collectives: 39.5 us -> 9.24 us
  waiting for transfers between devices: 58.8 us -> 37.9 us
  local copies, waits for them, and re-layouts: 19.5 us -> 5.89 us
  between operations: 16 us -> 2.57 us
  matrix products: 9.13 us -> 0 us
  starting transfers between devices: 0.08 us -> 7.59 us
  Pallas kernels: 0 us -> 6.53 us
  other arithmetic: 3.84 us -> 0.68 us
    psum x1 -> x0, blocking collectives: 39.5 us -> none  [per_device(): summed = lax.psum(local_sum, ('pair', 'aux'))]
    ppermute x0 -> x10, waiting for transfers between devices: none -> 37.9 us  [the longest x3 33.9 us: per_device(): following = lax.ppermute(mine, 'aux', onward) if step < chips - 1 else None]
    all_gather x1 -> x0, waiting for transfers between devices: 33.7 us -> none  [per_device(): piece = lax.all_gather(masked_flat, 'aux', axis=1, tiled=True)]
    unnamed x3 -> x0, waiting for transfers between devices: 25.1 us -> none
    reshape x2 -> x1, local copies, waits for them, and re-layouts: 11.1 us -> 0.49 us  [per_device(): whole = whole.transpose(1, 0, 2).reshape(nt * aux_here, aux_total)]
    all_to_all x0 -> x1, blocking collectives: none -> 9.24 us  [per_device(): everyone = lax.all_to_all(sums, ('pair', 'aux'), 0, 0, tiled=True)]
    dot_general x2 -> x0, matrix products: 9.13 us -> none  [the longest x1 5.92 us: per_device(): jnp.einsum('trpl,trql->tpq', occ_half, partner_half, preferred_element_ty...]
    ppermute x0 -> x10, starting transfers between devices: none -> 7.59 us  [the longest x3 4 us: per_device(): parts.append(lax.ppermute(piece.astype(jnp.bfloat16), 'pair', towards))]
  transfers between devices with their start and end apart: 2 -> 10, of which waited for: 2 -> 5; matrix products, arithmetic and copies ran while one was open for 5% -> 1% of each run, Pallas kernels for 0% -> 5%
where the time goes in v1:
time: 70.7 us; the launch traced here: 70.4 us
  waiting for transfers between devices  37.9 us (54%)
  blocking collectives  9.24 us (13%)
  starting transfers between devices  7.59 us (11%)
  Pallas kernels  6.53 us (9%)
  local copies, waits for them, and re-layouts  5.89 us (8%)
  between operations  2.57 us (4%)
    ppermute x3, waiting for transfers between devices, per_device(): following = lax.ppermute(mine, 'aux', onward) if step < chips - 1 else None  33.9 us
    all_to_all x1, blocking collectives, per_device(): everyone = lax.all_to_all(sums, ('pair', 'aux'), 0, 0, tiled=True)  9.24 us
    ppermute x3, starting transfers between devices, per_device(): parts.append(lax.ppermute(piece.astype(jnp.bfloat16), 'pair', towards))  4 us
    ppermute x3, waiting for transfers between devices, per_device(): parts.append(lax.ppermute(piece.astype(jnp.bfloat16), 'pair', towards))  3.96 us
    unnamed x12, local copies, waits for them, and re-layouts  3.43 us
    ppermute x3, starting transfers between devices, per_device(): following = lax.ppermute(mine, 'aux', onward) if step < chips - 1 else None  3.08 us
    pallas_call x4, Pallas kernels, chunk(): pl.pallas_call(chunk_kernel, out_shape=jax.ShapeDtypeStruct((z.shape[1],...  2.58 us
    pallas_call x1, Pallas kernels, transform(): pl.pallas_call(functools.partial(transform_kernel, nt), out_shape=jax.Sha...  1.43 us
  transfers between devices with their start and end apart: 10, of which 5 were waited for; matrix products, arithmetic and copies ran while one was open for 1% of the time, Pallas kernels for 5%

profile of v1, /device:TPU:0, one launch (start us, length us, event | category | flops | bytes accessed | tf_op | source)
XLA Modules:
  0.0 70.4 jit_solution(585952541945924274)
XLA Ops:
  0.6 0.0 copy-start
  0.6 0.0 copy-start.2
  0.6 1.0 %copy-done.2 = bf16[32,6144]{1,0:T(8,128)(2,1)S(1)} copy-done((bf16[32,6144]{1,0:T(8,128)(2,1)S(1)}, bf16[32,6144]{1,0:T(8,128)(2,1)}, u32[]{:S(2)}) %copy-start.2) | copy-done | bytes 393240
  1.7 0.0 copy-start.3
  1.7 0.7 copy-done.3
  2.4 1.2 %arrange.1.y_ref.mine_ref = bf16[8,96,256]{2,1,0:T(8,128)(2,1)S(1)} custom-call(bf16[32,6144]{1,0:T(8,128)(2,1)S(1)} %copy-done.2, s32[2,96]{1,0:T(2,128)S(1)} %copy-done.3), custom_call_target="tpu_custom_call" | custom-call | tf_op jit(solution)/shard_map/arrange/pallas_call | solution.py:42
  3.6 3.1 %collective-permute-start.1 = (bf16[8,96,256]{2,1,0:T(8,128)(2,1)S(1)}, bf16[8,96,256]{2,1,0:T(8,128)(2,1)S(1)}, u32[]{:S(2)}, u32[]{:S(2)}) collective-permute-start(bf16[8,96,256]{2,1,0:T(8,128)(2,1)S(1)} %arrange.1.y_ref.mine_ref), channel_id=1, source_target_pairs={{0,2},{1,3},{2,4},{3,5},{4,6},{5,7},{6,0},{7,1},{8,10},{9,11},{10,... | collective-permute-start | bytes 1179656 | tf_op jit(solution)/shard_map/ppermute | solution.py:175
  6.7 11.1 %collective-permute-done.1.mine_ref = bf16[8,96,256]{2,1,0:T(8,128)(2,1)S(1)} collective-permute-done((bf16[8,96,256]{2,1,0:T(8,128)(2,1)S(1)}, bf16[8,96,256]{2,1,0:T(8,128)(2,1)S(1)}, u32[]{:S(2)}, u32[]{:S(2)}) %collective-permute-start.1) | collective-permute-done | bytes 393248 | tf_op jit(solution)/shard_map/ppermute | solution.py:175
  17.8 0.0 collective-permute-start.3
  17.8 12.1 %collective-permute-done.3.mine_ref = bf16[8,96,256]{2,1,0:T(8,128)(2,1)S(1)} collective-permute-done((bf16[8,96,256]{2,1,0:T(8,128)(2,1)S(1)}, bf16[8,96,256]{2,1,0:T(8,128)(2,1)S(1)}, u32[]{:S(2)}, u32[]{:S(2)}) %collective-permute-start.3) | collective-permute-done | bytes 393248 | tf_op jit(solution)/shard_map/ppermute | solution.py:175
  29.9 0.0 collective-permute-start.5
  29.9 0.0 collective-permute-start
  29.9 0.5 collective-permute-start.2
  30.4 0.0 collective-permute-start.4
  30.5 10.7 %collective-permute-done.5.mine_ref = bf16[8,96,256]{2,1,0:T(8,128)(2,1)S(1)} collective-permute-done((bf16[8,96,256]{2,1,0:T(8,128)(2,1)S(1)}, bf16[8,96,256]{2,1,0:T(8,128)(2,1)S(1)}, u32[]{:S(2)}, u32[]{:S(2)}) %collective-permute-start.5) | collective-permute-done | bytes 393248 | tf_op jit(solution)/shard_map/ppermute | solution.py:175
  41.1 0.0 collective-permute-start.6
  41.1 0.0 copy-start.5
  41.1 0.7 copy-done.5
  41.8 0.6 dynamic_slice.15.atom_ref
  42.4 0.0 copy-done
  42.4 0.0 copy-start.1
  42.4 1.0 %copy-done.1 = bf16[2,16,64,64]{3,2,1,0:T(8,128)(2,1)S(1)} copy-done((bf16[2,16,64,64]{3,2,1,0:T(8,128)(2,1)S(1)}, bf16[2,16,64,64]{3,2,1,0:T(8,128)(2,1)}, u32[]{:S(2)}) %copy-start.1) | copy-done | bytes 262168
  43.4 1.4 %transform.1.z_ref = bf16[8,192,256]{2,1,0:T(8,128)(2,1)S(1)} custom-call(s32[1]{0:T(128)} %dynamic_slice.15.atom_ref, bf16[8,96,256]{2,1,0:T(8,128)(2,1)S(1)} %arrange.1.y_ref.mine_ref, bf16[2,16,64,64]{3,2,1,0:T(8,128)(2,1)S(1)} %copy-done, bf16[2,16,64,64]{3,2,1,0:T(8,128)(2,1)S(1)} %copy-done.1), custom_call_target="tpu_custom_call" | custom-call | tf_op jit(solution)/shard_map/transform/pallas_call | solution.py:79
  44.9 0.0 collective-permute-done.other_ref
  44.9 1.4 %chunk.4 = f32[192,192]{1,0:T(8,128)S(1)} custom-call(bf16[8,192,256]{2,1,0:T(8,128)(2,1)S(1)} %transform.1.z_ref, bf16[8,96,256]{2,1,0:T(8,128)(2,1)S(1)} %arrange.1.y_ref.mine_ref, bf16[8,96,256]{2,1,0:T(8,128)(2,1)} %collective-permute-done.other_ref), custom_call_target="tpu_custom_call" | custom-call | tf_op jit(solution)/shard_map/chunk/pallas_call | solution.py:115
  46.3 0.0 collective-permute-done.2.other_ref
  46.3 0.4 chunk.5
  46.7 0.0 collective-permute-done.4.other_ref
  46.7 0.4 chunk.6
  47.1 0.0 collective-permute-done.6.other_ref
  47.1 0.4 chunk.7
  47.5 0.1 pad_maximum_fusion
  47.6 0.6 gather_fusion
  48.2 0.5 copy.9
  48.7 0.5 reshape.58
  49.2 0.2 dynamic-slice_convert_fusion
  49.4 1.0 %collective-permute-start.7 = (bf16[192,192]{1,0:T(8,128)(2,1)S(1)}, bf16[192,192]{1,0:T(8,128)(2,1)S(1)}, u32[]{:S(2)}, u32[]{:S(2)}) collective-permute-start(bf16[192,192]{1,0:T(8,128)(2,1)S(1)} %get-tuple-element.8), channel_id=1, source_target_pairs={{0,8},{8,16},{16,24},{24,0},{1,9},{9,17},{17,25},{25,1},{2,10},{10... | collective-permute-start | bytes 221192 | tf_op jit(solution)/shard_map/ppermute | solution.py:187
  50.4 1.5 %collective-permute-start.8 = (bf16[192,192]{1,0:T(8,128)(2,1)S(1)}, bf16[192,192]{1,0:T(8,128)(2,1)S(1)}, u32[]{:S(2)}, u32[]{:S(2)}) collective-permute-start(bf16[192,192]{1,0:T(8,128)(2,1)S(1)} %get-tuple-element.7), channel_id=1, source_target_pairs={{0,16},{8,24},{16,0},{24,8},{1,17},{9,25},{17,1},{25,9},{2,18},{10... | collective-permute-start | bytes 221192 | tf_op jit(solution)/shard_map/ppermute | solution.py:187
  52.0 0.0 copy-start.4
  52.0 1.4 %collective-permute-start.9 = (bf16[192,192]{1,0:T(8,128)(2,1)S(1)}, bf16[192,192]{1,0:T(8,128)(2,1)S(1)}, u32[]{:S(2)}, u32[]{:S(2)}) collective-permute-start(bf16[192,192]{1,0:T(8,128)(2,1)S(1)} %get-tuple-element.6), channel_id=1, source_target_pairs={{0,24},{8,0},{16,8},{24,16},{1,25},{9,1},{17,9},{25,17},{2,26},{10... | collective-permute-start | bytes 221192 | tf_op jit(solution)/shard_map/ppermute | solution.py:187
  53.4 0.1 constant_dynamic-slice_fusion.refs_0_
  53.5 2.5 %collective-permute-done.7.refs_1_ = bf16[192,192]{1,0:T(8,128)(2,1)S(1)} collective-permute-done((bf16[192,192]{1,0:T(8,128)(2,1)S(1)}, bf16[192,192]{1,0:T(8,128)(2,1)S(1)}, u32[]{:S(2)}, u32[]{:S(2)}) %collective-permute-start.7) | collective-permute-done | bytes 73760 | tf_op jit(solution)/shard_map/ppermute | solution.py:187
  56.0 1.5 %collective-permute-done.8.refs_2_ = bf16[192,192]{1,0:T(8,128)(2,1)S(1)} collective-permute-done((bf16[192,192]{1,0:T(8,128)(2,1)S(1)}, bf16[192,192]{1,0:T(8,128)(2,1)S(1)}, u32[]{:S(2)}, u32[]{:S(2)}) %collective-permute-start.8) | collective-permute-done | bytes 73760 | tf_op jit(solution)/shard_map/ppermute | solution.py:187
  57.5 0.0 collective-permute-done.9.refs_3_
  57.5 0.0 copy-done.4
  57.5 1.3 %finish.1 = (f32[2,96,192]{2,1,0:T(8,128)}, f32[32,128]{1,0:T(8,128)S(1)}) custom-call(f32[2]{0:T(128)S(1)} %copy-done.4, f32[192,192]{1,0:T(8,128)S(1)} %constant_dynamic-slice_fusion.refs_0_, bf16[192,192]{1,0:T(8,128)(2,1)S(1)} %collective-permute-done.7.refs_1_, bf16[192,192]{1,0:T(8,128)(2,1)S(1)} %collective-permute-done.8.refs_2_, ...), custom_call_target="tpu_custom_call" | custom-call | tf_op jit(solution)/shard_map/finish/pallas_call | solution.py:143
  58.7 9.2 %all_to_all.12 = f32[32,1,128]{2,1,0:T(1,128)S(1)} all-to-all(f32[32,1,128]{2,1,0:T(1,128)S(1)} %bitcast.15), channel_id=1, replica_groups=mesh['pair'=4,'aux'=8] {'pair','aux'}, dimensions={0} | all-to-all | bytes 32768 | tf_op jit(solution)/shard_map/all_to_all | solution.py:190
  68.0 0.6 slice_reduce_fusion
  (2 shorter events, 0.0 us)
Async XLA Ops:
  0.6 41.7 %copy-start = (bf16[2,16,64,64]{3,2,1,0:T(8,128)(2,1)S(1)}, bf16[2,16,64,64]{3,2,1,0:T(8,128)(2,1)}, u32[]{:S(2)}) copy-start(bf16[2,16,64,64]{3,2,1,0:T(8,128)(2,1)} %occ_ref.1) | copy-start | bytes 786436
  0.6 1.1 %copy-start.2 = (bf16[32,6144]{1,0:T(8,128)(2,1)S(1)}, bf16[32,6144]{1,0:T(8,128)(2,1)}, u32[]{:S(2)}) copy-start(bf16[32,6144]{1,0:T(8,128)(2,1)} %x_ref.1) | copy-start | bytes 1179652
  1.7 0.7 copy-start.3
  3.6 14.2 %collective-permute-start.1 = (bf16[8,96,256]{2,1,0:T(8,128)(2,1)S(1)}, bf16[8,96,256]{2,1,0:T(8,128)(2,1)S(1)}, u32[]{:S(2)}, u32[]{:S(2)}) collective-permute-start(bf16[8,96,256]{2,1,0:T(8,128)(2,1)S(1)} %arrange.1.y_ref.mine_ref), channel_id=1, source_target_pairs={{0,2},{1,3},{2,4},{3,5},{4,6},{5,7},{6,0},{7,1},{8,10},{9,11},{10,... | collective-permute-start | bytes 1179656 | tf_op jit(solution)/shard_map/ppermute | solution.py:175
  17.8 12.1 %collective-permute-start.3 = (bf16[8,96,256]{2,1,0:T(8,128)(2,1)S(1)}, bf16[8,96,256]{2,1,0:T(8,128)(2,1)S(1)}, u32[]{:S(2)}, u32[]{:S(2)}) collective-permute-start(bf16[8,96,256]{2,1,0:T(8,128)(2,1)S(1)} %collective-permute-done.1.mine_ref), channel_id=1, source_target_pairs={{0,2},{1,3},{2,4},{3,5},{4,6},{5,7},{6,0},{7,1},{8,10},{9,11},{10,... | collective-permute-start | bytes 1179656 | tf_op jit(solution)/shard_map/ppermute | solution.py:175
  29.9 11.2 %collective-permute-start.5 = (bf16[8,96,256]{2,1,0:T(8,128)(2,1)S(1)}, bf16[8,96,256]{2,1,0:T(8,128)(2,1)S(1)}, u32[]{:S(2)}, u32[]{:S(2)}) collective-permute-start(bf16[8,96,256]{2,1,0:T(8,128)(2,1)S(1)} %collective-permute-done.3.mine_ref), channel_id=1, source_target_pairs={{0,2},{1,3},{2,4},{3,5},{4,6},{5,7},{6,0},{7,1},{8,10},{9,11},{10,... | collective-permute-start | bytes 1179656 | tf_op jit(solution)/shard_map/ppermute | solution.py:175
  29.9 14.9 %collective-permute-start = (bf16[8,96,256]{2,1,0:T(8,128)(2,1)S(1)}, bf16[8,96,256]{2,1,0:T(8,128)(2,1)}, u32[]{:S(2)}, u32[]{:S(2)}) collective-permute-start(bf16[8,96,256]{2,1,0:T(8,128)(2,1)S(1)} %arrange.1.y_ref.mine_ref), channel_id=1, source_target_pairs={{0,1},{1,0},{2,3},{3,2},{4,5},{5,4},{6,7},{7,6},{8,9},{9,8},{10,11... | collective-permute-start | bytes 1179656 | tf_op jit(solution)/shard_map/ppermute | solution.py:174
  29.9 16.3 %collective-permute-start.2 = (bf16[8,96,256]{2,1,0:T(8,128)(2,1)S(1)}, bf16[8,96,256]{2,1,0:T(8,128)(2,1)S(1)}, u32[]{:S(2)}, u32[]{:S(2)}) collective-permute-start(bf16[8,96,256]{2,1,0:T(8,128)(2,1)S(1)} %collective-permute-done.1.mine_ref), channel_id=1, source_target_pairs={{0,1},{1,0},{2,3},{3,2},{4,5},{5,4},{6,7},{7,6},{8,9},{9,8},{10,11... | collective-permute-start | bytes 1179656 | tf_op jit(solution)/shard_map/ppermute | solution.py:174
  30.4 16.2 %collective-permute-start.4 = (bf16[8,96,256]{2,1,0:T(8,128)(2,1)S(1)}, bf16[8,96,256]{2,1,0:T(8,128)(2,1)S(1)}, u32[]{:S(2)}, u32[]{:S(2)}) collective-permute-start(bf16[8,96,256]{2,1,0:T(8,128)(2,1)S(1)} %collective-permute-done.3.mine_ref), channel_id=1, source_target_pairs={{0,1},{1,0},{2,3},{3,2},{4,5},{5,4},{6,7},{7,6},{8,9},{9,8},{10,11... | collective-permute-start | bytes 1179656 | tf_op jit(solution)/shard_map/ppermute | solution.py:174
  41.1 6.0 %collective-permute-start.6 = (bf16[8,96,256]{2,1,0:T(8,128)(2,1)S(1)}, bf16[8,96,256]{2,1,0:T(8,128)(2,1)S(1)}, u32[]{:S(2)}, u32[]{:S(2)}) collective-permute-start(bf16[8,96,256]{2,1,0:T(8,128)(2,1)S(1)} %collective-permute-done.5.mine_ref), channel_id=1, source_target_pairs={{0,1},{1,0},{2,3},{3,2},{4,5},{5,4},{6,7},{7,6},{8,9},{9,8},{10,11... | collective-permute-start | bytes 1179656 | tf_op jit(solution)/shard_map/ppermute | solution.py:174
  41.1 0.7 copy-start.5
  42.4 1.0 %copy-start.1 = (bf16[2,16,64,64]{3,2,1,0:T(8,128)(2,1)S(1)}, bf16[2,16,64,64]{3,2,1,0:T(8,128)(2,1)}, u32[]{:S(2)}) copy-start(bf16[2,16,64,64]{3,2,1,0:T(8,128)(2,1)} %virt_ref.1) | copy-start | bytes 786436
  49.4 6.6 %collective-permute-start.7 = (bf16[192,192]{1,0:T(8,128)(2,1)S(1)}, bf16[192,192]{1,0:T(8,128)(2,1)S(1)}, u32[]{:S(2)}, u32[]{:S(2)}) collective-permute-start(bf16[192,192]{1,0:T(8,128)(2,1)S(1)} %get-tuple-element.8), channel_id=1, source_target_pairs={{0,8},{8,16},{16,24},{24,0},{1,9},{9,17},{17,25},{25,1},{2,10},{10... | collective-permute-start | bytes 221192 | tf_op jit(solution)/shard_map/ppermute | solution.py:187
  50.4 7.0 %collective-permute-start.8 = (bf16[192,192]{1,0:T(8,128)(2,1)S(1)}, bf16[192,192]{1,0:T(8,128)(2,1)S(1)}, u32[]{:S(2)}, u32[]{:S(2)}) collective-permute-start(bf16[192,192]{1,0:T(8,128)(2,1)S(1)} %get-tuple-element.7), channel_id=1, source_target_pairs={{0,16},{8,24},{16,0},{24,8},{1,17},{9,25},{17,1},{25,9},{2,18},{10... | collective-permute-start | bytes 221192 | tf_op jit(solution)/shard_map/ppermute | solution.py:187
  52.0 5.5 %copy-start.4 = (f32[2]{0:T(128)S(1)}, f32[2]{0:T(128)}, u32[]{:S(2)}) copy-start(f32[2]{0:T(128)} %weight_ref.1) | copy-start | bytes 28
  52.0 5.5 %collective-permute-start.9 = (bf16[192,192]{1,0:T(8,128)(2,1)S(1)}, bf16[192,192]{1,0:T(8,128)(2,1)S(1)}, u32[]{:S(2)}, u32[]{:S(2)}) collective-permute-start(bf16[192,192]{1,0:T(8,128)(2,1)S(1)} %get-tuple-element.6), channel_id=1, source_target_pairs={{0,24},{8,0},{16,8},{24,16},{1,25},{9,1},{17,9},{25,17},{2,26},{10... | collective-permute-start | bytes 221192 | tf_op jit(solution)/shard_map/ppermute | solution.py:187

commit v2 on v0

v2 whole, which is shorter than its diff:
```python
import functools
import jax
import jax.numpy as jnp
from jax import lax
from jax.experimental import pallas as pl
from jax.experimental.pallas import tpu as pltpu
from jax.sharding import PartitionSpec as P

BLK = 64
VMEM = pl.BlockSpec(memory_space=pltpu.VMEM)
SMEM = pl.BlockSpec(memory_space=pltpu.SMEM)
ANY = pl.BlockSpec(memory_space=pl.ANY)
NT_DIMS = (((1,), (1,)), ((), ()))


def call(kernel, name, flops, **settings):
    return pl.pallas_call(
        kernel,
        name=name,
        compiler_params=pltpu.CompilerParams(vmem_limit_bytes=40 * 1024 * 1024),
        cost_estimate=pl.CostEstimate(flops=flops, bytes_accessed=1 << 20, transcendentals=0),
        **settings,
    )


def chip_of():
    return lax.axis_index("aux") // 2


def early(chips, chip):
    return (chip < chips // 2).astype(jnp.int32)


def arrange_kernel(rows, aux, chips, second, x_ref, mask_ref, y_ref, x, wide, arrived):
    half = early(chips, chip_of())
    half = 1 - half if second else half
    start = pl.multiple_of(half * (rows // 2), rows // 2)
    copy = pltpu.make_async_copy(x_ref.at[pl.ds(start, rows // 2)], x, arrived)
    copy.start()
    block = lax.axis_index("pair") * rows // BLK
    low = lax.broadcasted_iota(jnp.int32, (8, 128), 1) < BLK
    copy.wait()
    for i in range(aux // 2):
        tile = x[:, i * 128:(i + 1) * 128].astype(jnp.float32)
        first, last = tile[:8], tile[8:]
        even = jnp.where(low, first, pltpu.roll(last, BLK, 1))
        odd = jnp.where(low, pltpu.roll(first, BLK, 1), last)
        even = jnp.where(mask_ref[block, 2 * i] > 0, even, 0.0)
        odd = jnp.where(mask_ref[block, 2 * i + 1] > 0, odd, 0.0)
        wide[pl.ds(2 * i, 8, stride=aux), :] = even
        wide[pl.ds(2 * i + 1, 8, stride=aux), :] = odd
    for s in range(8):
        lane = s % 2 * 128
        y_ref[s // 2, :, lane:lane + 128] = wide[s * aux:(s + 1) * aux, :].astype(y_ref.dtype)


def arrange(integrals, block_mask, chips, second):
    rows, width = integrals.shape
    aux = width // BLK
    return call(
        functools.partial(arrange_kernel, rows, aux, chips, second),
        "arrange",
        1 << 28,
        out_shape=jax.ShapeDtypeStruct((4, aux, 256), jnp.bfloat16),
        in_specs=[ANY, SMEM],
        out_specs=VMEM,
        scratch_shapes=[
            pltpu.VMEM((rows // 2, width), jnp.bfloat16),
            pltpu.VMEM((8 * aux, 128), jnp.float32),
            pltpu.SemaphoreType.DMA,
        ],
    )(integrals, block_mask)


def transform_kernel(nt, rows, atom_ref, occ_hbm, virt_hbm, y1, y2, o1, o2, z_ref, w_ref, occ_ref, virt_ref, arrived):
    steps, aux, wide = y1.shape
    copies = wide // BLK
    atom = atom_ref[lax.axis_index("pair") * rows // BLK]
    fetch = [
        pltpu.make_async_copy(occ_hbm.at[:, atom], occ_ref, arrived.at[0]),
        pltpu.make_async_copy(virt_hbm.at[:, atom], virt_ref, arrived.at[1]),
    ]
    for copy in fetch:
        copy.start()
    for copy in fetch:
        copy.wait()
    core = lax.rem(lax.axis_index("aux"), 2)
    same = (
        lax.broadcasted_iota(jnp.int32, (wide, wide), 0) // BLK
        == lax.broadcasted_iota(jnp.int32, (wide, wide), 1) // BLK
    )

    def diagonal(block):
        tall = jnp.concatenate([block.astype(jnp.float32)] * copies, axis=0)
        full = jnp.concatenate([tall] * copies, axis=1)
        return jnp.where(same, full, 0.0).astype(jnp.bfloat16)

    def through(y, first, second):
        half = jnp.dot(y, first, preferred_element_type=jnp.float32).astype(jnp.bfloat16)
        return lax.dot_general(half, second, NT_DIMS, preferred_element_type=jnp.float32).astype(jnp.bfloat16)

    for t in range(nt):
        occ, virt = diagonal(occ_ref[t]), diagonal(virt_ref[t])
        for half, (mine, other) in enumerate(((y1, o1), (y2, o2))):
            mine = mine[...].reshape(steps * aux, wide)
            other = other[...].reshape(steps * aux, wide)
            z = through(mine, occ, virt).reshape(steps, aux, wide)
            z_ref[half, :, t * aux:(t + 1) * aux, :] = z
            own = through(mine, virt, occ).reshape(steps, aux, wide)
            w_ref[half, t, :, pl.ds(pl.multiple_of(core * aux, aux), aux), :] = own
            sib = through(other, virt, occ).reshape(steps, aux, wide)
            w_ref[half, t, :, pl.ds(pl.multiple_of((1 - core) * aux, aux), aux), :] = sib


def transform(atom, green_occ, green_virt, rows, mine, other):
    nt = green_occ.shape[0]
    steps, aux, wide = mine[0].shape
    return call(
        functools.partial(transform_kernel, nt, rows),
        "transform",
        3 << 30,
        out_shape=(
            jax.ShapeDtypeStruct((2, steps, nt * aux, wide), jnp.bfloat16),
            jax.ShapeDtypeStruct((2, nt, steps, 2 * aux, wide), jnp.bfloat16),
        ),
        in_specs=[SMEM, ANY, ANY] + [VMEM] * 4,
        out_specs=(VMEM, VMEM),
        scratch_shapes=[
            pltpu.VMEM((nt, BLK, BLK), jnp.bfloat16),
            pltpu.VMEM((nt, BLK, BLK), jnp.bfloat16),
            pltpu.SemaphoreType.DMA((2,)),
        ],
    )(atom, green_occ, green_virt, *mine, *other)


def matching(chips, step, piece):
    chip = chip_of()
    source = lax.rem(chip + chips - step, chips)
    swap = early(chips, chip) != early(chips, source)
    return jnp.where(swap, 1 - piece, piece)


def near_kernel(chips, step, count, z_ref, *refs):
    mine, other, out_ref = refs[:count], refs[count:2 * count], refs[2 * count]
    halves = [matching(chips, step, piece) for piece in range(count)]

    def products(low, high):
        total = jnp.zeros(out_ref.shape, jnp.float32)
        for half, first, second in zip(halves, low, high):
            for j in range(z_ref.shape[1]):
                partner = jnp.concatenate([first[j], second[j]], axis=0)
                total += lax.dot_general(z_ref[half, j], partner, NT_DIMS, preferred_element_type=jnp.float32)
        out_ref[...] = total

    core = lax.rem(lax.axis_index("aux"), 2)
    pl.when(core == 0)(lambda: products(mine, other))
    pl.when(core == 1)(lambda: products(other, mine))


def near(z, chips, step, mine, other):
    size = z.shape[2]
    return call(
        functools.partial(near_kernel, chips, step, len(mine)),
        "near",
        1 << 30,
        out_shape=jax.ShapeDtypeStruct((size, 2 * mine[0].shape[1]), jnp.float32),
        in_specs=[VMEM] * (1 + 2 * len(mine)),
        out_specs=VMEM,
    )(z, *mine, *other)


def far_kernel(chips, step, count, w_ref, *refs):
    mine, out_ref = refs[:count], refs[count]
    nt, steps = w_ref.shape[1:3]
    aux = mine[0].shape[1]
    halves = [matching(chips, step, piece) for piece in range(count)]
    for t in range(nt):
        total = jnp.zeros((aux, out_ref.shape[1]), jnp.float32)
        for half, piece in zip(halves, mine):
            for j in range(steps):
                total += lax.dot_general(piece[j], w_ref[half, t, j], NT_DIMS, preferred_element_type=jnp.float32)
        out_ref[t * aux:(t + 1) * aux, :] = total.astype(out_ref.dtype)


def far(w, chips, step, mine):
    aux = mine[0].shape[1]
    return call(
        functools.partial(far_kernel, chips, step, len(mine)),
        "far",
        1 << 30,
        out_shape=jax.ShapeDtypeStruct((w.shape[1] * aux, w.shape[3]), jnp.bfloat16),
        in_specs=[VMEM] * (1 + len(mine)),
        out_specs=VMEM,
    )(w, *mine)


def pack_kernel(chips, *refs):
    backs, aheads, out_ref = refs[:chips // 2 + 1], refs[chips // 2 + 1:chips + 1], refs[chips + 1]
    chip = chip_of()
    for step in range(chips // 2):
        out_ref[lax.rem(chip + chips - step, chips)] = backs[step][...].astype(out_ref.dtype)
    for step in range(1, chips // 2):
        out_ref[lax.rem(chip + step, chips)] = aheads[step - 1][...]
    opposite = backs[-1][...] + aheads[-1][...].astype(jnp.float32)
    out_ref[lax.rem(chip + chips // 2, chips)] = opposite.astype(out_ref.dtype)


def pack(chips, backs, aheads):
    return call(
        functools.partial(pack_kernel, chips),
        "pack",
        1 << 28,
        out_shape=jax.ShapeDtypeStruct((chips,) + backs[0].shape, jnp.bfloat16),
        in_specs=[VMEM] * (chips + 1),
        out_specs=VMEM,
    )(*backs, *aheads)


def finish_kernel(scale, nt, weight_ref, part_ref, chi_ref, sum_ref):
    aux = chi_ref.shape[1]
    total = part_ref[0].astype(jnp.float32)
    for p in range(1, part_ref.shape[0]):
        total += part_ref[p].astype(jnp.float32)
    total *= scale
    local = jnp.zeros((1, 1), jnp.float32)
    for t in range(nt):
        chi = total[t * aux:(t + 1) * aux]
        chi_ref[t] = chi
        local += weight_ref[t] * jnp.sum(chi * chi, keepdims=True)
    sum_ref[...] = jnp.broadcast_to(local, sum_ref.shape)


def finish(scale, time_weights, parts, copies):
    nt = time_weights.shape[0]
    _, height, width = parts.shape
    return call(
        functools.partial(finish_kernel, scale, nt),
        "finish",
        1 << 28,
        out_shape=(
            jax.ShapeDtypeStruct((nt, height // nt, width), jnp.float32),
            jax.ShapeDtypeStruct((copies, 128), jnp.float32),
        ),
        in_specs=[SMEM, VMEM],
        out_specs=(VMEM, VMEM),
    )(time_weights, parts)


def per_device(integrals, block_mask, block_atom, green_occ, green_virt, time_weights):
    rows = integrals.shape[0]
    aux_here = integrals.shape[1] // BLK
    pairs, auxes = lax.axis_size("pair"), lax.axis_size("aux")
    chips = auxes // 2
    aux_total = aux_here * auxes
    columns = aux_total // pairs
    nt = green_occ.shape[0]

    def along(shift):
        return [(i, (i + 2 * shift) % auxes) for i in range(auxes)]

    def to_sibling(arrays):
        pairing = [(i, i ^ 1) for i in range(auxes)]
        return [lax.ppermute(a, "aux", pairing) for a in arrays]

    own = [arrange(integrals, block_mask, chips, second) for second in (False, True)]
    held = [own]
    for step in range(1, chips // 2 + 1):
        sent = held[-1] if step < chips // 2 else held[-1][:1]
        held.append([lax.ppermute(a, "aux", along(1)) for a in sent])
    others = [to_sibling(pieces) for pieces in held]
    z, w = transform(block_atom, green_occ, green_virt, rows, own, others[0])
    aheads = []
    for step in range(1, chips // 2 + 1):
        share = far(w, chips, step, held[step])
        aheads.append(lax.ppermute(share, "aux", along(-step)))
    backs = [near(z, chips, step, held[step], others[step]) for step in range(chips // 2 + 1)]
    parts = pack(chips, backs, aheads)
    if columns != 2 * aux_here:
        parts = parts.transpose(1, 0, 2).reshape(nt * aux_here, pairs, columns).transpose(1, 0, 2)
    parts = lax.all_to_all(parts, "pair", 0, 0)
    scale = float((rows * pairs * BLK) ** -0.5)
    chi, sums = finish(scale, time_weights, parts, auxes)
    level = jnp.sum(lax.all_to_all(sums, "aux", 0, 0, tiled=True), axis=0, keepdims=True)
    level = lax.all_to_all(jnp.broadcast_to(level, (pairs, 128)), "pair", 0, 0, tiled=True)
    energy = -jnp.sum(level[:, 0]) / jnp.float32(aux_total * aux_total)
    return chi, energy


def solution(mesh):
    placed = (P("pair", "aux"), P(None, "aux"), P(), P(), P(), P())
    return jax.shard_map(
        per_device,
        mesh=mesh,
        in_specs=placed,
        out_specs=(P(None, "aux", "pair"), P()),
        check_vma=False,
    )
```

time: 147 us -> 61.3 us (0.42)
  waiting for transfers between devices: 58.8 us -> 13.5 us
  local copies, waits for them, and re-layouts: 19.5 us -> 1.78 us
  between operations: 16 us -> 2.58 us
  blocking collectives: 39.5 us -> 26.7 us
  matrix products: 9.13 us -> 0 us
  Pallas kernels: 0 us -> 8.07 us
  starting transfers between devices: 0.08 us -> 7.79 us
  other arithmetic: 3.84 us -> 0.63 us
    psum x1 -> x0, blocking collectives: 39.5 us -> none  [per_device(): summed = lax.psum(local_sum, ('pair', 'aux'))]
    all_gather x1 -> x0, waiting for transfers between devices: 33.7 us -> none  [per_device(): piece = lax.all_gather(masked_flat, 'aux', axis=1, tiled=True)]
    all_to_all x0 -> x3, blocking collectives: none -> 26.7 us  [the longest x1 10.7 us: per_device(): parts = lax.all_to_all(parts, 'pair', 0, 0)]
    unnamed x3 -> x0, waiting for transfers between devices: 25.1 us -> none
    ppermute x0 -> x10, waiting for transfers between devices: none -> 13.5 us  [the longest x3 7.98 us: per_device(): held.append([lax.ppermute(a, 'aux', along(1)) for a in sent])]
    reshape x2 -> x0, local copies, waits for them, and re-layouts: 11.1 us -> none  [the longest x1 8.45 us: per_device(): partner = piece.reshape(rows, count, BLK)]
    dot_general x2 -> x0, matrix products: 9.13 us -> none  [the longest x1 5.92 us: per_device(): jnp.einsum('trpl,trql->tpq', occ_half, partner_half, preferred_element_ty...]
    pallas_call x0 -> x10, Pallas kernels: none -> 8.07 us  [the longest x2 2.44 us: arrange(): call(functools.partial(arrange_kernel, rows, aux, chips, second), 'arrang...]
  transfers between devices with their start and end apart: 2 -> 10, of which waited for: 2 -> 5; matrix products, arithmetic and copies ran while one was open for 5% -> 0% of each run, Pallas kernels for 0% -> 9%
where the time goes in v2:
time: 61.3 us; the launch traced here: 61 us
  blocking collectives  26.7 us (44%)
  waiting for transfers between devices  13.5 us (22%)
  Pallas kernels  8.07 us (13%)
  starting transfers between devices  7.79 us (13%)
  between operations  2.58 us (4%)
  local copies, waits for them, and re-layouts  1.78 us (3%)
  other arithmetic  0.63 us (1%)
    all_to_all x1, blocking collectives, per_device(): parts = lax.all_to_all(parts, 'pair', 0, 0)  10.7 us
    all_to_all x1, blocking collectives, per_device(): lax.all_to_all(sums, 'aux', 0, 0, tiled=True)  9.07 us
    ppermute x3, waiting for transfers between devices, per_device(): held.append([lax.ppermute(a, 'aux', along(1)) for a in sent])  7.98 us
    all_to_all x1, blocking collectives, per_device(): lax.all_to_all(jnp.broadcast_to(level, (pairs, 128)), 'pair', 0, 0, tiled...  6.98 us
    ppermute x2, waiting for transfers between devices, per_device(): aheads.append(lax.ppermute(share, 'aux', along(-step)))  4.97 us
    ppermute x3, starting transfers between devices, per_device(): held.append([lax.ppermute(a, 'aux', along(1)) for a in sent])  4.22 us
    pallas_call x2, Pallas kernels, arrange(): call(functools.partial(arrange_kernel, rows, aux, chips, second), 'arrang...  2.44 us
    ppermute x2, starting transfers between devices, per_device(): aheads.append(lax.ppermute(share, 'aux', along(-step)))  2.31 us
  transfers between devices with their start and end apart: 10, of which 5 were waited for; matrix products, arithmetic and copies ran while one was open for 0% of the time, Pallas kernels for 9%

profile of v2, /device:TPU:0, one launch (start us, length us, event | category | flops | bytes accessed | tf_op | source)
XLA Modules:
  0.0 61.0 jit_solution(1614823119939102127)
XLA Ops:
  0.6 0.0 copy-start
  0.6 0.0 copy-start.1
  0.7 0.0 copy-start.2
  0.7 1.1 %copy-done.2 = bf16[32,6144]{1,0:T(8,128)(2,1)S(1)} copy-done((bf16[32,6144]{1,0:T(8,128)(2,1)S(1)}, bf16[32,6144]{1,0:T(8,128)(2,1)}, u32[]{:S(2)}) %copy-start.2) | copy-done | bytes 393240
  1.7 0.0 copy-start.3
  1.7 0.7 %copy-done.3 = s32[2,96]{1,0:T(2,128)S(1)} copy-done((s32[2,96]{1,0:T(2,128)S(1)}, s32[2,96]{1,0:T(2,128)}, u32[]{:S(2)}) %copy-start.3) | copy-done | bytes 792
  2.4 0.0 copy-start.4
  2.4 1.2 %arrange.2.y1.refs_0_ = bf16[4,96,256]{2,1,0:T(8,128)(2,1)S(1)} custom-call(bf16[32,6144]{1,0:T(8,128)(2,1)S(1)} %copy-done.2, s32[2,96]{1,0:T(2,128)S(1)} %copy-done.3), custom_call_target="tpu_custom_call" | custom-call | flops 268435456 | bytes 1048576 | tf_op jit(solution)/shard_map/arrange/pallas_call | solution.py:60
  3.6 0.5 collective-permute-start
  4.2 2.6 %collective-permute-start.2 = (bf16[4,96,256]{2,1,0:T(8,128)(2,1)S(1)}, bf16[4,96,256]{2,1,0:T(8,128)(2,1)S(1)}, u32[]{:S(2)}, u32[]{:S(2)}) collective-permute-start(bf16[4,96,256]{2,1,0:T(8,128)(2,1)S(1)} %arrange.2.y1.refs_0_), channel_id=1, source_target_pairs={{0,2},{1,3},{2,4},{3,5},{4,6},{5,7},{6,0},{7,1},{8,10},{9,11},{10,... | collective-permute-start | bytes 589832 | tf_op jit(solution)/shard_map/ppermute | solution.py:269
  6.8 1.2 %arrange.3.y2.refs_1_ = bf16[4,96,256]{2,1,0:T(8,128)(2,1)S(1)} custom-call(bf16[32,6144]{1,0:T(8,128)(2,1)S(1)} %copy-done.2, s32[2,96]{1,0:T(2,128)S(1)} %copy-done.3), custom_call_target="tpu_custom_call" | custom-call | flops 268435456 | bytes 1048576 | tf_op jit(solution)/shard_map/arrange/pallas_call | solution.py:60
  8.0 0.2 collective-permute-start.1
  8.3 1.6 %collective-permute-start.3 = (bf16[4,96,256]{2,1,0:T(8,128)(2,1)S(1)}, bf16[4,96,256]{2,1,0:T(8,128)(2,1)S(1)}, u32[]{:S(2)}, u32[]{:S(2)}) collective-permute-start(bf16[4,96,256]{2,1,0:T(8,128)(2,1)S(1)} %arrange.3.y2.refs_1_), channel_id=1, source_target_pairs={{0,2},{1,3},{2,4},{3,5},{4,6},{5,7},{6,0},{7,1},{8,10},{9,11},{10,... | collective-permute-start | bytes 589832 | tf_op jit(solution)/shard_map/ppermute | solution.py:269
  9.8 4.7 %collective-permute-done.2.refs_0_ = bf16[4,96,256]{2,1,0:T(8,128)(2,1)S(1)} collective-permute-done((bf16[4,96,256]{2,1,0:T(8,128)(2,1)S(1)}, bf16[4,96,256]{2,1,0:T(8,128)(2,1)S(1)}, u32[]{:S(2)}, u32[]{:S(2)}) %collective-permute-start.2) | collective-permute-done | bytes 196640 | tf_op jit(solution)/shard_map/ppermute | solution.py:269
  14.6 0.0 collective-permute-start.6
  14.6 0.0 collective-permute-done.o1.refs_2_
  14.6 0.0 collective-permute-done.1.o2.refs_3_
  14.6 0.0 copy-done
  14.6 0.0 copy-done.1
  14.6 0.0 copy-done.4
  14.6 2.2 %transform.1 = (bf16[2,4,192,256]{3,2,1,0:T(8,128)(2,1)S(1)}, bf16[2,2,4,192,256]{4,3,2,1,0:T(8,128)(2,1)S(1)}) custom-call(s32[2]{0:T(128)S(1)} %copy-done.4, bf16[2,16,64,64]{3,2,1,0:T(8,128)(2,1)S(1)} %copy-done, bf16[2,16,64,64]{3,2,1,0:T(8,128)(2,1)S(1)} %copy-done.1, bf16[4,96,256]{2,1,0:T(8,128)(2,1)S(1)} %arrange.2.y1.refs_0_, ...), custom_call_target="tpu_custom_call" | custom-call | flops 3221225472 | bytes 1048576 | tf_op jit(solution)/shard_map/transform/pallas_call | solution.py:118
  16.8 1.7 %collective-permute-done.3.refs_1_ = bf16[4,96,256]{2,1,0:T(8,128)(2,1)S(1)} collective-permute-done((bf16[4,96,256]{2,1,0:T(8,128)(2,1)S(1)}, bf16[4,96,256]{2,1,0:T(8,128)(2,1)S(1)}, u32[]{:S(2)}, u32[]{:S(2)}) %collective-permute-start.3) | collective-permute-done | bytes 196640 | tf_op jit(solution)/shard_map/ppermute | solution.py:269
  18.5 0.6 %far.2 = bf16[192,192]{1,0:T(8,128)(2,1)S(1)} custom-call(bf16[2,2,4,192,256]{4,3,2,1,0:T(8,128)(2,1)S(1)} %get-tuple-element.7.w_ref, bf16[4,96,256]{2,1,0:T(8,128)(2,1)S(1)} %collective-permute-done.2.refs_0_, bf16[4,96,256]{2,1,0:T(8,128)(2,1)S(1)} %collective-permute-done.3.refs_1_), custom_call_target="tpu_custom_call" | custom-call | flops 1073741824 | bytes 1048576 | tf_op jit(solution)/shard_map/far/pallas_call | solution.py:187
  19.2 2.2 %collective-permute-start.8 = (bf16[192,192]{1,0:T(8,128)(2,1)S(1)}, bf16[192,192]{1,0:T(8,128)(2,1)S(1)}, u32[]{:S(2)}, u32[]{:S(2)}) collective-permute-start(bf16[192,192]{1,0:T(8,128)(2,1)S(1)} %far.2), channel_id=1, source_target_pairs={{0,6},{1,7},{2,0},{3,1},{4,2},{5,3},{6,4},{7,5},{8,14},{9,15},{10,... | collective-permute-start | bytes 221192 | tf_op jit(solution)/shard_map/ppermute | solution.py:275
  21.4 0.0 collective-permute-start.4
  21.4 0.5 collective-permute-start.5
  21.9 0.4 near.3.refs_0_
  22.3 1.5 %collective-permute-done.6.refs_0_ = bf16[4,96,256]{2,1,0:T(8,128)(2,1)S(1)} collective-permute-done((bf16[4,96,256]{2,1,0:T(8,128)(2,1)S(1)}, bf16[4,96,256]{2,1,0:T(8,128)(2,1)S(1)}, u32[]{:S(2)}, u32[]{:S(2)}) %collective-permute-start.6) | collective-permute-done | bytes 196640 | tf_op jit(solution)/shard_map/ppermute | solution.py:269
  23.9 0.0 collective-permute-start.7
  23.9 0.4 far.3
  24.2 0.1 collective-permute-start.9
  24.3 0.0 collective-permute-done.4.refs_2_
  24.3 0.0 collective-permute-done.5.refs_3_
  24.3 0.4 near.4.refs_1_
  24.8 0.5 collective-permute-done.7.refs_1_
  25.3 0.3 near.5.refs_2_
  25.6 0.0 copy-start.5
  25.6 0.0 collective-permute-done.8.refs_3_
  25.6 5.0 %collective-permute-done.9.refs_4_ = bf16[192,192]{1,0:T(8,128)(2,1)S(1)} collective-permute-done((bf16[192,192]{1,0:T(8,128)(2,1)S(1)}, bf16[192,192]{1,0:T(8,128)(2,1)S(1)}, u32[]{:S(2)}, u32[]{:S(2)}) %collective-permute-start.9) | collective-permute-done | bytes 73760 | tf_op jit(solution)/shard_map/ppermute | solution.py:275
  30.6 0.1 pack.1
  30.6 10.7 %all_to_all.23.part_ref = bf16[4,192,192]{2,1,0:T(8,128)(2,1)S(1)} all-to-all(bf16[4,192,192]{2,1,0:T(8,128)(2,1)S(1)} %pack.1), channel_id=1, replica_groups=mesh['pair'=4,'aux'=8] {'pair'}, dimensions={0} | all-to-all | bytes 589824 | tf_op jit(solution)/shard_map/all_to_all | solution.py:280
  41.3 0.0 copy-done.5
  41.3 1.3 %finish.1 = (f32[2,96,192]{2,1,0:T(8,128)}, f32[8,128]{1,0:T(8,128)S(1)}) custom-call(f32[2]{0:T(128)S(1)} %copy-done.5, bf16[4,192,192]{2,1,0:T(8,128)(2,1)S(1)} %all_to_all.23.part_ref), custom_call_target="tpu_custom_call" | custom-call | flops 268435456 | bytes 1048576 | tf_op jit(solution)/shard_map/finish/pallas_call | solution.py:236
  42.6 9.1 %all_to_all.24 = f32[8,1,128]{2,1,0:T(1,128)S(1)} all-to-all(f32[8,1,128]{2,1,0:T(1,128)S(1)} %bitcast.4), channel_id=1, replica_groups=mesh['pair'=4,'aux'=8] {'aux'}, dimensions={0} | all-to-all | bytes 8192 | tf_op jit(solution)/shard_map/all_to_all | solution.py:283
  51.7 7.0 %all_to_all.25 = f32[4,1,128]{2,1,0:T(1,128)S(1)} all-to-all(f32[4,1,128]{2,1,0:T(1,128)S(1)} %broadcast_in_dim.2), channel_id=1, replica_groups=mesh['pair'=4,'aux'=8] {'pair'}, dimensions={0} | all-to-all | bytes 4096 | tf_op jit(solution)/shard_map/all_to_all | solution.py:284
  58.7 0.6 slice_reduce_fusion
  (2 shorter events, 0.0 us)
Async XLA Ops:
  0.6 14.0 %copy-start = (bf16[2,16,64,64]{3,2,1,0:T(8,128)(2,1)S(1)}, bf16[2,16,64,64]{3,2,1,0:T(8,128)(2,1)}, u32[]{:S(2)}) copy-start(bf16[2,16,64,64]{3,2,1,0:T(8,128)(2,1)} %occ_hbm.1) | copy-start | bytes 786436
  0.6 14.0 %copy-start.1 = (bf16[2,16,64,64]{3,2,1,0:T(8,128)(2,1)S(1)}, bf16[2,16,64,64]{3,2,1,0:T(8,128)(2,1)}, u32[]{:S(2)}) copy-start(bf16[2,16,64,64]{3,2,1,0:T(8,128)(2,1)} %virt_hbm.1) | copy-start | bytes 786436
  0.7 1.1 %copy-start.2 = (bf16[32,6144]{1,0:T(8,128)(2,1)S(1)}, bf16[32,6144]{1,0:T(8,128)(2,1)}, u32[]{:S(2)}) copy-start(bf16[32,6144]{1,0:T(8,128)(2,1)} %x_ref.3) | copy-start | bytes 1179652
  1.7 0.7 %copy-start.3 = (s32[2,96]{1,0:T(2,128)S(1)}, s32[2,96]{1,0:T(2,128)}, u32[]{:S(2)}) copy-start(s32[2,96]{1,0:T(2,128)} %mask_ref.3) | copy-start | bytes 2308
  2.4 12.2 %copy-start.4 = (s32[2]{0:T(128)S(1)}, s32[2]{0:T(128)}, u32[]{:S(2)}) copy-start(s32[2]{0:T(128)} %atom_ref.1) | copy-start | bytes 28
  3.6 10.9 %collective-permute-start = (bf16[4,96,256]{2,1,0:T(8,128)(2,1)S(1)}, bf16[4,96,256]{2,1,0:T(8,128)(2,1)S(1)}, u32[]{:S(2)}, u32[]{:S(2)}) collective-permute-start(bf16[4,96,256]{2,1,0:T(8,128)(2,1)S(1)} %arrange.2.y1.refs_0_), channel_id=1, source_target_pairs={{0,1},{1,0},{2,3},{3,2},{4,5},{5,4},{6,7},{7,6},{8,9},{9,8},{10,11... | collective-permute-start | bytes 589832 | tf_op jit(solution)/shard_map/ppermute | solution.py:263
  4.2 10.4 %collective-permute-start.2 = (bf16[4,96,256]{2,1,0:T(8,128)(2,1)S(1)}, bf16[4,96,256]{2,1,0:T(8,128)(2,1)S(1)}, u32[]{:S(2)}, u32[]{:S(2)}) collective-permute-start(bf16[4,96,256]{2,1,0:T(8,128)(2,1)S(1)} %arrange.2.y1.refs_0_), channel_id=1, source_target_pairs={{0,2},{1,3},{2,4},{3,5},{4,6},{5,7},{6,0},{7,1},{8,10},{9,11},{10,... | collective-permute-start | bytes 589832 | tf_op jit(solution)/shard_map/ppermute | solution.py:269
  8.0 6.6 %collective-permute-start.1 = (bf16[4,96,256]{2,1,0:T(8,128)(2,1)S(1)}, bf16[4,96,256]{2,1,0:T(8,128)(2,1)S(1)}, u32[]{:S(2)}, u32[]{:S(2)}) collective-permute-start(bf16[4,96,256]{2,1,0:T(8,128)(2,1)S(1)} %arrange.3.y2.refs_1_), channel_id=1, source_target_pairs={{0,1},{1,0},{2,3},{3,2},{4,5},{5,4},{6,7},{7,6},{8,9},{9,8},{10,11... | collective-permute-start | bytes 589832 | tf_op jit(solution)/shard_map/ppermute | solution.py:263
  8.3 10.3 %collective-permute-start.3 = (bf16[4,96,256]{2,1,0:T(8,128)(2,1)S(1)}, bf16[4,96,256]{2,1,0:T(8,128)(2,1)S(1)}, u32[]{:S(2)}, u32[]{:S(2)}) collective-permute-start(bf16[4,96,256]{2,1,0:T(8,128)(2,1)S(1)} %arrange.3.y2.refs_1_), channel_id=1, source_target_pairs={{0,2},{1,3},{2,4},{3,5},{4,6},{5,7},{6,0},{7,1},{8,10},{9,11},{10,... | collective-permute-start | bytes 589832 | tf_op jit(solution)/shard_map/ppermute | solution.py:269
  14.6 9.3 %collective-permute-start.6 = (bf16[4,96,256]{2,1,0:T(8,128)(2,1)S(1)}, bf16[4,96,256]{2,1,0:T(8,128)(2,1)S(1)}, u32[]{:S(2)}, u32[]{:S(2)}) collective-permute-start(bf16[4,96,256]{2,1,0:T(8,128)(2,1)S(1)} %collective-permute-done.2.refs_0_), channel_id=1, source_target_pairs={{0,2},{1,3},{2,4},{3,5},{4,6},{5,7},{6,0},{7,1},{8,10},{9,11},{10,... | collective-permute-start | bytes 589832 | tf_op jit(solution)/shard_map/ppermute | solution.py:269
  19.2 6.4 %collective-permute-start.8 = (bf16[192,192]{1,0:T(8,128)(2,1)S(1)}, bf16[192,192]{1,0:T(8,128)(2,1)S(1)}, u32[]{:S(2)}, u32[]{:S(2)}) collective-permute-start(bf16[192,192]{1,0:T(8,128)(2,1)S(1)} %far.2), channel_id=1, source_target_pairs={{0,6},{1,7},{2,0},{3,1},{4,2},{5,3},{6,4},{7,5},{8,14},{9,15},{10,... | collective-permute-start | bytes 221192 | tf_op jit(solution)/shard_map/ppermute | solution.py:275
  21.4 2.9 %collective-permute-start.4 = (bf16[4,96,256]{2,1,0:T(8,128)(2,1)S(1)}, bf16[4,96,256]{2,1,0:T(8,128)(2,1)S(1)}, u32[]{:S(2)}, u32[]{:S(2)}) collective-permute-start(bf16[4,96,256]{2,1,0:T(8,128)(2,1)S(1)} %collective-permute-done.2.refs_0_), channel_id=1, source_target_pairs={{0,1},{1,0},{2,3},{3,2},{4,5},{5,4},{6,7},{7,6},{8,9},{9,8},{10,11... | collective-permute-start | bytes 589832 | tf_op jit(solution)/shard_map/ppermute | solution.py:263
  21.4 2.9 %collective-permute-start.5 = (bf16[4,96,256]{2,1,0:T(8,128)(2,1)S(1)}, bf16[4,96,256]{2,1,0:T(8,128)(2,1)S(1)}, u32[]{:S(2)}, u32[]{:S(2)}) collective-permute-start(bf16[4,96,256]{2,1,0:T(8,128)(2,1)S(1)} %collective-permute-done.3.refs_1_), channel_id=1, source_target_pairs={{0,1},{1,0},{2,3},{3,2},{4,5},{5,4},{6,7},{7,6},{8,9},{9,8},{10,11... | collective-permute-start | bytes 589832 | tf_op jit(solution)/shard_map/ppermute | solution.py:263
  23.9 1.4 %collective-permute-start.7 = (bf16[4,96,256]{2,1,0:T(8,128)(2,1)S(1)}, bf16[4,96,256]{2,1,0:T(8,128)(2,1)S(1)}, u32[]{:S(2)}, u32[]{:S(2)}) collective-permute-start(bf16[4,96,256]{2,1,0:T(8,128)(2,1)S(1)} %collective-permute-done.6.refs_0_), channel_id=1, source_target_pairs={{0,1},{1,0},{2,3},{3,2},{4,5},{5,4},{6,7},{7,6},{8,9},{9,8},{10,11... | collective-permute-start | bytes 589832 | tf_op jit(solution)/shard_map/ppermute | solution.py:263
  24.2 6.3 %collective-permute-start.9 = (bf16[192,192]{1,0:T(8,128)(2,1)S(1)}, bf16[192,192]{1,0:T(8,128)(2,1)S(1)}, u32[]{:S(2)}, u32[]{:S(2)}) collective-permute-start(bf16[192,192]{1,0:T(8,128)(2,1)S(1)} %far.3), channel_id=1, source_target_pairs={{0,4},{1,5},{2,6},{3,7},{4,0},{5,1},{6,2},{7,3},{8,12},{9,13},{10,... | collective-permute-start | bytes 221192 | tf_op jit(solution)/shard_map/ppermute | solution.py:275
  25.6 15.7 %copy-start.5 = (f32[2]{0:T(128)S(1)}, f32[2]{0:T(128)}, u32[]{:S(2)}) copy-start(f32[2]{0:T(128)} %weight_ref.1) | copy-start | bytes 28

commit v3 on v2

v3 whole, which is shorter than its diff:
```python
import functools
import jax
import jax.numpy as jnp
from jax import lax
from jax.experimental import pallas as pl
from jax.experimental.pallas import tpu as pltpu
from jax.sharding import PartitionSpec as P

BLK = 64
VMEM = pl.BlockSpec(memory_space=pltpu.VMEM)
SMEM = pl.BlockSpec(memory_space=pltpu.SMEM)
HBM = pl.BlockSpec(memory_space=pltpu.HBM)
NT_DIMS = (((1,), (1,)), ((), ()))


def call(kernel, name, flops, **settings):
    return pl.pallas_call(
        kernel,
        name=name,
        compiler_params=pltpu.CompilerParams(vmem_limit_bytes=40 * 1024 * 1024),
        cost_estimate=pl.CostEstimate(flops=flops // 16, bytes_accessed=1 << 10, transcendentals=0),
        **settings,
    )


def stay(array):
    return pltpu.with_memory_space_constraint(array, pltpu.HBM)


def chip_of():
    return lax.axis_index("aux") // 2


def early(chips, chip):
    return (chip < chips // 2).astype(jnp.int32)


def arrange_kernel(rows, aux, chips, second, x_hbm, mask_hbm, y_ref, x, mask, wide, arrived):
    half = early(chips, chip_of())
    half = 1 - half if second else half
    start = pl.multiple_of(half * (rows // 2), rows // 2)
    copies = [
        pltpu.make_async_copy(x_hbm.at[pl.ds(start, rows // 2)], x, arrived.at[0]),
        pltpu.make_async_copy(mask_hbm, mask, arrived.at[1]),
    ]
    for copy in copies:
        copy.start()
    block = lax.axis_index("pair") * rows // BLK
    low = lax.broadcasted_iota(jnp.int32, (8, 128), 1) < BLK
    for copy in copies:
        copy.wait()
    for i in range(aux // 2):
        tile = x[:, i * 128:(i + 1) * 128].astype(jnp.float32)
        first, last = tile[:8], tile[8:]
        even = jnp.where(low, first, pltpu.roll(last, BLK, 1))
        odd = jnp.where(low, pltpu.roll(first, BLK, 1), last)
        even = jnp.where(mask[block, 2 * i] > 0, even, 0.0)
        odd = jnp.where(mask[block, 2 * i + 1] > 0, odd, 0.0)
        wide[pl.ds(2 * i, 8, stride=aux), :] = even
        wide[pl.ds(2 * i + 1, 8, stride=aux), :] = odd
    for s in range(8):
        lane = s % 2 * 128
        y_ref[s // 2, :, lane:lane + 128] = wide[s * aux:(s + 1) * aux, :].astype(y_ref.dtype)


def arrange(integrals, block_mask, chips, second):
    rows, width = integrals.shape
    aux = width // BLK
    return call(
        functools.partial(arrange_kernel, rows, aux, chips, second),
        "arrange",
        1 << 28,
        out_shape=jax.ShapeDtypeStruct((4, aux, 256), jnp.bfloat16),
        in_specs=[HBM, HBM],
        out_specs=VMEM,
        scratch_shapes=[
            pltpu.VMEM((rows // 2, width), jnp.bfloat16),
            pltpu.SMEM(block_mask.shape, jnp.int32),
            pltpu.VMEM((8 * aux, 128), jnp.float32),
            pltpu.SemaphoreType.DMA((2,)),
        ],
    )(stay(integrals), stay(block_mask))


def transform_kernel(nt, rows, own, atom_hbm, occ_hbm, virt_hbm, *refs):
    parts, (w_ref, atom_ref, occ_ref, virt_ref, arrived) = refs[:-5], refs[-5:]
    pieces, z_ref = (parts[:2], parts[2]) if own else (parts[1:], None)
    steps, aux, wide = pieces[0].shape
    copies = wide // BLK
    copy = pltpu.make_async_copy(atom_hbm, atom_ref, arrived.at[0])
    copy.start()
    copy.wait()
    atom = atom_ref[lax.axis_index("pair") * rows // BLK]
    fetch = [
        pltpu.make_async_copy(occ_hbm.at[:, atom], occ_ref, arrived.at[0]),
        pltpu.make_async_copy(virt_hbm.at[:, atom], virt_ref, arrived.at[1]),
    ]
    for copy in fetch:
        copy.start()
    for copy in fetch:
        copy.wait()
    core = lax.rem(lax.axis_index("aux"), 2)
    core = core if own else 1 - core
    place = pl.ds(pl.multiple_of(core * aux, aux), aux)
    same = (
        lax.broadcasted_iota(jnp.int32, (wide, wide), 0) // BLK
        == lax.broadcasted_iota(jnp.int32, (wide, wide), 1) // BLK
    )

    def diagonal(block):
        tall = jnp.concatenate([block.astype(jnp.float32)] * copies, axis=0)
        full = jnp.concatenate([tall] * copies, axis=1)
        return jnp.where(same, full, 0.0).astype(jnp.bfloat16)

    def through(y, first, second):
        half = jnp.dot(y, first, preferred_element_type=jnp.float32).astype(jnp.bfloat16)
        full = lax.dot_general(half, second, NT_DIMS, preferred_element_type=jnp.float32)
        return full.astype(jnp.bfloat16).reshape(steps, aux, wide)

    for t in range(nt):
        occ, virt = diagonal(occ_ref[t]), diagonal(virt_ref[t])
        for half in range(2):
            y = pieces[half][...].reshape(steps * aux, wide)
            if own:
                z_ref[half, :, t * aux:(t + 1) * aux, :] = through(y, occ, virt)
            w_ref[half, t, :, place, :] = through(y, virt, occ)


def transform(atom, green_occ, green_virt, rows, pieces, before=None):
    nt = green_occ.shape[0]
    steps, aux, wide = pieces[0].shape
    own = before is None
    w_shape = jax.ShapeDtypeStruct((2, nt, steps, 2 * aux, wide), jnp.bfloat16)
    z_shape = jax.ShapeDtypeStruct((2, steps, nt * aux, wide), jnp.bfloat16)
    operands = (stay(atom), stay(green_occ), stay(green_virt), *(() if own else (before,)), *pieces)
    return call(
        functools.partial(transform_kernel, nt, rows, own),
        "transform",
        2 << 30,
        out_shape=(z_shape, w_shape) if own else w_shape,
        in_specs=[HBM] * 3 + [VMEM] * (len(operands) - 3),
        out_specs=(VMEM, VMEM) if own else VMEM,
        input_output_aliases={} if own else {3: 0},
        scratch_shapes=[
            pltpu.SMEM(atom.shape, jnp.int32),
            pltpu.VMEM((nt, BLK, BLK), jnp.bfloat16),
            pltpu.VMEM((nt, BLK, BLK), jnp.bfloat16),
            pltpu.SemaphoreType.DMA((2,)),
        ],
    )(*operands)


def matching(chips, step, piece):
    chip = chip_of()
    source = lax.rem(chip + chips - step, chips)
    swap = early(chips, chip) != early(chips, source)
    return jnp.where(swap, 1 - piece, piece)


def near_kernel(chips, step, count, z_ref, *refs):
    mine, other, out_ref = refs[:count], refs[count:2 * count], refs[-1]
    halves = [matching(chips, step, piece) for piece in range(count)]

    def products(low, high):
        total = jnp.zeros(out_ref.shape, jnp.float32)
        for half, first, second in zip(halves, low, high):
            for j in range(z_ref.shape[1]):
                partner = jnp.concatenate([first[j], second[j]], axis=0)
                total += lax.dot_general(z_ref[half, j], partner, NT_DIMS, preferred_element_type=jnp.float32)
        out_ref[...] = total

    core = lax.rem(lax.axis_index("aux"), 2)
    pl.when(core == 0)(lambda: products(mine, other))
    pl.when(core == 1)(lambda: products(other, mine))


def near(z, chips, step, mine, other):
    size = z.shape[2]
    return call(
        functools.partial(near_kernel, chips, step, len(mine)),
        "near",
        1 << 30,
        out_shape=jax.ShapeDtypeStruct((size, 2 * mine[0].shape[-2]), jnp.float32),
        in_specs=[VMEM] * (1 + 2 * len(mine)),
        out_specs=VMEM,
    )(z, *mine, *other)


def fold(x):
    high = x.shape[0] // 2
    past = jnp.concatenate([x[:high, 128:], x[high:, 128:]], axis=1)
    return jnp.concatenate([x[:, :128], past], axis=0)


def unfold(x):
    high = x.shape[0] // 3
    past = x[2 * high:]
    past = jnp.concatenate([past[:, :BLK], past[:, BLK:]], axis=0)
    return jnp.concatenate([x[:2 * high], past], axis=1)


def far_kernel(chips, step, count, w_ref, *refs):
    mine, out_ref = refs[:count], refs[count]
    nt, steps = w_ref.shape[1:3]
    aux = mine[0].shape[1]
    halves = [matching(chips, step, piece) for piece in range(count)]
    shares = []
    for t in range(nt):
        total = jnp.zeros((aux, w_ref.shape[3]), jnp.float32)
        for half, piece in zip(halves, mine):
            for j in range(steps):
                total += lax.dot_general(piece[j], w_ref[half, t, j], NT_DIMS, preferred_element_type=jnp.float32)
        shares.append(total)
    out_ref[...] = fold(jnp.concatenate(shares, axis=0)).astype(out_ref.dtype)


def far(w, chips, step, mine):
    aux = mine[0].shape[1]
    return call(
        functools.partial(far_kernel, chips, step, len(mine)),
        "far",
        1 << 30,
        out_shape=jax.ShapeDtypeStruct((w.shape[1] * aux * 3 // 2, 128), jnp.bfloat16),
        in_specs=[VMEM] * (1 + len(mine)),
        out_specs=VMEM,
    )(w, *mine)


def pack_kernel(chips, pairs, *refs):
    backs, aheads = refs[:chips // 2 + 1], refs[chips // 2 + 1:chips + 1]
    outs, shares = refs[chips + 1:-1], refs[-1]
    chip = chip_of()
    for step in range(chips // 2):
        shares[lax.rem(chip + chips - step, chips)] = fold(backs[step][...])
    for step in range(1, chips // 2):
        shares[lax.rem(chip + step, chips)] = aheads[step - 1][...].astype(jnp.float32)
    opposite = fold(backs[-1][...]) + aheads[-1][...].astype(jnp.float32)
    shares[lax.rem(chip + chips // 2, chips)] = opposite
    if pairs is None:
        for q in range(chips):
            outs[0][q] = unfold(shares[q]).astype(jnp.bfloat16)
    else:
        pair = lax.axis_index("pair")
        for j, out_ref in enumerate(outs):
            out_ref[...] = shares[lax.bitwise_xor(pair, j)].astype(out_ref.dtype)


def pack(chips, pairs, backs, aheads):
    height, width = backs[0].shape
    folded = (height * 3 // 2, 128)
    if pairs is None:
        out_shape = (jax.ShapeDtypeStruct((chips, height, width), jnp.bfloat16),)
    else:
        out_shape = (jax.ShapeDtypeStruct(folded, jnp.float32),)
        out_shape += (jax.ShapeDtypeStruct(folded, jnp.bfloat16),) * (pairs - 1)
    return call(
        functools.partial(pack_kernel, chips, pairs),
        "pack",
        1 << 28,
        out_shape=out_shape,
        in_specs=[VMEM] * (chips + 1),
        out_specs=(VMEM,) * len(out_shape),
        scratch_shapes=[pltpu.VMEM((chips,) + folded, jnp.float32)],
    )(*backs, *aheads)


def finish_kernel(scale, nt, folded, weight_ref, *refs):
    parts, (chi_ref, sum_ref) = refs[:-2], refs[-2:]
    aux = chi_ref.shape[1]
    if folded:
        total = parts[0][...]
        for part in parts[1:]:
            total += part[...].astype(jnp.float32)
        total = unfold(total * scale)
    else:
        total = parts[0][0].astype(jnp.float32)
        for p in range(1, parts[0].shape[0]):
            total += parts[0][p].astype(jnp.float32)
        total *= scale
    local = jnp.zeros((1, 1), jnp.float32)
    for t in range(nt):
        chi = total[t * aux:(t + 1) * aux]
        chi_ref[t] = chi
        local += weight_ref[t] * jnp.sum(chi * chi, keepdims=True)
    sum_ref[...] = jnp.broadcast_to(local, sum_ref.shape)


def finish(scale, time_weights, parts, chi_shape, copies):
    return call(
        functools.partial(finish_kernel, scale, chi_shape[0], len(parts) > 1),
        "finish",
        1 << 28,
        out_shape=(
            jax.ShapeDtypeStruct(chi_shape, jnp.float32),
            jax.ShapeDtypeStruct((copies, 128), jnp.float32),
        ),
        in_specs=[SMEM] + [VMEM] * len(parts),
        out_specs=(VMEM, VMEM),
    )(time_weights, *parts)


def per_device(integrals, block_mask, block_atom, green_occ, green_virt, time_weights):
    rows = integrals.shape[0]
    aux_here = integrals.shape[1] // BLK
    pairs, auxes = lax.axis_size("pair"), lax.axis_size("aux")
    chips = auxes // 2
    aux_total = aux_here * auxes
    columns = aux_total // pairs
    nt = green_occ.shape[0]

    def along(shift):
        return [(i, (i + 2 * shift) % auxes) for i in range(auxes)]

    def to_sibling(array):
        return lax.ppermute(array, "aux", [(i, i ^ 1) for i in range(auxes)])

    own = [arrange(integrals, block_mask, chips, second) for second in (False, True)]
    arriving = [lax.ppermute(a, "aux", along(1)) for a in own]
    z, w = transform(block_atom, green_occ, green_virt, rows, own)
    *later, z = lax.optimization_barrier((*own, z))
    arriving[0], z = lax.optimization_barrier((arriving[0], z))
    sibling = [to_sibling(a) for a in later]
    backs, aheads = [], []
    for step in range(1, chips // 2 + 1):
        held, last = arriving, step == chips // 2
        if not last:
            sent = held if step + 1 < chips // 2 else held[:1]
            arriving = [lax.ppermute(a, "aux", along(1)) for a in sent]
        other = [to_sibling(a) for a in held]
        if step == 1:
            w = transform(block_atom, green_occ, green_virt, rows, sibling, w)
        share = far(w, chips, step, held)
        aheads.append(lax.ppermute(share, "aux", along(-step)))
        if step == 1:
            backs.append(near(z, chips, 0, own, sibling))
        back = near(z, chips, step, held, other)
        if not last:
            arriving[0], share, back = lax.optimization_barrier((arriving[0], share, back))
        backs.append(back)
    if columns == 2 * aux_here and pairs & (pairs - 1) == 0:
        mine, *sends = pack(chips, pairs, backs, aheads)
        parts = [mine]
        for j in range(pairs - 1, 0, -1):
            parts.append(lax.ppermute(sends[j - 1], "pair", [(i, i ^ j) for i in range(pairs)]))
    else:
        (shares,) = pack(chips, None, backs, aheads)
        shares = shares.transpose(1, 0, 2).reshape(nt * aux_here, pairs, columns).transpose(1, 0, 2)
        parts = [lax.all_to_all(shares, "pair", 0, 0)]
    scale = float((rows * pairs * BLK) ** -0.5)
    chi, sums = finish(scale, time_weights, parts, (nt, aux_here, columns), pairs * auxes)
    everyone = lax.all_to_all(sums, ("pair", "aux"), 0, 0, tiled=True)
    energy = -jnp.sum(everyone[:, 0]) / jnp.float32(aux_total * aux_total)
    return chi, energy


def solution(mesh):
    placed = (P("pair", "aux"), P(None, "aux"), P(), P(), P(), P())
    return jax.shard_map(
        per_device,
        mesh=mesh,
        in_specs=placed,
        out_specs=(P(None, "aux", "pair"), P()),
        check_vma=False,
    )
```

time: 61.3 us -> 55.1 us (0.90)
  blocking collectives: 26.7 us -> 10.5 us
  waiting for transfers between devices: 13.5 us -> 21 us
  Pallas kernels: 8.07 us -> 11.3 us
  local copies, waits for them, and re-layouts: 1.78 us -> 0.01 us
  starting transfers between devices: 7.79 us -> 8.91 us
    all_to_all x3 -> x1, blocking collectives: 26.7 us -> 10.5 us  [per_device(): everyone = lax.all_to_all(sums, ('pair', 'aux'), 0, 0, tiled=True)]
    ppermute x8 -> x11, waiting for transfers between devices: 8.53 us -> 15 us  [the longest x1 5.72 us: per_device(): arriving = [lax.ppermute(a, 'aux', along(1)) for a in sent]]
    ppermute x8 -> x11, starting transfers between devices: 5.48 us -> 8.84 us  [the longest x2 4.71 us: per_device(): arriving = [lax.ppermute(a, 'aux', along(1)) for a in own]]
    pallas_call x3 -> x4, Pallas kernels: 3.53 us -> 6.31 us  [the longest x2 4.86 us: transform(): call(functools.partial(transform_kernel, nt, rows, own), 'transform', 2 <...]
    ppermute x2, starting transfers between devices: 2.31 us -> 0.07 us  [per_device(): aheads.append(lax.ppermute(share, 'aux', along(-step)))]
    unnamed x12 -> x2, local copies, waits for them, and re-layouts: 1.77 us -> 0.01 us
    ppermute x2, waiting for transfers between devices: 4.97 us -> 6 us  [per_device(): aheads.append(lax.ppermute(share, 'aux', along(-step)))]
  transfers between devices with their start and end apart: 10 -> 13, of which waited for: 5 -> 9; matrix products, arithmetic and copies ran while one was open for 0% -> 0% of each run, Pallas kernels for 9% -> 15%
where the time goes in v3:
time: 55.1 us; the launch traced here: 54.7 us
  waiting for transfers between devices  21 us (38%)
  Pallas kernels  11.3 us (21%)
  blocking collectives  10.5 us (19%)
  starting transfers between devices  8.91 us (16%)
  between operations  2.53 us (5%)
  other arithmetic  0.6 us (1%)
    all_to_all x1, blocking collectives, per_device(): everyone = lax.all_to_all(sums, ('pair', 'aux'), 0, 0, tiled=True)  10.5 us
    ppermute x2, waiting for transfers between devices, per_device(): aheads.append(lax.ppermute(share, 'aux', along(-step)))  6 us
    ppermute x1, waiting for transfers between devices, per_device(): arriving = [lax.ppermute(a, 'aux', along(1)) for a in sent]  5.72 us
    ppermute x2, waiting for transfers between devices, per_device(): arriving = [lax.ppermute(a, 'aux', along(1)) for a in own]  4.95 us
    pallas_call x2, Pallas kernels, transform(): call(functools.partial(transform_kernel, nt, rows, own), 'transform', 2 <...  4.86 us
    ppermute x2, starting transfers between devices, per_device(): arriving = [lax.ppermute(a, 'aux', along(1)) for a in own]  4.71 us
    ppermute x3, waiting for transfers between devices, per_device(): lax.ppermute(sends[j - 1], 'pair', [(i, i ^ j) for i in range(pairs)])  3.82 us
    ppermute x3, starting transfers between devices, per_device(): lax.ppermute(sends[j - 1], 'pair', [(i, i ^ j) for i in range(pairs)])  3.55 us
  transfers between devices with their start and end apart: 13, of which 9 were waited for; matrix products, arithmetic and copies ran while one was open for 0% of the time, Pallas kernels for 15%

profile of v3, /device:TPU:0, one launch (start us, length us, event | category | flops | bytes accessed | tf_op | source)
XLA Modules:
  0.0 54.7 jit_solution(11029199043727782547)
XLA Ops:
  0.6 1.4 %arrange.2.refs_0_ = bf16[4,96,256]{2,1,0:T(8,128)(2,1)S(1)} custom-call(bf16[32,6144]{1,0:T(8,128)(2,1)} %x_hbm.3, s32[2,96]{1,0:T(2,128)} %mask_hbm.3), custom_call_target="tpu_custom_call" | custom-call | flops 16777216 | bytes 1024 | tf_op jit(solution)/shard_map/arrange/pallas_call | solution.py:69
  2.0 3.1 %collective-permute-start = (bf16[4,96,256]{2,1,0:T(8,128)(2,1)S(1)}, bf16[4,96,256]{2,1,0:T(8,128)(2,1)S(1)}, u32[]{:S(2)}, u32[]{:S(2)}) collective-permute-start(bf16[4,96,256]{2,1,0:T(8,128)(2,1)S(1)} %arrange.2.refs_0_), channel_id=1, source_target_pairs={{0,2},{1,3},{2,4},{3,5},{4,6},{5,7},{6,0},{7,1},{8,10},{9,11},{10,... | collective-permute-start | bytes 589832 | tf_op jit(solution)/shard_map/ppermute | solution.py:318
  5.1 1.3 %arrange.3.refs_1_ = bf16[4,96,256]{2,1,0:T(8,128)(2,1)S(1)} custom-call(bf16[32,6144]{1,0:T(8,128)(2,1)} %x_hbm.3, s32[2,96]{1,0:T(2,128)} %mask_hbm.3), custom_call_target="tpu_custom_call" | custom-call | flops 16777216 | bytes 1024 | tf_op jit(solution)/shard_map/arrange/pallas_call | solution.py:69
  6.4 1.6 %collective-permute-start.4 = (bf16[4,96,256]{2,1,0:T(8,128)(2,1)S(1)}, bf16[4,96,256]{2,1,0:T(8,128)(2,1)S(1)}, u32[]{:S(2)}, u32[]{:S(2)}) collective-permute-start(bf16[4,96,256]{2,1,0:T(8,128)(2,1)S(1)} %arrange.3.refs_1_), channel_id=1, source_target_pairs={{0,2},{1,3},{2,4},{3,5},{4,6},{5,7},{6,0},{7,1},{8,10},{9,11},{10,... | collective-permute-start | bytes 589832 | tf_op jit(solution)/shard_map/ppermute | solution.py:318
  8.0 2.6 %transform.2 = (bf16[2,4,192,256]{3,2,1,0:T(8,128)(2,1)S(1)}, bf16[2,2,4,192,256]{4,3,2,1,0:T(8,128)(2,1)S(1)}) custom-call(s32[2]{0:T(128)} %atom_hbm.3, bf16[2,16,64,64]{3,2,1,0:T(8,128)(2,1)} %occ_hbm.3, bf16[2,16,64,64]{3,2,1,0:T(8,128)(2,1)} %virt_hbm.3, bf16[4,96,256]{2,1,0:T(8,128)(2,1)S(1)} %arrange.2.refs_0_, bf16[4,96,256]{2,1,0:T(8,128)(2,1)S(1)} %arrange.3.refs_1_), custom_call_target="tpu_custom_call" | custom-call | flops 134217728 | bytes 1024 | tf_op jit(solution)/shard_map/transform/pallas_call | solution.py:136
  10.7 0.1 collective-permute-start.1
  10.8 0.5 collective-permute-start.2
  11.2 1.6 %collective-permute-done.refs_0_ = bf16[4,96,256]{2,1,0:T(8,128)(2,1)S(1)} collective-permute-done((bf16[4,96,256]{2,1,0:T(8,128)(2,1)S(1)}, bf16[4,96,256]{2,1,0:T(8,128)(2,1)S(1)}, u32[]{:S(2)}, u32[]{:S(2)}) %collective-permute-start) | collective-permute-done | bytes 196640 | tf_op jit(solution)/shard_map/ppermute | solution.py:318
  12.8 0.0 collective-permute-start.5
  12.8 3.4 %collective-permute-done.4.refs_1_ = bf16[4,96,256]{2,1,0:T(8,128)(2,1)S(1)} collective-permute-done((bf16[4,96,256]{2,1,0:T(8,128)(2,1)S(1)}, bf16[4,96,256]{2,1,0:T(8,128)(2,1)S(1)}, u32[]{:S(2)}, u32[]{:S(2)}) %collective-permute-start.4) | collective-permute-done | bytes 196640 | tf_op jit(solution)/shard_map/ppermute | solution.py:318
  16.2 0.0 collective-permute-start.6
  16.2 0.0 collective-permute-start.3
  16.2 0.0 collective-permute-done.1.refs_2_.refs_1_
  16.2 0.0 collective-permute-done.2.refs_3_.refs_2_
  16.2 2.2 %transform.3.w_ref = bf16[2,2,4,192,256]{4,3,2,1,0:T(8,128)(2,1)S(1)} custom-call(s32[2]{0:T(128)} %atom_hbm.3, bf16[2,16,64,64]{3,2,1,0:T(8,128)(2,1)} %occ_hbm.3, bf16[2,16,64,64]{3,2,1,0:T(8,128)(2,1)} %virt_hbm.3, bf16[2,2,4,192,256]{4,3,2,1,0:T(8,128)(2,1)S(1)} %get-tuple-element.23.refs_0_, ...), custom_call_target="tpu_custom_call", output_to_operand_aliasing={{}: (3, {})} | custom-call | flops 134217728 | bytes 1024 | tf_op jit(solution)/shard_map/transform/pallas_call | solution.py:136
  18.5 0.7 %far.2 = bf16[288,128]{1,0:T(8,128)(2,1)S(1)} custom-call(bf16[2,2,4,192,256]{4,3,2,1,0:T(8,128)(2,1)S(1)} %transform.3.w_ref, bf16[4,96,256]{2,1,0:T(8,128)(2,1)S(1)} %collective-permute-done.refs_0_, bf16[4,96,256]{2,1,0:T(8,128)(2,1)S(1)} %collective-permute-done.4.refs_1_), custom_call_target="tpu_custom_call" | custom-call | flops 67108864 | bytes 1024 | tf_op jit(solution)/shard_map/far/pallas_call | solution.py:219
  19.2 0.0 collective-permute-done.5.refs_2_
  19.2 0.0 collective-permute-done.6.refs_3_
  19.2 0.4 near.4.refs_1_
  19.6 5.7 %collective-permute-done.3.refs_0_ = bf16[4,96,256]{2,1,0:T(8,128)(2,1)S(1)} collective-permute-done((bf16[4,96,256]{2,1,0:T(8,128)(2,1)S(1)}, bf16[4,96,256]{2,1,0:T(8,128)(2,1)S(1)}, u32[]{:S(2)}, u32[]{:S(2)}) %collective-permute-start.3) | collective-permute-done | bytes 196640 | tf_op jit(solution)/shard_map/ppermute | solution.py:328
  25.3 0.0 collective-permute-start.7
  25.3 0.0 collective-permute-start.8
  25.3 0.5 far.3
  25.8 0.0 copy-start
  25.8 0.1 collective-permute-start.9
  25.9 0.4 near.3.refs_0_
  26.3 0.5 collective-permute-done.7.refs_1_
  26.8 0.3 near.5.refs_2_
  27.1 4.2 %collective-permute-done.8.refs_3_ = bf16[288,128]{1,0:T(8,128)(2,1)S(1)} collective-permute-done((bf16[288,128]{1,0:T(8,128)(2,1)S(1)}, bf16[288,128]{1,0:T(8,128)(2,1)S(1)}, u32[]{:S(2)}, u32[]{:S(2)}) %collective-permute-start.8) | collective-permute-done | bytes 73760 | tf_op jit(solution)/shard_map/ppermute | solution.py:333
  31.2 1.8 %collective-permute-done.9.refs_4_ = bf16[288,128]{1,0:T(8,128)(2,1)S(1)} collective-permute-done((bf16[288,128]{1,0:T(8,128)(2,1)S(1)}, bf16[288,128]{1,0:T(8,128)(2,1)S(1)}, u32[]{:S(2)}, u32[]{:S(2)}) %collective-permute-start.9) | collective-permute-done | bytes 73760 | tf_op jit(solution)/shard_map/ppermute | solution.py:333
  33.1 0.1 pack.1
  33.2 2.5 %collective-permute-start.10 = (bf16[288,128]{1,0:T(8,128)(2,1)S(1)}, bf16[288,128]{1,0:T(8,128)(2,1)S(1)}, u32[]{:S(2)}, u32[]{:S(2)}) collective-permute-start(bf16[288,128]{1,0:T(8,128)(2,1)S(1)} %get-tuple-element.27), channel_id=1, source_target_pairs={{0,24},{8,16},{16,8},{24,0},{1,25},{9,17},{17,9},{25,1},{2,26},{10... | collective-permute-start | bytes 221192 | tf_op jit(solution)/shard_map/ppermute | solution.py:344
  35.7 0.5 collective-permute-start.11
  36.2 0.5 collective-permute-start.12
  36.8 2.2 %collective-permute-done.10.refs_1_ = bf16[288,128]{1,0:T(8,128)(2,1)S(1)} collective-permute-done((bf16[288,128]{1,0:T(8,128)(2,1)S(1)}, bf16[288,128]{1,0:T(8,128)(2,1)S(1)}, u32[]{:S(2)}, u32[]{:S(2)}) %collective-permute-start.10) | collective-permute-done | bytes 73760 | tf_op jit(solution)/shard_map/ppermute | solution.py:344
  38.9 1.1 %collective-permute-done.11.refs_2_ = bf16[288,128]{1,0:T(8,128)(2,1)S(1)} collective-permute-done((bf16[288,128]{1,0:T(8,128)(2,1)S(1)}, bf16[288,128]{1,0:T(8,128)(2,1)S(1)}, u32[]{:S(2)}, u32[]{:S(2)}) %collective-permute-start.11) | collective-permute-done | bytes 73760 | tf_op jit(solution)/shard_map/ppermute | solution.py:344
  40.1 0.5 collective-permute-done.12.refs_3_
  40.6 0.0 copy-done
  40.6 1.3 %finish.1 = (f32[2,96,192]{2,1,0:T(8,128)}, f32[32,128]{1,0:T(8,128)S(1)}) custom-call(f32[2]{0:T(128)S(1)} %copy-done, f32[288,128]{1,0:T(8,128)S(1)} %get-tuple-element.26.refs_0_, bf16[288,128]{1,0:T(8,128)(2,1)S(1)} %collective-permute-done.10.refs_1_, bf16[288,128]{1,0:T(8,128)(2,1)S(1)} %collective-permute-done.11.refs_2_, ...), custom_call_target="tpu_custom_call" | custom-call | flops 16777216 | bytes 1024 | tf_op jit(solution)/shard_map/finish/pallas_call | solution.py:289
  41.9 10.5 %all_to_all.12 = f32[32,1,128]{2,1,0:T(1,128)S(1)} all-to-all(f32[32,1,128]{2,1,0:T(1,128)S(1)} %bitcast.4), channel_id=1, replica_groups=mesh['pair'=4,'aux'=8] {'pair','aux'}, dimensions={0} | all-to-all | bytes 32768 | tf_op jit(solution)/shard_map/all_to_all | solution.py:351
  52.3 0.6 %slice_reduce_fusion = f32[]{:T(128)} fusion(f32[32,128]{1,0:T(8,128)S(1)} %bitcast.5), kind=kLoop, calls=%fused_computation | loop fusion | flops 31 | bytes 132 | tf_op jit(solution)/shard_map/reduce_sum | solution.py:352
Async XLA Ops:
  2.0 10.8 %collective-permute-start = (bf16[4,96,256]{2,1,0:T(8,128)(2,1)S(1)}, bf16[4,96,256]{2,1,0:T(8,128)(2,1)S(1)}, u32[]{:S(2)}, u32[]{:S(2)}) collective-permute-start(bf16[4,96,256]{2,1,0:T(8,128)(2,1)S(1)} %arrange.2.refs_0_), channel_id=1, source_target_pairs={{0,2},{1,3},{2,4},{3,5},{4,6},{5,7},{6,0},{7,1},{8,10},{9,11},{10,... | collective-permute-start | bytes 589832 | tf_op jit(solution)/shard_map/ppermute | solution.py:318
  6.4 9.8 %collective-permute-start.4 = (bf16[4,96,256]{2,1,0:T(8,128)(2,1)S(1)}, bf16[4,96,256]{2,1,0:T(8,128)(2,1)S(1)}, u32[]{:S(2)}, u32[]{:S(2)}) collective-permute-start(bf16[4,96,256]{2,1,0:T(8,128)(2,1)S(1)} %arrange.3.refs_1_), channel_id=1, source_target_pairs={{0,2},{1,3},{2,4},{3,5},{4,6},{5,7},{6,0},{7,1},{8,10},{9,11},{10,... | collective-permute-start | bytes 589832 | tf_op jit(solution)/shard_map/ppermute | solution.py:318
  10.7 5.5 %collective-permute-start.1 = (bf16[4,96,256]{2,1,0:T(8,128)(2,1)S(1)}, bf16[4,96,256]{2,1,0:T(8,128)(2,1)S(1)}, u32[]{:S(2)}, u32[]{:S(2)}) collective-permute-start(bf16[4,96,256]{2,1,0:T(8,128)(2,1)S(1)} %arrange.2.refs_0_), channel_id=1, source_target_pairs={{0,1},{1,0},{2,3},{3,2},{4,5},{5,4},{6,7},{7,6},{8,9},{9,8},{10,11... | collective-permute-start | bytes 589832 | tf_op jit(solution)/shard_map/ppermute | solution.py:315
  10.8 5.5 %collective-permute-start.2 = (bf16[4,96,256]{2,1,0:T(8,128)(2,1)S(1)}, bf16[4,96,256]{2,1,0:T(8,128)(2,1)S(1)}, u32[]{:S(2)}, u32[]{:S(2)}) collective-permute-start(bf16[4,96,256]{2,1,0:T(8,128)(2,1)S(1)} %arrange.3.refs_1_), channel_id=1, source_target_pairs={{0,1},{1,0},{2,3},{3,2},{4,5},{5,4},{6,7},{7,6},{8,9},{9,8},{10,11... | collective-permute-start | bytes 589832 | tf_op jit(solution)/shard_map/ppermute | solution.py:315
  12.8 6.4 %collective-permute-start.5 = (bf16[4,96,256]{2,1,0:T(8,128)(2,1)S(1)}, bf16[4,96,256]{2,1,0:T(8,128)(2,1)S(1)}, u32[]{:S(2)}, u32[]{:S(2)}) collective-permute-start(bf16[4,96,256]{2,1,0:T(8,128)(2,1)S(1)} %collective-permute-done.refs_0_), channel_id=1, source_target_pairs={{0,1},{1,0},{2,3},{3,2},{4,5},{5,4},{6,7},{7,6},{8,9},{9,8},{10,11... | collective-permute-start | bytes 589832 | tf_op jit(solution)/shard_map/ppermute | solution.py:315
  16.2 3.0 %collective-permute-start.6 = (bf16[4,96,256]{2,1,0:T(8,128)(2,1)S(1)}, bf16[4,96,256]{2,1,0:T(8,128)(2,1)S(1)}, u32[]{:S(2)}, u32[]{:S(2)}) collective-permute-start(bf16[4,96,256]{2,1,0:T(8,128)(2,1)S(1)} %collective-permute-done.4.refs_1_), channel_id=1, source_target_pairs={{0,1},{1,0},{2,3},{3,2},{4,5},{5,4},{6,7},{7,6},{8,9},{9,8},{10,11... | collective-permute-start | bytes 589832 | tf_op jit(solution)/shard_map/ppermute | solution.py:315
  16.2 9.1 %collective-permute-start.3 = (bf16[4,96,256]{2,1,0:T(8,128)(2,1)S(1)}, bf16[4,96,256]{2,1,0:T(8,128)(2,1)S(1)}, u32[]{:S(2)}, u32[]{:S(2)}) collective-permute-start(bf16[4,96,256]{2,1,0:T(8,128)(2,1)S(1)} %collective-permute-done.refs_0_), channel_id=1, source_target_pairs={{0,2},{1,3},{2,4},{3,5},{4,6},{5,7},{6,0},{7,1},{8,10},{9,11},{10,... | collective-permute-start | bytes 589832 | tf_op jit(solution)/shard_map/ppermute | solution.py:328
  25.3 1.4 %collective-permute-start.7 = (bf16[4,96,256]{2,1,0:T(8,128)(2,1)S(1)}, bf16[4,96,256]{2,1,0:T(8,128)(2,1)S(1)}, u32[]{:S(2)}, u32[]{:S(2)}) collective-permute-start(bf16[4,96,256]{2,1,0:T(8,128)(2,1)S(1)} %collective-permute-done.3.refs_0_), channel_id=1, source_target_pairs={{0,1},{1,0},{2,3},{3,2},{4,5},{5,4},{6,7},{7,6},{8,9},{9,8},{10,11... | collective-permute-start | bytes 589832 | tf_op jit(solution)/shard_map/ppermute | solution.py:315
  25.3 5.9 %collective-permute-start.8 = (bf16[288,128]{1,0:T(8,128)(2,1)S(1)}, bf16[288,128]{1,0:T(8,128)(2,1)S(1)}, u32[]{:S(2)}, u32[]{:S(2)}) collective-permute-start(bf16[288,128]{1,0:T(8,128)(2,1)S(1)} %far.2), channel_id=1, source_target_pairs={{0,6},{1,7},{2,0},{3,1},{4,2},{5,3},{6,4},{7,5},{8,14},{9,15},{10,... | collective-permute-start | bytes 221192 | tf_op jit(solution)/shard_map/ppermute | solution.py:333
  25.8 14.8 %copy-start = (f32[2]{0:T(128)S(1)}, f32[2]{0:T(128)}, u32[]{:S(2)}) copy-start(f32[2]{0:T(128)} %weight_ref.1) | copy-start | bytes 28
  25.8 7.3 %collective-permute-start.9 = (bf16[288,128]{1,0:T(8,128)(2,1)S(1)}, bf16[288,128]{1,0:T(8,128)(2,1)S(1)}, u32[]{:S(2)}, u32[]{:S(2)}) collective-permute-start(bf16[288,128]{1,0:T(8,128)(2,1)S(1)} %far.3), channel_id=1, source_target_pairs={{0,4},{1,5},{2,6},{3,7},{4,0},{5,1},{6,2},{7,3},{8,12},{9,13},{10,... | collective-permute-start | bytes 221192 | tf_op jit(solution)/shard_map/ppermute | solution.py:333
  33.2 5.7 %collective-permute-start.10 = (bf16[288,128]{1,0:T(8,128)(2,1)S(1)}, bf16[288,128]{1,0:T(8,128)(2,1)S(1)}, u32[]{:S(2)}, u32[]{:S(2)}) collective-permute-start(bf16[288,128]{1,0:T(8,128)(2,1)S(1)} %get-tuple-element.27), channel_id=1, source_target_pairs={{0,24},{8,16},{16,8},{24,0},{1,25},{9,17},{17,9},{25,1},{2,26},{10... | collective-permute-start | bytes 221192 | tf_op jit(solution)/shard_map/ppermute | solution.py:344
  35.7 4.4 %collective-permute-start.11 = (bf16[288,128]{1,0:T(8,128)(2,1)S(1)}, bf16[288,128]{1,0:T(8,128)(2,1)S(1)}, u32[]{:S(2)}, u32[]{:S(2)}) collective-permute-start(bf16[288,128]{1,0:T(8,128)(2,1)S(1)} %get-tuple-element.28), channel_id=1, source_target_pairs={{0,16},{8,24},{16,0},{24,8},{1,17},{9,25},{17,1},{25,9},{2,18},{10... | collective-permute-start | bytes 221192 | tf_op jit(solution)/shard_map/ppermute | solution.py:344
  36.2 4.4 %collective-permute-start.12 = (bf16[288,128]{1,0:T(8,128)(2,1)S(1)}, bf16[288,128]{1,0:T(8,128)(2,1)S(1)}, u32[]{:S(2)}, u32[]{:S(2)}) collective-permute-start(bf16[288,128]{1,0:T(8,128)(2,1)S(1)} %get-tuple-element.29), channel_id=1, source_target_pairs={{0,8},{8,0},{16,24},{24,16},{1,9},{9,1},{17,25},{25,17},{2,10},{10... | collective-permute-start | bytes 221192 | tf_op jit(solution)/shard_map/ppermute | solution.py:344

commit v4 on v3

--- a/solution.py
+++ b/solution.py
@@ -18,7 +18,7 @@
         kernel,
         name=name,
         compiler_params=pltpu.CompilerParams(vmem_limit_bytes=40 * 1024 * 1024),
-        cost_estimate=pl.CostEstimate(flops=flops // 16, bytes_accessed=1 << 10, transcendentals=0),
+        cost_estimate=pl.CostEstimate(flops=flops, bytes_accessed=1 << 8, transcendentals=0),
         **settings,
     )
 
@@ -326,16 +326,20 @@
         if not last:
             sent = held if step + 1 < chips // 2 else held[:1]
             arriving = [lax.ppermute(a, "aux", along(1)) for a in sent]
-        other = [to_sibling(a) for a in held]
         if step == 1:
             w = transform(block_atom, green_occ, green_virt, rows, sibling, w)
         share = far(w, chips, step, held)
-        aheads.append(lax.ppermute(share, "aux", along(-step)))
+        onward = held
+        if last:
+            *onward, share = lax.optimization_barrier((*held, share))
+        other = [to_sibling(a) for a in onward]
+        ahead = lax.ppermute(share, "aux", along(-step))
         if step == 1:
             backs.append(near(z, chips, 0, own, sibling))
         back = near(z, chips, step, held, other)
         if not last:
-            arriving[0], share, back = lax.optimization_barrier((arriving[0], share, back))
+            arriving[0], ahead, back, backs[-1] = lax.optimization_barrier((arriving[0], ahead, back, backs[-1]))
+        aheads.append(ahead)
         backs.append(back)
     if columns == 2 * aux_here and pairs & (pairs - 1) == 0:
         mine, *sends = pack(chips, pairs, backs, aheads)

time: 55.1 us -> 54.5 us (0.989)
  waiting for transfers between devices: 21 us -> 14.3 us
  starting transfers between devices: 8.91 us -> 13 us
  blocking collectives: 10.5 us -> 12.5 us
    ppermute x1, waiting for transfers between devices: 5.72 us -> 0.01 us  [per_device(): arriving = [lax.ppermute(a, 'aux', along(1)) for a in sent]]
    ppermute x2, starting transfers between devices: 0.07 us -> 4.05 us  [per_device(): ahead = lax.ppermute(share, 'aux', along(-step))]
    all_to_all x1, blocking collectives: 10.5 us -> 12.5 us  [per_device(): everyone = lax.all_to_all(sums, ('pair', 'aux'), 0, 0, tiled=True)]
    ppermute x2, waiting for transfers between devices: 6 us -> 5.13 us  [per_device(): ahead = lax.ppermute(share, 'aux', along(-step))]
  transfers between devices with their start and end apart: 13 -> 13, of which waited for: 9 -> 7; matrix products, arithmetic and copies ran while one was open for 0% -> 0% of each run, Pallas kernels for 15% -> 15%
where the time goes in v4:
time: 54.5 us; the launch traced here: 54.2 us
  waiting for transfers between devices  14.3 us (26%)
  starting transfers between devices  13 us (24%)
  blocking collectives  12.5 us (23%)
  Pallas kernels  11.2 us (21%)
  between operations  2.52 us (5%)
  other arithmetic  0.6 us (1%)
    all_to_all x1, blocking collectives, per_device(): everyone = lax.all_to_all(sums, ('pair', 'aux'), 0, 0, tiled=True)  12.5 us
    ppermute x2, waiting for transfers between devices, per_device(): arriving = [lax.ppermute(a, 'aux', along(1)) for a in own]  5.33 us
    ppermute x2, waiting for transfers between devices, per_device(): ahead = lax.ppermute(share, 'aux', along(-step))  5.13 us
    pallas_call x2, Pallas kernels, transform(): call(functools.partial(transform_kernel, nt, rows, own), 'transform', 2 <...  4.86 us
    ppermute x2, starting transfers between devices, per_device(): arriving = [lax.ppermute(a, 'aux', along(1)) for a in own]  4.71 us
    ppermute x2, starting transfers between devices, per_device(): ahead = lax.ppermute(share, 'aux', along(-step))  4.05 us
    ppermute x3, waiting for transfers between devices, per_device(): lax.ppermute(sends[j - 1], 'pair', [(i, i ^ j) for i in range(pairs)])  3.82 us
    ppermute x3, starting transfers between devices, per_device(): lax.ppermute(sends[j - 1], 'pair', [(i, i ^ j) for i in range(pairs)])  3.55 us
  transfers between devices with their start and end apart: 13, of which 7 were waited for; matrix products, arithmetic and copies ran while one was open for 0% of the time, Pallas kernels for 15%

profile of v4, /device:TPU:0, one launch (start us, length us, event | category | flops | bytes accessed | tf_op | source)
XLA Modules:
  0.0 54.2 jit_solution(6780190600148749179)
XLA Ops:
  0.6 1.4 %arrange.2.refs_0_ = bf16[4,96,256]{2,1,0:T(8,128)(2,1)S(1)} custom-call(bf16[32,6144]{1,0:T(8,128)(2,1)} %x_hbm.3, s32[2,96]{1,0:T(2,128)} %mask_hbm.3), custom_call_target="tpu_custom_call" | custom-call | flops 268435456 | bytes 256 | tf_op jit(solution)/shard_map/arrange/pallas_call | solution.py:69
  2.0 3.1 %collective-permute-start = (bf16[4,96,256]{2,1,0:T(8,128)(2,1)S(1)}, bf16[4,96,256]{2,1,0:T(8,128)(2,1)S(1)}, u32[]{:S(2)}, u32[]{:S(2)}) collective-permute-start(bf16[4,96,256]{2,1,0:T(8,128)(2,1)S(1)} %arrange.2.refs_0_), channel_id=1, source_target_pairs={{0,2},{1,3},{2,4},{3,5},{4,6},{5,7},{6,0},{7,1},{8,10},{9,11},{10,... | collective-permute-start | bytes 589832 | tf_op jit(solution)/shard_map/ppermute | solution.py:318
  5.1 1.3 %arrange.3.refs_1_ = bf16[4,96,256]{2,1,0:T(8,128)(2,1)S(1)} custom-call(bf16[32,6144]{1,0:T(8,128)(2,1)} %x_hbm.3, s32[2,96]{1,0:T(2,128)} %mask_hbm.3), custom_call_target="tpu_custom_call" | custom-call | flops 268435456 | bytes 256 | tf_op jit(solution)/shard_map/arrange/pallas_call | solution.py:69
  6.4 1.6 %collective-permute-start.4 = (bf16[4,96,256]{2,1,0:T(8,128)(2,1)S(1)}, bf16[4,96,256]{2,1,0:T(8,128)(2,1)S(1)}, u32[]{:S(2)}, u32[]{:S(2)}) collective-permute-start(bf16[4,96,256]{2,1,0:T(8,128)(2,1)S(1)} %arrange.3.refs_1_), channel_id=1, source_target_pairs={{0,2},{1,3},{2,4},{3,5},{4,6},{5,7},{6,0},{7,1},{8,10},{9,11},{10,... | collective-permute-start | bytes 589832 | tf_op jit(solution)/shard_map/ppermute | solution.py:318
  8.0 2.6 %transform.2 = (bf16[2,4,192,256]{3,2,1,0:T(8,128)(2,1)S(1)}, bf16[2,2,4,192,256]{4,3,2,1,0:T(8,128)(2,1)S(1)}) custom-call(s32[2]{0:T(128)} %atom_hbm.3, bf16[2,16,64,64]{3,2,1,0:T(8,128)(2,1)} %occ_hbm.3, bf16[2,16,64,64]{3,2,1,0:T(8,128)(2,1)} %virt_hbm.3, bf16[4,96,256]{2,1,0:T(8,128)(2,1)S(1)} %arrange.2.refs_0_, bf16[4,96,256]{2,1,0:T(8,128)(2,1)S(1)} %arrange.3.refs_1_), custom_call_target="tpu_custom_call" | custom-call | flops 2147483648 | bytes 256 | tf_op jit(solution)/shard_map/transform/pallas_call | solution.py:136
  10.7 0.1 collective-permute-start.2
  10.8 0.5 collective-permute-start.3
  11.2 1.6 %collective-permute-done.refs_0_ = bf16[4,96,256]{2,1,0:T(8,128)(2,1)S(1)} collective-permute-done((bf16[4,96,256]{2,1,0:T(8,128)(2,1)S(1)}, bf16[4,96,256]{2,1,0:T(8,128)(2,1)S(1)}, u32[]{:S(2)}, u32[]{:S(2)}) %collective-permute-start) | collective-permute-done | bytes 196640 | tf_op jit(solution)/shard_map/ppermute | solution.py:318
  12.8 0.0 collective-permute-start.1
  12.9 0.0 collective-permute-start.6
  12.9 3.8 %collective-permute-done.4.refs_1_ = bf16[4,96,256]{2,1,0:T(8,128)(2,1)S(1)} collective-permute-done((bf16[4,96,256]{2,1,0:T(8,128)(2,1)S(1)}, bf16[4,96,256]{2,1,0:T(8,128)(2,1)S(1)}, u32[]{:S(2)}, u32[]{:S(2)}) %collective-permute-start.4) | collective-permute-done | bytes 196640 | tf_op jit(solution)/shard_map/ppermute | solution.py:318
  16.6 0.0 collective-permute-start.7
  16.6 0.0 collective-permute-done.2.refs_1_.refs_2_
  16.6 0.0 collective-permute-done.3.refs_2_.refs_3_
  16.6 2.2 %transform.3.w_ref = bf16[2,2,4,192,256]{4,3,2,1,0:T(8,128)(2,1)S(1)} custom-call(s32[2]{0:T(128)} %atom_hbm.3, bf16[2,16,64,64]{3,2,1,0:T(8,128)(2,1)} %occ_hbm.3, bf16[2,16,64,64]{3,2,1,0:T(8,128)(2,1)} %virt_hbm.3, bf16[2,2,4,192,256]{4,3,2,1,0:T(8,128)(2,1)S(1)} %get-tuple-element.24.refs_0_, ...), custom_call_target="tpu_custom_call", output_to_operand_aliasing={{}: (3, {})} | custom-call | flops 2147483648 | bytes 256 | tf_op jit(solution)/shard_map/transform/pallas_call | solution.py:136
  18.9 0.7 %far.2 = bf16[288,128]{1,0:T(8,128)(2,1)S(1)} custom-call(bf16[2,2,4,192,256]{4,3,2,1,0:T(8,128)(2,1)S(1)} %transform.3.w_ref, bf16[4,96,256]{2,1,0:T(8,128)(2,1)S(1)} %collective-permute-done.refs_0_, bf16[4,96,256]{2,1,0:T(8,128)(2,1)S(1)} %collective-permute-done.4.refs_1_), custom_call_target="tpu_custom_call" | custom-call | flops 1073741824 | bytes 256 | tf_op jit(solution)/shard_map/far/pallas_call | solution.py:219
  19.6 2.5 %collective-permute-start.5 = (bf16[288,128]{1,0:T(8,128)(2,1)S(1)}, bf16[288,128]{1,0:T(8,128)(2,1)S(1)}, u32[]{:S(2)}, u32[]{:S(2)}) collective-permute-start(bf16[288,128]{1,0:T(8,128)(2,1)S(1)} %far.2), channel_id=1, source_target_pairs={{0,6},{1,7},{2,0},{3,1},{4,2},{5,3},{6,4},{7,5},{8,14},{9,15},{10,... | collective-permute-start | bytes 221192 | tf_op jit(solution)/shard_map/ppermute | solution.py:336
  22.1 0.4 near.4.refs_0_
  22.5 0.0 collective-permute-done.6.refs_2_
  22.5 0.0 collective-permute-done.7.refs_3_
  22.5 0.4 near.3.refs_1_
  22.9 1.4 %collective-permute-done.5.refs_3_ = bf16[288,128]{1,0:T(8,128)(2,1)S(1)} collective-permute-done((bf16[288,128]{1,0:T(8,128)(2,1)S(1)}, bf16[288,128]{1,0:T(8,128)(2,1)S(1)}, u32[]{:S(2)}, u32[]{:S(2)}) %collective-permute-start.5) | collective-permute-done | bytes 73760 | tf_op jit(solution)/shard_map/ppermute | solution.py:336
  24.3 0.0 collective-permute-done.1.refs_0_
  24.3 0.4 far.3
  24.7 0.0 copy-start
  24.8 0.1 collective-permute-start.8
  24.8 1.5 %collective-permute-start.9 = (bf16[288,128]{1,0:T(8,128)(2,1)S(1)}, bf16[288,128]{1,0:T(8,128)(2,1)S(1)}, u32[]{:S(2)}, u32[]{:S(2)}) collective-permute-start(bf16[288,128]{1,0:T(8,128)(2,1)S(1)} %far.3), channel_id=1, source_target_pairs={{0,4},{1,5},{2,6},{3,7},{4,0},{5,1},{6,2},{7,3},{8,12},{9,13},{10,... | collective-permute-start | bytes 221192 | tf_op jit(solution)/shard_map/ppermute | solution.py:336
  26.4 0.0 collective-permute-done.8.refs_1_
  26.4 0.3 near.5.refs_2_
  26.7 3.8 %collective-permute-done.9.refs_4_ = bf16[288,128]{1,0:T(8,128)(2,1)S(1)} collective-permute-done((bf16[288,128]{1,0:T(8,128)(2,1)S(1)}, bf16[288,128]{1,0:T(8,128)(2,1)S(1)}, u32[]{:S(2)}, u32[]{:S(2)}) %collective-permute-start.9) | collective-permute-done | bytes 73760 | tf_op jit(solution)/shard_map/ppermute | solution.py:336
  30.4 0.1 pack.1
  30.6 2.5 %collective-permute-start.10 = (bf16[288,128]{1,0:T(8,128)(2,1)S(1)}, bf16[288,128]{1,0:T(8,128)(2,1)S(1)}, u32[]{:S(2)}, u32[]{:S(2)}) collective-permute-start(bf16[288,128]{1,0:T(8,128)(2,1)S(1)} %get-tuple-element.35), channel_id=1, source_target_pairs={{0,24},{8,16},{16,8},{24,0},{1,25},{9,17},{17,9},{25,1},{2,26},{10... | collective-permute-start | bytes 221192 | tf_op jit(solution)/shard_map/ppermute | solution.py:348
  33.1 0.5 collective-permute-start.11
  33.6 0.5 collective-permute-start.12
  34.1 1.9 %collective-permute-done.10.refs_1_ = bf16[288,128]{1,0:T(8,128)(2,1)S(1)} collective-permute-done((bf16[288,128]{1,0:T(8,128)(2,1)S(1)}, bf16[288,128]{1,0:T(8,128)(2,1)S(1)}, u32[]{:S(2)}, u32[]{:S(2)}) %collective-permute-start.10) | collective-permute-done | bytes 73760 | tf_op jit(solution)/shard_map/ppermute | solution.py:348
  36.0 1.4 %collective-permute-done.11.refs_2_ = bf16[288,128]{1,0:T(8,128)(2,1)S(1)} collective-permute-done((bf16[288,128]{1,0:T(8,128)(2,1)S(1)}, bf16[288,128]{1,0:T(8,128)(2,1)S(1)}, u32[]{:S(2)}, u32[]{:S(2)}) %collective-permute-start.11) | collective-permute-done | bytes 73760 | tf_op jit(solution)/shard_map/ppermute | solution.py:348
  37.4 0.5 collective-permute-done.12.refs_3_
  37.9 0.0 copy-done
  37.9 1.3 %finish.1 = (f32[2,96,192]{2,1,0:T(8,128)}, f32[32,128]{1,0:T(8,128)S(1)}) custom-call(f32[2]{0:T(128)S(1)} %copy-done, f32[288,128]{1,0:T(8,128)S(1)} %get-tuple-element.34.refs_0_, bf16[288,128]{1,0:T(8,128)(2,1)S(1)} %collective-permute-done.10.refs_1_, bf16[288,128]{1,0:T(8,128)(2,1)S(1)} %collective-permute-done.11.refs_2_, ...), custom_call_target="tpu_custom_call" | custom-call | flops 268435456 | bytes 256 | tf_op jit(solution)/shard_map/finish/pallas_call | solution.py:289
  39.3 12.5 %all_to_all.12 = f32[32,1,128]{2,1,0:T(1,128)S(1)} all-to-all(f32[32,1,128]{2,1,0:T(1,128)S(1)} %bitcast.4), channel_id=1, replica_groups=mesh['pair'=4,'aux'=8] {'pair','aux'}, dimensions={0} | all-to-all | bytes 32768 | tf_op jit(solution)/shard_map/all_to_all | solution.py:355
  51.8 0.6 %slice_reduce_fusion = f32[]{:T(128)} fusion(f32[32,128]{1,0:T(8,128)S(1)} %bitcast.5), kind=kLoop, calls=%fused_computation | loop fusion | flops 31 | bytes 132 | tf_op jit(solution)/shard_map/reduce_sum | solution.py:356
Async XLA Ops:
  2.0 10.8 %collective-permute-start = (bf16[4,96,256]{2,1,0:T(8,128)(2,1)S(1)}, bf16[4,96,256]{2,1,0:T(8,128)(2,1)S(1)}, u32[]{:S(2)}, u32[]{:S(2)}) collective-permute-start(bf16[4,96,256]{2,1,0:T(8,128)(2,1)S(1)} %arrange.2.refs_0_), channel_id=1, source_target_pairs={{0,2},{1,3},{2,4},{3,5},{4,6},{5,7},{6,0},{7,1},{8,10},{9,11},{10,... | collective-permute-start | bytes 589832 | tf_op jit(solution)/shard_map/ppermute | solution.py:318
  6.4 10.2 %collective-permute-start.4 = (bf16[4,96,256]{2,1,0:T(8,128)(2,1)S(1)}, bf16[4,96,256]{2,1,0:T(8,128)(2,1)S(1)}, u32[]{:S(2)}, u32[]{:S(2)}) collective-permute-start(bf16[4,96,256]{2,1,0:T(8,128)(2,1)S(1)} %arrange.3.refs_1_), channel_id=1, source_target_pairs={{0,2},{1,3},{2,4},{3,5},{4,6},{5,7},{6,0},{7,1},{8,10},{9,11},{10,... | collective-permute-start | bytes 589832 | tf_op jit(solution)/shard_map/ppermute | solution.py:318
  10.7 5.9 %collective-permute-start.2 = (bf16[4,96,256]{2,1,0:T(8,128)(2,1)S(1)}, bf16[4,96,256]{2,1,0:T(8,128)(2,1)S(1)}, u32[]{:S(2)}, u32[]{:S(2)}) collective-permute-start(bf16[4,96,256]{2,1,0:T(8,128)(2,1)S(1)} %arrange.2.refs_0_), channel_id=1, source_target_pairs={{0,1},{1,0},{2,3},{3,2},{4,5},{5,4},{6,7},{7,6},{8,9},{9,8},{10,11... | collective-permute-start | bytes 589832 | tf_op jit(solution)/shard_map/ppermute | solution.py:315
  10.8 5.9 %collective-permute-start.3 = (bf16[4,96,256]{2,1,0:T(8,128)(2,1)S(1)}, bf16[4,96,256]{2,1,0:T(8,128)(2,1)S(1)}, u32[]{:S(2)}, u32[]{:S(2)}) collective-permute-start(bf16[4,96,256]{2,1,0:T(8,128)(2,1)S(1)} %arrange.3.refs_1_), channel_id=1, source_target_pairs={{0,1},{1,0},{2,3},{3,2},{4,5},{5,4},{6,7},{7,6},{8,9},{9,8},{10,11... | collective-permute-start | bytes 589832 | tf_op jit(solution)/shard_map/ppermute | solution.py:315
  12.8 11.5 %collective-permute-start.1 = (bf16[4,96,256]{2,1,0:T(8,128)(2,1)S(1)}, bf16[4,96,256]{2,1,0:T(8,128)(2,1)S(1)}, u32[]{:S(2)}, u32[]{:S(2)}) collective-permute-start(bf16[4,96,256]{2,1,0:T(8,128)(2,1)S(1)} %collective-permute-done.refs_0_), channel_id=1, source_target_pairs={{0,2},{1,3},{2,4},{3,5},{4,6},{5,7},{6,0},{7,1},{8,10},{9,11},{10,... | collective-permute-start | bytes 589832 | tf_op jit(solution)/shard_map/ppermute | solution.py:328
  12.9 9.6 %collective-permute-start.6 = (bf16[4,96,256]{2,1,0:T(8,128)(2,1)S(1)}, bf16[4,96,256]{2,1,0:T(8,128)(2,1)S(1)}, u32[]{:S(2)}, u32[]{:S(2)}) collective-permute-start(bf16[4,96,256]{2,1,0:T(8,128)(2,1)S(1)} %collective-permute-done.refs_0_), channel_id=1, source_target_pairs={{0,1},{1,0},{2,3},{3,2},{4,5},{5,4},{6,7},{7,6},{8,9},{9,8},{10,11... | collective-permute-start | bytes 589832 | tf_op jit(solution)/shard_map/ppermute | solution.py:315
  16.6 5.9 %collective-permute-start.7 = (bf16[4,96,256]{2,1,0:T(8,128)(2,1)S(1)}, bf16[4,96,256]{2,1,0:T(8,128)(2,1)S(1)}, u32[]{:S(2)}, u32[]{:S(2)}) collective-permute-start(bf16[4,96,256]{2,1,0:T(8,128)(2,1)S(1)} %collective-permute-done.4.refs_1_), channel_id=1, source_target_pairs={{0,1},{1,0},{2,3},{3,2},{4,5},{5,4},{6,7},{7,6},{8,9},{9,8},{10,11... | collective-permute-start | bytes 589832 | tf_op jit(solution)/shard_map/ppermute | solution.py:315
  19.6 4.7 %collective-permute-start.5 = (bf16[288,128]{1,0:T(8,128)(2,1)S(1)}, bf16[288,128]{1,0:T(8,128)(2,1)S(1)}, u32[]{:S(2)}, u32[]{:S(2)}) collective-permute-start(bf16[288,128]{1,0:T(8,128)(2,1)S(1)} %far.2), channel_id=1, source_target_pairs={{0,6},{1,7},{2,0},{3,1},{4,2},{5,3},{6,4},{7,5},{8,14},{9,15},{10,... | collective-permute-start | bytes 221192 | tf_op jit(solution)/shard_map/ppermute | solution.py:336
  24.7 13.2 %copy-start = (f32[2]{0:T(128)S(1)}, f32[2]{0:T(128)}, u32[]{:S(2)}) copy-start(f32[2]{0:T(128)} %weight_ref.1) | copy-start | bytes 28
  24.8 1.6 %collective-permute-start.8 = (bf16[4,96,256]{2,1,0:T(8,128)(2,1)S(1)}, bf16[4,96,256]{2,1,0:T(8,128)(2,1)S(1)}, u32[]{:S(2)}, u32[]{:S(2)}) collective-permute-start(bf16[4,96,256]{2,1,0:T(8,128)(2,1)S(1)} %collective-permute-done.1.refs_0_), channel_id=1, source_target_pairs={{0,1},{1,0},{2,3},{3,2},{4,5},{5,4},{6,7},{7,6},{8,9},{9,8},{10,11... | collective-permute-start | bytes 589832 | tf_op jit(solution)/shard_map/ppermute | solution.py:315
  24.8 5.6 %collective-permute-start.9 = (bf16[288,128]{1,0:T(8,128)(2,1)S(1)}, bf16[288,128]{1,0:T(8,128)(2,1)S(1)}, u32[]{:S(2)}, u32[]{:S(2)}) collective-permute-start(bf16[288,128]{1,0:T(8,128)(2,1)S(1)} %far.3), channel_id=1, source_target_pairs={{0,4},{1,5},{2,6},{3,7},{4,0},{5,1},{6,2},{7,3},{8,12},{9,13},{10,... | collective-permute-start | bytes 221192 | tf_op jit(solution)/shard_map/ppermute | solution.py:336
  30.6 5.4 %collective-permute-start.10 = (bf16[288,128]{1,0:T(8,128)(2,1)S(1)}, bf16[288,128]{1,0:T(8,128)(2,1)S(1)}, u32[]{:S(2)}, u32[]{:S(2)}) collective-permute-start(bf16[288,128]{1,0:T(8,128)(2,1)S(1)} %get-tuple-element.35), channel_id=1, source_target_pairs={{0,24},{8,16},{16,8},{24,0},{1,25},{9,17},{17,9},{25,1},{2,26},{10... | collective-permute-start | bytes 221192 | tf_op jit(solution)/shard_map/ppermute | solution.py:348
  33.1 4.4 %collective-permute-start.11 = (bf16[288,128]{1,0:T(8,128)(2,1)S(1)}, bf16[288,128]{1,0:T(8,128)(2,1)S(1)}, u32[]{:S(2)}, u32[]{:S(2)}) collective-permute-start(bf16[288,128]{1,0:T(8,128)(2,1)S(1)} %get-tuple-element.36), channel_id=1, source_target_pairs={{0,16},{8,24},{16,0},{24,8},{1,17},{9,25},{17,1},{25,9},{2,18},{10... | collective-permute-start | bytes 221192 | tf_op jit(solution)/shard_map/ppermute | solution.py:348
  33.6 4.4 %collective-permute-start.12 = (bf16[288,128]{1,0:T(8,128)(2,1)S(1)}, bf16[288,128]{1,0:T(8,128)(2,1)S(1)}, u32[]{:S(2)}, u32[]{:S(2)}) collective-permute-start(bf16[288,128]{1,0:T(8,128)(2,1)S(1)} %get-tuple-element.37), channel_id=1, source_target_pairs={{0,8},{8,0},{16,24},{24,16},{1,9},{9,1},{17,25},{25,17},{2,10},{10... | collective-permute-start | bytes 221192 | tf_op jit(solution)/shard_map/ppermute | solution.py:348

commit v5 on v4

--- a/solution.py
+++ b/solution.py
@@ -338,22 +338,30 @@
             backs.append(near(z, chips, 0, own, sibling))
         back = near(z, chips, step, held, other)
         if not last:
-            arriving[0], ahead, back, backs[-1] = lax.optimization_barrier((arriving[0], ahead, back, backs[-1]))
+            arriving[0], _, back, backs[-1] = lax.optimization_barrier((arriving[0], share, back, backs[-1]))
         aheads.append(ahead)
         backs.append(back)
     if columns == 2 * aux_here and pairs & (pairs - 1) == 0:
         mine, *sends = pack(chips, pairs, backs, aheads)
         parts = [mine]
-        for j in range(pairs - 1, 0, -1):
+        for j in range(1, pairs):
             parts.append(lax.ppermute(sends[j - 1], "pair", [(i, i ^ j) for i in range(pairs)]))
     else:
         (shares,) = pack(chips, None, backs, aheads)
         shares = shares.transpose(1, 0, 2).reshape(nt * aux_here, pairs, columns).transpose(1, 0, 2)
         parts = [lax.all_to_all(shares, "pair", 0, 0)]
     scale = float((rows * pairs * BLK) ** -0.5)
-    chi, sums = finish(scale, time_weights, parts, (nt, aux_here, columns), pairs * auxes)
-    everyone = lax.all_to_all(sums, ("pair", "aux"), 0, 0, tiled=True)
-    energy = -jnp.sum(everyone[:, 0]) / jnp.float32(aux_total * aux_total)
+    doubling = pairs & (pairs - 1) == 0 and auxes & (auxes - 1) == 0
+    copies = 8 if doubling else pairs * auxes
+    chi, sums = finish(scale, time_weights, parts, (nt, aux_here, columns), copies)
+    if doubling:
+        for axis, size in (("pair", pairs), ("aux", auxes)):
+            for bit in range(size.bit_length() - 1):
+                sums += lax.ppermute(sums, axis, [(i, i ^ 1 << bit) for i in range(size)])
+        total = sums[0, 0]
+    else:
+        total = jnp.sum(lax.all_to_all(sums, ("pair", "aux"), 0, 0, tiled=True)[:, 0])
+    energy = -total / jnp.float32(aux_total * aux_total)
     return chi, energy
 
 

time: 54.5 us -> 58.8 us (1.079)
  waiting for transfers between devices: 14.3 us -> 30.1 us
  blocking collectives: 12.5 us -> 0 us
  starting transfers between devices: 13 us -> 14.1 us
    ppermute x0 -> x5, waiting for transfers between devices: none -> 14.3 us  [per_device(): sums += lax.ppermute(sums, axis, [(i, i ^ 1 << bit) for i in range(size)])]
    all_to_all x1 -> x0, blocking collectives: 12.5 us -> none  [per_device(): everyone = lax.all_to_all(sums, ('pair', 'aux'), 0, 0, tiled=True)]
    ppermute x0 -> x5, starting transfers between devices: none -> 2.19 us  [per_device(): sums += lax.ppermute(sums, axis, [(i, i ^ 1 << bit) for i in range(size)])]
    ppermute x2, starting transfers between devices: 4.05 us -> 2.48 us  [per_device(): ahead = lax.ppermute(share, 'aux', along(-step))]
    ppermute x3, waiting for transfers between devices: 3.82 us -> 4.78 us  [per_device(): lax.ppermute(sends[j - 1], 'pair', [(i, i ^ j) for i in range(pairs)])]
    reduce_sum x1 -> x0, other arithmetic: 0.6 us -> none  [per_device(): energy = -jnp.sum(everyone[:, 0]) / jnp.float32(aux_total * aux_total)]
  transfers between devices with their start and end apart: 13 -> 18, of which waited for: 7 -> 12; matrix products, arithmetic and copies ran while one was open for 0% -> 0% of each run, Pallas kernels for 15% -> 14%
where the time goes in v5:
time: 58.8 us; the launch traced here: 58.5 us
  waiting for transfers between devices  30.1 us (51%)
  starting transfers between devices  14.1 us (24%)
  Pallas kernels  11.3 us (19%)
  between operations  2.52 us (4%)
    ppermute x5, waiting for transfers between devices, per_device(): sums += lax.ppermute(sums, axis, [(i, i ^ 1 << bit) for i in range(size)])  14.3 us
    ppermute x2, waiting for transfers between devices, per_device(): ahead = lax.ppermute(share, 'aux', along(-step))  5.63 us
    ppermute x2, waiting for transfers between devices, per_device(): arriving = [lax.ppermute(a, 'aux', along(1)) for a in own]  5.33 us
    pallas_call x2, Pallas kernels, transform(): call(functools.partial(transform_kernel, nt, rows, own), 'transform', 2 <...  4.86 us
    ppermute x3, waiting for transfers between devices, per_device(): lax.ppermute(sends[j - 1], 'pair', [(i, i ^ j) for i in range(pairs)])  4.78 us
    ppermute x2, starting transfers between devices, per_device(): arriving = [lax.ppermute(a, 'aux', along(1)) for a in own]  4.71 us
    ppermute x3, starting transfers between devices, per_device(): lax.ppermute(sends[j - 1], 'pair', [(i, i ^ j) for i in range(pairs)])  3.55 us
    pallas_call x2, Pallas kernels, arrange(): call(functools.partial(arrange_kernel, rows, aux, chips, second), 'arrang...  2.68 us
  transfers between devices with their start and end apart: 18, of which 12 were waited for; matrix products, arithmetic and copies ran while one was open for 0% of the time, Pallas kernels for 14%

profile of v5, /device:TPU:0, one launch (start us, length us, event | category | flops | bytes accessed | tf_op | source)
XLA Modules:
  0.0 58.5 jit_solution(9987930527959799121)
XLA Ops:
  0.6 1.4 %arrange.2.refs_0_ = bf16[4,96,256]{2,1,0:T(8,128)(2,1)S(1)} custom-call(bf16[32,6144]{1,0:T(8,128)(2,1)} %x_hbm.3, s32[2,96]{1,0:T(2,128)} %mask_hbm.3), custom_call_target="tpu_custom_call" | custom-call | flops 268435456 | bytes 256 | tf_op jit(solution)/shard_map/arrange/pallas_call | solution.py:69
  2.0 3.1 %collective-permute-start = (bf16[4,96,256]{2,1,0:T(8,128)(2,1)S(1)}, bf16[4,96,256]{2,1,0:T(8,128)(2,1)S(1)}, u32[]{:S(2)}, u32[]{:S(2)}) collective-permute-start(bf16[4,96,256]{2,1,0:T(8,128)(2,1)S(1)} %arrange.2.refs_0_), channel_id=1, source_target_pairs={{0,2},{1,3},{2,4},{3,5},{4,6},{5,7},{6,0},{7,1},{8,10},{9,11},{10,... | collective-permute-start | bytes 589832 | tf_op jit(solution)/shard_map/ppermute | solution.py:318
  5.1 1.3 %arrange.3.refs_1_ = bf16[4,96,256]{2,1,0:T(8,128)(2,1)S(1)} custom-call(bf16[32,6144]{1,0:T(8,128)(2,1)} %x_hbm.3, s32[2,96]{1,0:T(2,128)} %mask_hbm.3), custom_call_target="tpu_custom_call" | custom-call | flops 268435456 | bytes 256 | tf_op jit(solution)/shard_map/arrange/pallas_call | solution.py:69
  6.4 1.6 %collective-permute-start.4 = (bf16[4,96,256]{2,1,0:T(8,128)(2,1)S(1)}, bf16[4,96,256]{2,1,0:T(8,128)(2,1)S(1)}, u32[]{:S(2)}, u32[]{:S(2)}) collective-permute-start(bf16[4,96,256]{2,1,0:T(8,128)(2,1)S(1)} %arrange.3.refs_1_), channel_id=1, source_target_pairs={{0,2},{1,3},{2,4},{3,5},{4,6},{5,7},{6,0},{7,1},{8,10},{9,11},{10,... | collective-permute-start | bytes 589832 | tf_op jit(solution)/shard_map/ppermute | solution.py:318
  8.0 2.6 %transform.2 = (bf16[2,4,192,256]{3,2,1,0:T(8,128)(2,1)S(1)}, bf16[2,2,4,192,256]{4,3,2,1,0:T(8,128)(2,1)S(1)}) custom-call(s32[2]{0:T(128)} %atom_hbm.3, bf16[2,16,64,64]{3,2,1,0:T(8,128)(2,1)} %occ_hbm.3, bf16[2,16,64,64]{3,2,1,0:T(8,128)(2,1)} %virt_hbm.3, bf16[4,96,256]{2,1,0:T(8,128)(2,1)S(1)} %arrange.2.refs_0_, bf16[4,96,256]{2,1,0:T(8,128)(2,1)S(1)} %arrange.3.refs_1_), custom_call_target="tpu_custom_call" | custom-call | flops 2147483648 | bytes 256 | tf_op jit(solution)/shard_map/transform/pallas_call | solution.py:136
  10.7 0.1 collective-permute-start.2
  10.8 0.5 collective-permute-start.3
  11.2 1.6 %collective-permute-done.refs_0_ = bf16[4,96,256]{2,1,0:T(8,128)(2,1)S(1)} collective-permute-done((bf16[4,96,256]{2,1,0:T(8,128)(2,1)S(1)}, bf16[4,96,256]{2,1,0:T(8,128)(2,1)S(1)}, u32[]{:S(2)}, u32[]{:S(2)}) %collective-permute-start) | collective-permute-done | bytes 196640 | tf_op jit(solution)/shard_map/ppermute | solution.py:318
  12.8 0.0 collective-permute-start.1
  12.9 0.0 collective-permute-start.5
  12.9 3.8 %collective-permute-done.4.refs_1_ = bf16[4,96,256]{2,1,0:T(8,128)(2,1)S(1)} collective-permute-done((bf16[4,96,256]{2,1,0:T(8,128)(2,1)S(1)}, bf16[4,96,256]{2,1,0:T(8,128)(2,1)S(1)}, u32[]{:S(2)}, u32[]{:S(2)}) %collective-permute-start.4) | collective-permute-done | bytes 196640 | tf_op jit(solution)/shard_map/ppermute | solution.py:318
  16.6 0.0 collective-permute-start.6
  16.6 0.0 collective-permute-done.2.refs_1_.refs_2_
  16.6 0.0 collective-permute-done.3.refs_2_.refs_3_
  16.6 2.2 %transform.3.w_ref = bf16[2,2,4,192,256]{4,3,2,1,0:T(8,128)(2,1)S(1)} custom-call(s32[2]{0:T(128)} %atom_hbm.3, bf16[2,16,64,64]{3,2,1,0:T(8,128)(2,1)} %occ_hbm.3, bf16[2,16,64,64]{3,2,1,0:T(8,128)(2,1)} %virt_hbm.3, bf16[2,2,4,192,256]{4,3,2,1,0:T(8,128)(2,1)S(1)} %get-tuple-element.23.refs_0_, ...), custom_call_target="tpu_custom_call", output_to_operand_aliasing={{}: (3, {})} | custom-call | flops 2147483648 | bytes 256 | tf_op jit(solution)/shard_map/transform/pallas_call | solution.py:136
  18.9 0.7 %far.2 = bf16[288,128]{1,0:T(8,128)(2,1)S(1)} custom-call(bf16[2,2,4,192,256]{4,3,2,1,0:T(8,128)(2,1)S(1)} %transform.3.w_ref, bf16[4,96,256]{2,1,0:T(8,128)(2,1)S(1)} %collective-permute-done.refs_0_, bf16[4,96,256]{2,1,0:T(8,128)(2,1)S(1)} %collective-permute-done.4.refs_1_), custom_call_target="tpu_custom_call" | custom-call | flops 1073741824 | bytes 256 | tf_op jit(solution)/shard_map/far/pallas_call | solution.py:219
  19.6 0.4 near.4.refs_0_
  20.0 0.0 collective-permute-done.5.refs_2_
  20.0 0.0 collective-permute-done.6.refs_3_
  20.0 0.4 near.3.refs_1_
  20.4 0.0 collective-permute-done.1.refs_0_
  20.4 0.5 far.3
  20.9 0.0 copy-start
  20.9 0.6 collective-permute-start.7
  21.5 2.5 %collective-permute-start.8 = (bf16[288,128]{1,0:T(8,128)(2,1)S(1)}, bf16[288,128]{1,0:T(8,128)(2,1)S(1)}, u32[]{:S(2)}, u32[]{:S(2)}) collective-permute-start(bf16[288,128]{1,0:T(8,128)(2,1)S(1)} %far.2), channel_id=1, source_target_pairs={{0,6},{1,7},{2,0},{3,1},{4,2},{5,3},{6,4},{7,5},{8,14},{9,15},{10,... | collective-permute-start | bytes 221192 | tf_op jit(solution)/shard_map/ppermute | solution.py:336
  24.0 0.0 collective-permute-start.9
  24.0 0.0 collective-permute-done.7.refs_1_
  24.0 0.3 near.5.refs_2_
  24.3 2.3 %collective-permute-done.8.refs_3_ = bf16[288,128]{1,0:T(8,128)(2,1)S(1)} collective-permute-done((bf16[288,128]{1,0:T(8,128)(2,1)S(1)}, bf16[288,128]{1,0:T(8,128)(2,1)S(1)}, u32[]{:S(2)}, u32[]{:S(2)}) %collective-permute-start.8) | collective-permute-done | bytes 73760 | tf_op jit(solution)/shard_map/ppermute | solution.py:336
  26.5 3.3 %collective-permute-done.9.refs_4_ = bf16[288,128]{1,0:T(8,128)(2,1)S(1)} collective-permute-done((bf16[288,128]{1,0:T(8,128)(2,1)S(1)}, bf16[288,128]{1,0:T(8,128)(2,1)S(1)}, u32[]{:S(2)}, u32[]{:S(2)}) %collective-permute-start.9) | collective-permute-done | bytes 73760 | tf_op jit(solution)/shard_map/ppermute | solution.py:336
  29.9 0.1 pack.1
  30.0 1.6 %collective-permute-start.10 = (bf16[288,128]{1,0:T(8,128)(2,1)S(1)}, bf16[288,128]{1,0:T(8,128)(2,1)S(1)}, u32[]{:S(2)}, u32[]{:S(2)}) collective-permute-start(bf16[288,128]{1,0:T(8,128)(2,1)S(1)} %get-tuple-element.33), channel_id=1, source_target_pairs={{0,8},{8,0},{16,24},{24,16},{1,9},{9,1},{17,25},{25,17},{2,10},{10... | collective-permute-start | bytes 221192 | tf_op jit(solution)/shard_map/ppermute | solution.py:348
  31.6 1.5 %collective-permute-start.11 = (bf16[288,128]{1,0:T(8,128)(2,1)S(1)}, bf16[288,128]{1,0:T(8,128)(2,1)S(1)}, u32[]{:S(2)}, u32[]{:S(2)}) collective-permute-start(bf16[288,128]{1,0:T(8,128)(2,1)S(1)} %get-tuple-element.34), channel_id=1, source_target_pairs={{0,16},{8,24},{16,0},{24,8},{1,17},{9,25},{17,1},{25,9},{2,18},{10... | collective-permute-start | bytes 221192 | tf_op jit(solution)/shard_map/ppermute | solution.py:348
  33.1 0.5 collective-permute-start.12
  33.6 0.9 %collective-permute-done.10.refs_1_ = bf16[288,128]{1,0:T(8,128)(2,1)S(1)} collective-permute-done((bf16[288,128]{1,0:T(8,128)(2,1)S(1)}, bf16[288,128]{1,0:T(8,128)(2,1)S(1)}, u32[]{:S(2)}, u32[]{:S(2)}) %collective-permute-start.10) | collective-permute-done | bytes 73760 | tf_op jit(solution)/shard_map/ppermute | solution.py:348
  34.4 1.5 %collective-permute-done.11.refs_2_ = bf16[288,128]{1,0:T(8,128)(2,1)S(1)} collective-permute-done((bf16[288,128]{1,0:T(8,128)(2,1)S(1)}, bf16[288,128]{1,0:T(8,128)(2,1)S(1)}, u32[]{:S(2)}, u32[]{:S(2)}) %collective-permute-start.11) | collective-permute-done | bytes 73760 | tf_op jit(solution)/shard_map/ppermute | solution.py:348
  35.9 2.4 %collective-permute-done.12.refs_3_ = bf16[288,128]{1,0:T(8,128)(2,1)S(1)} collective-permute-done((bf16[288,128]{1,0:T(8,128)(2,1)S(1)}, bf16[288,128]{1,0:T(8,128)(2,1)S(1)}, u32[]{:S(2)}, u32[]{:S(2)}) %collective-permute-start.12) | collective-permute-done | bytes 73760 | tf_op jit(solution)/shard_map/ppermute | solution.py:348
  38.4 0.0 copy-done
  38.4 1.3 %finish.1 = (f32[2,96,192]{2,1,0:T(8,128)}, f32[8,128]{1,0:T(8,128)S(1)}) custom-call(f32[2]{0:T(128)S(1)} %copy-done, f32[288,128]{1,0:T(8,128)S(1)} %get-tuple-element.32.refs_0_, bf16[288,128]{1,0:T(8,128)(2,1)S(1)} %collective-permute-done.10.refs_1_, bf16[288,128]{1,0:T(8,128)(2,1)S(1)} %collective-permute-done.11.refs_2_, ...), custom_call_target="tpu_custom_call" | custom-call | flops 268435456 | bytes 256 | tf_op jit(solution)/shard_map/finish/pallas_call | solution.py:289
  39.7 0.6 collective-permute-start.13
  40.2 3.1 %collective-permute-done.13 = f32[8,128]{1,0:T(8,128)S(1)} collective-permute-done((f32[8,128]{1,0:T(8,128)S(1)}, f32[8,128]{1,0:T(8,128)S(1)}, u32[]{:S(2)}, u32[]{:S(2)}) %collective-permute-start.13) | collective-permute-done | bytes 4128 | tf_op jit(solution)/shard_map/ppermute | solution.py:360
  43.3 0.6 collective-permute-start.14
  43.8 3.0 %collective-permute-done.14 = f32[8,128]{1,0:T(8,128)S(1)} collective-permute-done((f32[8,128]{1,0:T(8,128)S(1)}, f32[8,128]{1,0:T(8,128)S(1)}, u32[]{:S(2)}, u32[]{:S(2)}) %collective-permute-start.14) | collective-permute-done | bytes 4128 | tf_op jit(solution)/shard_map/ppermute | solution.py:360
  46.9 0.0 collective-permute-start.15
  46.9 1.2 %collective-permute-done.15 = f32[8,128]{1,0:T(8,128)S(1)} collective-permute-done((f32[8,128]{1,0:T(8,128)S(1)}, f32[8,128]{1,0:T(8,128)S(1)}, u32[]{:S(2)}, u32[]{:S(2)}) %collective-permute-start.15) | collective-permute-done | bytes 4128 | tf_op jit(solution)/shard_map/ppermute | solution.py:360
  48.1 0.0 collective-permute-start.16
  48.1 3.6 %collective-permute-done.16 = f32[8,128]{1,0:T(8,128)S(1)} collective-permute-done((f32[8,128]{1,0:T(8,128)S(1)}, f32[8,128]{1,0:T(8,128)S(1)}, u32[]{:S(2)}, u32[]{:S(2)}) %collective-permute-start.16) | collective-permute-done | bytes 4128 | tf_op jit(solution)/shard_map/ppermute | solution.py:360
  51.7 1.1 %collective-permute-start.17 = (f32[8,128]{1,0:T(8,128)S(1)}, f32[8,128]{1,0:T(8,128)S(1)}, u32[]{:S(2)}, u32[]{:S(2)}) collective-permute-start(f32[8,128]{1,0:T(8,128)S(1)} %add.18), channel_id=1, source_target_pairs={{0,4},{1,5},{2,6},{3,7},{4,0},{5,1},{6,2},{7,3},{8,12},{9,13},{10,... | collective-permute-start | bytes 12296 | tf_op jit(solution)/shard_map/ppermute | solution.py:360
  52.8 3.4 %collective-permute-done.17 = f32[8,128]{1,0:T(8,128)S(1)} collective-permute-done((f32[8,128]{1,0:T(8,128)S(1)}, f32[8,128]{1,0:T(8,128)S(1)}, u32[]{:S(2)}, u32[]{:S(2)}) %collective-permute-start.17) | collective-permute-done | bytes 4128 | tf_op jit(solution)/shard_map/ppermute | solution.py:360
  56.2 0.5 slice.3
  (5 shorter events, 0.0 us)
Async XLA Ops:
  2.0 10.8 %collective-permute-start = (bf16[4,96,256]{2,1,0:T(8,128)(2,1)S(1)}, bf16[4,96,256]{2,1,0:T(8,128)(2,1)S(1)}, u32[]{:S(2)}, u32[]{:S(2)}) collective-permute-start(bf16[4,96,256]{2,1,0:T(8,128)(2,1)S(1)} %arrange.2.refs_0_), channel_id=1, source_target_pairs={{0,2},{1,3},{2,4},{3,5},{4,6},{5,7},{6,0},{7,1},{8,10},{9,11},{10,... | collective-permute-start | bytes 589832 | tf_op jit(solution)/shard_map/ppermute | solution.py:318
  6.4 10.2 %collective-permute-start.4 = (bf16[4,96,256]{2,1,0:T(8,128)(2,1)S(1)}, bf16[4,96,256]{2,1,0:T(8,128)(2,1)S(1)}, u32[]{:S(2)}, u32[]{:S(2)}) collective-permute-start(bf16[4,96,256]{2,1,0:T(8,128)(2,1)S(1)} %arrange.3.refs_1_), channel_id=1, source_target_pairs={{0,2},{1,3},{2,4},{3,5},{4,6},{5,7},{6,0},{7,1},{8,10},{9,11},{10,... | collective-permute-start | bytes 589832 | tf_op jit(solution)/shard_map/ppermute | solution.py:318
  10.7 5.9 %collective-permute-start.2 = (bf16[4,96,256]{2,1,0:T(8,128)(2,1)S(1)}, bf16[4,96,256]{2,1,0:T(8,128)(2,1)S(1)}, u32[]{:S(2)}, u32[]{:S(2)}) collective-permute-start(bf16[4,96,256]{2,1,0:T(8,128)(2,1)S(1)} %arrange.2.refs_0_), channel_id=1, source_target_pairs={{0,1},{1,0},{2,3},{3,2},{4,5},{5,4},{6,7},{7,6},{8,9},{9,8},{10,11... | collective-permute-start | bytes 589832 | tf_op jit(solution)/shard_map/ppermute | solution.py:315
  10.8 5.9 %collective-permute-start.3 = (bf16[4,96,256]{2,1,0:T(8,128)(2,1)S(1)}, bf16[4,96,256]{2,1,0:T(8,128)(2,1)S(1)}, u32[]{:S(2)}, u32[]{:S(2)}) collective-permute-start(bf16[4,96,256]{2,1,0:T(8,128)(2,1)S(1)} %arrange.3.refs_1_), channel_id=1, source_target_pairs={{0,1},{1,0},{2,3},{3,2},{4,5},{5,4},{6,7},{7,6},{8,9},{9,8},{10,11... | collective-permute-start | bytes 589832 | tf_op jit(solution)/shard_map/ppermute | solution.py:315
  12.8 7.6 %collective-permute-start.1 = (bf16[4,96,256]{2,1,0:T(8,128)(2,1)S(1)}, bf16[4,96,256]{2,1,0:T(8,128)(2,1)S(1)}, u32[]{:S(2)}, u32[]{:S(2)}) collective-permute-start(bf16[4,96,256]{2,1,0:T(8,128)(2,1)S(1)} %collective-permute-done.refs_0_), channel_id=1, source_target_pairs={{0,2},{1,3},{2,4},{3,5},{4,6},{5,7},{6,0},{7,1},{8,10},{9,11},{10,... | collective-permute-start | bytes 589832 | tf_op jit(solution)/shard_map/ppermute | solution.py:328
  12.9 7.1 %collective-permute-start.5 = (bf16[4,96,256]{2,1,0:T(8,128)(2,1)S(1)}, bf16[4,96,256]{2,1,0:T(8,128)(2,1)S(1)}, u32[]{:S(2)}, u32[]{:S(2)}) collective-permute-start(bf16[4,96,256]{2,1,0:T(8,128)(2,1)S(1)} %collective-permute-done.refs_0_), channel_id=1, source_target_pairs={{0,1},{1,0},{2,3},{3,2},{4,5},{5,4},{6,7},{7,6},{8,9},{9,8},{10,11... | collective-permute-start | bytes 589832 | tf_op jit(solution)/shard_map/ppermute | solution.py:315
  16.6 3.4 %collective-permute-start.6 = (bf16[4,96,256]{2,1,0:T(8,128)(2,1)S(1)}, bf16[4,96,256]{2,1,0:T(8,128)(2,1)S(1)}, u32[]{:S(2)}, u32[]{:S(2)}) collective-permute-start(bf16[4,96,256]{2,1,0:T(8,128)(2,1)S(1)} %collective-permute-done.4.refs_1_), channel_id=1, source_target_pairs={{0,1},{1,0},{2,3},{3,2},{4,5},{5,4},{6,7},{7,6},{8,9},{9,8},{10,11... | collective-permute-start | bytes 589832 | tf_op jit(solution)/shard_map/ppermute | solution.py:315
  20.9 17.5 %copy-start = (f32[2]{0:T(128)S(1)}, f32[2]{0:T(128)}, u32[]{:S(2)}) copy-start(f32[2]{0:T(128)} %weight_ref.1) | copy-start | bytes 28
  20.9 3.1 %collective-permute-start.7 = (bf16[4,96,256]{2,1,0:T(8,128)(2,1)S(1)}, bf16[4,96,256]{2,1,0:T(8,128)(2,1)S(1)}, u32[]{:S(2)}, u32[]{:S(2)}) collective-permute-start(bf16[4,96,256]{2,1,0:T(8,128)(2,1)S(1)} %collective-permute-done.1.refs_0_), channel_id=1, source_target_pairs={{0,1},{1,0},{2,3},{3,2},{4,5},{5,4},{6,7},{7,6},{8,9},{9,8},{10,11... | collective-permute-start | bytes 589832 | tf_op jit(solution)/shard_map/ppermute | solution.py:315
  21.5 5.1 %collective-permute-start.8 = (bf16[288,128]{1,0:T(8,128)(2,1)S(1)}, bf16[288,128]{1,0:T(8,128)(2,1)S(1)}, u32[]{:S(2)}, u32[]{:S(2)}) collective-permute-start(bf16[288,128]{1,0:T(8,128)(2,1)S(1)} %far.2), channel_id=1, source_target_pairs={{0,6},{1,7},{2,0},{3,1},{4,2},{5,3},{6,4},{7,5},{8,14},{9,15},{10,... | collective-permute-start | bytes 221192 | tf_op jit(solution)/shard_map/ppermute | solution.py:336
  24.0 5.9 %collective-permute-start.9 = (bf16[288,128]{1,0:T(8,128)(2,1)S(1)}, bf16[288,128]{1,0:T(8,128)(2,1)S(1)}, u32[]{:S(2)}, u32[]{:S(2)}) collective-permute-start(bf16[288,128]{1,0:T(8,128)(2,1)S(1)} %far.3), channel_id=1, source_target_pairs={{0,4},{1,5},{2,6},{3,7},{4,0},{5,1},{6,2},{7,3},{8,12},{9,13},{10,... | collective-permute-start | bytes 221192 | tf_op jit(solution)/shard_map/ppermute | solution.py:336
  30.0 4.4 %collective-permute-start.10 = (bf16[288,128]{1,0:T(8,128)(2,1)S(1)}, bf16[288,128]{1,0:T(8,128)(2,1)S(1)}, u32[]{:S(2)}, u32[]{:S(2)}) collective-permute-start(bf16[288,128]{1,0:T(8,128)(2,1)S(1)} %get-tuple-element.33), channel_id=1, source_target_pairs={{0,8},{8,0},{16,24},{24,16},{1,9},{9,1},{17,25},{25,17},{2,10},{10... | collective-permute-start | bytes 221192 | tf_op jit(solution)/shard_map/ppermute | solution.py:348
  31.6 4.4 %collective-permute-start.11 = (bf16[288,128]{1,0:T(8,128)(2,1)S(1)}, bf16[288,128]{1,0:T(8,128)(2,1)S(1)}, u32[]{:S(2)}, u32[]{:S(2)}) collective-permute-start(bf16[288,128]{1,0:T(8,128)(2,1)S(1)} %get-tuple-element.34), channel_id=1, source_target_pairs={{0,16},{8,24},{16,0},{24,8},{1,17},{9,25},{17,1},{25,9},{2,18},{10... | collective-permute-start | bytes 221192 | tf_op jit(solution)/shard_map/ppermute | solution.py:348
  33.1 5.3 %collective-permute-start.12 = (bf16[288,128]{1,0:T(8,128)(2,1)S(1)}, bf16[288,128]{1,0:T(8,128)(2,1)S(1)}, u32[]{:S(2)}, u32[]{:S(2)}) collective-permute-start(bf16[288,128]{1,0:T(8,128)(2,1)S(1)} %get-tuple-element.35), channel_id=1, source_target_pairs={{0,24},{8,16},{16,8},{24,0},{1,25},{9,17},{17,9},{25,1},{2,26},{10... | collective-permute-start | bytes 221192 | tf_op jit(solution)/shard_map/ppermute | solution.py:348
  39.7 3.6 %collective-permute-start.13 = (f32[8,128]{1,0:T(8,128)S(1)}, f32[8,128]{1,0:T(8,128)S(1)}, u32[]{:S(2)}, u32[]{:S(2)}) collective-permute-start(f32[8,128]{1,0:T(8,128)S(1)} %get-tuple-element.37), channel_id=1, source_target_pairs={{0,8},{8,0},{16,24},{24,16},{1,9},{9,1},{17,25},{25,17},{2,10},{10... | collective-permute-start | bytes 12296 | tf_op jit(solution)/shard_map/ppermute | solution.py:360
  43.3 3.6 %collective-permute-start.14 = (f32[8,128]{1,0:T(8,128)S(1)}, f32[8,128]{1,0:T(8,128)S(1)}, u32[]{:S(2)}, u32[]{:S(2)}) collective-permute-start(f32[8,128]{1,0:T(8,128)S(1)} %add.15), channel_id=1, source_target_pairs={{0,16},{8,24},{16,0},{24,8},{1,17},{9,25},{17,1},{25,9},{2,18},{10... | collective-permute-start | bytes 12296 | tf_op jit(solution)/shard_map/ppermute | solution.py:360
  46.9 1.2 %collective-permute-start.15 = (f32[8,128]{1,0:T(8,128)S(1)}, f32[8,128]{1,0:T(8,128)S(1)}, u32[]{:S(2)}, u32[]{:S(2)}) collective-permute-start(f32[8,128]{1,0:T(8,128)S(1)} %add.16), channel_id=1, source_target_pairs={{0,1},{1,0},{2,3},{3,2},{4,5},{5,4},{6,7},{7,6},{8,9},{9,8},{10,11... | collective-permute-start | bytes 12296 | tf_op jit(solution)/shard_map/ppermute | solution.py:360
  48.1 3.6 %collective-permute-start.16 = (f32[8,128]{1,0:T(8,128)S(1)}, f32[8,128]{1,0:T(8,128)S(1)}, u32[]{:S(2)}, u32[]{:S(2)}) collective-permute-start(f32[8,128]{1,0:T(8,128)S(1)} %add.17), channel_id=1, source_target_pairs={{0,2},{1,3},{2,0},{3,1},{4,6},{5,7},{6,4},{7,5},{8,10},{9,11},{10,... | collective-permute-start | bytes 12296 | tf_op jit(solution)/shard_map/ppermute | solution.py:360
  51.7 4.5 %collective-permute-start.17 = (f32[8,128]{1,0:T(8,128)S(1)}, f32[8,128]{1,0:T(8,128)S(1)}, u32[]{:S(2)}, u32[]{:S(2)}) collective-permute-start(f32[8,128]{1,0:T(8,128)S(1)} %add.18), channel_id=1, source_target_pairs={{0,4},{1,5},{2,6},{3,7},{4,0},{5,1},{6,2},{7,3},{8,12},{9,13},{10,... | collective-permute-start | bytes 12296 | tf_op jit(solution)/shard_map/ppermute | solution.py:360

commit v6 on v4

--- a/solution.py
+++ b/solution.py
@@ -31,16 +31,9 @@
     return lax.axis_index("aux") // 2
 
 
-def early(chips, chip):
-    return (chip < chips // 2).astype(jnp.int32)
-
-
-def arrange_kernel(rows, aux, chips, second, x_hbm, mask_hbm, y_ref, x, mask, wide, arrived):
-    half = early(chips, chip_of())
-    half = 1 - half if second else half
-    start = pl.multiple_of(half * (rows // 2), rows // 2)
+def arrange_kernel(rows, aux, second, x_hbm, mask_hbm, y_ref, x, mask, wide, arrived):
     copies = [
-        pltpu.make_async_copy(x_hbm.at[pl.ds(start, rows // 2)], x, arrived.at[0]),
+        pltpu.make_async_copy(x_hbm.at[pl.ds(second * (rows // 2), rows // 2)], x, arrived.at[0]),
         pltpu.make_async_copy(mask_hbm, mask, arrived.at[1]),
     ]
     for copy in copies:
@@ -63,11 +56,11 @@
         y_ref[s // 2, :, lane:lane + 128] = wide[s * aux:(s + 1) * aux, :].astype(y_ref.dtype)
 
 
-def arrange(integrals, block_mask, chips, second):
+def arrange(integrals, block_mask, second):
     rows, width = integrals.shape
     aux = width // BLK
     return call(
-        functools.partial(arrange_kernel, rows, aux, chips, second),
+        functools.partial(arrange_kernel, rows, aux, second),
         "arrange",
         1 << 28,
         out_shape=jax.ShapeDtypeStruct((4, aux, 256), jnp.bfloat16),
@@ -150,20 +143,12 @@
     )(*operands)
 
 
-def matching(chips, step, piece):
-    chip = chip_of()
-    source = lax.rem(chip + chips - step, chips)
-    swap = early(chips, chip) != early(chips, source)
-    return jnp.where(swap, 1 - piece, piece)
-
-
-def near_kernel(chips, step, count, z_ref, *refs):
+def near_kernel(count, start, z_ref, *refs):
     mine, other, out_ref = refs[:count], refs[count:2 * count], refs[-1]
-    halves = [matching(chips, step, piece) for piece in range(count)]
 
     def products(low, high):
         total = jnp.zeros(out_ref.shape, jnp.float32)
-        for half, first, second in zip(halves, low, high):
+        for half, (first, second) in enumerate(zip(low, high), start):
             for j in range(z_ref.shape[1]):
                 partner = jnp.concatenate([first[j], second[j]], axis=0)
                 total += lax.dot_general(z_ref[half, j], partner, NT_DIMS, preferred_element_type=jnp.float32)
@@ -174,10 +159,10 @@
     pl.when(core == 1)(lambda: products(other, mine))
 
 
-def near(z, chips, step, mine, other):
+def near(z, mine, other, start=0):
     size = z.shape[2]
     return call(
-        functools.partial(near_kernel, chips, step, len(mine)),
+        functools.partial(near_kernel, len(mine), start),
         "near",
         1 << 30,
         out_shape=jax.ShapeDtypeStruct((size, 2 * mine[0].shape[-2]), jnp.float32),
@@ -199,25 +184,24 @@
     return jnp.concatenate([x[:2 * high], past], axis=1)
 
 
-def far_kernel(chips, step, count, w_ref, *refs):
-    mine, out_ref = refs[:count], refs[count]
+def far_kernel(w_ref, *refs):
+    mine, out_ref = refs[:-1], refs[-1]
     nt, steps = w_ref.shape[1:3]
     aux = mine[0].shape[1]
-    halves = [matching(chips, step, piece) for piece in range(count)]
     shares = []
     for t in range(nt):
         total = jnp.zeros((aux, w_ref.shape[3]), jnp.float32)
-        for half, piece in zip(halves, mine):
+        for half, piece in enumerate(mine):
             for j in range(steps):
                 total += lax.dot_general(piece[j], w_ref[half, t, j], NT_DIMS, preferred_element_type=jnp.float32)
         shares.append(total)
     out_ref[...] = fold(jnp.concatenate(shares, axis=0)).astype(out_ref.dtype)
 
 
-def far(w, chips, step, mine):
+def far(w, mine):
     aux = mine[0].shape[1]
     return call(
-        functools.partial(far_kernel, chips, step, len(mine)),
+        far_kernel,
         "far",
         1 << 30,
         out_shape=jax.ShapeDtypeStruct((w.shape[1] * aux * 3 // 2, 128), jnp.bfloat16),
@@ -227,15 +211,14 @@
 
 
 def pack_kernel(chips, pairs, *refs):
-    backs, aheads = refs[:chips // 2 + 1], refs[chips // 2 + 1:chips + 1]
+    backs, lower, aheads = refs[:chips // 2 + 1], refs[chips // 2 + 1], refs[chips // 2 + 2:chips + 1]
     outs, shares = refs[chips + 1:-1], refs[-1]
     chip = chip_of()
-    for step in range(chips // 2):
-        shares[lax.rem(chip + chips - step, chips)] = fold(backs[step][...])
+    for step in range(chips // 2 + 1):
+        share = backs[step][...] if step < chips // 2 else backs[step][...] + lower[...]
+        shares[lax.rem(chip + chips - step, chips)] = fold(share)
     for step in range(1, chips // 2):
         shares[lax.rem(chip + step, chips)] = aheads[step - 1][...].astype(jnp.float32)
-    opposite = fold(backs[-1][...]) + aheads[-1][...].astype(jnp.float32)
-    shares[lax.rem(chip + chips // 2, chips)] = opposite
     if pairs is None:
         for q in range(chips):
             outs[0][q] = unfold(shares[q]).astype(jnp.bfloat16)
@@ -314,7 +297,7 @@
     def to_sibling(array):
         return lax.ppermute(array, "aux", [(i, i ^ 1) for i in range(auxes)])
 
-    own = [arrange(integrals, block_mask, chips, second) for second in (False, True)]
+    own = [arrange(integrals, block_mask, second) for second in (False, True)]
     arriving = [lax.ppermute(a, "aux", along(1)) for a in own]
     z, w = transform(block_atom, green_occ, green_virt, rows, own)
     *later, z = lax.optimization_barrier((*own, z))
@@ -324,23 +307,23 @@
     for step in range(1, chips // 2 + 1):
         held, last = arriving, step == chips // 2
         if not last:
-            sent = held if step + 1 < chips // 2 else held[:1]
-            arriving = [lax.ppermute(a, "aux", along(1)) for a in sent]
+            arriving = [lax.ppermute(a, "aux", along(1)) for a in held]
+        if last:
+            upper = near(z, held[:1], [to_sibling(held[0])])
+            later, upper = lax.optimization_barrier((held[1], upper))
+            backs += [upper, near(z, [later], [to_sibling(later)], 1)]
+            continue
+        other = [to_sibling(a) for a in held]
         if step == 1:
             w = transform(block_atom, green_occ, green_virt, rows, sibling, w)
-        share = far(w, chips, step, held)
-        onward = held
-        if last:
-            *onward, share = lax.optimization_barrier((*held, share))
-        other = [to_sibling(a) for a in onward]
+        share = far(w, held)
         ahead = lax.ppermute(share, "aux", along(-step))
         if step == 1:
-            backs.append(near(z, chips, 0, own, sibling))
-        back = near(z, chips, step, held, other)
-        if not last:
-            arriving[0], ahead, back, backs[-1] = lax.optimization_barrier((arriving[0], ahead, back, backs[-1]))
+            backs.append(near(z, own, sibling))
+        backs.append(near(z, held, other))
+        arriving[0], _, backs[-1], backs[-2] = lax.optimization_barrier((arriving[0], share, backs[-1], backs[-2]))
+        arriving[1], ahead = lax.optimization_barrier((arriving[1], ahead))
         aheads.append(ahead)
-        backs.append(back)
     if columns == 2 * aux_here and pairs & (pairs - 1) == 0:
         mine, *sends = pack(chips, pairs, backs, aheads)
         parts = [mine]
@@ -352,8 +335,8 @@
         parts = [lax.all_to_all(shares, "pair", 0, 0)]
     scale = float((rows * pairs * BLK) ** -0.5)
     chi, sums = finish(scale, time_weights, parts, (nt, aux_here, columns), pairs * auxes)
-    everyone = lax.all_to_all(sums, ("pair", "aux"), 0, 0, tiled=True)
-    energy = -jnp.sum(everyone[:, 0]) / jnp.float32(aux_total * aux_total)
+    total = jnp.sum(lax.all_to_all(sums, ("pair", "aux"), 0, 0, tiled=True)[:, 0])
+    energy = -total / jnp.float32(aux_total * aux_total)
     return chi, energy
 
 

time: 54.5 us -> 52.7 us (0.967)
  waiting for transfers between devices: 14.3 us -> 13.4 us
  blocking collectives: 12.5 us -> 11.7 us
    ppermute x2 -> x1, waiting for transfers between devices: 5.13 us -> 2.8 us  [per_device(): ahead = lax.ppermute(share, 'aux', along(-step))]
    ppermute x5 -> x6, waiting for transfers between devices: 0.01 us -> 1.41 us  [to_sibling(): return lax.ppermute(array, 'aux', [(i, i ^ 1) for i in range(auxes)])]
    all_to_all x1, blocking collectives: 12.5 us -> 11.7 us  [per_device(): lax.all_to_all(sums, ('pair', 'aux'), 0, 0, tiled=True)[:, 0]]
    ppermute x5 -> x6, starting transfers between devices: 0.64 us -> 1.24 us  [to_sibling(): return lax.ppermute(array, 'aux', [(i, i ^ 1) for i in range(auxes)])]
    ppermute x2 -> x1, starting transfers between devices: 4.05 us -> 3.53 us  [per_device(): ahead = lax.ppermute(share, 'aux', along(-step))]
  transfers between devices with their start and end apart: 13 -> 14, of which waited for: 7 -> 7; matrix products, arithmetic and copies ran while one was open for 0% -> 0% of each run, Pallas kernels for 15% -> 15%
where the time goes in v6:
time: 52.7 us; the launch traced here: 52.4 us
  waiting for transfers between devices  13.4 us (25%)
  starting transfers between devices  13.1 us (25%)
  blocking collectives  11.7 us (22%)
  Pallas kernels  11.1 us (21%)
  between operations  2.54 us (5%)
  other arithmetic  0.6 us (1%)
    all_to_all x1, blocking collectives, per_device(): lax.all_to_all(sums, ('pair', 'aux'), 0, 0, tiled=True)[:, 0]  11.7 us
    ppermute x2, waiting for transfers between devices, per_device(): arriving = [lax.ppermute(a, 'aux', along(1)) for a in own]  5.33 us
    pallas_call x2, Pallas kernels, transform(): call(functools.partial(transform_kernel, nt, rows, own), 'transform', 2 <...  4.86 us
    ppermute x2, starting transfers between devices, per_device(): arriving = [lax.ppermute(a, 'aux', along(1)) for a in own]  4.71 us
    ppermute x3, waiting for transfers between devices, per_device(): lax.ppermute(sends[j - 1], 'pair', [(i, i ^ j) for i in range(pairs)])  3.83 us
    ppermute x3, starting transfers between devices, per_device(): lax.ppermute(sends[j - 1], 'pair', [(i, i ^ j) for i in range(pairs)])  3.55 us
    ppermute x1, starting transfers between devices, per_device(): ahead = lax.ppermute(share, 'aux', along(-step))  3.53 us
    ppermute x1, waiting for transfers between devices, per_device(): ahead = lax.ppermute(share, 'aux', along(-step))  2.8 us
  transfers between devices with their start and end apart: 14, of which 7 were waited for; matrix products, arithmetic and copies ran while one was open for 0% of the time, Pallas kernels for 15%

profile of v6, /device:TPU:0, one launch (start us, length us, event | category | flops | bytes accessed | tf_op | source)
XLA Modules:
  0.0 52.4 jit_solution(17849196003669786212)
XLA Ops:
  0.6 1.3 %arrange.2.refs_0_ = bf16[4,96,256]{2,1,0:T(8,128)(2,1)S(1)} custom-call(bf16[32,6144]{1,0:T(8,128)(2,1)} %x_hbm.3, s32[2,96]{1,0:T(2,128)} %mask_hbm.3), custom_call_target="tpu_custom_call" | custom-call | flops 268435456 | bytes 256 | tf_op jit(solution)/shard_map/arrange/pallas_call | solution.py:62
  2.0 3.1 %collective-permute-start = (bf16[4,96,256]{2,1,0:T(8,128)(2,1)S(1)}, bf16[4,96,256]{2,1,0:T(8,128)(2,1)S(1)}, u32[]{:S(2)}, u32[]{:S(2)}) collective-permute-start(bf16[4,96,256]{2,1,0:T(8,128)(2,1)S(1)} %arrange.2.refs_0_), channel_id=1, source_target_pairs={{0,2},{1,3},{2,4},{3,5},{4,6},{5,7},{6,0},{7,1},{8,10},{9,11},{10,... | collective-permute-start | bytes 589832 | tf_op jit(solution)/shard_map/ppermute | solution.py:301
  5.0 1.3 %arrange.3.refs_1_ = bf16[4,96,256]{2,1,0:T(8,128)(2,1)S(1)} custom-call(bf16[32,6144]{1,0:T(8,128)(2,1)} %x_hbm.3, s32[2,96]{1,0:T(2,128)} %mask_hbm.3), custom_call_target="tpu_custom_call" | custom-call | flops 268435456 | bytes 256 | tf_op jit(solution)/shard_map/arrange/pallas_call | solution.py:62
  6.4 1.6 %collective-permute-start.4 = (bf16[4,96,256]{2,1,0:T(8,128)(2,1)S(1)}, bf16[4,96,256]{2,1,0:T(8,128)(2,1)S(1)}, u32[]{:S(2)}, u32[]{:S(2)}) collective-permute-start(bf16[4,96,256]{2,1,0:T(8,128)(2,1)S(1)} %arrange.3.refs_1_), channel_id=1, source_target_pairs={{0,2},{1,3},{2,4},{3,5},{4,6},{5,7},{6,0},{7,1},{8,10},{9,11},{10,... | collective-permute-start | bytes 589832 | tf_op jit(solution)/shard_map/ppermute | solution.py:301
  8.0 2.6 %transform.2 = (bf16[2,4,192,256]{3,2,1,0:T(8,128)(2,1)S(1)}, bf16[2,2,4,192,256]{4,3,2,1,0:T(8,128)(2,1)S(1)}) custom-call(s32[2]{0:T(128)} %atom_hbm.3, bf16[2,16,64,64]{3,2,1,0:T(8,128)(2,1)} %occ_hbm.3, bf16[2,16,64,64]{3,2,1,0:T(8,128)(2,1)} %virt_hbm.3, bf16[4,96,256]{2,1,0:T(8,128)(2,1)S(1)} %arrange.2.refs_0_, bf16[4,96,256]{2,1,0:T(8,128)(2,1)S(1)} %arrange.3.refs_1_), custom_call_target="tpu_custom_call" | custom-call | flops 2147483648 | bytes 256 | tf_op jit(solution)/shard_map/transform/pallas_call | solution.py:129
  10.7 0.1 collective-permute-start.2
  10.7 0.5 collective-permute-start.3
  11.2 1.6 %collective-permute-done.refs_0_ = bf16[4,96,256]{2,1,0:T(8,128)(2,1)S(1)} collective-permute-done((bf16[4,96,256]{2,1,0:T(8,128)(2,1)S(1)}, bf16[4,96,256]{2,1,0:T(8,128)(2,1)S(1)}, u32[]{:S(2)}, u32[]{:S(2)}) %collective-permute-start) | collective-permute-done | bytes 196640 | tf_op jit(solution)/shard_map/ppermute | solution.py:301
  12.8 0.0 collective-permute-start.1
  12.8 0.0 collective-permute-start.5
  12.8 3.8 %collective-permute-done.4.refs_1_ = bf16[4,96,256]{2,1,0:T(8,128)(2,1)S(1)} collective-permute-done((bf16[4,96,256]{2,1,0:T(8,128)(2,1)S(1)}, bf16[4,96,256]{2,1,0:T(8,128)(2,1)S(1)}, u32[]{:S(2)}, u32[]{:S(2)}) %collective-permute-start.4) | collective-permute-done | bytes 196640 | tf_op jit(solution)/shard_map/ppermute | solution.py:301
  16.6 0.0 collective-permute-start.6
  16.6 0.0 collective-permute-done.2.refs_1_.refs_2_
  16.6 0.0 collective-permute-start.7
  16.6 0.0 collective-permute-done.3.refs_2_.refs_3_
  16.6 2.2 %transform.3.w_ref = bf16[2,2,4,192,256]{4,3,2,1,0:T(8,128)(2,1)S(1)} custom-call(s32[2]{0:T(128)} %atom_hbm.3, bf16[2,16,64,64]{3,2,1,0:T(8,128)(2,1)} %occ_hbm.3, bf16[2,16,64,64]{3,2,1,0:T(8,128)(2,1)} %virt_hbm.3, bf16[2,2,4,192,256]{4,3,2,1,0:T(8,128)(2,1)S(1)} %get-tuple-element.25.refs_0_, ...), custom_call_target="tpu_custom_call", output_to_operand_aliasing={{}: (3, {})} | custom-call | flops 2147483648 | bytes 256 | tf_op jit(solution)/shard_map/transform/pallas_call | solution.py:129
  18.9 0.7 %far.1 = bf16[288,128]{1,0:T(8,128)(2,1)S(1)} custom-call(bf16[2,2,4,192,256]{4,3,2,1,0:T(8,128)(2,1)S(1)} %transform.3.w_ref, bf16[4,96,256]{2,1,0:T(8,128)(2,1)S(1)} %collective-permute-done.refs_0_, bf16[4,96,256]{2,1,0:T(8,128)(2,1)S(1)} %collective-permute-done.4.refs_1_), custom_call_target="tpu_custom_call" | custom-call | flops 1073741824 | bytes 256 | tf_op jit(solution)/shard_map/far/pallas_call | solution.py:203
  19.6 0.4 near.5.refs_0_
  20.0 0.0 collective-permute-done.5.refs_2_
  20.0 0.0 collective-permute-done.6.refs_3_
  20.0 0.4 near.4.refs_1_
  20.4 0.0 collective-permute-done.1.refs_0_
  20.4 0.6 %collective-permute-start.9 = (bf16[4,96,256]{2,1,0:T(8,128)(2,1)S(1)}, bf16[4,96,256]{2,1,0:T(8,128)(2,1)S(1)}, u32[]{:S(2)}, u32[]{:S(2)}) collective-permute-start(bf16[4,96,256]{2,1,0:T(8,128)(2,1)S(1)} %collective-permute-done.1.refs_0_), channel_id=1, source_target_pairs={{0,1},{1,0},{2,3},{3,2},{4,5},{5,4},{6,7},{7,6},{8,9},{9,8},{10,11... | collective-permute-start | bytes 589832 | tf_op jit(solution)/shard_map/ppermute | solution.py:298
  21.0 3.5 %collective-permute-start.8 = (bf16[288,128]{1,0:T(8,128)(2,1)S(1)}, bf16[288,128]{1,0:T(8,128)(2,1)S(1)}, u32[]{:S(2)}, u32[]{:S(2)}) collective-permute-start(bf16[288,128]{1,0:T(8,128)(2,1)S(1)} %far.1), channel_id=1, source_target_pairs={{0,6},{1,7},{2,0},{3,1},{4,2},{5,3},{6,4},{7,5},{8,14},{9,15},{10,... | collective-permute-start | bytes 221192 | tf_op jit(solution)/shard_map/ppermute | solution.py:320
  24.5 2.8 %collective-permute-done.8.refs_4_ = bf16[288,128]{1,0:T(8,128)(2,1)S(1)} collective-permute-done((bf16[288,128]{1,0:T(8,128)(2,1)S(1)}, bf16[288,128]{1,0:T(8,128)(2,1)S(1)}, u32[]{:S(2)}, u32[]{:S(2)}) %collective-permute-start.8) | collective-permute-done | bytes 73760 | tf_op jit(solution)/shard_map/ppermute | solution.py:320
  27.3 0.0 collective-permute-done.7.refs_0_
  27.3 0.0 collective-permute-done.9.refs_1_
  27.3 0.3 near.6.refs_2_
  27.6 0.0 copy-start
  27.6 0.1 collective-permute-start.10
  27.7 1.4 %collective-permute-done.10.refs_1_ = bf16[4,96,256]{2,1,0:T(8,128)(2,1)S(1)} collective-permute-done((bf16[4,96,256]{2,1,0:T(8,128)(2,1)S(1)}, bf16[4,96,256]{2,1,0:T(8,128)(2,1)S(1)}, u32[]{:S(2)}, u32[]{:S(2)}) %collective-permute-start.10) | collective-permute-done | bytes 196640 | tf_op jit(solution)/shard_map/ppermute | solution.py:298
  29.1 0.3 near.7.refs_3_
  29.4 0.1 pack.1
  29.6 2.5 %collective-permute-start.11 = (bf16[288,128]{1,0:T(8,128)(2,1)S(1)}, bf16[288,128]{1,0:T(8,128)(2,1)S(1)}, u32[]{:S(2)}, u32[]{:S(2)}) collective-permute-start(bf16[288,128]{1,0:T(8,128)(2,1)S(1)} %get-tuple-element.37), channel_id=1, source_target_pairs={{0,24},{8,16},{16,8},{24,0},{1,25},{9,17},{17,9},{25,1},{2,26},{10... | collective-permute-start | bytes 221192 | tf_op jit(solution)/shard_map/ppermute | solution.py:331
  32.1 0.5 collective-permute-start.12
  32.6 0.5 collective-permute-start.13
  33.1 1.8 %collective-permute-done.11.refs_1_ = bf16[288,128]{1,0:T(8,128)(2,1)S(1)} collective-permute-done((bf16[288,128]{1,0:T(8,128)(2,1)S(1)}, bf16[288,128]{1,0:T(8,128)(2,1)S(1)}, u32[]{:S(2)}, u32[]{:S(2)}) %collective-permute-start.11) | collective-permute-done | bytes 73760 | tf_op jit(solution)/shard_map/ppermute | solution.py:331
  34.9 1.5 %collective-permute-done.12.refs_2_ = bf16[288,128]{1,0:T(8,128)(2,1)S(1)} collective-permute-done((bf16[288,128]{1,0:T(8,128)(2,1)S(1)}, bf16[288,128]{1,0:T(8,128)(2,1)S(1)}, u32[]{:S(2)}, u32[]{:S(2)}) %collective-permute-start.12) | collective-permute-done | bytes 73760 | tf_op jit(solution)/shard_map/ppermute | solution.py:331
  36.5 0.5 collective-permute-done.13.refs_3_
  37.0 0.0 copy-done
  37.0 1.3 %finish.1 = (f32[2,96,192]{2,1,0:T(8,128)}, f32[32,128]{1,0:T(8,128)S(1)}) custom-call(f32[2]{0:T(128)S(1)} %copy-done, f32[288,128]{1,0:T(8,128)S(1)} %get-tuple-element.36.refs_0_, bf16[288,128]{1,0:T(8,128)(2,1)S(1)} %collective-permute-done.11.refs_1_, bf16[288,128]{1,0:T(8,128)(2,1)S(1)} %collective-permute-done.12.refs_2_, ...), custom_call_target="tpu_custom_call" | custom-call | flops 268435456 | bytes 256 | tf_op jit(solution)/shard_map/finish/pallas_call | solution.py:272
  38.3 11.7 %all_to_all.12 = f32[32,1,128]{2,1,0:T(1,128)S(1)} all-to-all(f32[32,1,128]{2,1,0:T(1,128)S(1)} %bitcast.4), channel_id=1, replica_groups=mesh['pair'=4,'aux'=8] {'pair','aux'}, dimensions={0} | all-to-all | bytes 32768 | tf_op jit(solution)/shard_map/all_to_all | solution.py:338
  50.0 0.6 %slice_reduce_fusion = f32[]{:T(128)} fusion(f32[32,128]{1,0:T(8,128)S(1)} %bitcast.5), kind=kLoop, calls=%fused_computation | loop fusion | flops 31 | bytes 132 | tf_op jit(solution)/shard_map/reduce_sum | solution.py:338
Async XLA Ops:
  2.0 10.8 %collective-permute-start = (bf16[4,96,256]{2,1,0:T(8,128)(2,1)S(1)}, bf16[4,96,256]{2,1,0:T(8,128)(2,1)S(1)}, u32[]{:S(2)}, u32[]{:S(2)}) collective-permute-start(bf16[4,96,256]{2,1,0:T(8,128)(2,1)S(1)} %arrange.2.refs_0_), channel_id=1, source_target_pairs={{0,2},{1,3},{2,4},{3,5},{4,6},{5,7},{6,0},{7,1},{8,10},{9,11},{10,... | collective-permute-start | bytes 589832 | tf_op jit(solution)/shard_map/ppermute | solution.py:301
  6.4 10.2 %collective-permute-start.4 = (bf16[4,96,256]{2,1,0:T(8,128)(2,1)S(1)}, bf16[4,96,256]{2,1,0:T(8,128)(2,1)S(1)}, u32[]{:S(2)}, u32[]{:S(2)}) collective-permute-start(bf16[4,96,256]{2,1,0:T(8,128)(2,1)S(1)} %arrange.3.refs_1_), channel_id=1, source_target_pairs={{0,2},{1,3},{2,4},{3,5},{4,6},{5,7},{6,0},{7,1},{8,10},{9,11},{10,... | collective-permute-start | bytes 589832 | tf_op jit(solution)/shard_map/ppermute | solution.py:301
  10.7 5.9 %collective-permute-start.2 = (bf16[4,96,256]{2,1,0:T(8,128)(2,1)S(1)}, bf16[4,96,256]{2,1,0:T(8,128)(2,1)S(1)}, u32[]{:S(2)}, u32[]{:S(2)}) collective-permute-start(bf16[4,96,256]{2,1,0:T(8,128)(2,1)S(1)} %arrange.2.refs_0_), channel_id=1, source_target_pairs={{0,1},{1,0},{2,3},{3,2},{4,5},{5,4},{6,7},{7,6},{8,9},{9,8},{10,11... | collective-permute-start | bytes 589832 | tf_op jit(solution)/shard_map/ppermute | solution.py:298
  10.7 5.9 %collective-permute-start.3 = (bf16[4,96,256]{2,1,0:T(8,128)(2,1)S(1)}, bf16[4,96,256]{2,1,0:T(8,128)(2,1)S(1)}, u32[]{:S(2)}, u32[]{:S(2)}) collective-permute-start(bf16[4,96,256]{2,1,0:T(8,128)(2,1)S(1)} %arrange.3.refs_1_), channel_id=1, source_target_pairs={{0,1},{1,0},{2,3},{3,2},{4,5},{5,4},{6,7},{7,6},{8,9},{9,8},{10,11... | collective-permute-start | bytes 589832 | tf_op jit(solution)/shard_map/ppermute | solution.py:298
  12.8 7.6 %collective-permute-start.1 = (bf16[4,96,256]{2,1,0:T(8,128)(2,1)S(1)}, bf16[4,96,256]{2,1,0:T(8,128)(2,1)S(1)}, u32[]{:S(2)}, u32[]{:S(2)}) collective-permute-start(bf16[4,96,256]{2,1,0:T(8,128)(2,1)S(1)} %collective-permute-done.refs_0_), channel_id=1, source_target_pairs={{0,2},{1,3},{2,4},{3,5},{4,6},{5,7},{6,0},{7,1},{8,10},{9,11},{10,... | collective-permute-start | bytes 589832 | tf_op jit(solution)/shard_map/ppermute | solution.py:310
  12.8 7.1 %collective-permute-start.5 = (bf16[4,96,256]{2,1,0:T(8,128)(2,1)S(1)}, bf16[4,96,256]{2,1,0:T(8,128)(2,1)S(1)}, u32[]{:S(2)}, u32[]{:S(2)}) collective-permute-start(bf16[4,96,256]{2,1,0:T(8,128)(2,1)S(1)} %collective-permute-done.refs_0_), channel_id=1, source_target_pairs={{0,1},{1,0},{2,3},{3,2},{4,5},{5,4},{6,7},{7,6},{8,9},{9,8},{10,11... | collective-permute-start | bytes 589832 | tf_op jit(solution)/shard_map/ppermute | solution.py:298
  16.6 3.4 %collective-permute-start.6 = (bf16[4,96,256]{2,1,0:T(8,128)(2,1)S(1)}, bf16[4,96,256]{2,1,0:T(8,128)(2,1)S(1)}, u32[]{:S(2)}, u32[]{:S(2)}) collective-permute-start(bf16[4,96,256]{2,1,0:T(8,128)(2,1)S(1)} %collective-permute-done.4.refs_1_), channel_id=1, source_target_pairs={{0,1},{1,0},{2,3},{3,2},{4,5},{5,4},{6,7},{7,6},{8,9},{9,8},{10,11... | collective-permute-start | bytes 589832 | tf_op jit(solution)/shard_map/ppermute | solution.py:298
  16.6 10.7 %collective-permute-start.7 = (bf16[4,96,256]{2,1,0:T(8,128)(2,1)S(1)}, bf16[4,96,256]{2,1,0:T(8,128)(2,1)S(1)}, u32[]{:S(2)}, u32[]{:S(2)}) collective-permute-start(bf16[4,96,256]{2,1,0:T(8,128)(2,1)S(1)} %collective-permute-done.4.refs_1_), channel_id=1, source_target_pairs={{0,2},{1,3},{2,4},{3,5},{4,6},{5,7},{6,0},{7,1},{8,10},{9,11},{10,... | collective-permute-start | bytes 589832 | tf_op jit(solution)/shard_map/ppermute | solution.py:310
  20.4 6.9 %collective-permute-start.9 = (bf16[4,96,256]{2,1,0:T(8,128)(2,1)S(1)}, bf16[4,96,256]{2,1,0:T(8,128)(2,1)S(1)}, u32[]{:S(2)}, u32[]{:S(2)}) collective-permute-start(bf16[4,96,256]{2,1,0:T(8,128)(2,1)S(1)} %collective-permute-done.1.refs_0_), channel_id=1, source_target_pairs={{0,1},{1,0},{2,3},{3,2},{4,5},{5,4},{6,7},{7,6},{8,9},{9,8},{10,11... | collective-permute-start | bytes 589832 | tf_op jit(solution)/shard_map/ppermute | solution.py:298
  21.0 6.3 %collective-permute-start.8 = (bf16[288,128]{1,0:T(8,128)(2,1)S(1)}, bf16[288,128]{1,0:T(8,128)(2,1)S(1)}, u32[]{:S(2)}, u32[]{:S(2)}) collective-permute-start(bf16[288,128]{1,0:T(8,128)(2,1)S(1)} %far.1), channel_id=1, source_target_pairs={{0,6},{1,7},{2,0},{3,1},{4,2},{5,3},{6,4},{7,5},{8,14},{9,15},{10,... | collective-permute-start | bytes 221192 | tf_op jit(solution)/shard_map/ppermute | solution.py:320
  27.6 9.3 %copy-start = (f32[2]{0:T(128)S(1)}, f32[2]{0:T(128)}, u32[]{:S(2)}) copy-start(f32[2]{0:T(128)} %weight_ref.1) | copy-start | bytes 28
  27.6 1.5 %collective-permute-start.10 = (bf16[4,96,256]{2,1,0:T(8,128)(2,1)S(1)}, bf16[4,96,256]{2,1,0:T(8,128)(2,1)S(1)}, u32[]{:S(2)}, u32[]{:S(2)}) collective-permute-start(bf16[4,96,256]{2,1,0:T(8,128)(2,1)S(1)} %collective-permute-done.7.refs_0_), channel_id=1, source_target_pairs={{0,1},{1,0},{2,3},{3,2},{4,5},{5,4},{6,7},{7,6},{8,9},{9,8},{10,11... | collective-permute-start | bytes 589832 | tf_op jit(solution)/shard_map/ppermute | solution.py:298
  29.6 5.4 %collective-permute-start.11 = (bf16[288,128]{1,0:T(8,128)(2,1)S(1)}, bf16[288,128]{1,0:T(8,128)(2,1)S(1)}, u32[]{:S(2)}, u32[]{:S(2)}) collective-permute-start(bf16[288,128]{1,0:T(8,128)(2,1)S(1)} %get-tuple-element.37), channel_id=1, source_target_pairs={{0,24},{8,16},{16,8},{24,0},{1,25},{9,17},{17,9},{25,1},{2,26},{10... | collective-permute-start | bytes 221192 | tf_op jit(solution)/shard_map/ppermute | solution.py:331
  32.1 4.4 %collective-permute-start.12 = (bf16[288,128]{1,0:T(8,128)(2,1)S(1)}, bf16[288,128]{1,0:T(8,128)(2,1)S(1)}, u32[]{:S(2)}, u32[]{:S(2)}) collective-permute-start(bf16[288,128]{1,0:T(8,128)(2,1)S(1)} %get-tuple-element.38), channel_id=1, source_target_pairs={{0,16},{8,24},{16,0},{24,8},{1,17},{9,25},{17,1},{25,9},{2,18},{10... | collective-permute-start | bytes 221192 | tf_op jit(solution)/shard_map/ppermute | solution.py:331
  32.6 4.4 %collective-permute-start.13 = (bf16[288,128]{1,0:T(8,128)(2,1)S(1)}, bf16[288,128]{1,0:T(8,128)(2,1)S(1)}, u32[]{:S(2)}, u32[]{:S(2)}) collective-permute-start(bf16[288,128]{1,0:T(8,128)(2,1)S(1)} %get-tuple-element.39), channel_id=1, source_target_pairs={{0,8},{8,0},{16,24},{24,16},{1,9},{9,1},{17,25},{25,17},{2,10},{10... | collective-permute-start | bytes 221192 | tf_op jit(solution)/shard_map/ppermute | solution.py:331

commit v7 on v6

--- a/solution.py
+++ b/solution.py
@@ -75,10 +75,9 @@
     )(stay(integrals), stay(block_mask))
 
 
-def transform_kernel(nt, rows, own, atom_hbm, occ_hbm, virt_hbm, *refs):
-    parts, (w_ref, atom_ref, occ_ref, virt_ref, arrived) = refs[:-5], refs[-5:]
-    pieces, z_ref = (parts[:2], parts[2]) if own else (parts[1:], None)
-    steps, aux, wide = pieces[0].shape
+def transform_kernel(nt, rows, atom_hbm, occ_hbm, virt_hbm, y1, y2, o1, o2, z_ref, w_ref, *scratch):
+    atom_ref, occ_ref, virt_ref, arrived = scratch
+    steps, aux, wide = y1.shape
     copies = wide // BLK
     copy = pltpu.make_async_copy(atom_hbm, atom_ref, arrived.at[0])
     copy.start()
@@ -93,8 +92,6 @@
     for copy in fetch:
         copy.wait()
     core = lax.rem(lax.axis_index("aux"), 2)
-    core = core if own else 1 - core
-    place = pl.ds(pl.multiple_of(core * aux, aux), aux)
     same = (
         lax.broadcasted_iota(jnp.int32, (wide, wide), 0) // BLK
         == lax.broadcasted_iota(jnp.int32, (wide, wide), 1) // BLK
@@ -112,43 +109,43 @@
 
     for t in range(nt):
         occ, virt = diagonal(occ_ref[t]), diagonal(virt_ref[t])
-        for half in range(2):
-            y = pieces[half][...].reshape(steps * aux, wide)
-            if own:
-                z_ref[half, :, t * aux:(t + 1) * aux, :] = through(y, occ, virt)
-            w_ref[half, t, :, place, :] = through(y, virt, occ)
-
-
-def transform(atom, green_occ, green_virt, rows, pieces, before=None):
+        for half, pieces in enumerate(((y1, o1), (y2, o2))):
+            for which, piece in enumerate(pieces):
+                y = piece[...].reshape(steps * aux, wide)
+                if which == 0:
+                    z_ref[half, :, t * aux:(t + 1) * aux, :] = through(y, occ, virt)
+                place = jnp.bitwise_xor(core, which) * aux
+                w_ref[half, t, :, pl.ds(pl.multiple_of(place, aux), aux), :] = through(y, virt, occ)
+
+
+def transform(atom, green_occ, green_virt, rows, own, sibling):
     nt = green_occ.shape[0]
-    steps, aux, wide = pieces[0].shape
-    own = before is None
-    w_shape = jax.ShapeDtypeStruct((2, nt, steps, 2 * aux, wide), jnp.bfloat16)
-    z_shape = jax.ShapeDtypeStruct((2, steps, nt * aux, wide), jnp.bfloat16)
-    operands = (stay(atom), stay(green_occ), stay(green_virt), *(() if own else (before,)), *pieces)
-    return call(
-        functools.partial(transform_kernel, nt, rows, own),
+    steps, aux, wide = own[0].shape
+    return call(
+        functools.partial(transform_kernel, nt, rows),
         "transform",
         2 << 30,
-        out_shape=(z_shape, w_shape) if own else w_shape,
-        in_specs=[HBM] * 3 + [VMEM] * (len(operands) - 3),
-        out_specs=(VMEM, VMEM) if own else VMEM,
-        input_output_aliases={} if own else {3: 0},
+        out_shape=(
+            jax.ShapeDtypeStruct((2, steps, nt * aux, wide), jnp.bfloat16),
+            jax.ShapeDtypeStruct((2, nt, steps, 2 * aux, wide), jnp.bfloat16),
+        ),
+        in_specs=[HBM] * 3 + [VMEM] * 4,
+        out_specs=(VMEM, VMEM),
         scratch_shapes=[
             pltpu.SMEM(atom.shape, jnp.int32),
             pltpu.VMEM((nt, BLK, BLK), jnp.bfloat16),
             pltpu.VMEM((nt, BLK, BLK), jnp.bfloat16),
             pltpu.SemaphoreType.DMA((2,)),
         ],
-    )(*operands)
-
-
-def near_kernel(count, start, z_ref, *refs):
+    )(stay(atom), stay(green_occ), stay(green_virt), *own, *sibling)
+
+
+def near_kernel(count, z_ref, *refs):
     mine, other, out_ref = refs[:count], refs[count:2 * count], refs[-1]
 
     def products(low, high):
         total = jnp.zeros(out_ref.shape, jnp.float32)
-        for half, (first, second) in enumerate(zip(low, high), start):
+        for half, (first, second) in enumerate(zip(low, high)):
             for j in range(z_ref.shape[1]):
                 partner = jnp.concatenate([first[j], second[j]], axis=0)
                 total += lax.dot_general(z_ref[half, j], partner, NT_DIMS, preferred_element_type=jnp.float32)
@@ -159,10 +156,10 @@
     pl.when(core == 1)(lambda: products(other, mine))
 
 
-def near(z, mine, other, start=0):
+def near(z, mine, other):
     size = z.shape[2]
     return call(
-        functools.partial(near_kernel, len(mine), start),
+        functools.partial(near_kernel, len(mine)),
         "near",
         1 << 30,
         out_shape=jax.ShapeDtypeStruct((size, 2 * mine[0].shape[-2]), jnp.float32),
@@ -211,12 +208,11 @@
 
 
 def pack_kernel(chips, pairs, *refs):
-    backs, lower, aheads = refs[:chips // 2 + 1], refs[chips // 2 + 1], refs[chips // 2 + 2:chips + 1]
-    outs, shares = refs[chips + 1:-1], refs[-1]
+    backs, aheads = refs[:chips // 2 + 1], refs[chips // 2 + 1:chips]
+    outs, shares = refs[chips:-1], refs[-1]
     chip = chip_of()
     for step in range(chips // 2 + 1):
-        share = backs[step][...] if step < chips // 2 else backs[step][...] + lower[...]
-        shares[lax.rem(chip + chips - step, chips)] = fold(share)
+        shares[lax.rem(chip + chips - step, chips)] = fold(backs[step][...])
     for step in range(1, chips // 2):
         shares[lax.rem(chip + step, chips)] = aheads[step - 1][...].astype(jnp.float32)
     if pairs is None:
@@ -241,7 +237,7 @@
         "pack",
         1 << 28,
         out_shape=out_shape,
-        in_specs=[VMEM] * (chips + 1),
+        in_specs=[VMEM] * chips,
         out_specs=(VMEM,) * len(out_shape),
         scratch_shapes=[pltpu.VMEM((chips,) + folded, jnp.float32)],
     )(*backs, *aheads)
@@ -299,30 +295,24 @@
 
     own = [arrange(integrals, block_mask, second) for second in (False, True)]
     arriving = [lax.ppermute(a, "aux", along(1)) for a in own]
-    z, w = transform(block_atom, green_occ, green_virt, rows, own)
-    *later, z = lax.optimization_barrier((*own, z))
-    arriving[0], z = lax.optimization_barrier((arriving[0], z))
+    *later, arriving[0] = lax.optimization_barrier((*own, arriving[0]))
     sibling = [to_sibling(a) for a in later]
+    z, w = transform(block_atom, green_occ, green_virt, rows, own, sibling)
     backs, aheads = [], []
     for step in range(1, chips // 2 + 1):
         held, last = arriving, step == chips // 2
         if not last:
             arriving = [lax.ppermute(a, "aux", along(1)) for a in held]
         if last:
-            upper = near(z, held[:1], [to_sibling(held[0])])
-            later, upper = lax.optimization_barrier((held[1], upper))
-            backs += [upper, near(z, [later], [to_sibling(later)], 1)]
+            backs.append(near(z, held, [to_sibling(a) for a in held]))
             continue
         other = [to_sibling(a) for a in held]
-        if step == 1:
-            w = transform(block_atom, green_occ, green_virt, rows, sibling, w)
         share = far(w, held)
         ahead = lax.ppermute(share, "aux", along(-step))
         if step == 1:
             backs.append(near(z, own, sibling))
         backs.append(near(z, held, other))
-        arriving[0], _, backs[-1], backs[-2] = lax.optimization_barrier((arriving[0], share, backs[-1], backs[-2]))
-        arriving[1], ahead = lax.optimization_barrier((arriving[1], ahead))
+        *arriving, ahead, backs[-1], backs[-2] = lax.optimization_barrier((*arriving, ahead, backs[-1], backs[-2]))
         aheads.append(ahead)
     if columns == 2 * aux_here and pairs & (pairs - 1) == 0:
         mine, *sends = pack(chips, pairs, backs, aheads)

time: 52.7 us -> 52.2 us (level)
  waiting for transfers between devices: 13.4 us -> 16 us
  Pallas kernels: 11.1 us -> 9.04 us
  blocking collectives: 11.7 us -> 10.6 us
    ppermute x2, waiting for transfers between devices: 5.33 us -> 7.62 us  [per_device(): arriving = [lax.ppermute(a, 'aux', along(1)) for a in own]]
    ppermute x2, waiting for transfers between devices: 0.01 us -> 2.27 us  [per_device(): arriving = [lax.ppermute(a, 'aux', along(1)) for a in held]]
    ppermute x1, waiting for transfers between devices: 2.8 us -> 0.78 us  [per_device(): ahead = lax.ppermute(share, 'aux', along(-step))]
    pallas_call x6 -> x4, Pallas kernels: 6.23 us -> 4.22 us  [the longest x1 3.05 us: transform(): call(functools.partial(transform_kernel, nt, rows), 'transform', 2 << 30,...]
    all_to_all x1, blocking collectives: 11.7 us -> 10.6 us  [per_device(): lax.all_to_all(sums, ('pair', 'aux'), 0, 0, tiled=True)[:, 0]]
  transfers between devices with their start and end apart: 14 -> 14, of which waited for: 7 -> 9; matrix products, arithmetic and copies ran while one was open for 0% -> 0% of each run, Pallas kernels for 15% -> 11%
where the time goes in v7:
time: 52.2 us; the launch traced here: 51.9 us
  waiting for transfers between devices  16 us (31%)
  starting transfers between devices  13.2 us (25%)
  blocking collectives  10.6 us (20%)
  Pallas kernels  9.04 us (17%)
  between operations  2.52 us (5%)
  other arithmetic  0.6 us (1%)
    all_to_all x1, blocking collectives, per_device(): lax.all_to_all(sums, ('pair', 'aux'), 0, 0, tiled=True)[:, 0]  10.6 us
    ppermute x2, waiting for transfers between devices, per_device(): arriving = [lax.ppermute(a, 'aux', along(1)) for a in own]  7.62 us
    ppermute x2, starting transfers between devices, per_device(): arriving = [lax.ppermute(a, 'aux', along(1)) for a in own]  4.71 us
    ppermute x3, waiting for transfers between devices, per_device(): lax.ppermute(sends[j - 1], 'pair', [(i, i ^ j) for i in range(pairs)])  4.07 us
    ppermute x1, starting transfers between devices, per_device(): ahead = lax.ppermute(share, 'aux', along(-step))  3.85 us
    ppermute x3, starting transfers between devices, per_device(): lax.ppermute(sends[j - 1], 'pair', [(i, i ^ j) for i in range(pairs)])  3.55 us
    pallas_call x1, Pallas kernels, transform(): call(functools.partial(transform_kernel, nt, rows), 'transform', 2 << 30,...  3.05 us
    pallas_call x2, Pallas kernels, arrange(): call(functools.partial(arrange_kernel, rows, aux, second), 'arrange', 1 <...  2.67 us
  transfers between devices with their start and end apart: 14, of which 9 were waited for; matrix products, arithmetic and copies ran while one was open for 0% of the time, Pallas kernels for 11%

profile of v7, /device:TPU:0, one launch (start us, length us, event | category | flops | bytes accessed | tf_op | source)
XLA Modules:
  0.0 51.9 jit_solution(4643696601182875033)
XLA Ops:
  0.6 1.3 %arrange.2.y1.refs_0_ = bf16[4,96,256]{2,1,0:T(8,128)(2,1)S(1)} custom-call(bf16[32,6144]{1,0:T(8,128)(2,1)} %x_hbm.3, s32[2,96]{1,0:T(2,128)} %mask_hbm.3), custom_call_target="tpu_custom_call" | custom-call | flops 268435456 | bytes 256 | tf_op jit(solution)/shard_map/arrange/pallas_call | solution.py:62
  2.0 3.1 %collective-permute-start = (bf16[4,96,256]{2,1,0:T(8,128)(2,1)S(1)}, bf16[4,96,256]{2,1,0:T(8,128)(2,1)S(1)}, u32[]{:S(2)}, u32[]{:S(2)}) collective-permute-start(bf16[4,96,256]{2,1,0:T(8,128)(2,1)S(1)} %arrange.2.y1.refs_0_), channel_id=1, source_target_pairs={{0,2},{1,3},{2,4},{3,5},{4,6},{5,7},{6,0},{7,1},{8,10},{9,11},{10,... | collective-permute-start | bytes 589832 | tf_op jit(solution)/shard_map/ppermute | solution.py:297
  5.0 1.3 %arrange.3.y2.refs_1_ = bf16[4,96,256]{2,1,0:T(8,128)(2,1)S(1)} custom-call(bf16[32,6144]{1,0:T(8,128)(2,1)} %x_hbm.3, s32[2,96]{1,0:T(2,128)} %mask_hbm.3), custom_call_target="tpu_custom_call" | custom-call | flops 268435456 | bytes 256 | tf_op jit(solution)/shard_map/arrange/pallas_call | solution.py:62
  6.4 1.6 %collective-permute-start.2 = (bf16[4,96,256]{2,1,0:T(8,128)(2,1)S(1)}, bf16[4,96,256]{2,1,0:T(8,128)(2,1)S(1)}, u32[]{:S(2)}, u32[]{:S(2)}) collective-permute-start(bf16[4,96,256]{2,1,0:T(8,128)(2,1)S(1)} %arrange.3.y2.refs_1_), channel_id=1, source_target_pairs={{0,2},{1,3},{2,4},{3,5},{4,6},{5,7},{6,0},{7,1},{8,10},{9,11},{10,... | collective-permute-start | bytes 589832 | tf_op jit(solution)/shard_map/ppermute | solution.py:297
  8.0 4.8 %collective-permute-done.refs_0_ = bf16[4,96,256]{2,1,0:T(8,128)(2,1)S(1)} collective-permute-done((bf16[4,96,256]{2,1,0:T(8,128)(2,1)S(1)}, bf16[4,96,256]{2,1,0:T(8,128)(2,1)S(1)}, u32[]{:S(2)}, u32[]{:S(2)}) %collective-permute-start) | collective-permute-done | bytes 196640 | tf_op jit(solution)/shard_map/ppermute | solution.py:297
  12.8 0.0 collective-permute-start.4
  12.8 0.5 collective-permute-start.5
  13.3 0.0 collective-permute-start.1
  13.3 0.0 collective-permute-start.7
  13.4 2.8 %collective-permute-done.2.refs_1_ = bf16[4,96,256]{2,1,0:T(8,128)(2,1)S(1)} collective-permute-done((bf16[4,96,256]{2,1,0:T(8,128)(2,1)S(1)}, bf16[4,96,256]{2,1,0:T(8,128)(2,1)S(1)}, u32[]{:S(2)}, u32[]{:S(2)}) %collective-permute-start.2) | collective-permute-done | bytes 196640 | tf_op jit(solution)/shard_map/ppermute | solution.py:297
  16.2 0.0 collective-permute-start.3
  16.2 0.0 collective-permute-done.4.o1.refs_2_
  16.2 0.0 collective-permute-start.8
  16.2 0.0 collective-permute-done.5.o2.refs_3_
  16.2 3.0 %transform.1 = (bf16[2,4,192,256]{3,2,1,0:T(8,128)(2,1)S(1)}, bf16[2,2,4,192,256]{4,3,2,1,0:T(8,128)(2,1)S(1)}) custom-call(s32[2]{0:T(128)} %atom_hbm.1, bf16[2,16,64,64]{3,2,1,0:T(8,128)(2,1)} %occ_hbm.1, bf16[2,16,64,64]{3,2,1,0:T(8,128)(2,1)} %virt_hbm.1, bf16[4,96,256]{2,1,0:T(8,128)(2,1)S(1)} %arrange.2.y1.refs_0_, ...), custom_call_target="tpu_custom_call" | custom-call | flops 2147483648 | bytes 256 | tf_op jit(solution)/shard_map/transform/pallas_call | solution.py:124
  19.3 0.7 %far.1 = bf16[288,128]{1,0:T(8,128)(2,1)S(1)} custom-call(bf16[2,2,4,192,256]{4,3,2,1,0:T(8,128)(2,1)S(1)} %get-tuple-element.21.w_ref, bf16[4,96,256]{2,1,0:T(8,128)(2,1)S(1)} %collective-permute-done.refs_0_, bf16[4,96,256]{2,1,0:T(8,128)(2,1)S(1)} %collective-permute-done.2.refs_1_), custom_call_target="tpu_custom_call" | custom-call | flops 1073741824 | bytes 256 | tf_op jit(solution)/shard_map/far/pallas_call | solution.py:200
  20.0 3.9 %collective-permute-start.6 = (bf16[288,128]{1,0:T(8,128)(2,1)S(1)}, bf16[288,128]{1,0:T(8,128)(2,1)S(1)}, u32[]{:S(2)}, u32[]{:S(2)}) collective-permute-start(bf16[288,128]{1,0:T(8,128)(2,1)S(1)} %far.1), channel_id=1, source_target_pairs={{0,6},{1,7},{2,0},{3,1},{4,2},{5,3},{6,4},{7,5},{8,14},{9,15},{10,... | collective-permute-start | bytes 221192 | tf_op jit(solution)/shard_map/ppermute | solution.py:311
  23.8 0.4 near.4.refs_0_
  24.2 0.0 collective-permute-done.7.refs_2_
  24.2 0.0 collective-permute-done.8.refs_3_
  24.2 0.4 near.3.refs_1_
  24.6 0.0 copy-start
  24.7 0.0 collective-permute-done.1.refs_0_
  24.7 2.3 %collective-permute-done.3.refs_1_ = bf16[4,96,256]{2,1,0:T(8,128)(2,1)S(1)} collective-permute-done((bf16[4,96,256]{2,1,0:T(8,128)(2,1)S(1)}, bf16[4,96,256]{2,1,0:T(8,128)(2,1)S(1)}, u32[]{:S(2)}, u32[]{:S(2)}) %collective-permute-start.3) | collective-permute-done | bytes 196640 | tf_op jit(solution)/shard_map/ppermute | solution.py:305
  26.9 0.8 %collective-permute-done.6.refs_3_ = bf16[288,128]{1,0:T(8,128)(2,1)S(1)} collective-permute-done((bf16[288,128]{1,0:T(8,128)(2,1)S(1)}, bf16[288,128]{1,0:T(8,128)(2,1)S(1)}, u32[]{:S(2)}, u32[]{:S(2)}) %collective-permute-start.6) | collective-permute-done | bytes 73760 | tf_op jit(solution)/shard_map/ppermute | solution.py:311
  27.7 0.1 collective-permute-start.9
  27.8 0.4 collective-permute-start.10
  28.2 0.9 %collective-permute-done.9.refs_2_ = bf16[4,96,256]{2,1,0:T(8,128)(2,1)S(1)} collective-permute-done((bf16[4,96,256]{2,1,0:T(8,128)(2,1)S(1)}, bf16[4,96,256]{2,1,0:T(8,128)(2,1)S(1)}, u32[]{:S(2)}, u32[]{:S(2)}) %collective-permute-start.9) | collective-permute-done | bytes 196640 | tf_op jit(solution)/shard_map/ppermute | solution.py:294
  29.2 0.3 collective-permute-done.10.refs_3_
  29.4 0.4 near.5.refs_2_
  29.8 0.1 pack.1
  30.0 2.8 %collective-permute-start.11 = (bf16[288,128]{1,0:T(8,128)(2,1)S(1)}, bf16[288,128]{1,0:T(8,128)(2,1)S(1)}, u32[]{:S(2)}, u32[]{:S(2)}) collective-permute-start(bf16[288,128]{1,0:T(8,128)(2,1)S(1)} %get-tuple-element.29), channel_id=1, source_target_pairs={{0,24},{8,16},{16,8},{24,0},{1,25},{9,17},{17,9},{25,1},{2,26},{10... | collective-permute-start | bytes 221192 | tf_op jit(solution)/shard_map/ppermute | solution.py:321
  32.7 0.5 collective-permute-start.12
  33.3 0.3 collective-permute-start.13
  33.5 1.9 %collective-permute-done.11.refs_1_ = bf16[288,128]{1,0:T(8,128)(2,1)S(1)} collective-permute-done((bf16[288,128]{1,0:T(8,128)(2,1)S(1)}, bf16[288,128]{1,0:T(8,128)(2,1)S(1)}, u32[]{:S(2)}, u32[]{:S(2)}) %collective-permute-start.11) | collective-permute-done | bytes 73760 | tf_op jit(solution)/shard_map/ppermute | solution.py:321
  35.4 1.7 %collective-permute-done.12.refs_2_ = bf16[288,128]{1,0:T(8,128)(2,1)S(1)} collective-permute-done((bf16[288,128]{1,0:T(8,128)(2,1)S(1)}, bf16[288,128]{1,0:T(8,128)(2,1)S(1)}, u32[]{:S(2)}, u32[]{:S(2)}) %collective-permute-start.12) | collective-permute-done | bytes 73760 | tf_op jit(solution)/shard_map/ppermute | solution.py:321
  37.1 0.5 collective-permute-done.13.refs_3_
  37.6 0.0 copy-done
  37.6 1.3 %finish.1 = (f32[2,96,192]{2,1,0:T(8,128)}, f32[32,128]{1,0:T(8,128)S(1)}) custom-call(f32[2]{0:T(128)S(1)} %copy-done, f32[288,128]{1,0:T(8,128)S(1)} %get-tuple-element.28.refs_0_, bf16[288,128]{1,0:T(8,128)(2,1)S(1)} %collective-permute-done.11.refs_1_, bf16[288,128]{1,0:T(8,128)(2,1)S(1)} %collective-permute-done.12.refs_2_, ...), custom_call_target="tpu_custom_call" | custom-call | flops 268435456 | bytes 256 | tf_op jit(solution)/shard_map/finish/pallas_call | solution.py:268
  38.9 10.6 %all_to_all.12 = f32[32,1,128]{2,1,0:T(1,128)S(1)} all-to-all(f32[32,1,128]{2,1,0:T(1,128)S(1)} %bitcast.4), channel_id=1, replica_groups=mesh['pair'=4,'aux'=8] {'pair','aux'}, dimensions={0} | all-to-all | bytes 32768 | tf_op jit(solution)/shard_map/all_to_all | solution.py:328
  49.5 0.6 %slice_reduce_fusion = f32[]{:T(128)} fusion(f32[32,128]{1,0:T(8,128)S(1)} %bitcast.5), kind=kLoop, calls=%fused_computation | loop fusion | flops 31 | bytes 132 | tf_op jit(solution)/shard_map/reduce_sum | solution.py:328
Async XLA Ops:
  2.0 10.8 %collective-permute-start = (bf16[4,96,256]{2,1,0:T(8,128)(2,1)S(1)}, bf16[4,96,256]{2,1,0:T(8,128)(2,1)S(1)}, u32[]{:S(2)}, u32[]{:S(2)}) collective-permute-start(bf16[4,96,256]{2,1,0:T(8,128)(2,1)S(1)} %arrange.2.y1.refs_0_), channel_id=1, source_target_pairs={{0,2},{1,3},{2,4},{3,5},{4,6},{5,7},{6,0},{7,1},{8,10},{9,11},{10,... | collective-permute-start | bytes 589832 | tf_op jit(solution)/shard_map/ppermute | solution.py:297
  6.4 9.8 %collective-permute-start.2 = (bf16[4,96,256]{2,1,0:T(8,128)(2,1)S(1)}, bf16[4,96,256]{2,1,0:T(8,128)(2,1)S(1)}, u32[]{:S(2)}, u32[]{:S(2)}) collective-permute-start(bf16[4,96,256]{2,1,0:T(8,128)(2,1)S(1)} %arrange.3.y2.refs_1_), channel_id=1, source_target_pairs={{0,2},{1,3},{2,4},{3,5},{4,6},{5,7},{6,0},{7,1},{8,10},{9,11},{10,... | collective-permute-start | bytes 589832 | tf_op jit(solution)/shard_map/ppermute | solution.py:297
  12.8 3.4 %collective-permute-start.4 = (bf16[4,96,256]{2,1,0:T(8,128)(2,1)S(1)}, bf16[4,96,256]{2,1,0:T(8,128)(2,1)S(1)}, u32[]{:S(2)}, u32[]{:S(2)}) collective-permute-start(bf16[4,96,256]{2,1,0:T(8,128)(2,1)S(1)} %arrange.2.y1.refs_0_), channel_id=1, source_target_pairs={{0,1},{1,0},{2,3},{3,2},{4,5},{5,4},{6,7},{7,6},{8,9},{9,8},{10,11... | collective-permute-start | bytes 589832 | tf_op jit(solution)/shard_map/ppermute | solution.py:294
  12.8 3.4 %collective-permute-start.5 = (bf16[4,96,256]{2,1,0:T(8,128)(2,1)S(1)}, bf16[4,96,256]{2,1,0:T(8,128)(2,1)S(1)}, u32[]{:S(2)}, u32[]{:S(2)}) collective-permute-start(bf16[4,96,256]{2,1,0:T(8,128)(2,1)S(1)} %arrange.3.y2.refs_1_), channel_id=1, source_target_pairs={{0,1},{1,0},{2,3},{3,2},{4,5},{5,4},{6,7},{7,6},{8,9},{9,8},{10,11... | collective-permute-start | bytes 589832 | tf_op jit(solution)/shard_map/ppermute | solution.py:294
  13.3 11.3 %collective-permute-start.1 = (bf16[4,96,256]{2,1,0:T(8,128)(2,1)S(1)}, bf16[4,96,256]{2,1,0:T(8,128)(2,1)S(1)}, u32[]{:S(2)}, u32[]{:S(2)}) collective-permute-start(bf16[4,96,256]{2,1,0:T(8,128)(2,1)S(1)} %collective-permute-done.refs_0_), channel_id=1, source_target_pairs={{0,2},{1,3},{2,4},{3,5},{4,6},{5,7},{6,0},{7,1},{8,10},{9,11},{10,... | collective-permute-start | bytes 589832 | tf_op jit(solution)/shard_map/ppermute | solution.py:305
  13.3 10.9 %collective-permute-start.7 = (bf16[4,96,256]{2,1,0:T(8,128)(2,1)S(1)}, bf16[4,96,256]{2,1,0:T(8,128)(2,1)S(1)}, u32[]{:S(2)}, u32[]{:S(2)}) collective-permute-start(bf16[4,96,256]{2,1,0:T(8,128)(2,1)S(1)} %collective-permute-done.refs_0_), channel_id=1, source_target_pairs={{0,1},{1,0},{2,3},{3,2},{4,5},{5,4},{6,7},{7,6},{8,9},{9,8},{10,11... | collective-permute-start | bytes 589832 | tf_op jit(solution)/shard_map/ppermute | solution.py:294
  16.2 10.7 %collective-permute-start.3 = (bf16[4,96,256]{2,1,0:T(8,128)(2,1)S(1)}, bf16[4,96,256]{2,1,0:T(8,128)(2,1)S(1)}, u32[]{:S(2)}, u32[]{:S(2)}) collective-permute-start(bf16[4,96,256]{2,1,0:T(8,128)(2,1)S(1)} %collective-permute-done.2.refs_1_), channel_id=1, source_target_pairs={{0,2},{1,3},{2,4},{3,5},{4,6},{5,7},{6,0},{7,1},{8,10},{9,11},{10,... | collective-permute-start | bytes 589832 | tf_op jit(solution)/shard_map/ppermute | solution.py:305
  16.2 8.0 %collective-permute-start.8 = (bf16[4,96,256]{2,1,0:T(8,128)(2,1)S(1)}, bf16[4,96,256]{2,1,0:T(8,128)(2,1)S(1)}, u32[]{:S(2)}, u32[]{:S(2)}) collective-permute-start(bf16[4,96,256]{2,1,0:T(8,128)(2,1)S(1)} %collective-permute-done.2.refs_1_), channel_id=1, source_target_pairs={{0,1},{1,0},{2,3},{3,2},{4,5},{5,4},{6,7},{7,6},{8,9},{9,8},{10,11... | collective-permute-start | bytes 589832 | tf_op jit(solution)/shard_map/ppermute | solution.py:294
  20.0 7.8 %collective-permute-start.6 = (bf16[288,128]{1,0:T(8,128)(2,1)S(1)}, bf16[288,128]{1,0:T(8,128)(2,1)S(1)}, u32[]{:S(2)}, u32[]{:S(2)}) collective-permute-start(bf16[288,128]{1,0:T(8,128)(2,1)S(1)} %far.1), channel_id=1, source_target_pairs={{0,6},{1,7},{2,0},{3,1},{4,2},{5,3},{6,4},{7,5},{8,14},{9,15},{10,... | collective-permute-start | bytes 221192 | tf_op jit(solution)/shard_map/ppermute | solution.py:311
  24.6 13.0 %copy-start = (f32[2]{0:T(128)S(1)}, f32[2]{0:T(128)}, u32[]{:S(2)}) copy-start(f32[2]{0:T(128)} %weight_ref.1) | copy-start | bytes 28
  27.7 1.4 %collective-permute-start.9 = (bf16[4,96,256]{2,1,0:T(8,128)(2,1)S(1)}, bf16[4,96,256]{2,1,0:T(8,128)(2,1)S(1)}, u32[]{:S(2)}, u32[]{:S(2)}) collective-permute-start(bf16[4,96,256]{2,1,0:T(8,128)(2,1)S(1)} %collective-permute-done.1.refs_0_), channel_id=1, source_target_pairs={{0,1},{1,0},{2,3},{3,2},{4,5},{5,4},{6,7},{7,6},{8,9},{9,8},{10,11... | collective-permute-start | bytes 589832 | tf_op jit(solution)/shard_map/ppermute | solution.py:294
  27.8 1.7 %collective-permute-start.10 = (bf16[4,96,256]{2,1,0:T(8,128)(2,1)S(1)}, bf16[4,96,256]{2,1,0:T(8,128)(2,1)S(1)}, u32[]{:S(2)}, u32[]{:S(2)}) collective-permute-start(bf16[4,96,256]{2,1,0:T(8,128)(2,1)S(1)} %collective-permute-done.3.refs_1_), channel_id=1, source_target_pairs={{0,1},{1,0},{2,3},{3,2},{4,5},{5,4},{6,7},{7,6},{8,9},{9,8},{10,11... | collective-permute-start | bytes 589832 | tf_op jit(solution)/shard_map/ppermute | solution.py:294
  30.0 5.4 %collective-permute-start.11 = (bf16[288,128]{1,0:T(8,128)(2,1)S(1)}, bf16[288,128]{1,0:T(8,128)(2,1)S(1)}, u32[]{:S(2)}, u32[]{:S(2)}) collective-permute-start(bf16[288,128]{1,0:T(8,128)(2,1)S(1)} %get-tuple-element.29), channel_id=1, source_target_pairs={{0,24},{8,16},{16,8},{24,0},{1,25},{9,17},{17,9},{25,1},{2,26},{10... | collective-permute-start | bytes 221192 | tf_op jit(solution)/shard_map/ppermute | solution.py:321
  32.7 4.4 %collective-permute-start.12 = (bf16[288,128]{1,0:T(8,128)(2,1)S(1)}, bf16[288,128]{1,0:T(8,128)(2,1)S(1)}, u32[]{:S(2)}, u32[]{:S(2)}) collective-permute-start(bf16[288,128]{1,0:T(8,128)(2,1)S(1)} %get-tuple-element.30), channel_id=1, source_target_pairs={{0,16},{8,24},{16,0},{24,8},{1,17},{9,25},{17,1},{25,9},{2,18},{10... | collective-permute-start | bytes 221192 | tf_op jit(solution)/shard_map/ppermute | solution.py:321
  33.3 4.4 %collective-permute-start.13 = (bf16[288,128]{1,0:T(8,128)(2,1)S(1)}, bf16[288,128]{1,0:T(8,128)(2,1)S(1)}, u32[]{:S(2)}, u32[]{:S(2)}) collective-permute-start(bf16[288,128]{1,0:T(8,128)(2,1)S(1)} %get-tuple-element.31), channel_id=1, source_target_pairs={{0,8},{8,0},{16,24},{24,16},{1,9},{9,1},{17,25},{25,17},{2,10},{10... | collective-permute-start | bytes 221192 | tf_op jit(solution)/shard_map/ppermute | solution.py:321

commit v8 on v7

--- a/solution.py
+++ b/solution.py
@@ -75,9 +75,22 @@
     )(stay(integrals), stay(block_mask))
 
 
-def transform_kernel(nt, rows, atom_hbm, occ_hbm, virt_hbm, y1, y2, o1, o2, z_ref, w_ref, *scratch):
+def through(y, first, second):
+    steps, aux, wide = y.shape
+    y = y[...].reshape(steps * aux, wide)
+    half = jnp.dot(y, first, preferred_element_type=jnp.float32).astype(jnp.bfloat16)
+    full = lax.dot_general(half, second, NT_DIMS, preferred_element_type=jnp.float32)
+    return full.astype(jnp.bfloat16).reshape(steps, aux, wide)
+
+
+def core_rows(aux, other):
+    core = jnp.bitwise_xor(lax.rem(lax.axis_index("aux"), 2), other)
+    return pl.ds(pl.multiple_of(core * aux, aux), aux)
+
+
+def transform_kernel(nt, rows, atom_hbm, occ_hbm, virt_hbm, y1, y2, z_ref, w_ref, green_ref, *scratch):
     atom_ref, occ_ref, virt_ref, arrived = scratch
-    steps, aux, wide = y1.shape
+    aux, wide = y1.shape[1:]
     copies = wide // BLK
     copy = pltpu.make_async_copy(atom_hbm, atom_ref, arrived.at[0])
     copy.start()
@@ -91,7 +104,6 @@
         copy.start()
     for copy in fetch:
         copy.wait()
-    core = lax.rem(lax.axis_index("aux"), 2)
     same = (
         lax.broadcasted_iota(jnp.int32, (wide, wide), 0) // BLK
         == lax.broadcasted_iota(jnp.int32, (wide, wide), 1) // BLK
@@ -102,23 +114,15 @@
         full = jnp.concatenate([tall] * copies, axis=1)
         return jnp.where(same, full, 0.0).astype(jnp.bfloat16)
 
-    def through(y, first, second):
-        half = jnp.dot(y, first, preferred_element_type=jnp.float32).astype(jnp.bfloat16)
-        full = lax.dot_general(half, second, NT_DIMS, preferred_element_type=jnp.float32)
-        return full.astype(jnp.bfloat16).reshape(steps, aux, wide)
-
     for t in range(nt):
         occ, virt = diagonal(occ_ref[t]), diagonal(virt_ref[t])
-        for half, pieces in enumerate(((y1, o1), (y2, o2))):
-            for which, piece in enumerate(pieces):
-                y = piece[...].reshape(steps * aux, wide)
-                if which == 0:
-                    z_ref[half, :, t * aux:(t + 1) * aux, :] = through(y, occ, virt)
-                place = jnp.bitwise_xor(core, which) * aux
-                w_ref[half, t, :, pl.ds(pl.multiple_of(place, aux), aux), :] = through(y, virt, occ)
-
-
-def transform(atom, green_occ, green_virt, rows, own, sibling):
+        green_ref[t, 0], green_ref[t, 1] = occ, virt
+        for half, y in enumerate((y1, y2)):
+            z_ref[half, :, t * aux:(t + 1) * aux, :] = through(y, occ, virt)
+            w_ref[half, t, :, core_rows(aux, 0), :] = through(y, virt, occ)
+
+
+def transform(atom, green_occ, green_virt, rows, own):
     nt = green_occ.shape[0]
     steps, aux, wide = own[0].shape
     return call(
@@ -128,16 +132,36 @@
         out_shape=(
             jax.ShapeDtypeStruct((2, steps, nt * aux, wide), jnp.bfloat16),
             jax.ShapeDtypeStruct((2, nt, steps, 2 * aux, wide), jnp.bfloat16),
+            jax.ShapeDtypeStruct((nt, 2, wide, wide), jnp.bfloat16),
         ),
-        in_specs=[HBM] * 3 + [VMEM] * 4,
-        out_specs=(VMEM, VMEM),
+        in_specs=[HBM] * 3 + [VMEM] * 2,
+        out_specs=(VMEM,) * 3,
         scratch_shapes=[
             pltpu.SMEM(atom.shape, jnp.int32),
             pltpu.VMEM((nt, BLK, BLK), jnp.bfloat16),
             pltpu.VMEM((nt, BLK, BLK), jnp.bfloat16),
             pltpu.SemaphoreType.DMA((2,)),
         ],
-    )(stay(atom), stay(green_occ), stay(green_virt), *own, *sibling)
+    )(stay(atom), stay(green_occ), stay(green_virt), *own)
+
+
+def complete_kernel(before_ref, green_ref, y1, y2, w_ref):
+    aux = y1.shape[1]
+    for t in range(green_ref.shape[0]):
+        for half, y in enumerate((y1, y2)):
+            w_ref[half, t, :, core_rows(aux, 1), :] = through(y, green_ref[t, 1], green_ref[t, 0])
+
+
+def complete(w, greens, sibling):
+    return call(
+        complete_kernel,
+        "complete",
+        1 << 30,
+        out_shape=jax.ShapeDtypeStruct(w.shape, w.dtype),
+        in_specs=[VMEM] * 4,
+        out_specs=VMEM,
+        input_output_aliases={0: 0},
+    )(w, greens, *sibling)
 
 
 def near_kernel(count, z_ref, *refs):
@@ -161,7 +185,7 @@
     return call(
         functools.partial(near_kernel, len(mine)),
         "near",
-        1 << 30,
+        1 << 29,
         out_shape=jax.ShapeDtypeStruct((size, 2 * mine[0].shape[-2]), jnp.float32),
         in_specs=[VMEM] * (1 + 2 * len(mine)),
         out_specs=VMEM,
@@ -200,7 +224,7 @@
     return call(
         far_kernel,
         "far",
-        1 << 30,
+        1 << 29,
         out_shape=jax.ShapeDtypeStruct((w.shape[1] * aux * 3 // 2, 128), jnp.bfloat16),
         in_specs=[VMEM] * (1 + len(mine)),
         out_specs=VMEM,
@@ -295,9 +319,11 @@
 
     own = [arrange(integrals, block_mask, second) for second in (False, True)]
     arriving = [lax.ppermute(a, "aux", along(1)) for a in own]
-    *later, arriving[0] = lax.optimization_barrier((*own, arriving[0]))
+    z, w, greens = transform(block_atom, green_occ, green_virt, rows, own)
+    *later, z = lax.optimization_barrier((*own, z))
+    arriving[0], z = lax.optimization_barrier((arriving[0], z))
     sibling = [to_sibling(a) for a in later]
-    z, w = transform(block_atom, green_occ, green_virt, rows, own, sibling)
+    w = complete(w, greens, sibling)
     backs, aheads = [], []
     for step in range(1, chips // 2 + 1):
         held, last = arriving, step == chips // 2

time: 52.2 us -> 50.5 us (0.967)
  blocking collectives: 10.6 us -> 8.86 us
    ppermute x1, waiting for transfers between devices: 0.78 us -> 5.42 us  [per_device(): ahead = lax.ppermute(share, 'aux', along(-step))]
    ppermute x2, waiting for transfers between devices: 7.62 us -> 4.79 us  [per_device(): arriving = [lax.ppermute(a, 'aux', along(1)) for a in own]]
    ppermute x2, waiting for transfers between devices: 2.27 us -> 0.01 us  [per_device(): arriving = [lax.ppermute(a, 'aux', along(1)) for a in held]]
    all_to_all x1, blocking collectives: 10.6 us -> 8.86 us  [per_device(): lax.all_to_all(sums, ('pair', 'aux'), 0, 0, tiled=True)[:, 0]]
    pallas_call x4 -> x5, Pallas kernels: 1.87 us -> 2.55 us  [the longest x3 1.18 us: near(): call(functools.partial(near_kernel, len(mine)), 'near', 1 << 29, out_shap...]
  transfers between devices with their start and end apart: 14 -> 14, of which waited for: 9 -> 8; matrix products, arithmetic and copies ran while one was open for 0% -> 0% of each run, Pallas kernels for 11% -> 12%
where the time goes in v8:
time: 50.5 us; the launch traced here: 50.2 us
  waiting for transfers between devices  15.5 us (31%)
  starting transfers between devices  13.3 us (26%)
  Pallas kernels  9.34 us (18%)
  blocking collectives  8.86 us (18%)
  between operations  2.53 us (5%)
  other arithmetic  0.6 us (1%)
    all_to_all x1, blocking collectives, per_device(): lax.all_to_all(sums, ('pair', 'aux'), 0, 0, tiled=True)[:, 0]  8.86 us
    ppermute x1, waiting for transfers between devices, per_device(): ahead = lax.ppermute(share, 'aux', along(-step))  5.42 us
    ppermute x2, waiting for transfers between devices, per_device(): arriving = [lax.ppermute(a, 'aux', along(1)) for a in own]  4.79 us
    ppermute x2, starting transfers between devices, per_device(): arriving = [lax.ppermute(a, 'aux', along(1)) for a in own]  4.71 us
    ppermute x3, waiting for transfers between devices, per_device(): lax.ppermute(sends[j - 1], 'pair', [(i, i ^ j) for i in range(pairs)])  4.08 us
    ppermute x1, starting transfers between devices, per_device(): ahead = lax.ppermute(share, 'aux', along(-step))  3.86 us
    ppermute x3, starting transfers between devices, per_device(): lax.ppermute(sends[j - 1], 'pair', [(i, i ^ j) for i in range(pairs)])  3.55 us
    pallas_call x2, Pallas kernels, arrange(): call(functools.partial(arrange_kernel, rows, aux, second), 'arrange', 1 <...  2.67 us
  transfers between devices with their start and end apart: 14, of which 8 were waited for; matrix products, arithmetic and copies ran while one was open for 0% of the time, Pallas kernels for 12%

profile of v8, /device:TPU:0, one launch (start us, length us, event | category | flops | bytes accessed | tf_op | source)
XLA Modules:
  0.0 50.2 jit_solution(1694448252270302245)
XLA Ops:
  0.6 1.3 %arrange.2.y1.refs_0_ = bf16[4,96,256]{2,1,0:T(8,128)(2,1)S(1)} custom-call(bf16[32,6144]{1,0:T(8,128)(2,1)} %x_hbm.3, s32[2,96]{1,0:T(2,128)} %mask_hbm.3), custom_call_target="tpu_custom_call" | custom-call | flops 268435456 | bytes 256 | tf_op jit(solution)/shard_map/arrange/pallas_call | solution.py:62
  2.0 3.1 %collective-permute-start = (bf16[4,96,256]{2,1,0:T(8,128)(2,1)S(1)}, bf16[4,96,256]{2,1,0:T(8,128)(2,1)S(1)}, u32[]{:S(2)}, u32[]{:S(2)}) collective-permute-start(bf16[4,96,256]{2,1,0:T(8,128)(2,1)S(1)} %arrange.2.y1.refs_0_), channel_id=1, source_target_pairs={{0,2},{1,3},{2,4},{3,5},{4,6},{5,7},{6,0},{7,1},{8,10},{9,11},{10,... | collective-permute-start | bytes 589832 | tf_op jit(solution)/shard_map/ppermute | solution.py:321
  5.0 1.3 %arrange.3.y2.refs_1_ = bf16[4,96,256]{2,1,0:T(8,128)(2,1)S(1)} custom-call(bf16[32,6144]{1,0:T(8,128)(2,1)} %x_hbm.3, s32[2,96]{1,0:T(2,128)} %mask_hbm.3), custom_call_target="tpu_custom_call" | custom-call | flops 268435456 | bytes 256 | tf_op jit(solution)/shard_map/arrange/pallas_call | solution.py:62
  6.4 1.6 %collective-permute-start.2 = (bf16[4,96,256]{2,1,0:T(8,128)(2,1)S(1)}, bf16[4,96,256]{2,1,0:T(8,128)(2,1)S(1)}, u32[]{:S(2)}, u32[]{:S(2)}) collective-permute-start(bf16[4,96,256]{2,1,0:T(8,128)(2,1)S(1)} %arrange.3.y2.refs_1_), channel_id=1, source_target_pairs={{0,2},{1,3},{2,4},{3,5},{4,6},{5,7},{6,0},{7,1},{8,10},{9,11},{10,... | collective-permute-start | bytes 589832 | tf_op jit(solution)/shard_map/ppermute | solution.py:321
  8.0 2.7 %transform.1 = (bf16[2,4,192,256]{3,2,1,0:T(8,128)(2,1)S(1)}, bf16[2,2,4,192,256]{4,3,2,1,0:T(8,128)(2,1)S(1)}, bf16[2,2,256,256]{3,2,1,0:T(8,128)(2,1)S(1)}) custom-call(s32[2]{0:T(128)} %atom_hbm.1, bf16[2,16,64,64]{3,2,1,0:T(8,128)(2,1)} %occ_hbm.1, bf16[2,16,64,64]{3,2,1,0:T(8,128)(2,1)} %virt_hbm.1, bf16[4,96,256]{2,1,0:T(8,128)(2,1)S(1)} %arrange.2.y1.refs_0_, ...), custom_call_target="tpu_custom_call" | custom-call | flops 2147483648 | bytes 256 | tf_op jit(solution)/shard_map/transform/pallas_call | solution.py:128
  10.7 0.1 collective-permute-start.4
  10.8 0.5 collective-permute-start.5
  11.3 1.5 %collective-permute-done.refs_0_ = bf16[4,96,256]{2,1,0:T(8,128)(2,1)S(1)} collective-permute-done((bf16[4,96,256]{2,1,0:T(8,128)(2,1)S(1)}, bf16[4,96,256]{2,1,0:T(8,128)(2,1)S(1)}, u32[]{:S(2)}, u32[]{:S(2)}) %collective-permute-start) | collective-permute-done | bytes 196640 | tf_op jit(solution)/shard_map/ppermute | solution.py:321
  12.8 0.0 collective-permute-start.7
  12.8 0.1 collective-permute-start.1
  12.9 3.3 %collective-permute-done.2.refs_1_ = bf16[4,96,256]{2,1,0:T(8,128)(2,1)S(1)} collective-permute-done((bf16[4,96,256]{2,1,0:T(8,128)(2,1)S(1)}, bf16[4,96,256]{2,1,0:T(8,128)(2,1)S(1)}, u32[]{:S(2)}, u32[]{:S(2)}) %collective-permute-start.2) | collective-permute-done | bytes 196640 | tf_op jit(solution)/shard_map/ppermute | solution.py:321
  16.2 0.0 collective-permute-start.8
  16.2 0.0 collective-permute-done.4.y1.refs_2_
  16.2 0.0 collective-permute-start.3
  16.2 0.0 collective-permute-done.5.y2.refs_3_
  16.2 0.7 %complete.1.w_ref = bf16[2,2,4,192,256]{4,3,2,1,0:T(8,128)(2,1)S(1)} custom-call(bf16[2,2,4,192,256]{4,3,2,1,0:T(8,128)(2,1)S(1)} %get-tuple-element.24.before_ref, bf16[2,2,256,256]{3,2,1,0:T(8,128)(2,1)S(1)} %get-tuple-element.25.green_ref, bf16[4,96,256]{2,1,0:T(8,128)(2,1)S(1)} %collective-permute-done.4.y1.refs_2_, ...), custom_call_target="tpu_custom_call", output_to_operand_aliasing={{}: (0, {})} | custom-call | flops 1073741824 | bytes 256 | tf_op jit(solution)/shard_map/complete/pallas_call | solution.py:156
  16.9 0.7 %far.1 = bf16[288,128]{1,0:T(8,128)(2,1)S(1)} custom-call(bf16[2,2,4,192,256]{4,3,2,1,0:T(8,128)(2,1)S(1)} %complete.1.w_ref, bf16[4,96,256]{2,1,0:T(8,128)(2,1)S(1)} %collective-permute-done.refs_0_, bf16[4,96,256]{2,1,0:T(8,128)(2,1)S(1)} %collective-permute-done.2.refs_1_), custom_call_target="tpu_custom_call" | custom-call | flops 536870912 | bytes 256 | tf_op jit(solution)/shard_map/far/pallas_call | solution.py:224
  17.6 3.9 %collective-permute-start.6 = (bf16[288,128]{1,0:T(8,128)(2,1)S(1)}, bf16[288,128]{1,0:T(8,128)(2,1)S(1)}, u32[]{:S(2)}, u32[]{:S(2)}) collective-permute-start(bf16[288,128]{1,0:T(8,128)(2,1)S(1)} %far.1), channel_id=1, source_target_pairs={{0,6},{1,7},{2,0},{3,1},{4,2},{5,3},{6,4},{7,5},{8,14},{9,15},{10,... | collective-permute-start | bytes 221192 | tf_op jit(solution)/shard_map/ppermute | solution.py:337
  21.5 0.4 near.4.refs_0_
  21.8 0.0 collective-permute-done.7.refs_2_
  21.9 0.0 collective-permute-done.8.refs_3_
  21.9 0.4 near.3.refs_1_
  22.3 0.0 copy-start
  22.3 5.4 %collective-permute-done.6.refs_3_ = bf16[288,128]{1,0:T(8,128)(2,1)S(1)} collective-permute-done((bf16[288,128]{1,0:T(8,128)(2,1)S(1)}, bf16[288,128]{1,0:T(8,128)(2,1)S(1)}, u32[]{:S(2)}, u32[]{:S(2)}) %collective-permute-start.6) | collective-permute-done | bytes 73760 | tf_op jit(solution)/shard_map/ppermute | solution.py:337
  27.7 0.0 collective-permute-done.1.refs_0_
  27.7 0.0 collective-permute-done.3.refs_1_
  27.7 0.1 collective-permute-start.10
  27.8 0.4 collective-permute-start.9
  28.2 0.9 %collective-permute-done.10.refs_3_ = bf16[4,96,256]{2,1,0:T(8,128)(2,1)S(1)} collective-permute-done((bf16[4,96,256]{2,1,0:T(8,128)(2,1)S(1)}, bf16[4,96,256]{2,1,0:T(8,128)(2,1)S(1)}, u32[]{:S(2)}, u32[]{:S(2)}) %collective-permute-start.10) | collective-permute-done | bytes 196640 | tf_op jit(solution)/shard_map/ppermute | solution.py:318
  29.2 0.3 collective-permute-done.9.refs_2_
  29.4 0.4 near.5.refs_2_
  29.8 0.1 pack.1
  30.0 2.8 %collective-permute-start.11 = (bf16[288,128]{1,0:T(8,128)(2,1)S(1)}, bf16[288,128]{1,0:T(8,128)(2,1)S(1)}, u32[]{:S(2)}, u32[]{:S(2)}) collective-permute-start(bf16[288,128]{1,0:T(8,128)(2,1)S(1)} %get-tuple-element.35), channel_id=1, source_target_pairs={{0,24},{8,16},{16,8},{24,0},{1,25},{9,17},{17,9},{25,1},{2,26},{10... | collective-permute-start | bytes 221192 | tf_op jit(solution)/shard_map/ppermute | solution.py:347
  32.7 0.5 %collective-permute-start.12 = (bf16[288,128]{1,0:T(8,128)(2,1)S(1)}, bf16[288,128]{1,0:T(8,128)(2,1)S(1)}, u32[]{:S(2)}, u32[]{:S(2)}) collective-permute-start(bf16[288,128]{1,0:T(8,128)(2,1)S(1)} %get-tuple-element.36), channel_id=1, source_target_pairs={{0,16},{8,24},{16,0},{24,8},{1,17},{9,25},{17,1},{25,9},{2,18},{10... | collective-permute-start | bytes 221192 | tf_op jit(solution)/shard_map/ppermute | solution.py:347
  33.3 0.3 collective-permute-start.13
  33.5 1.9 %collective-permute-done.11.refs_1_ = bf16[288,128]{1,0:T(8,128)(2,1)S(1)} collective-permute-done((bf16[288,128]{1,0:T(8,128)(2,1)S(1)}, bf16[288,128]{1,0:T(8,128)(2,1)S(1)}, u32[]{:S(2)}, u32[]{:S(2)}) %collective-permute-start.11) | collective-permute-done | bytes 73760 | tf_op jit(solution)/shard_map/ppermute | solution.py:347
  35.4 1.7 %collective-permute-done.12.refs_2_ = bf16[288,128]{1,0:T(8,128)(2,1)S(1)} collective-permute-done((bf16[288,128]{1,0:T(8,128)(2,1)S(1)}, bf16[288,128]{1,0:T(8,128)(2,1)S(1)}, u32[]{:S(2)}, u32[]{:S(2)}) %collective-permute-start.12) | collective-permute-done | bytes 73760 | tf_op jit(solution)/shard_map/ppermute | solution.py:347
  37.1 0.5 %collective-permute-done.13.refs_3_ = bf16[288,128]{1,0:T(8,128)(2,1)S(1)} collective-permute-done((bf16[288,128]{1,0:T(8,128)(2,1)S(1)}, bf16[288,128]{1,0:T(8,128)(2,1)S(1)}, u32[]{:S(2)}, u32[]{:S(2)}) %collective-permute-start.13) | collective-permute-done | bytes 73760 | tf_op jit(solution)/shard_map/ppermute | solution.py:347
  37.6 0.0 copy-done
  37.6 1.3 %finish.1 = (f32[2,96,192]{2,1,0:T(8,128)}, f32[32,128]{1,0:T(8,128)S(1)}) custom-call(f32[2]{0:T(128)S(1)} %copy-done, f32[288,128]{1,0:T(8,128)S(1)} %get-tuple-element.34.refs_0_, bf16[288,128]{1,0:T(8,128)(2,1)S(1)} %collective-permute-done.11.refs_1_, bf16[288,128]{1,0:T(8,128)(2,1)S(1)} %collective-permute-done.12.refs_2_, ...), custom_call_target="tpu_custom_call" | custom-call | flops 268435456 | bytes 256 | tf_op jit(solution)/shard_map/finish/pallas_call | solution.py:292
  38.9 8.9 %all_to_all.12 = f32[32,1,128]{2,1,0:T(1,128)S(1)} all-to-all(f32[32,1,128]{2,1,0:T(1,128)S(1)} %bitcast.4), channel_id=1, replica_groups=mesh['pair'=4,'aux'=8] {'pair','aux'}, dimensions={0} | all-to-all | bytes 32768 | tf_op jit(solution)/shard_map/all_to_all | solution.py:354
  47.8 0.6 %slice_reduce_fusion = f32[]{:T(128)} fusion(f32[32,128]{1,0:T(8,128)S(1)} %bitcast.5), kind=kLoop, calls=%fused_computation | loop fusion | flops 31 | bytes 132 | tf_op jit(solution)/shard_map/reduce_sum | solution.py:354
Async XLA Ops:
  2.0 10.8 %collective-permute-start = (bf16[4,96,256]{2,1,0:T(8,128)(2,1)S(1)}, bf16[4,96,256]{2,1,0:T(8,128)(2,1)S(1)}, u32[]{:S(2)}, u32[]{:S(2)}) collective-permute-start(bf16[4,96,256]{2,1,0:T(8,128)(2,1)S(1)} %arrange.2.y1.refs_0_), channel_id=1, source_target_pairs={{0,2},{1,3},{2,4},{3,5},{4,6},{5,7},{6,0},{7,1},{8,10},{9,11},{10,... | collective-permute-start | bytes 589832 | tf_op jit(solution)/shard_map/ppermute | solution.py:321
  6.4 9.8 %collective-permute-start.2 = (bf16[4,96,256]{2,1,0:T(8,128)(2,1)S(1)}, bf16[4,96,256]{2,1,0:T(8,128)(2,1)S(1)}, u32[]{:S(2)}, u32[]{:S(2)}) collective-permute-start(bf16[4,96,256]{2,1,0:T(8,128)(2,1)S(1)} %arrange.3.y2.refs_1_), channel_id=1, source_target_pairs={{0,2},{1,3},{2,4},{3,5},{4,6},{5,7},{6,0},{7,1},{8,10},{9,11},{10,... | collective-permute-start | bytes 589832 | tf_op jit(solution)/shard_map/ppermute | solution.py:321
  10.7 5.5 %collective-permute-start.4 = (bf16[4,96,256]{2,1,0:T(8,128)(2,1)S(1)}, bf16[4,96,256]{2,1,0:T(8,128)(2,1)S(1)}, u32[]{:S(2)}, u32[]{:S(2)}) collective-permute-start(bf16[4,96,256]{2,1,0:T(8,128)(2,1)S(1)} %arrange.2.y1.refs_0_), channel_id=1, source_target_pairs={{0,1},{1,0},{2,3},{3,2},{4,5},{5,4},{6,7},{7,6},{8,9},{9,8},{10,11... | collective-permute-start | bytes 589832 | tf_op jit(solution)/shard_map/ppermute | solution.py:318
  10.8 5.4 %collective-permute-start.5 = (bf16[4,96,256]{2,1,0:T(8,128)(2,1)S(1)}, bf16[4,96,256]{2,1,0:T(8,128)(2,1)S(1)}, u32[]{:S(2)}, u32[]{:S(2)}) collective-permute-start(bf16[4,96,256]{2,1,0:T(8,128)(2,1)S(1)} %arrange.3.y2.refs_1_), channel_id=1, source_target_pairs={{0,1},{1,0},{2,3},{3,2},{4,5},{5,4},{6,7},{7,6},{8,9},{9,8},{10,11... | collective-permute-start | bytes 589832 | tf_op jit(solution)/shard_map/ppermute | solution.py:318
  12.8 9.0 %collective-permute-start.7 = (bf16[4,96,256]{2,1,0:T(8,128)(2,1)S(1)}, bf16[4,96,256]{2,1,0:T(8,128)(2,1)S(1)}, u32[]{:S(2)}, u32[]{:S(2)}) collective-permute-start(bf16[4,96,256]{2,1,0:T(8,128)(2,1)S(1)} %collective-permute-done.refs_0_), channel_id=1, source_target_pairs={{0,1},{1,0},{2,3},{3,2},{4,5},{5,4},{6,7},{7,6},{8,9},{9,8},{10,11... | collective-permute-start | bytes 589832 | tf_op jit(solution)/shard_map/ppermute | solution.py:318
  12.8 14.9 %collective-permute-start.1 = (bf16[4,96,256]{2,1,0:T(8,128)(2,1)S(1)}, bf16[4,96,256]{2,1,0:T(8,128)(2,1)S(1)}, u32[]{:S(2)}, u32[]{:S(2)}) collective-permute-start(bf16[4,96,256]{2,1,0:T(8,128)(2,1)S(1)} %collective-permute-done.refs_0_), channel_id=1, source_target_pairs={{0,2},{1,3},{2,4},{3,5},{4,6},{5,7},{6,0},{7,1},{8,10},{9,11},{10,... | collective-permute-start | bytes 589832 | tf_op jit(solution)/shard_map/ppermute | solution.py:331
  16.2 5.7 %collective-permute-start.8 = (bf16[4,96,256]{2,1,0:T(8,128)(2,1)S(1)}, bf16[4,96,256]{2,1,0:T(8,128)(2,1)S(1)}, u32[]{:S(2)}, u32[]{:S(2)}) collective-permute-start(bf16[4,96,256]{2,1,0:T(8,128)(2,1)S(1)} %collective-permute-done.2.refs_1_), channel_id=1, source_target_pairs={{0,1},{1,0},{2,3},{3,2},{4,5},{5,4},{6,7},{7,6},{8,9},{9,8},{10,11... | collective-permute-start | bytes 589832 | tf_op jit(solution)/shard_map/ppermute | solution.py:318
  16.2 11.5 %collective-permute-start.3 = (bf16[4,96,256]{2,1,0:T(8,128)(2,1)S(1)}, bf16[4,96,256]{2,1,0:T(8,128)(2,1)S(1)}, u32[]{:S(2)}, u32[]{:S(2)}) collective-permute-start(bf16[4,96,256]{2,1,0:T(8,128)(2,1)S(1)} %collective-permute-done.2.refs_1_), channel_id=1, source_target_pairs={{0,2},{1,3},{2,4},{3,5},{4,6},{5,7},{6,0},{7,1},{8,10},{9,11},{10,... | collective-permute-start | bytes 589832 | tf_op jit(solution)/shard_map/ppermute | solution.py:331
  17.6 10.1 %collective-permute-start.6 = (bf16[288,128]{1,0:T(8,128)(2,1)S(1)}, bf16[288,128]{1,0:T(8,128)(2,1)S(1)}, u32[]{:S(2)}, u32[]{:S(2)}) collective-permute-start(bf16[288,128]{1,0:T(8,128)(2,1)S(1)} %far.1), channel_id=1, source_target_pairs={{0,6},{1,7},{2,0},{3,1},{4,2},{5,3},{6,4},{7,5},{8,14},{9,15},{10,... | collective-permute-start | bytes 221192 | tf_op jit(solution)/shard_map/ppermute | solution.py:337
  22.3 15.3 %copy-start = (f32[2]{0:T(128)S(1)}, f32[2]{0:T(128)}, u32[]{:S(2)}) copy-start(f32[2]{0:T(128)} %weight_ref.1) | copy-start | bytes 28
  27.7 1.4 %collective-permute-start.10 = (bf16[4,96,256]{2,1,0:T(8,128)(2,1)S(1)}, bf16[4,96,256]{2,1,0:T(8,128)(2,1)S(1)}, u32[]{:S(2)}, u32[]{:S(2)}) collective-permute-start(bf16[4,96,256]{2,1,0:T(8,128)(2,1)S(1)} %collective-permute-done.3.refs_1_), channel_id=1, source_target_pairs={{0,1},{1,0},{2,3},{3,2},{4,5},{5,4},{6,7},{7,6},{8,9},{9,8},{10,11... | collective-permute-start | bytes 589832 | tf_op jit(solution)/shard_map/ppermute | solution.py:318
  27.8 1.7 %collective-permute-start.9 = (bf16[4,96,256]{2,1,0:T(8,128)(2,1)S(1)}, bf16[4,96,256]{2,1,0:T(8,128)(2,1)S(1)}, u32[]{:S(2)}, u32[]{:S(2)}) collective-permute-start(bf16[4,96,256]{2,1,0:T(8,128)(2,1)S(1)} %collective-permute-done.1.refs_0_), channel_id=1, source_target_pairs={{0,1},{1,0},{2,3},{3,2},{4,5},{5,4},{6,7},{7,6},{8,9},{9,8},{10,11... | collective-permute-start | bytes 589832 | tf_op jit(solution)/shard_map/ppermute | solution.py:318
  30.0 5.4 %collective-permute-start.11 = (bf16[288,128]{1,0:T(8,128)(2,1)S(1)}, bf16[288,128]{1,0:T(8,128)(2,1)S(1)}, u32[]{:S(2)}, u32[]{:S(2)}) collective-permute-start(bf16[288,128]{1,0:T(8,128)(2,1)S(1)} %get-tuple-element.35), channel_id=1, source_target_pairs={{0,24},{8,16},{16,8},{24,0},{1,25},{9,17},{17,9},{25,1},{2,26},{10... | collective-permute-start | bytes 221192 | tf_op jit(solution)/shard_map/ppermute | solution.py:347
  32.7 4.4 %collective-permute-start.12 = (bf16[288,128]{1,0:T(8,128)(2,1)S(1)}, bf16[288,128]{1,0:T(8,128)(2,1)S(1)}, u32[]{:S(2)}, u32[]{:S(2)}) collective-permute-start(bf16[288,128]{1,0:T(8,128)(2,1)S(1)} %get-tuple-element.36), channel_id=1, source_target_pairs={{0,16},{8,24},{16,0},{24,8},{1,17},{9,25},{17,1},{25,9},{2,18},{10... | collective-permute-start | bytes 221192 | tf_op jit(solution)/shard_map/ppermute | solution.py:347
  33.3 4.4 %collective-permute-start.13 = (bf16[288,128]{1,0:T(8,128)(2,1)S(1)}, bf16[288,128]{1,0:T(8,128)(2,1)S(1)}, u32[]{:S(2)}, u32[]{:S(2)}) collective-permute-start(bf16[288,128]{1,0:T(8,128)(2,1)S(1)} %get-tuple-element.37), channel_id=1, source_target_pairs={{0,8},{8,0},{16,24},{24,16},{1,9},{9,1},{17,25},{25,17},{2,10},{10... | collective-permute-start | bytes 221192 | tf_op jit(solution)/shard_map/ppermute | solution.py:347

commit v9 on v8

--- a/solution.py
+++ b/solution.py
@@ -49,11 +49,11 @@
         odd = jnp.where(low, pltpu.roll(first, BLK, 1), last)
         even = jnp.where(mask[block, 2 * i] > 0, even, 0.0)
         odd = jnp.where(mask[block, 2 * i + 1] > 0, odd, 0.0)
-        wide[pl.ds(2 * i, 8, stride=aux), :] = even
-        wide[pl.ds(2 * i + 1, 8, stride=aux), :] = odd
+        wide[pl.ds(2 * i, 8, stride=aux + 1), :] = even
+        wide[pl.ds(2 * i + 1, 8, stride=aux + 1), :] = odd
     for s in range(8):
         lane = s % 2 * 128
-        y_ref[s // 2, :, lane:lane + 128] = wide[s * aux:(s + 1) * aux, :].astype(y_ref.dtype)
+        y_ref[s // 2, :, lane:lane + 128] = wide[s * (aux + 1):s * (aux + 1) + aux, :].astype(y_ref.dtype)
 
 
 def arrange(integrals, block_mask, second):
@@ -69,7 +69,7 @@
         scratch_shapes=[
             pltpu.VMEM((rows // 2, width), jnp.bfloat16),
             pltpu.SMEM(block_mask.shape, jnp.int32),
-            pltpu.VMEM((8 * aux, 128), jnp.float32),
+            pltpu.VMEM((8 * (aux + 1), 128), jnp.float32),
             pltpu.SemaphoreType.DMA((2,)),
         ],
     )(stay(integrals), stay(block_mask))
@@ -268,7 +268,7 @@
 
 
 def finish_kernel(scale, nt, folded, weight_ref, *refs):
-    parts, (chi_ref, sum_ref) = refs[:-2], refs[-2:]
+    parts, (chi_hbm, sum_ref, chi_ref, leaving) = refs[:-4], refs[-4:]
     aux = chi_ref.shape[1]
     if folded:
         total = parts[0][...]
@@ -280,12 +280,16 @@
         for p in range(1, parts[0].shape[0]):
             total += parts[0][p].astype(jnp.float32)
         total *= scale
+    for t in range(nt):
+        chi_ref[t] = total[t * aux:(t + 1) * aux]
+    copy = pltpu.make_async_copy(chi_ref, chi_hbm, leaving)
+    copy.start()
     local = jnp.zeros((1, 1), jnp.float32)
     for t in range(nt):
         chi = total[t * aux:(t + 1) * aux]
-        chi_ref[t] = chi
-        local += weight_ref[t] * jnp.sum(chi * chi, keepdims=True)
+        local += weight_ref[:, t:t + 1] * jnp.sum(chi * chi, keepdims=True)
     sum_ref[...] = jnp.broadcast_to(local, sum_ref.shape)
+    copy.wait()
 
 
 def finish(scale, time_weights, parts, chi_shape, copies):
@@ -297,9 +301,10 @@
             jax.ShapeDtypeStruct(chi_shape, jnp.float32),
             jax.ShapeDtypeStruct((copies, 128), jnp.float32),
         ),
-        in_specs=[SMEM] + [VMEM] * len(parts),
-        out_specs=(VMEM, VMEM),
-    )(time_weights, *parts)
+        in_specs=[VMEM] * (1 + len(parts)),
+        out_specs=(HBM, VMEM),
+        scratch_shapes=[pltpu.VMEM(chi_shape, jnp.float32), pltpu.SemaphoreType.DMA],
+    )(time_weights[None], *parts)
 
 
 def per_device(integrals, block_mask, block_atom, green_occ, green_virt, time_weights):

time: 50.5 us -> 49.8 us (0.986)
  Pallas kernels: 9.34 us -> 8.43 us
    pallas_call x1, Pallas kernels: 1.32 us -> 0.78 us  [finish(): call(functools.partial(finish_kernel, scale, chi_shape[0], len(parts) > 1...]
where the time goes in v9:
time: 49.8 us; the launch traced here: 49.5 us
  waiting for transfers between devices  15.8 us (32%)
  starting transfers between devices  13.2 us (27%)
  blocking collectives  8.87 us (18%)
  Pallas kernels  8.43 us (17%)
  between operations  2.53 us (5%)
  other arithmetic  0.6 us (1%)
    all_to_all x1, blocking collectives, per_device(): lax.all_to_all(sums, ('pair', 'aux'), 0, 0, tiled=True)[:, 0]  8.87 us
    ppermute x1, waiting for transfers between devices, per_device(): ahead = lax.ppermute(share, 'aux', along(-step))  5.42 us
    ppermute x2, waiting for transfers between devices, per_device(): arriving = [lax.ppermute(a, 'aux', along(1)) for a in own]  5.07 us
    ppermute x2, starting transfers between devices, per_device(): arriving = [lax.ppermute(a, 'aux', along(1)) for a in own]  4.71 us
    ppermute x3, waiting for transfers between devices, per_device(): lax.ppermute(sends[j - 1], 'pair', [(i, i ^ j) for i in range(pairs)])  4.08 us
    ppermute x1, starting transfers between devices, per_device(): ahead = lax.ppermute(share, 'aux', along(-step))  3.86 us
    ppermute x3, starting transfers between devices, per_device(): lax.ppermute(sends[j - 1], 'pair', [(i, i ^ j) for i in range(pairs)])  3.55 us
    pallas_call x1, Pallas kernels, transform(): call(functools.partial(transform_kernel, nt, rows), 'transform', 2 << 30,...  2.67 us
  transfers between devices with their start and end apart: 14, of which 8 were waited for; matrix products, arithmetic and copies ran while one was open for 0% of the time, Pallas kernels for 12%

profile of v9, /device:TPU:0, one launch (start us, length us, event | category | flops | bytes accessed | tf_op | source)
XLA Modules:
  0.0 49.5 jit_solution(16315913554029033567)
XLA Ops:
  0.6 1.1 %arrange.2.y1.refs_0_ = bf16[4,96,256]{2,1,0:T(8,128)(2,1)S(1)} custom-call(bf16[32,6144]{1,0:T(8,128)(2,1)} %x_hbm.3, s32[2,96]{1,0:T(2,128)} %mask_hbm.3), custom_call_target="tpu_custom_call" | custom-call | flops 268435456 | bytes 256 | tf_op jit(solution)/shard_map/arrange/pallas_call | solution.py:62
  1.8 3.1 %collective-permute-start = (bf16[4,96,256]{2,1,0:T(8,128)(2,1)S(1)}, bf16[4,96,256]{2,1,0:T(8,128)(2,1)S(1)}, u32[]{:S(2)}, u32[]{:S(2)}) collective-permute-start(bf16[4,96,256]{2,1,0:T(8,128)(2,1)S(1)} %arrange.2.y1.refs_0_), channel_id=1, source_target_pairs={{0,2},{1,3},{2,4},{3,5},{4,6},{5,7},{6,0},{7,1},{8,10},{9,11},{10,... | collective-permute-start | bytes 589832 | tf_op jit(solution)/shard_map/ppermute | solution.py:326
  4.9 1.1 %arrange.3.y2.refs_1_ = bf16[4,96,256]{2,1,0:T(8,128)(2,1)S(1)} custom-call(bf16[32,6144]{1,0:T(8,128)(2,1)} %x_hbm.3, s32[2,96]{1,0:T(2,128)} %mask_hbm.3), custom_call_target="tpu_custom_call" | custom-call | flops 268435456 | bytes 256 | tf_op jit(solution)/shard_map/arrange/pallas_call | solution.py:62
  6.0 1.6 %collective-permute-start.2 = (bf16[4,96,256]{2,1,0:T(8,128)(2,1)S(1)}, bf16[4,96,256]{2,1,0:T(8,128)(2,1)S(1)}, u32[]{:S(2)}, u32[]{:S(2)}) collective-permute-start(bf16[4,96,256]{2,1,0:T(8,128)(2,1)S(1)} %arrange.3.y2.refs_1_), channel_id=1, source_target_pairs={{0,2},{1,3},{2,4},{3,5},{4,6},{5,7},{6,0},{7,1},{8,10},{9,11},{10,... | collective-permute-start | bytes 589832 | tf_op jit(solution)/shard_map/ppermute | solution.py:326
  7.6 2.7 %transform.1 = (bf16[2,4,192,256]{3,2,1,0:T(8,128)(2,1)S(1)}, bf16[2,2,4,192,256]{4,3,2,1,0:T(8,128)(2,1)S(1)}, bf16[2,2,256,256]{3,2,1,0:T(8,128)(2,1)S(1)}) custom-call(s32[2]{0:T(128)} %atom_hbm.1, bf16[2,16,64,64]{3,2,1,0:T(8,128)(2,1)} %occ_hbm.1, bf16[2,16,64,64]{3,2,1,0:T(8,128)(2,1)} %virt_hbm.1, bf16[4,96,256]{2,1,0:T(8,128)(2,1)S(1)} %arrange.2.y1.refs_0_, ...), custom_call_target="tpu_custom_call" | custom-call | flops 2147483648 | bytes 256 | tf_op jit(solution)/shard_map/transform/pallas_call | solution.py:128
  10.3 0.1 collective-permute-start.4
  10.4 0.5 %collective-permute-start.5 = (bf16[4,96,256]{2,1,0:T(8,128)(2,1)S(1)}, bf16[4,96,256]{2,1,0:T(8,128)(2,1)S(1)}, u32[]{:S(2)}, u32[]{:S(2)}) collective-permute-start(bf16[4,96,256]{2,1,0:T(8,128)(2,1)S(1)} %arrange.3.y2.refs_1_), channel_id=1, source_target_pairs={{0,1},{1,0},{2,3},{3,2},{4,5},{5,4},{6,7},{7,6},{8,9},{9,8},{10,11... | collective-permute-start | bytes 589832 | tf_op jit(solution)/shard_map/ppermute | solution.py:323
  10.9 1.7 %collective-permute-done.refs_0_ = bf16[4,96,256]{2,1,0:T(8,128)(2,1)S(1)} collective-permute-done((bf16[4,96,256]{2,1,0:T(8,128)(2,1)S(1)}, bf16[4,96,256]{2,1,0:T(8,128)(2,1)S(1)}, u32[]{:S(2)}, u32[]{:S(2)}) %collective-permute-start) | collective-permute-done | bytes 196640 | tf_op jit(solution)/shard_map/ppermute | solution.py:326
  12.6 0.0 collective-permute-start.7
  12.6 0.0 collective-permute-start.1
  12.7 3.3 %collective-permute-done.2.refs_1_ = bf16[4,96,256]{2,1,0:T(8,128)(2,1)S(1)} collective-permute-done((bf16[4,96,256]{2,1,0:T(8,128)(2,1)S(1)}, bf16[4,96,256]{2,1,0:T(8,128)(2,1)S(1)}, u32[]{:S(2)}, u32[]{:S(2)}) %collective-permute-start.2) | collective-permute-done | bytes 196640 | tf_op jit(solution)/shard_map/ppermute | solution.py:326
  16.0 0.0 collective-permute-start.8
  16.0 0.0 collective-permute-done.4.y1.refs_2_
  16.0 0.0 collective-permute-start.3
  16.0 0.0 collective-permute-done.5.y2.refs_3_
  16.0 0.7 %complete.1.w_ref = bf16[2,2,4,192,256]{4,3,2,1,0:T(8,128)(2,1)S(1)} custom-call(bf16[2,2,4,192,256]{4,3,2,1,0:T(8,128)(2,1)S(1)} %get-tuple-element.24.before_ref, bf16[2,2,256,256]{3,2,1,0:T(8,128)(2,1)S(1)} %get-tuple-element.25.green_ref, bf16[4,96,256]{2,1,0:T(8,128)(2,1)S(1)} %collective-permute-done.4.y1.refs_2_, ...), custom_call_target="tpu_custom_call", output_to_operand_aliasing={{}: (0, {})} | custom-call | flops 1073741824 | bytes 256 | tf_op jit(solution)/shard_map/complete/pallas_call | solution.py:156
  16.7 0.7 %far.1 = bf16[288,128]{1,0:T(8,128)(2,1)S(1)} custom-call(bf16[2,2,4,192,256]{4,3,2,1,0:T(8,128)(2,1)S(1)} %complete.1.w_ref, bf16[4,96,256]{2,1,0:T(8,128)(2,1)S(1)} %collective-permute-done.refs_0_, bf16[4,96,256]{2,1,0:T(8,128)(2,1)S(1)} %collective-permute-done.2.refs_1_), custom_call_target="tpu_custom_call" | custom-call | flops 536870912 | bytes 256 | tf_op jit(solution)/shard_map/far/pallas_call | solution.py:224
  17.4 3.9 %collective-permute-start.6 = (bf16[288,128]{1,0:T(8,128)(2,1)S(1)}, bf16[288,128]{1,0:T(8,128)(2,1)S(1)}, u32[]{:S(2)}, u32[]{:S(2)}) collective-permute-start(bf16[288,128]{1,0:T(8,128)(2,1)S(1)} %far.1), channel_id=1, source_target_pairs={{0,6},{1,7},{2,0},{3,1},{4,2},{5,3},{6,4},{7,5},{8,14},{9,15},{10,... | collective-permute-start | bytes 221192 | tf_op jit(solution)/shard_map/ppermute | solution.py:342
  21.3 0.4 near.4.refs_0_
  21.7 0.0 collective-permute-done.7.refs_2_
  21.7 0.0 collective-permute-done.8.refs_3_
  21.7 0.4 near.3.refs_1_
  22.1 0.0 copy-start
  22.1 5.4 %collective-permute-done.6.refs_3_ = bf16[288,128]{1,0:T(8,128)(2,1)S(1)} collective-permute-done((bf16[288,128]{1,0:T(8,128)(2,1)S(1)}, bf16[288,128]{1,0:T(8,128)(2,1)S(1)}, u32[]{:S(2)}, u32[]{:S(2)}) %collective-permute-start.6) | collective-permute-done | bytes 73760 | tf_op jit(solution)/shard_map/ppermute | solution.py:342
  27.5 0.0 collective-permute-done.1.refs_0_
  27.5 0.0 collective-permute-done.3.refs_1_
  27.5 0.1 collective-permute-start.10
  27.6 0.4 collective-permute-start.9
  28.0 0.9 %collective-permute-done.10.refs_3_ = bf16[4,96,256]{2,1,0:T(8,128)(2,1)S(1)} collective-permute-done((bf16[4,96,256]{2,1,0:T(8,128)(2,1)S(1)}, bf16[4,96,256]{2,1,0:T(8,128)(2,1)S(1)}, u32[]{:S(2)}, u32[]{:S(2)}) %collective-permute-start.10) | collective-permute-done | bytes 196640 | tf_op jit(solution)/shard_map/ppermute | solution.py:323
  29.0 0.3 collective-permute-done.9.refs_2_
  29.3 0.4 near.5.refs_2_
  29.7 0.1 pack.1
  29.8 2.8 %collective-permute-start.11 = (bf16[288,128]{1,0:T(8,128)(2,1)S(1)}, bf16[288,128]{1,0:T(8,128)(2,1)S(1)}, u32[]{:S(2)}, u32[]{:S(2)}) collective-permute-start(bf16[288,128]{1,0:T(8,128)(2,1)S(1)} %get-tuple-element.35), channel_id=1, source_target_pairs={{0,24},{8,16},{16,8},{24,0},{1,25},{9,17},{17,9},{25,1},{2,26},{10... | collective-permute-start | bytes 221192 | tf_op jit(solution)/shard_map/ppermute | solution.py:352
  32.6 0.5 %collective-permute-start.12 = (bf16[288,128]{1,0:T(8,128)(2,1)S(1)}, bf16[288,128]{1,0:T(8,128)(2,1)S(1)}, u32[]{:S(2)}, u32[]{:S(2)}) collective-permute-start(bf16[288,128]{1,0:T(8,128)(2,1)S(1)} %get-tuple-element.36), channel_id=1, source_target_pairs={{0,16},{8,24},{16,0},{24,8},{1,17},{9,25},{17,1},{25,9},{2,18},{10... | collective-permute-start | bytes 221192 | tf_op jit(solution)/shard_map/ppermute | solution.py:352
  33.1 0.3 collective-permute-start.13
  33.4 1.9 %collective-permute-done.11.refs_1_ = bf16[288,128]{1,0:T(8,128)(2,1)S(1)} collective-permute-done((bf16[288,128]{1,0:T(8,128)(2,1)S(1)}, bf16[288,128]{1,0:T(8,128)(2,1)S(1)}, u32[]{:S(2)}, u32[]{:S(2)}) %collective-permute-start.11) | collective-permute-done | bytes 73760 | tf_op jit(solution)/shard_map/ppermute | solution.py:352
  35.2 1.7 %collective-permute-done.12.refs_2_ = bf16[288,128]{1,0:T(8,128)(2,1)S(1)} collective-permute-done((bf16[288,128]{1,0:T(8,128)(2,1)S(1)}, bf16[288,128]{1,0:T(8,128)(2,1)S(1)}, u32[]{:S(2)}, u32[]{:S(2)}) %collective-permute-start.12) | collective-permute-done | bytes 73760 | tf_op jit(solution)/shard_map/ppermute | solution.py:352
  36.9 0.5 %collective-permute-done.13.refs_3_ = bf16[288,128]{1,0:T(8,128)(2,1)S(1)} collective-permute-done((bf16[288,128]{1,0:T(8,128)(2,1)S(1)}, bf16[288,128]{1,0:T(8,128)(2,1)S(1)}, u32[]{:S(2)}, u32[]{:S(2)}) %collective-permute-start.13) | collective-permute-done | bytes 73760 | tf_op jit(solution)/shard_map/ppermute | solution.py:352
  37.4 0.0 copy-done
  37.4 0.8 %finish.1 = (f32[2,96,192]{2,1,0:T(8,128)}, f32[32,128]{1,0:T(8,128)S(1)}) custom-call(f32[1,2]{1,0:T(1,128)S(1)} %bitcast.6, f32[288,128]{1,0:T(8,128)S(1)} %get-tuple-element.34.refs_0_, bf16[288,128]{1,0:T(8,128)(2,1)S(1)} %collective-permute-done.11.refs_1_, bf16[288,128]{1,0:T(8,128)(2,1)S(1)} %collective-permute-done.12.refs_2_, ...), custom_call_target="tpu_custom_call" | custom-call | flops 268435456 | bytes 256 | tf_op jit(solution)/shard_map/finish/pallas_call | solution.py:296
  38.2 8.9 %all_to_all.12 = f32[32,1,128]{2,1,0:T(1,128)S(1)} all-to-all(f32[32,1,128]{2,1,0:T(1,128)S(1)} %bitcast.5), channel_id=1, replica_groups=mesh['pair'=4,'aux'=8] {'pair','aux'}, dimensions={0} | all-to-all | bytes 32768 | tf_op jit(solution)/shard_map/all_to_all | solution.py:359
  47.1 0.6 %slice_reduce_fusion = f32[]{:T(128)} fusion(f32[32,128]{1,0:T(8,128)S(1)} %bitcast.7), kind=kLoop, calls=%fused_computation | loop fusion | flops 31 | bytes 132 | tf_op jit(solution)/shard_map/reduce_sum | solution.py:359
Async XLA Ops:
  1.8 10.8 %collective-permute-start = (bf16[4,96,256]{2,1,0:T(8,128)(2,1)S(1)}, bf16[4,96,256]{2,1,0:T(8,128)(2,1)S(1)}, u32[]{:S(2)}, u32[]{:S(2)}) collective-permute-start(bf16[4,96,256]{2,1,0:T(8,128)(2,1)S(1)} %arrange.2.y1.refs_0_), channel_id=1, source_target_pairs={{0,2},{1,3},{2,4},{3,5},{4,6},{5,7},{6,0},{7,1},{8,10},{9,11},{10,... | collective-permute-start | bytes 589832 | tf_op jit(solution)/shard_map/ppermute | solution.py:326
  6.0 10.0 %collective-permute-start.2 = (bf16[4,96,256]{2,1,0:T(8,128)(2,1)S(1)}, bf16[4,96,256]{2,1,0:T(8,128)(2,1)S(1)}, u32[]{:S(2)}, u32[]{:S(2)}) collective-permute-start(bf16[4,96,256]{2,1,0:T(8,128)(2,1)S(1)} %arrange.3.y2.refs_1_), channel_id=1, source_target_pairs={{0,2},{1,3},{2,4},{3,5},{4,6},{5,7},{6,0},{7,1},{8,10},{9,11},{10,... | collective-permute-start | bytes 589832 | tf_op jit(solution)/shard_map/ppermute | solution.py:326
  10.3 5.7 %collective-permute-start.4 = (bf16[4,96,256]{2,1,0:T(8,128)(2,1)S(1)}, bf16[4,96,256]{2,1,0:T(8,128)(2,1)S(1)}, u32[]{:S(2)}, u32[]{:S(2)}) collective-permute-start(bf16[4,96,256]{2,1,0:T(8,128)(2,1)S(1)} %arrange.2.y1.refs_0_), channel_id=1, source_target_pairs={{0,1},{1,0},{2,3},{3,2},{4,5},{5,4},{6,7},{7,6},{8,9},{9,8},{10,11... | collective-permute-start | bytes 589832 | tf_op jit(solution)/shard_map/ppermute | solution.py:323
  10.4 5.6 %collective-permute-start.5 = (bf16[4,96,256]{2,1,0:T(8,128)(2,1)S(1)}, bf16[4,96,256]{2,1,0:T(8,128)(2,1)S(1)}, u32[]{:S(2)}, u32[]{:S(2)}) collective-permute-start(bf16[4,96,256]{2,1,0:T(8,128)(2,1)S(1)} %arrange.3.y2.refs_1_), channel_id=1, source_target_pairs={{0,1},{1,0},{2,3},{3,2},{4,5},{5,4},{6,7},{7,6},{8,9},{9,8},{10,11... | collective-permute-start | bytes 589832 | tf_op jit(solution)/shard_map/ppermute | solution.py:323
  12.6 9.0 %collective-permute-start.7 = (bf16[4,96,256]{2,1,0:T(8,128)(2,1)S(1)}, bf16[4,96,256]{2,1,0:T(8,128)(2,1)S(1)}, u32[]{:S(2)}, u32[]{:S(2)}) collective-permute-start(bf16[4,96,256]{2,1,0:T(8,128)(2,1)S(1)} %collective-permute-done.refs_0_), channel_id=1, source_target_pairs={{0,1},{1,0},{2,3},{3,2},{4,5},{5,4},{6,7},{7,6},{8,9},{9,8},{10,11... | collective-permute-start | bytes 589832 | tf_op jit(solution)/shard_map/ppermute | solution.py:323
  12.6 14.9 %collective-permute-start.1 = (bf16[4,96,256]{2,1,0:T(8,128)(2,1)S(1)}, bf16[4,96,256]{2,1,0:T(8,128)(2,1)S(1)}, u32[]{:S(2)}, u32[]{:S(2)}) collective-permute-start(bf16[4,96,256]{2,1,0:T(8,128)(2,1)S(1)} %collective-permute-done.refs_0_), channel_id=1, source_target_pairs={{0,2},{1,3},{2,4},{3,5},{4,6},{5,7},{6,0},{7,1},{8,10},{9,11},{10,... | collective-permute-start | bytes 589832 | tf_op jit(solution)/shard_map/ppermute | solution.py:336
  16.0 5.7 %collective-permute-start.8 = (bf16[4,96,256]{2,1,0:T(8,128)(2,1)S(1)}, bf16[4,96,256]{2,1,0:T(8,128)(2,1)S(1)}, u32[]{:S(2)}, u32[]{:S(2)}) collective-permute-start(bf16[4,96,256]{2,1,0:T(8,128)(2,1)S(1)} %collective-permute-done.2.refs_1_), channel_id=1, source_target_pairs={{0,1},{1,0},{2,3},{3,2},{4,5},{5,4},{6,7},{7,6},{8,9},{9,8},{10,11... | collective-permute-start | bytes 589832 | tf_op jit(solution)/shard_map/ppermute | solution.py:323
  16.0 11.5 %collective-permute-start.3 = (bf16[4,96,256]{2,1,0:T(8,128)(2,1)S(1)}, bf16[4,96,256]{2,1,0:T(8,128)(2,1)S(1)}, u32[]{:S(2)}, u32[]{:S(2)}) collective-permute-start(bf16[4,96,256]{2,1,0:T(8,128)(2,1)S(1)} %collective-permute-done.2.refs_1_), channel_id=1, source_target_pairs={{0,2},{1,3},{2,4},{3,5},{4,6},{5,7},{6,0},{7,1},{8,10},{9,11},{10,... | collective-permute-start | bytes 589832 | tf_op jit(solution)/shard_map/ppermute | solution.py:336
  17.4 10.1 %collective-permute-start.6 = (bf16[288,128]{1,0:T(8,128)(2,1)S(1)}, bf16[288,128]{1,0:T(8,128)(2,1)S(1)}, u32[]{:S(2)}, u32[]{:S(2)}) collective-permute-start(bf16[288,128]{1,0:T(8,128)(2,1)S(1)} %far.1), channel_id=1, source_target_pairs={{0,6},{1,7},{2,0},{3,1},{4,2},{5,3},{6,4},{7,5},{8,14},{9,15},{10,... | collective-permute-start | bytes 221192 | tf_op jit(solution)/shard_map/ppermute | solution.py:342
  22.1 15.3 %copy-start = (f32[2]{0:T(128)S(1)}, f32[2]{0:T(128)}, u32[]{:S(2)}) copy-start(f32[2]{0:T(128)} %param.11) | copy-start | bytes 28
  27.5 1.4 %collective-permute-start.10 = (bf16[4,96,256]{2,1,0:T(8,128)(2,1)S(1)}, bf16[4,96,256]{2,1,0:T(8,128)(2,1)S(1)}, u32[]{:S(2)}, u32[]{:S(2)}) collective-permute-start(bf16[4,96,256]{2,1,0:T(8,128)(2,1)S(1)} %collective-permute-done.3.refs_1_), channel_id=1, source_target_pairs={{0,1},{1,0},{2,3},{3,2},{4,5},{5,4},{6,7},{7,6},{8,9},{9,8},{10,11... | collective-permute-start | bytes 589832 | tf_op jit(solution)/shard_map/ppermute | solution.py:323
  27.6 1.7 %collective-permute-start.9 = (bf16[4,96,256]{2,1,0:T(8,128)(2,1)S(1)}, bf16[4,96,256]{2,1,0:T(8,128)(2,1)S(1)}, u32[]{:S(2)}, u32[]{:S(2)}) collective-permute-start(bf16[4,96,256]{2,1,0:T(8,128)(2,1)S(1)} %collective-permute-done.1.refs_0_), channel_id=1, source_target_pairs={{0,1},{1,0},{2,3},{3,2},{4,5},{5,4},{6,7},{7,6},{8,9},{9,8},{10,11... | collective-permute-start | bytes 589832 | tf_op jit(solution)/shard_map/ppermute | solution.py:323
  29.8 5.4 %collective-permute-start.11 = (bf16[288,128]{1,0:T(8,128)(2,1)S(1)}, bf16[288,128]{1,0:T(8,128)(2,1)S(1)}, u32[]{:S(2)}, u32[]{:S(2)}) collective-permute-start(bf16[288,128]{1,0:T(8,128)(2,1)S(1)} %get-tuple-element.35), channel_id=1, source_target_pairs={{0,24},{8,16},{16,8},{24,0},{1,25},{9,17},{17,9},{25,1},{2,26},{10... | collective-permute-start | bytes 221192 | tf_op jit(solution)/shard_map/ppermute | solution.py:352
  32.6 4.4 %collective-permute-start.12 = (bf16[288,128]{1,0:T(8,128)(2,1)S(1)}, bf16[288,128]{1,0:T(8,128)(2,1)S(1)}, u32[]{:S(2)}, u32[]{:S(2)}) collective-permute-start(bf16[288,128]{1,0:T(8,128)(2,1)S(1)} %get-tuple-element.36), channel_id=1, source_target_pairs={{0,16},{8,24},{16,0},{24,8},{1,17},{9,25},{17,1},{25,9},{2,18},{10... | collective-permute-start | bytes 221192 | tf_op jit(solution)/shard_map/ppermute | solution.py:352
  33.1 4.4 %collective-permute-start.13 = (bf16[288,128]{1,0:T(8,128)(2,1)S(1)}, bf16[288,128]{1,0:T(8,128)(2,1)S(1)}, u32[]{:S(2)}, u32[]{:S(2)}) collective-permute-start(bf16[288,128]{1,0:T(8,128)(2,1)S(1)} %get-tuple-element.37), channel_id=1, source_target_pairs={{0,8},{8,0},{16,24},{24,16},{1,9},{9,1},{17,25},{25,17},{2,10},{10... | collective-permute-start | bytes 221192 | tf_op jit(solution)/shard_map/ppermute | solution.py:352

commit v10 on v9

--- a/solution.py
+++ b/solution.py
@@ -164,6 +164,46 @@
     )(w, greens, *sibling)
 
 
+def mirror_kernel(green_ref, y1, y2, z_ref):
+    aux = y1.shape[1]
+    for t in range(green_ref.shape[0]):
+        for half, y in enumerate((y1, y2)):
+            z_ref[half, :, t * aux:(t + 1) * aux, :] = through(y, green_ref[t, 0], green_ref[t, 1])
+
+
+def mirror(greens, sibling):
+    steps, aux, wide = sibling[0].shape
+    return call(
+        mirror_kernel,
+        "mirror",
+        1 << 29,
+        out_shape=jax.ShapeDtypeStruct((2, steps, greens.shape[0] * aux, wide), jnp.bfloat16),
+        in_specs=[VMEM] * 3,
+        out_specs=VMEM,
+    )(greens, *sibling)
+
+
+def both_kernel(z_ref, sibling_ref, y1, y2, mine_ref, theirs_ref):
+    for operand, out_ref in ((sibling_ref, theirs_ref), (z_ref, mine_ref)):
+        total = jnp.zeros(out_ref.shape, jnp.float32)
+        for half, y in enumerate((y1, y2)):
+            for j in range(y.shape[0]):
+                total += lax.dot_general(operand[half, j], y[j], NT_DIMS, preferred_element_type=jnp.float32)
+        out_ref[...] = total
+
+
+def both(z, z_sibling, pieces):
+    share = jax.ShapeDtypeStruct((z.shape[2], pieces[0].shape[1]), jnp.float32)
+    return call(
+        both_kernel,
+        "both",
+        1 << 29,
+        out_shape=(share, share),
+        in_specs=[VMEM] * 4,
+        out_specs=(VMEM, VMEM),
+    )(z, z_sibling, *pieces)
+
+
 def near_kernel(count, z_ref, *refs):
     mine, other, out_ref = refs[:count], refs[count:2 * count], refs[-1]
 
@@ -232,11 +272,15 @@
 
 
 def pack_kernel(chips, pairs, *refs):
-    backs, aheads = refs[:chips // 2 + 1], refs[chips // 2 + 1:chips]
-    outs, shares = refs[chips:-1], refs[-1]
+    backs, aheads = refs[:chips // 2], refs[chips // 2 + 2:chips + 1]
+    mine, other = refs[chips // 2][...], refs[chips // 2 + 1][...]
+    outs, shares = refs[chips + 1:-1], refs[-1]
     chip = chip_of()
-    for step in range(chips // 2 + 1):
+    for step in range(chips // 2):
         shares[lax.rem(chip + chips - step, chips)] = fold(backs[step][...])
+    first = lax.rem(lax.axis_index("aux"), 2) == 0
+    pieces = [jnp.where(first, mine, other), jnp.where(first, other, mine)]
+    shares[lax.rem(chip + chips // 2, chips)] = fold(jnp.concatenate(pieces, axis=1))
     for step in range(1, chips // 2):
         shares[lax.rem(chip + step, chips)] = aheads[step - 1][...].astype(jnp.float32)
     if pairs is None:
@@ -261,7 +305,7 @@
         "pack",
         1 << 28,
         out_shape=out_shape,
-        in_specs=[VMEM] * chips,
+        in_specs=[VMEM] * (chips + 1),
         out_specs=(VMEM,) * len(out_shape),
         scratch_shapes=[pltpu.VMEM((chips,) + folded, jnp.float32)],
     )(*backs, *aheads)
@@ -335,7 +379,8 @@
         if not last:
             arriving = [lax.ppermute(a, "aux", along(1)) for a in held]
         if last:
-            backs.append(near(z, held, [to_sibling(a) for a in held]))
+            mine, theirs = both(z, z_sibling, held)
+            backs += [mine, to_sibling(theirs)]
             continue
         other = [to_sibling(a) for a in held]
         share = far(w, held)
@@ -343,7 +388,12 @@
         if step == 1:
             backs.append(near(z, own, sibling))
         backs.append(near(z, held, other))
-        *arriving, ahead, backs[-1], backs[-2] = lax.optimization_barrier((*arriving, ahead, backs[-1], backs[-2]))
+        if step == 1:
+            *sibling, _ = lax.optimization_barrier((*sibling, share))
+            z_sibling = mirror(greens, sibling)
+        *arriving, ahead, backs[-1], backs[-2], z_sibling = lax.optimization_barrier(
+            (*arriving, ahead, backs[-1], backs[-2], z_sibling)
+        )
         aheads.append(ahead)
     if columns == 2 * aux_here and pairs & (pairs - 1) == 0:
         mine, *sends = pack(chips, pairs, backs, aheads)

time: 49.8 us -> 49.6 us (level)
  Pallas kernels: 8.43 us -> 9.33 us
  waiting for transfers between devices: 15.8 us -> 15.1 us
    pallas_call x0 -> x2, Pallas kernels: none -> 1.21 us  [the longest x1 0.67 us: mirror(): call(mirror_kernel, 'mirror', 1 << 29, out_shape=jax.ShapeDtypeStruct((2,...]
    ppermute x1, waiting for transfers between devices: 5.42 us -> 4.73 us  [per_device(): ahead = lax.ppermute(share, 'aux', along(-step))]
    pallas_call x3 -> x2, Pallas kernels: 1.18 us -> 0.81 us  [near(): call(functools.partial(near_kernel, len(mine)), 'near', 1 << 29, out_shap...]
    ppermute x6 -> x5, starting transfers between devices: 1.09 us -> 0.72 us  [to_sibling(): return lax.ppermute(array, 'aux', [(i, i ^ 1) for i in range(auxes)])]
    ppermute x6 -> x5, waiting for transfers between devices: 1.22 us -> 1.23 us  [to_sibling(): return lax.ppermute(array, 'aux', [(i, i ^ 1) for i in range(auxes)])]
  transfers between devices with their start and end apart: 14 -> 13, of which waited for: 8 -> 7; matrix products, arithmetic and copies ran while one was open for 0% -> 0% of each run, Pallas kernels for 12% -> 14%
where the time goes in v10:
time: 49.6 us; the launch traced here: 49.3 us
  waiting for transfers between devices  15.1 us (30%)
  starting transfers between devices  12.9 us (26%)
  Pallas kernels  9.33 us (19%)
  blocking collectives  8.87 us (18%)
  between operations  2.54 us (5%)
  other arithmetic  0.6 us (1%)
    all_to_all x1, blocking collectives, per_device(): lax.all_to_all(sums, ('pair', 'aux'), 0, 0, tiled=True)[:, 0]  8.87 us
    ppermute x2, waiting for transfers between devices, per_device(): arriving = [lax.ppermute(a, 'aux', along(1)) for a in own]  5.07 us
    ppermute x1, waiting for transfers between devices, per_device(): ahead = lax.ppermute(share, 'aux', along(-step))  4.73 us
    ppermute x2, starting transfers between devices, per_device(): arriving = [lax.ppermute(a, 'aux', along(1)) for a in own]  4.71 us
    ppermute x3, waiting for transfers between devices, per_device(): lax.ppermute(sends[j - 1], 'pair', [(i, i ^ j) for i in range(pairs)])  4.08 us
    ppermute x1, starting transfers between devices, per_device(): ahead = lax.ppermute(share, 'aux', along(-step))  3.85 us
    ppermute x3, starting transfers between devices, per_device(): lax.ppermute(sends[j - 1], 'pair', [(i, i ^ j) for i in range(pairs)])  3.55 us
    pallas_call x1, Pallas kernels, transform(): call(functools.partial(transform_kernel, nt, rows), 'transform', 2 << 30,...  2.67 us
  transfers between devices with their start and end apart: 13, of which 7 were waited for; matrix products, arithmetic and copies ran while one was open for 0% of the time, Pallas kernels for 14%

profile of v10, /device:TPU:0, one launch (start us, length us, event | category | flops | bytes accessed | tf_op | source)
XLA Modules:
  0.0 49.3 jit_solution(75516587569402654)
XLA Ops:
  0.6 1.1 %arrange.2.y1.refs_0_ = bf16[4,96,256]{2,1,0:T(8,128)(2,1)S(1)} custom-call(bf16[32,6144]{1,0:T(8,128)(2,1)} %x_hbm.3, s32[2,96]{1,0:T(2,128)} %mask_hbm.3), custom_call_target="tpu_custom_call" | custom-call | flops 268435456 | bytes 256 | tf_op jit(solution)/shard_map/arrange/pallas_call | solution.py:62
  1.8 3.1 %collective-permute-start = (bf16[4,96,256]{2,1,0:T(8,128)(2,1)S(1)}, bf16[4,96,256]{2,1,0:T(8,128)(2,1)S(1)}, u32[]{:S(2)}, u32[]{:S(2)}) collective-permute-start(bf16[4,96,256]{2,1,0:T(8,128)(2,1)S(1)} %arrange.2.y1.refs_0_), channel_id=1, source_target_pairs={{0,2},{1,3},{2,4},{3,5},{4,6},{5,7},{6,0},{7,1},{8,10},{9,11},{10,... | collective-permute-start | bytes 589832 | tf_op jit(solution)/shard_map/ppermute | solution.py:370
  4.9 1.1 %arrange.3.y2.refs_1_ = bf16[4,96,256]{2,1,0:T(8,128)(2,1)S(1)} custom-call(bf16[32,6144]{1,0:T(8,128)(2,1)} %x_hbm.3, s32[2,96]{1,0:T(2,128)} %mask_hbm.3), custom_call_target="tpu_custom_call" | custom-call | flops 268435456 | bytes 256 | tf_op jit(solution)/shard_map/arrange/pallas_call | solution.py:62
  6.0 1.6 %collective-permute-start.2 = (bf16[4,96,256]{2,1,0:T(8,128)(2,1)S(1)}, bf16[4,96,256]{2,1,0:T(8,128)(2,1)S(1)}, u32[]{:S(2)}, u32[]{:S(2)}) collective-permute-start(bf16[4,96,256]{2,1,0:T(8,128)(2,1)S(1)} %arrange.3.y2.refs_1_), channel_id=1, source_target_pairs={{0,2},{1,3},{2,4},{3,5},{4,6},{5,7},{6,0},{7,1},{8,10},{9,11},{10,... | collective-permute-start | bytes 589832 | tf_op jit(solution)/shard_map/ppermute | solution.py:370
  7.6 2.7 %transform.1 = (bf16[2,4,192,256]{3,2,1,0:T(8,128)(2,1)S(1)}, bf16[2,2,4,192,256]{4,3,2,1,0:T(8,128)(2,1)S(1)}, bf16[2,2,256,256]{3,2,1,0:T(8,128)(2,1)S(1)}) custom-call(s32[2]{0:T(128)} %atom_hbm.1, bf16[2,16,64,64]{3,2,1,0:T(8,128)(2,1)} %occ_hbm.1, bf16[2,16,64,64]{3,2,1,0:T(8,128)(2,1)} %virt_hbm.1, bf16[4,96,256]{2,1,0:T(8,128)(2,1)S(1)} %arrange.2.y1.refs_0_, ...), custom_call_target="tpu_custom_call" | custom-call | flops 2147483648 | bytes 256 | tf_op jit(solution)/shard_map/transform/pallas_call | solution.py:128
  10.3 0.1 collective-permute-start.4
  10.4 0.5 %collective-permute-start.5 = (bf16[4,96,256]{2,1,0:T(8,128)(2,1)S(1)}, bf16[4,96,256]{2,1,0:T(8,128)(2,1)S(1)}, u32[]{:S(2)}, u32[]{:S(2)}) collective-permute-start(bf16[4,96,256]{2,1,0:T(8,128)(2,1)S(1)} %arrange.3.y2.refs_1_), channel_id=1, source_target_pairs={{0,1},{1,0},{2,3},{3,2},{4,5},{5,4},{6,7},{7,6},{8,9},{9,8},{10,11... | collective-permute-start | bytes 589832 | tf_op jit(solution)/shard_map/ppermute | solution.py:367
  10.9 1.7 %collective-permute-done.refs_0_ = bf16[4,96,256]{2,1,0:T(8,128)(2,1)S(1)} collective-permute-done((bf16[4,96,256]{2,1,0:T(8,128)(2,1)S(1)}, bf16[4,96,256]{2,1,0:T(8,128)(2,1)S(1)}, u32[]{:S(2)}, u32[]{:S(2)}) %collective-permute-start) | collective-permute-done | bytes 196640 | tf_op jit(solution)/shard_map/ppermute | solution.py:370
  12.6 0.0 collective-permute-start.7
  12.6 0.0 collective-permute-start.1
  12.7 3.3 %collective-permute-done.2.refs_1_ = bf16[4,96,256]{2,1,0:T(8,128)(2,1)S(1)} collective-permute-done((bf16[4,96,256]{2,1,0:T(8,128)(2,1)S(1)}, bf16[4,96,256]{2,1,0:T(8,128)(2,1)S(1)}, u32[]{:S(2)}, u32[]{:S(2)}) %collective-permute-start.2) | collective-permute-done | bytes 196640 | tf_op jit(solution)/shard_map/ppermute | solution.py:370
  16.0 0.0 collective-permute-start.8
  16.0 0.0 collective-permute-done.4.y1.refs_2_
  16.0 0.0 collective-permute-start.3
  16.0 0.0 collective-permute-done.5.y2.refs_3_
  16.0 0.7 %complete.1.w_ref = bf16[2,2,4,192,256]{4,3,2,1,0:T(8,128)(2,1)S(1)} custom-call(bf16[2,2,4,192,256]{4,3,2,1,0:T(8,128)(2,1)S(1)} %get-tuple-element.29.before_ref, bf16[2,2,256,256]{3,2,1,0:T(8,128)(2,1)S(1)} %get-tuple-element.30.green_ref, bf16[4,96,256]{2,1,0:T(8,128)(2,1)S(1)} %collective-permute-done.4.y1.refs_2_, ...), custom_call_target="tpu_custom_call", output_to_operand_aliasing={{}: (0, {})} | custom-call | flops 1073741824 | bytes 256 | tf_op jit(solution)/shard_map/complete/pallas_call | solution.py:156
  16.7 0.7 %far.1 = bf16[288,128]{1,0:T(8,128)(2,1)S(1)} custom-call(bf16[2,2,4,192,256]{4,3,2,1,0:T(8,128)(2,1)S(1)} %complete.1.w_ref, bf16[4,96,256]{2,1,0:T(8,128)(2,1)S(1)} %collective-permute-done.refs_0_, bf16[4,96,256]{2,1,0:T(8,128)(2,1)S(1)} %collective-permute-done.2.refs_1_), custom_call_target="tpu_custom_call" | custom-call | flops 536870912 | bytes 256 | tf_op jit(solution)/shard_map/far/pallas_call | solution.py:264
  17.4 3.8 %collective-permute-start.6 = (bf16[288,128]{1,0:T(8,128)(2,1)S(1)}, bf16[288,128]{1,0:T(8,128)(2,1)S(1)}, u32[]{:S(2)}, u32[]{:S(2)}) collective-permute-start(bf16[288,128]{1,0:T(8,128)(2,1)S(1)} %far.1), channel_id=1, source_target_pairs={{0,6},{1,7},{2,0},{3,1},{4,2},{5,3},{6,4},{7,5},{8,14},{9,15},{10,... | collective-permute-start | bytes 221192 | tf_op jit(solution)/shard_map/ppermute | solution.py:387
  21.3 0.7 %mirror.1.sibling_ref = bf16[2,4,192,256]{3,2,1,0:T(8,128)(2,1)S(1)} custom-call(bf16[2,2,256,256]{3,2,1,0:T(8,128)(2,1)S(1)} %get-tuple-element.30.green_ref, bf16[4,96,256]{2,1,0:T(8,128)(2,1)S(1)} %collective-permute-done.4.y1.refs_2_, bf16[4,96,256]{2,1,0:T(8,128)(2,1)S(1)} %collective-permute-done.5.y2.refs_3_), custom_call_target="tpu_custom_call" | custom-call | flops 536870912 | bytes 256 | tf_op jit(solution)/shard_map/mirror/pallas_call | solution.py:176
  21.9 0.4 near.3.refs_0_
  22.4 0.0 collective-permute-done.7.refs_2_
  22.4 0.0 collective-permute-done.8.refs_3_
  22.4 0.4 near.2.refs_1_
  22.8 0.0 copy-start
  22.8 4.7 %collective-permute-done.6.refs_4_ = bf16[288,128]{1,0:T(8,128)(2,1)S(1)} collective-permute-done((bf16[288,128]{1,0:T(8,128)(2,1)S(1)}, bf16[288,128]{1,0:T(8,128)(2,1)S(1)}, u32[]{:S(2)}, u32[]{:S(2)}) %collective-permute-start.6) | collective-permute-done | bytes 73760 | tf_op jit(solution)/shard_map/ppermute | solution.py:387
  27.5 0.0 collective-permute-done.1.y1
  27.5 0.0 collective-permute-done.3.y2
  27.5 0.5 %both.1 = (f32[192,96]{1,0:T(8,128)S(1)}, f32[192,96]{1,0:T(8,128)S(1)}) custom-call(bf16[2,4,192,256]{3,2,1,0:T(8,128)(2,1)S(1)} %get-tuple-element.33.z_ref, bf16[2,4,192,256]{3,2,1,0:T(8,128)(2,1)S(1)} %mirror.1.sibling_ref, bf16[4,96,256]{2,1,0:T(8,128)(2,1)S(1)} %collective-permute-done.1.y1, bf16[4,96,256]{2,1,0:T(8,128)(2,1)S(1)} %collective-permute-done.3.y2), custom_call_target="tpu_custom_call" | custom-call | flops 536870912 | bytes 256 | tf_op jit(solution)/shard_map/both/pallas_call | solution.py:197
  28.1 0.1 collective-permute-start.9
  28.2 1.2 %collective-permute-done.9.refs_3_ = f32[192,96]{1,0:T(8,128)S(1)} collective-permute-done((f32[192,96]{1,0:T(8,128)S(1)}, f32[192,96]{1,0:T(8,128)S(1)}, u32[]{:S(2)}, u32[]{:S(2)}) %collective-permute-start.9) | collective-permute-done | bytes 73760 | tf_op jit(solution)/shard_map/ppermute | solution.py:367
  29.4 0.2 pack.1
  29.6 2.8 %collective-permute-start.10 = (bf16[288,128]{1,0:T(8,128)(2,1)S(1)}, bf16[288,128]{1,0:T(8,128)(2,1)S(1)}, u32[]{:S(2)}, u32[]{:S(2)}) collective-permute-start(bf16[288,128]{1,0:T(8,128)(2,1)S(1)} %get-tuple-element.45), channel_id=1, source_target_pairs={{0,24},{8,16},{16,8},{24,0},{1,25},{9,17},{17,9},{25,1},{2,26},{10... | collective-permute-start | bytes 221192 | tf_op jit(solution)/shard_map/ppermute | solution.py:402
  32.4 0.5 %collective-permute-start.11 = (bf16[288,128]{1,0:T(8,128)(2,1)S(1)}, bf16[288,128]{1,0:T(8,128)(2,1)S(1)}, u32[]{:S(2)}, u32[]{:S(2)}) collective-permute-start(bf16[288,128]{1,0:T(8,128)(2,1)S(1)} %get-tuple-element.46), channel_id=1, source_target_pairs={{0,16},{8,24},{16,0},{24,8},{1,17},{9,25},{17,1},{25,9},{2,18},{10... | collective-permute-start | bytes 221192 | tf_op jit(solution)/shard_map/ppermute | solution.py:402
  32.9 0.3 collective-permute-start.12
  33.2 1.8 %collective-permute-done.10.refs_1_ = bf16[288,128]{1,0:T(8,128)(2,1)S(1)} collective-permute-done((bf16[288,128]{1,0:T(8,128)(2,1)S(1)}, bf16[288,128]{1,0:T(8,128)(2,1)S(1)}, u32[]{:S(2)}, u32[]{:S(2)}) %collective-permute-start.10) | collective-permute-done | bytes 73760 | tf_op jit(solution)/shard_map/ppermute | solution.py:402
  35.0 1.7 %collective-permute-done.11.refs_2_ = bf16[288,128]{1,0:T(8,128)(2,1)S(1)} collective-permute-done((bf16[288,128]{1,0:T(8,128)(2,1)S(1)}, bf16[288,128]{1,0:T(8,128)(2,1)S(1)}, u32[]{:S(2)}, u32[]{:S(2)}) %collective-permute-start.11) | collective-permute-done | bytes 73760 | tf_op jit(solution)/shard_map/ppermute | solution.py:402
  36.8 0.5 %collective-permute-done.12.refs_3_ = bf16[288,128]{1,0:T(8,128)(2,1)S(1)} collective-permute-done((bf16[288,128]{1,0:T(8,128)(2,1)S(1)}, bf16[288,128]{1,0:T(8,128)(2,1)S(1)}, u32[]{:S(2)}, u32[]{:S(2)}) %collective-permute-start.12) | collective-permute-done | bytes 73760 | tf_op jit(solution)/shard_map/ppermute | solution.py:402
  37.3 0.0 copy-done
  37.3 0.8 %finish.1 = (f32[2,96,192]{2,1,0:T(8,128)}, f32[32,128]{1,0:T(8,128)S(1)}) custom-call(f32[1,2]{1,0:T(1,128)S(1)} %bitcast.6, f32[288,128]{1,0:T(8,128)S(1)} %get-tuple-element.44.refs_0_, bf16[288,128]{1,0:T(8,128)(2,1)S(1)} %collective-permute-done.10.refs_1_, bf16[288,128]{1,0:T(8,128)(2,1)S(1)} %collective-permute-done.11.refs_2_, ...), custom_call_target="tpu_custom_call" | custom-call | flops 268435456 | bytes 256 | tf_op jit(solution)/shard_map/finish/pallas_call | solution.py:340
  38.1 8.9 %all_to_all.12 = f32[32,1,128]{2,1,0:T(1,128)S(1)} all-to-all(f32[32,1,128]{2,1,0:T(1,128)S(1)} %bitcast.5), channel_id=1, replica_groups=mesh['pair'=4,'aux'=8] {'pair','aux'}, dimensions={0} | all-to-all | bytes 32768 | tf_op jit(solution)/shard_map/all_to_all | solution.py:409
  46.9 0.6 %slice_reduce_fusion = f32[]{:T(128)} fusion(f32[32,128]{1,0:T(8,128)S(1)} %bitcast.7), kind=kLoop, calls=%fused_computation | loop fusion | flops 31 | bytes 132 | tf_op jit(solution)/shard_map/reduce_sum | solution.py:409
Async XLA Ops:
  1.8 10.8 %collective-permute-start = (bf16[4,96,256]{2,1,0:T(8,128)(2,1)S(1)}, bf16[4,96,256]{2,1,0:T(8,128)(2,1)S(1)}, u32[]{:S(2)}, u32[]{:S(2)}) collective-permute-start(bf16[4,96,256]{2,1,0:T(8,128)(2,1)S(1)} %arrange.2.y1.refs_0_), channel_id=1, source_target_pairs={{0,2},{1,3},{2,4},{3,5},{4,6},{5,7},{6,0},{7,1},{8,10},{9,11},{10,... | collective-permute-start | bytes 589832 | tf_op jit(solution)/shard_map/ppermute | solution.py:370
  6.0 10.0 %collective-permute-start.2 = (bf16[4,96,256]{2,1,0:T(8,128)(2,1)S(1)}, bf16[4,96,256]{2,1,0:T(8,128)(2,1)S(1)}, u32[]{:S(2)}, u32[]{:S(2)}) collective-permute-start(bf16[4,96,256]{2,1,0:T(8,128)(2,1)S(1)} %arrange.3.y2.refs_1_), channel_id=1, source_target_pairs={{0,2},{1,3},{2,4},{3,5},{4,6},{5,7},{6,0},{7,1},{8,10},{9,11},{10,... | collective-permute-start | bytes 589832 | tf_op jit(solution)/shard_map/ppermute | solution.py:370
  10.3 5.7 %collective-permute-start.4 = (bf16[4,96,256]{2,1,0:T(8,128)(2,1)S(1)}, bf16[4,96,256]{2,1,0:T(8,128)(2,1)S(1)}, u32[]{:S(2)}, u32[]{:S(2)}) collective-permute-start(bf16[4,96,256]{2,1,0:T(8,128)(2,1)S(1)} %arrange.2.y1.refs_0_), channel_id=1, source_target_pairs={{0,1},{1,0},{2,3},{3,2},{4,5},{5,4},{6,7},{7,6},{8,9},{9,8},{10,11... | collective-permute-start | bytes 589832 | tf_op jit(solution)/shard_map/ppermute | solution.py:367
  10.4 5.6 %collective-permute-start.5 = (bf16[4,96,256]{2,1,0:T(8,128)(2,1)S(1)}, bf16[4,96,256]{2,1,0:T(8,128)(2,1)S(1)}, u32[]{:S(2)}, u32[]{:S(2)}) collective-permute-start(bf16[4,96,256]{2,1,0:T(8,128)(2,1)S(1)} %arrange.3.y2.refs_1_), channel_id=1, source_target_pairs={{0,1},{1,0},{2,3},{3,2},{4,5},{5,4},{6,7},{7,6},{8,9},{9,8},{10,11... | collective-permute-start | bytes 589832 | tf_op jit(solution)/shard_map/ppermute | solution.py:367
  12.6 9.7 %collective-permute-start.7 = (bf16[4,96,256]{2,1,0:T(8,128)(2,1)S(1)}, bf16[4,96,256]{2,1,0:T(8,128)(2,1)S(1)}, u32[]{:S(2)}, u32[]{:S(2)}) collective-permute-start(bf16[4,96,256]{2,1,0:T(8,128)(2,1)S(1)} %collective-permute-done.refs_0_), channel_id=1, source_target_pairs={{0,1},{1,0},{2,3},{3,2},{4,5},{5,4},{6,7},{7,6},{8,9},{9,8},{10,11... | collective-permute-start | bytes 589832 | tf_op jit(solution)/shard_map/ppermute | solution.py:367
  12.6 14.9 %collective-permute-start.1 = (bf16[4,96,256]{2,1,0:T(8,128)(2,1)S(1)}, bf16[4,96,256]{2,1,0:T(8,128)(2,1)S(1)}, u32[]{:S(2)}, u32[]{:S(2)}) collective-permute-start(bf16[4,96,256]{2,1,0:T(8,128)(2,1)S(1)} %collective-permute-done.refs_0_), channel_id=1, source_target_pairs={{0,2},{1,3},{2,4},{3,5},{4,6},{5,7},{6,0},{7,1},{8,10},{9,11},{10,... | collective-permute-start | bytes 589832 | tf_op jit(solution)/shard_map/ppermute | solution.py:380
  16.0 6.4 %collective-permute-start.8 = (bf16[4,96,256]{2,1,0:T(8,128)(2,1)S(1)}, bf16[4,96,256]{2,1,0:T(8,128)(2,1)S(1)}, u32[]{:S(2)}, u32[]{:S(2)}) collective-permute-start(bf16[4,96,256]{2,1,0:T(8,128)(2,1)S(1)} %collective-permute-done.2.refs_1_), channel_id=1, source_target_pairs={{0,1},{1,0},{2,3},{3,2},{4,5},{5,4},{6,7},{7,6},{8,9},{9,8},{10,11... | collective-permute-start | bytes 589832 | tf_op jit(solution)/shard_map/ppermute | solution.py:367
  16.0 11.5 %collective-permute-start.3 = (bf16[4,96,256]{2,1,0:T(8,128)(2,1)S(1)}, bf16[4,96,256]{2,1,0:T(8,128)(2,1)S(1)}, u32[]{:S(2)}, u32[]{:S(2)}) collective-permute-start(bf16[4,96,256]{2,1,0:T(8,128)(2,1)S(1)} %collective-permute-done.2.refs_1_), channel_id=1, source_target_pairs={{0,2},{1,3},{2,4},{3,5},{4,6},{5,7},{6,0},{7,1},{8,10},{9,11},{10,... | collective-permute-start | bytes 589832 | tf_op jit(solution)/shard_map/ppermute | solution.py:380
  17.4 10.1 %collective-permute-start.6 = (bf16[288,128]{1,0:T(8,128)(2,1)S(1)}, bf16[288,128]{1,0:T(8,128)(2,1)S(1)}, u32[]{:S(2)}, u32[]{:S(2)}) collective-permute-start(bf16[288,128]{1,0:T(8,128)(2,1)S(1)} %far.1), channel_id=1, source_target_pairs={{0,6},{1,7},{2,0},{3,1},{4,2},{5,3},{6,4},{7,5},{8,14},{9,15},{10,... | collective-permute-start | bytes 221192 | tf_op jit(solution)/shard_map/ppermute | solution.py:387
  22.8 14.5 %copy-start = (f32[2]{0:T(128)S(1)}, f32[2]{0:T(128)}, u32[]{:S(2)}) copy-start(f32[2]{0:T(128)} %param.11) | copy-start | bytes 28
  28.1 1.4 %collective-permute-start.9 = (f32[192,96]{1,0:T(8,128)S(1)}, f32[192,96]{1,0:T(8,128)S(1)}, u32[]{:S(2)}, u32[]{:S(2)}) collective-permute-start(f32[192,96]{1,0:T(8,128)S(1)} %get-tuple-element.42), channel_id=1, source_target_pairs={{0,1},{1,0},{2,3},{3,2},{4,5},{5,4},{6,7},{7,6},{8,9},{9,8},{10,11... | collective-permute-start | bytes 221192 | tf_op jit(solution)/shard_map/ppermute | solution.py:367
  29.6 5.4 %collective-permute-start.10 = (bf16[288,128]{1,0:T(8,128)(2,1)S(1)}, bf16[288,128]{1,0:T(8,128)(2,1)S(1)}, u32[]{:S(2)}, u32[]{:S(2)}) collective-permute-start(bf16[288,128]{1,0:T(8,128)(2,1)S(1)} %get-tuple-element.45), channel_id=1, source_target_pairs={{0,24},{8,16},{16,8},{24,0},{1,25},{9,17},{17,9},{25,1},{2,26},{10... | collective-permute-start | bytes 221192 | tf_op jit(solution)/shard_map/ppermute | solution.py:402
  32.4 4.4 %collective-permute-start.11 = (bf16[288,128]{1,0:T(8,128)(2,1)S(1)}, bf16[288,128]{1,0:T(8,128)(2,1)S(1)}, u32[]{:S(2)}, u32[]{:S(2)}) collective-permute-start(bf16[288,128]{1,0:T(8,128)(2,1)S(1)} %get-tuple-element.46), channel_id=1, source_target_pairs={{0,16},{8,24},{16,0},{24,8},{1,17},{9,25},{17,1},{25,9},{2,18},{10... | collective-permute-start | bytes 221192 | tf_op jit(solution)/shard_map/ppermute | solution.py:402
  32.9 4.4 %collective-permute-start.12 = (bf16[288,128]{1,0:T(8,128)(2,1)S(1)}, bf16[288,128]{1,0:T(8,128)(2,1)S(1)}, u32[]{:S(2)}, u32[]{:S(2)}) collective-permute-start(bf16[288,128]{1,0:T(8,128)(2,1)S(1)} %get-tuple-element.47), channel_id=1, source_target_pairs={{0,8},{8,0},{16,24},{24,16},{1,9},{9,1},{17,25},{25,17},{2,10},{10... | collective-permute-start | bytes 221192 | tf_op jit(solution)/shard_map/ppermute | solution.py:402

commit v11 on v10

--- a/solution.py
+++ b/solution.py
@@ -271,10 +271,10 @@
     )(w, *mine)
 
 
-def pack_kernel(chips, pairs, *refs):
+def pack_kernel(chips, folded, *refs):
     backs, aheads = refs[:chips // 2], refs[chips // 2 + 2:chips + 1]
     mine, other = refs[chips // 2][...], refs[chips // 2 + 1][...]
-    outs, shares = refs[chips + 1:-1], refs[-1]
+    out_ref, shares = refs[-2:]
     chip = chip_of()
     for step in range(chips // 2):
         shares[lax.rem(chip + chips - step, chips)] = fold(backs[step][...])
@@ -283,47 +283,32 @@
     shares[lax.rem(chip + chips // 2, chips)] = fold(jnp.concatenate(pieces, axis=1))
     for step in range(1, chips // 2):
         shares[lax.rem(chip + step, chips)] = aheads[step - 1][...].astype(jnp.float32)
-    if pairs is None:
-        for q in range(chips):
-            outs[0][q] = unfold(shares[q]).astype(jnp.bfloat16)
-    else:
-        pair = lax.axis_index("pair")
-        for j, out_ref in enumerate(outs):
-            out_ref[...] = shares[lax.bitwise_xor(pair, j)].astype(out_ref.dtype)
-
-
-def pack(chips, pairs, backs, aheads):
+    for q in range(chips):
+        out_ref[q] = (shares[q] if folded else unfold(shares[q])).astype(out_ref.dtype)
+
+
+def pack(chips, folded, backs, aheads):
     height, width = backs[0].shape
-    folded = (height * 3 // 2, 128)
-    if pairs is None:
-        out_shape = (jax.ShapeDtypeStruct((chips, height, width), jnp.bfloat16),)
-    else:
-        out_shape = (jax.ShapeDtypeStruct(folded, jnp.float32),)
-        out_shape += (jax.ShapeDtypeStruct(folded, jnp.bfloat16),) * (pairs - 1)
-    return call(
-        functools.partial(pack_kernel, chips, pairs),
+    narrow = (chips, height * 3 // 2, 128)
+    return call(
+        functools.partial(pack_kernel, chips, folded),
         "pack",
         1 << 28,
-        out_shape=out_shape,
+        out_shape=jax.ShapeDtypeStruct(narrow if folded else (chips, height, width), jnp.bfloat16),
         in_specs=[VMEM] * (chips + 1),
-        out_specs=(VMEM,) * len(out_shape),
-        scratch_shapes=[pltpu.VMEM((chips,) + folded, jnp.float32)],
+        out_specs=VMEM,
+        scratch_shapes=[pltpu.VMEM(narrow, jnp.float32)],
     )(*backs, *aheads)
 
 
-def finish_kernel(scale, nt, folded, weight_ref, *refs):
-    parts, (chi_hbm, sum_ref, chi_ref, leaving) = refs[:-4], refs[-4:]
+def finish_kernel(scale, nt, folded, weight_ref, part_ref, chi_hbm, sum_ref, chi_ref, leaving):
     aux = chi_ref.shape[1]
+    total = part_ref[0].astype(jnp.float32)
+    for p in range(1, part_ref.shape[0]):
+        total += part_ref[p].astype(jnp.float32)
+    total *= scale
     if folded:
-        total = parts[0][...]
-        for part in parts[1:]:
-            total += part[...].astype(jnp.float32)
-        total = unfold(total * scale)
-    else:
-        total = parts[0][0].astype(jnp.float32)
-        for p in range(1, parts[0].shape[0]):
-            total += parts[0][p].astype(jnp.float32)
-        total *= scale
+        total = unfold(total)
     for t in range(nt):
         chi_ref[t] = total[t * aux:(t + 1) * aux]
     copy = pltpu.make_async_copy(chi_ref, chi_hbm, leaving)
@@ -336,19 +321,19 @@
     copy.wait()
 
 
-def finish(scale, time_weights, parts, chi_shape, copies):
-    return call(
-        functools.partial(finish_kernel, scale, chi_shape[0], len(parts) > 1),
+def finish(scale, folded, time_weights, parts, chi_shape, copies):
+    return call(
+        functools.partial(finish_kernel, scale, chi_shape[0], folded),
         "finish",
         1 << 28,
         out_shape=(
             jax.ShapeDtypeStruct(chi_shape, jnp.float32),
             jax.ShapeDtypeStruct((copies, 128), jnp.float32),
         ),
-        in_specs=[VMEM] * (1 + len(parts)),
+        in_specs=[VMEM] * 2,
         out_specs=(HBM, VMEM),
         scratch_shapes=[pltpu.VMEM(chi_shape, jnp.float32), pltpu.SemaphoreType.DMA],
-    )(time_weights[None], *parts)
+    )(time_weights[None], parts)
 
 
 def per_device(integrals, block_mask, block_atom, green_occ, green_virt, time_weights):
@@ -395,17 +380,13 @@
             (*arriving, ahead, backs[-1], backs[-2], z_sibling)
         )
         aheads.append(ahead)
-    if columns == 2 * aux_here and pairs & (pairs - 1) == 0:
-        mine, *sends = pack(chips, pairs, backs, aheads)
-        parts = [mine]
-        for j in range(pairs - 1, 0, -1):
-            parts.append(lax.ppermute(sends[j - 1], "pair", [(i, i ^ j) for i in range(pairs)]))
-    else:
-        (shares,) = pack(chips, None, backs, aheads)
+    folded = columns == 2 * aux_here
+    shares = pack(chips, folded, backs, aheads)
+    if not folded:
         shares = shares.transpose(1, 0, 2).reshape(nt * aux_here, pairs, columns).transpose(1, 0, 2)
-        parts = [lax.all_to_all(shares, "pair", 0, 0)]
+    parts = lax.all_to_all(shares, "pair", 0, 0)
     scale = float((rows * pairs * BLK) ** -0.5)
-    chi, sums = finish(scale, time_weights, parts, (nt, aux_here, columns), pairs * auxes)
+    chi, sums = finish(scale, folded, time_weights, parts, (nt, aux_here, columns), pairs * auxes)
     total = jnp.sum(lax.all_to_all(sums, ("pair", "aux"), 0, 0, tiled=True)[:, 0])
     energy = -total / jnp.float32(aux_total * aux_total)
     return chi, energy

time: 49.6 us -> 52.4 us (1.056)
  blocking collectives: 8.87 us -> 19.3 us
  waiting for transfers between devices: 15.1 us -> 11 us
  starting transfers between devices: 12.9 us -> 9.31 us
    all_to_all x0 -> x1, blocking collectives: none -> 10.4 us  [per_device(): parts = lax.all_to_all(shares, 'pair', 0, 0)]
    ppermute x3 -> x0, waiting for transfers between devices: 4.08 us -> none  [per_device(): lax.ppermute(sends[j - 1], 'pair', [(i, i ^ j) for i in range(pairs)])]
    ppermute x3 -> x0, starting transfers between devices: 3.55 us -> none  [per_device(): lax.ppermute(sends[j - 1], 'pair', [(i, i ^ j) for i in range(pairs)])]
  transfers between devices with their start and end apart: 13 -> 10, of which waited for: 7 -> 4; matrix products, arithmetic and copies ran while one was open for 0% -> 0% of each run, Pallas kernels for 14% -> 13%
where the time goes in v11:
time: 52.4 us; the launch traced here: 52.1 us
  blocking collectives  19.3 us (37%)
  waiting for transfers between devices  11 us (21%)
  Pallas kernels  9.36 us (18%)
  starting transfers between devices  9.31 us (18%)
  between operations  2.54 us (5%)
  other arithmetic  0.6 us (1%)
    all_to_all x1, blocking collectives, per_device(): parts = lax.all_to_all(shares, 'pair', 0, 0)  10.4 us
    all_to_all x1, blocking collectives, per_device(): lax.all_to_all(sums, ('pair', 'aux'), 0, 0, tiled=True)[:, 0]  8.84 us
    ppermute x2, waiting for transfers between devices, per_device(): arriving = [lax.ppermute(a, 'aux', along(1)) for a in own]  5.07 us
    ppermute x1, waiting for transfers between devices, per_device(): ahead = lax.ppermute(share, 'aux', along(-step))  4.73 us
    ppermute x2, starting transfers between devices, per_device(): arriving = [lax.ppermute(a, 'aux', along(1)) for a in own]  4.71 us
    ppermute x1, starting transfers between devices, per_device(): ahead = lax.ppermute(share, 'aux', along(-step))  3.85 us
    pallas_call x1, Pallas kernels, transform(): call(functools.partial(transform_kernel, nt, rows), 'transform', 2 << 30,...  2.67 us
    pallas_call x2, Pallas kernels, arrange(): call(functools.partial(arrange_kernel, rows, aux, second), 'arrange', 1 <...  2.29 us
  transfers between devices with their start and end apart: 10, of which 4 were waited for; matrix products, arithmetic and copies ran while one was open for 0% of the time, Pallas kernels for 13%

profile of v11, /device:TPU:0, one launch (start us, length us, event | category | flops | bytes accessed | tf_op | source)
XLA Modules:
  0.0 52.1 jit_solution(3352150124170954230)
XLA Ops:
  0.6 1.1 %arrange.2.y1.refs_0_ = bf16[4,96,256]{2,1,0:T(8,128)(2,1)S(1)} custom-call(bf16[32,6144]{1,0:T(8,128)(2,1)} %x_hbm.3, s32[2,96]{1,0:T(2,128)} %mask_hbm.3), custom_call_target="tpu_custom_call" | custom-call | flops 268435456 | bytes 256 | tf_op jit(solution)/shard_map/arrange/pallas_call | solution.py:62
  1.8 3.1 %collective-permute-start = (bf16[4,96,256]{2,1,0:T(8,128)(2,1)S(1)}, bf16[4,96,256]{2,1,0:T(8,128)(2,1)S(1)}, u32[]{:S(2)}, u32[]{:S(2)}) collective-permute-start(bf16[4,96,256]{2,1,0:T(8,128)(2,1)S(1)} %arrange.2.y1.refs_0_), channel_id=1, source_target_pairs={{0,2},{1,3},{2,4},{3,5},{4,6},{5,7},{6,0},{7,1},{8,10},{9,11},{10,... | collective-permute-start | bytes 589832 | tf_op jit(solution)/shard_map/ppermute | solution.py:355
  4.9 1.1 %arrange.3.y2.refs_1_ = bf16[4,96,256]{2,1,0:T(8,128)(2,1)S(1)} custom-call(bf16[32,6144]{1,0:T(8,128)(2,1)} %x_hbm.3, s32[2,96]{1,0:T(2,128)} %mask_hbm.3), custom_call_target="tpu_custom_call" | custom-call | flops 268435456 | bytes 256 | tf_op jit(solution)/shard_map/arrange/pallas_call | solution.py:62
  6.0 1.6 %collective-permute-start.2 = (bf16[4,96,256]{2,1,0:T(8,128)(2,1)S(1)}, bf16[4,96,256]{2,1,0:T(8,128)(2,1)S(1)}, u32[]{:S(2)}, u32[]{:S(2)}) collective-permute-start(bf16[4,96,256]{2,1,0:T(8,128)(2,1)S(1)} %arrange.3.y2.refs_1_), channel_id=1, source_target_pairs={{0,2},{1,3},{2,4},{3,5},{4,6},{5,7},{6,0},{7,1},{8,10},{9,11},{10,... | collective-permute-start | bytes 589832 | tf_op jit(solution)/shard_map/ppermute | solution.py:355
  7.6 2.7 %transform.1 = (bf16[2,4,192,256]{3,2,1,0:T(8,128)(2,1)S(1)}, bf16[2,2,4,192,256]{4,3,2,1,0:T(8,128)(2,1)S(1)}, bf16[2,2,256,256]{3,2,1,0:T(8,128)(2,1)S(1)}) custom-call(s32[2]{0:T(128)} %atom_hbm.1, bf16[2,16,64,64]{3,2,1,0:T(8,128)(2,1)} %occ_hbm.1, bf16[2,16,64,64]{3,2,1,0:T(8,128)(2,1)} %virt_hbm.1, bf16[4,96,256]{2,1,0:T(8,128)(2,1)S(1)} %arrange.2.y1.refs_0_, ...), custom_call_target="tpu_custom_call" | custom-call | flops 2147483648 | bytes 256 | tf_op jit(solution)/shard_map/transform/pallas_call | solution.py:128
  10.3 0.1 collective-permute-start.4
  10.4 0.5 collective-permute-start.5
  10.9 1.7 %collective-permute-done.refs_0_ = bf16[4,96,256]{2,1,0:T(8,128)(2,1)S(1)} collective-permute-done((bf16[4,96,256]{2,1,0:T(8,128)(2,1)S(1)}, bf16[4,96,256]{2,1,0:T(8,128)(2,1)S(1)}, u32[]{:S(2)}, u32[]{:S(2)}) %collective-permute-start) | collective-permute-done | bytes 196640 | tf_op jit(solution)/shard_map/ppermute | solution.py:355
  12.6 0.0 collective-permute-start.7
  12.6 0.0 collective-permute-start.1
  12.7 3.3 %collective-permute-done.2.refs_1_ = bf16[4,96,256]{2,1,0:T(8,128)(2,1)S(1)} collective-permute-done((bf16[4,96,256]{2,1,0:T(8,128)(2,1)S(1)}, bf16[4,96,256]{2,1,0:T(8,128)(2,1)S(1)}, u32[]{:S(2)}, u32[]{:S(2)}) %collective-permute-start.2) | collective-permute-done | bytes 196640 | tf_op jit(solution)/shard_map/ppermute | solution.py:355
  16.0 0.0 collective-permute-start.8
  16.0 0.0 collective-permute-done.4.y1.refs_2_
  16.0 0.0 collective-permute-start.3
  16.0 0.0 collective-permute-done.5.y2.refs_3_
  16.0 0.7 %complete.1.w_ref = bf16[2,2,4,192,256]{4,3,2,1,0:T(8,128)(2,1)S(1)} custom-call(bf16[2,2,4,192,256]{4,3,2,1,0:T(8,128)(2,1)S(1)} %get-tuple-element.25.before_ref, bf16[2,2,256,256]{3,2,1,0:T(8,128)(2,1)S(1)} %get-tuple-element.26.green_ref, bf16[4,96,256]{2,1,0:T(8,128)(2,1)S(1)} %collective-permute-done.4.y1.refs_2_, ...), custom_call_target="tpu_custom_call", output_to_operand_aliasing={{}: (0, {})} | custom-call | flops 1073741824 | bytes 256 | tf_op jit(solution)/shard_map/complete/pallas_call | solution.py:156
  16.7 0.7 %far.1 = bf16[288,128]{1,0:T(8,128)(2,1)S(1)} custom-call(bf16[2,2,4,192,256]{4,3,2,1,0:T(8,128)(2,1)S(1)} %complete.1.w_ref, bf16[4,96,256]{2,1,0:T(8,128)(2,1)S(1)} %collective-permute-done.refs_0_, bf16[4,96,256]{2,1,0:T(8,128)(2,1)S(1)} %collective-permute-done.2.refs_1_), custom_call_target="tpu_custom_call" | custom-call | flops 536870912 | bytes 256 | tf_op jit(solution)/shard_map/far/pallas_call | solution.py:264
  17.4 3.8 %collective-permute-start.6 = (bf16[288,128]{1,0:T(8,128)(2,1)S(1)}, bf16[288,128]{1,0:T(8,128)(2,1)S(1)}, u32[]{:S(2)}, u32[]{:S(2)}) collective-permute-start(bf16[288,128]{1,0:T(8,128)(2,1)S(1)} %far.1), channel_id=1, source_target_pairs={{0,6},{1,7},{2,0},{3,1},{4,2},{5,3},{6,4},{7,5},{8,14},{9,15},{10,... | collective-permute-start | bytes 221192 | tf_op jit(solution)/shard_map/ppermute | solution.py:372
  21.3 0.7 %mirror.1.sibling_ref = bf16[2,4,192,256]{3,2,1,0:T(8,128)(2,1)S(1)} custom-call(bf16[2,2,256,256]{3,2,1,0:T(8,128)(2,1)S(1)} %get-tuple-element.26.green_ref, bf16[4,96,256]{2,1,0:T(8,128)(2,1)S(1)} %collective-permute-done.4.y1.refs_2_, bf16[4,96,256]{2,1,0:T(8,128)(2,1)S(1)} %collective-permute-done.5.y2.refs_3_), custom_call_target="tpu_custom_call" | custom-call | flops 536870912 | bytes 256 | tf_op jit(solution)/shard_map/mirror/pallas_call | solution.py:176
  21.9 0.4 near.3.refs_0_
  22.4 0.0 collective-permute-done.7.refs_2_
  22.4 0.0 collective-permute-done.8.refs_3_
  22.4 0.4 near.2.refs_1_
  22.8 0.0 copy-start
  22.8 4.7 %collective-permute-done.6.refs_4_ = bf16[288,128]{1,0:T(8,128)(2,1)S(1)} collective-permute-done((bf16[288,128]{1,0:T(8,128)(2,1)S(1)}, bf16[288,128]{1,0:T(8,128)(2,1)S(1)}, u32[]{:S(2)}, u32[]{:S(2)}) %collective-permute-start.6) | collective-permute-done | bytes 73760 | tf_op jit(solution)/shard_map/ppermute | solution.py:372
  27.5 0.0 collective-permute-done.1.y1
  27.5 0.0 collective-permute-done.3.y2
  27.5 0.5 %both.1 = (f32[192,96]{1,0:T(8,128)S(1)}, f32[192,96]{1,0:T(8,128)S(1)}) custom-call(bf16[2,4,192,256]{3,2,1,0:T(8,128)(2,1)S(1)} %get-tuple-element.29.z_ref, bf16[2,4,192,256]{3,2,1,0:T(8,128)(2,1)S(1)} %mirror.1.sibling_ref, bf16[4,96,256]{2,1,0:T(8,128)(2,1)S(1)} %collective-permute-done.1.y1, bf16[4,96,256]{2,1,0:T(8,128)(2,1)S(1)} %collective-permute-done.3.y2), custom_call_target="tpu_custom_call" | custom-call | flops 536870912 | bytes 256 | tf_op jit(solution)/shard_map/both/pallas_call | solution.py:197
  28.1 0.1 collective-permute-start.9
  28.2 1.2 %collective-permute-done.9.refs_3_ = f32[192,96]{1,0:T(8,128)S(1)} collective-permute-done((f32[192,96]{1,0:T(8,128)S(1)}, f32[192,96]{1,0:T(8,128)S(1)}, u32[]{:S(2)}, u32[]{:S(2)}) %collective-permute-start.9) | collective-permute-done | bytes 73760 | tf_op jit(solution)/shard_map/ppermute | solution.py:352
  29.4 0.2 pack.1
  29.7 10.4 %all_to_all.17.part_ref = bf16[4,288,128]{2,1,0:T(8,128)(2,1)S(1)} all-to-all(bf16[4,288,128]{2,1,0:T(8,128)(2,1)S(1)} %pack.1), channel_id=1, replica_groups=mesh['pair'=4,'aux'=8] {'pair'}, dimensions={0} | all-to-all | bytes 589824 | tf_op jit(solution)/shard_map/all_to_all | solution.py:387
  40.1 0.0 copy-done
  40.1 0.8 %finish.1 = (f32[2,96,192]{2,1,0:T(8,128)}, f32[32,128]{1,0:T(8,128)S(1)}) custom-call(f32[1,2]{1,0:T(1,128)S(1)} %bitcast.6, bf16[4,288,128]{2,1,0:T(8,128)(2,1)S(1)} %all_to_all.17.part_ref), custom_call_target="tpu_custom_call" | custom-call | flops 268435456 | bytes 256 | tf_op jit(solution)/shard_map/finish/pallas_call | solution.py:325
  40.9 8.8 %all_to_all.18 = f32[32,1,128]{2,1,0:T(1,128)S(1)} all-to-all(f32[32,1,128]{2,1,0:T(1,128)S(1)} %bitcast.5), channel_id=1, replica_groups=mesh['pair'=4,'aux'=8] {'pair','aux'}, dimensions={0} | all-to-all | bytes 32768 | tf_op jit(solution)/shard_map/all_to_all | solution.py:390
  49.7 0.6 %slice_reduce_fusion = f32[]{:T(128)} fusion(f32[32,128]{1,0:T(8,128)S(1)} %bitcast.7), kind=kLoop, calls=%fused_computation | loop fusion | flops 31 | bytes 132 | tf_op jit(solution)/shard_map/reduce_sum | solution.py:390
Async XLA Ops:
  1.8 10.8 %collective-permute-start = (bf16[4,96,256]{2,1,0:T(8,128)(2,1)S(1)}, bf16[4,96,256]{2,1,0:T(8,128)(2,1)S(1)}, u32[]{:S(2)}, u32[]{:S(2)}) collective-permute-start(bf16[4,96,256]{2,1,0:T(8,128)(2,1)S(1)} %arrange.2.y1.refs_0_), channel_id=1, source_target_pairs={{0,2},{1,3},{2,4},{3,5},{4,6},{5,7},{6,0},{7,1},{8,10},{9,11},{10,... | collective-permute-start | bytes 589832 | tf_op jit(solution)/shard_map/ppermute | solution.py:355
  6.0 10.0 %collective-permute-start.2 = (bf16[4,96,256]{2,1,0:T(8,128)(2,1)S(1)}, bf16[4,96,256]{2,1,0:T(8,128)(2,1)S(1)}, u32[]{:S(2)}, u32[]{:S(2)}) collective-permute-start(bf16[4,96,256]{2,1,0:T(8,128)(2,1)S(1)} %arrange.3.y2.refs_1_), channel_id=1, source_target_pairs={{0,2},{1,3},{2,4},{3,5},{4,6},{5,7},{6,0},{7,1},{8,10},{9,11},{10,... | collective-permute-start | bytes 589832 | tf_op jit(solution)/shard_map/ppermute | solution.py:355
  10.3 5.7 %collective-permute-start.4 = (bf16[4,96,256]{2,1,0:T(8,128)(2,1)S(1)}, bf16[4,96,256]{2,1,0:T(8,128)(2,1)S(1)}, u32[]{:S(2)}, u32[]{:S(2)}) collective-permute-start(bf16[4,96,256]{2,1,0:T(8,128)(2,1)S(1)} %arrange.2.y1.refs_0_), channel_id=1, source_target_pairs={{0,1},{1,0},{2,3},{3,2},{4,5},{5,4},{6,7},{7,6},{8,9},{9,8},{10,11... | collective-permute-start | bytes 589832 | tf_op jit(solution)/shard_map/ppermute | solution.py:352
  10.4 5.6 %collective-permute-start.5 = (bf16[4,96,256]{2,1,0:T(8,128)(2,1)S(1)}, bf16[4,96,256]{2,1,0:T(8,128)(2,1)S(1)}, u32[]{:S(2)}, u32[]{:S(2)}) collective-permute-start(bf16[4,96,256]{2,1,0:T(8,128)(2,1)S(1)} %arrange.3.y2.refs_1_), channel_id=1, source_target_pairs={{0,1},{1,0},{2,3},{3,2},{4,5},{5,4},{6,7},{7,6},{8,9},{9,8},{10,11... | collective-permute-start | bytes 589832 | tf_op jit(solution)/shard_map/ppermute | solution.py:352
  12.6 9.7 %collective-permute-start.7 = (bf16[4,96,256]{2,1,0:T(8,128)(2,1)S(1)}, bf16[4,96,256]{2,1,0:T(8,128)(2,1)S(1)}, u32[]{:S(2)}, u32[]{:S(2)}) collective-permute-start(bf16[4,96,256]{2,1,0:T(8,128)(2,1)S(1)} %collective-permute-done.refs_0_), channel_id=1, source_target_pairs={{0,1},{1,0},{2,3},{3,2},{4,5},{5,4},{6,7},{7,6},{8,9},{9,8},{10,11... | collective-permute-start | bytes 589832 | tf_op jit(solution)/shard_map/ppermute | solution.py:352
  12.6 14.9 %collective-permute-start.1 = (bf16[4,96,256]{2,1,0:T(8,128)(2,1)S(1)}, bf16[4,96,256]{2,1,0:T(8,128)(2,1)S(1)}, u32[]{:S(2)}, u32[]{:S(2)}) collective-permute-start(bf16[4,96,256]{2,1,0:T(8,128)(2,1)S(1)} %collective-permute-done.refs_0_), channel_id=1, source_target_pairs={{0,2},{1,3},{2,4},{3,5},{4,6},{5,7},{6,0},{7,1},{8,10},{9,11},{10,... | collective-permute-start | bytes 589832 | tf_op jit(solution)/shard_map/ppermute | solution.py:365
  16.0 6.4 %collective-permute-start.8 = (bf16[4,96,256]{2,1,0:T(8,128)(2,1)S(1)}, bf16[4,96,256]{2,1,0:T(8,128)(2,1)S(1)}, u32[]{:S(2)}, u32[]{:S(2)}) collective-permute-start(bf16[4,96,256]{2,1,0:T(8,128)(2,1)S(1)} %collective-permute-done.2.refs_1_), channel_id=1, source_target_pairs={{0,1},{1,0},{2,3},{3,2},{4,5},{5,4},{6,7},{7,6},{8,9},{9,8},{10,11... | collective-permute-start | bytes 589832 | tf_op jit(solution)/shard_map/ppermute | solution.py:352
  16.0 11.5 %collective-permute-start.3 = (bf16[4,96,256]{2,1,0:T(8,128)(2,1)S(1)}, bf16[4,96,256]{2,1,0:T(8,128)(2,1)S(1)}, u32[]{:S(2)}, u32[]{:S(2)}) collective-permute-start(bf16[4,96,256]{2,1,0:T(8,128)(2,1)S(1)} %collective-permute-done.2.refs_1_), channel_id=1, source_target_pairs={{0,2},{1,3},{2,4},{3,5},{4,6},{5,7},{6,0},{7,1},{8,10},{9,11},{10,... | collective-permute-start | bytes 589832 | tf_op jit(solution)/shard_map/ppermute | solution.py:365
  17.4 10.1 %collective-permute-start.6 = (bf16[288,128]{1,0:T(8,128)(2,1)S(1)}, bf16[288,128]{1,0:T(8,128)(2,1)S(1)}, u32[]{:S(2)}, u32[]{:S(2)}) collective-permute-start(bf16[288,128]{1,0:T(8,128)(2,1)S(1)} %far.1), channel_id=1, source_target_pairs={{0,6},{1,7},{2,0},{3,1},{4,2},{5,3},{6,4},{7,5},{8,14},{9,15},{10,... | collective-permute-start | bytes 221192 | tf_op jit(solution)/shard_map/ppermute | solution.py:372
  22.8 17.3 %copy-start = (f32[2]{0:T(128)S(1)}, f32[2]{0:T(128)}, u32[]{:S(2)}) copy-start(f32[2]{0:T(128)} %param.11) | copy-start | bytes 28
  28.1 1.4 %collective-permute-start.9 = (f32[192,96]{1,0:T(8,128)S(1)}, f32[192,96]{1,0:T(8,128)S(1)}, u32[]{:S(2)}, u32[]{:S(2)}) collective-permute-start(f32[192,96]{1,0:T(8,128)S(1)} %get-tuple-element.38), channel_id=1, source_target_pairs={{0,1},{1,0},{2,3},{3,2},{4,5},{5,4},{6,7},{7,6},{8,9},{9,8},{10,11... | collective-permute-start | bytes 221192 | tf_op jit(solution)/shard_map/ppermute | solution.py:352

commit v12 on v10

--- a/solution.py
+++ b/solution.py
@@ -311,8 +311,8 @@
     )(*backs, *aheads)
 
 
-def finish_kernel(scale, nt, folded, weight_ref, *refs):
-    parts, (chi_hbm, sum_ref, chi_ref, leaving) = refs[:-4], refs[-4:]
+def combine_kernel(scale, nt, folded, weight_ref, *refs):
+    parts, (chi_ref, sum_ref) = refs[:-2], refs[-2:]
     aux = chi_ref.shape[1]
     if folded:
         total = parts[0][...]
@@ -324,31 +324,49 @@
         for p in range(1, parts[0].shape[0]):
             total += parts[0][p].astype(jnp.float32)
         total *= scale
-    for t in range(nt):
-        chi_ref[t] = total[t * aux:(t + 1) * aux]
-    copy = pltpu.make_async_copy(chi_ref, chi_hbm, leaving)
-    copy.start()
     local = jnp.zeros((1, 1), jnp.float32)
     for t in range(nt):
         chi = total[t * aux:(t + 1) * aux]
+        chi_ref[t] = chi
         local += weight_ref[:, t:t + 1] * jnp.sum(chi * chi, keepdims=True)
     sum_ref[...] = jnp.broadcast_to(local, sum_ref.shape)
-    copy.wait()
-
-
-def finish(scale, time_weights, parts, chi_shape, copies):
-    return call(
-        functools.partial(finish_kernel, scale, chi_shape[0], len(parts) > 1),
-        "finish",
+
+
+def combine(scale, time_weights, parts, chi_shape, copies):
+    return call(
+        functools.partial(combine_kernel, scale, chi_shape[0], len(parts) > 1),
+        "combine",
         1 << 28,
         out_shape=(
             jax.ShapeDtypeStruct(chi_shape, jnp.float32),
             jax.ShapeDtypeStruct((copies, 128), jnp.float32),
         ),
         in_specs=[VMEM] * (1 + len(parts)),
+        out_specs=(VMEM, VMEM),
+    )(time_weights[None], *parts)
+
+
+def close_kernel(norm, tile_ref, sums_ref, chi_hbm, energy_ref, leaving):
+    copy = pltpu.make_async_copy(tile_ref, chi_hbm, leaving)
+    copy.start()
+    total = jnp.sum(sums_ref[...], axis=0, keepdims=True)
+    energy_ref[...] = -total[:, :1] / norm
+    copy.wait()
+
+
+def close(norm, tile, sums):
+    return call(
+        functools.partial(close_kernel, norm),
+        "close",
+        1 << 28,
+        out_shape=(
+            jax.ShapeDtypeStruct(tile.shape, jnp.float32),
+            jax.ShapeDtypeStruct((1, 1), jnp.float32),
+        ),
+        in_specs=[VMEM, VMEM],
         out_specs=(HBM, VMEM),
-        scratch_shapes=[pltpu.VMEM(chi_shape, jnp.float32), pltpu.SemaphoreType.DMA],
-    )(time_weights[None], *parts)
+        scratch_shapes=[pltpu.SemaphoreType.DMA],
+    )(tile, sums)
 
 
 def per_device(integrals, block_mask, block_atom, green_occ, green_virt, time_weights):
@@ -405,10 +423,10 @@
         shares = shares.transpose(1, 0, 2).reshape(nt * aux_here, pairs, columns).transpose(1, 0, 2)
         parts = [lax.all_to_all(shares, "pair", 0, 0)]
     scale = float((rows * pairs * BLK) ** -0.5)
-    chi, sums = finish(scale, time_weights, parts, (nt, aux_here, columns), pairs * auxes)
-    total = jnp.sum(lax.all_to_all(sums, ("pair", "aux"), 0, 0, tiled=True)[:, 0])
-    energy = -total / jnp.float32(aux_total * aux_total)
-    return chi, energy
+    tile, sums = combine(scale, time_weights, parts, (nt, aux_here, columns), pairs * auxes)
+    everyone = lax.all_to_all(sums, ("pair", "aux"), 0, 0, tiled=True)
+    chi, energy = close(float(aux_total * aux_total), tile, everyone)
+    return chi, energy[0, 0]
 
 
 def solution(mesh):

time: 49.6 us -> 47.9 us (0.966)
  between operations: 2.54 us -> 0.76 us
  Pallas kernels: 9.33 us -> 10.1 us
  other arithmetic: 0.6 us -> 0 us
    pallas_call x1 -> x2, Pallas kernels: 0.78 us -> 1.55 us  [the longest x1 1.19 us: close(): call(functools.partial(close_kernel, norm), 'close', 1 << 28, out_shape=(...]
    reduce_sum x1 -> x0, other arithmetic: 0.6 us -> none  [per_device(): jnp.sum(lax.all_to_all(sums, ('pair', 'aux'), 0, 0, tiled=True)[:, 0])]
where the time goes in v12:
time: 47.9 us; the launch traced here: 47.7 us
  waiting for transfers between devices  15.1 us (32%)
  starting transfers between devices  12.9 us (27%)
  Pallas kernels  10.1 us (21%)
  blocking collectives  8.86 us (18%)
  between operations  0.76 us (2%)
    all_to_all x1, blocking collectives, per_device(): everyone = lax.all_to_all(sums, ('pair', 'aux'), 0, 0, tiled=True)  8.86 us
    ppermute x2, waiting for transfers between devices, per_device(): arriving = [lax.ppermute(a, 'aux', along(1)) for a in own]  5.07 us
    ppermute x1, waiting for transfers between devices, per_device(): ahead = lax.ppermute(share, 'aux', along(-step))  4.73 us
    ppermute x2, starting transfers between devices, per_device(): arriving = [lax.ppermute(a, 'aux', along(1)) for a in own]  4.71 us
    ppermute x3, waiting for transfers between devices, per_device(): lax.ppermute(sends[j - 1], 'pair', [(i, i ^ j) for i in range(pairs)])  4.08 us
    ppermute x1, starting transfers between devices, per_device(): ahead = lax.ppermute(share, 'aux', along(-step))  3.85 us
    ppermute x3, starting transfers between devices, per_device(): lax.ppermute(sends[j - 1], 'pair', [(i, i ^ j) for i in range(pairs)])  3.55 us
    pallas_call x1, Pallas kernels, transform(): call(functools.partial(transform_kernel, nt, rows), 'transform', 2 << 30,...  2.67 us
  transfers between devices with their start and end apart: 13, of which 7 were waited for; matrix products, arithmetic and copies ran while one was open for 0% of the time, Pallas kernels for 14%

profile of v12, /device:TPU:0, one launch (start us, length us, event | category | flops | bytes accessed | tf_op | source)
XLA Modules:
  0.0 47.7 jit_solution(16245746288307405998)
XLA Ops:
  0.6 1.1 %arrange.2.y1.refs_0_ = bf16[4,96,256]{2,1,0:T(8,128)(2,1)S(1)} custom-call(bf16[32,6144]{1,0:T(8,128)(2,1)} %x_hbm.3, s32[2,96]{1,0:T(2,128)} %mask_hbm.3), custom_call_target="tpu_custom_call" | custom-call | flops 268435456 | bytes 256 | tf_op jit(solution)/shard_map/arrange/pallas_call | solution.py:62
  1.8 3.1 %collective-permute-start = (bf16[4,96,256]{2,1,0:T(8,128)(2,1)S(1)}, bf16[4,96,256]{2,1,0:T(8,128)(2,1)S(1)}, u32[]{:S(2)}, u32[]{:S(2)}) collective-permute-start(bf16[4,96,256]{2,1,0:T(8,128)(2,1)S(1)} %arrange.2.y1.refs_0_), channel_id=1, source_target_pairs={{0,2},{1,3},{2,4},{3,5},{4,6},{5,7},{6,0},{7,1},{8,10},{9,11},{10,... | collective-permute-start | bytes 589832 | tf_op jit(solution)/shard_map/ppermute | solution.py:388
  4.9 1.1 %arrange.3.y2.refs_1_ = bf16[4,96,256]{2,1,0:T(8,128)(2,1)S(1)} custom-call(bf16[32,6144]{1,0:T(8,128)(2,1)} %x_hbm.3, s32[2,96]{1,0:T(2,128)} %mask_hbm.3), custom_call_target="tpu_custom_call" | custom-call | flops 268435456 | bytes 256 | tf_op jit(solution)/shard_map/arrange/pallas_call | solution.py:62
  6.0 1.6 %collective-permute-start.2 = (bf16[4,96,256]{2,1,0:T(8,128)(2,1)S(1)}, bf16[4,96,256]{2,1,0:T(8,128)(2,1)S(1)}, u32[]{:S(2)}, u32[]{:S(2)}) collective-permute-start(bf16[4,96,256]{2,1,0:T(8,128)(2,1)S(1)} %arrange.3.y2.refs_1_), channel_id=1, source_target_pairs={{0,2},{1,3},{2,4},{3,5},{4,6},{5,7},{6,0},{7,1},{8,10},{9,11},{10,... | collective-permute-start | bytes 589832 | tf_op jit(solution)/shard_map/ppermute | solution.py:388
  7.6 2.7 %transform.1 = (bf16[2,4,192,256]{3,2,1,0:T(8,128)(2,1)S(1)}, bf16[2,2,4,192,256]{4,3,2,1,0:T(8,128)(2,1)S(1)}, bf16[2,2,256,256]{3,2,1,0:T(8,128)(2,1)S(1)}) custom-call(s32[2]{0:T(128)} %atom_hbm.1, bf16[2,16,64,64]{3,2,1,0:T(8,128)(2,1)} %occ_hbm.1, bf16[2,16,64,64]{3,2,1,0:T(8,128)(2,1)} %virt_hbm.1, bf16[4,96,256]{2,1,0:T(8,128)(2,1)S(1)} %arrange.2.y1.refs_0_, ...), custom_call_target="tpu_custom_call" | custom-call | flops 2147483648 | bytes 256 | tf_op jit(solution)/shard_map/transform/pallas_call | solution.py:128
  10.3 0.1 collective-permute-start.4
  10.4 0.5 %collective-permute-start.5 = (bf16[4,96,256]{2,1,0:T(8,128)(2,1)S(1)}, bf16[4,96,256]{2,1,0:T(8,128)(2,1)S(1)}, u32[]{:S(2)}, u32[]{:S(2)}) collective-permute-start(bf16[4,96,256]{2,1,0:T(8,128)(2,1)S(1)} %arrange.3.y2.refs_1_), channel_id=1, source_target_pairs={{0,1},{1,0},{2,3},{3,2},{4,5},{5,4},{6,7},{7,6},{8,9},{9,8},{10,11... | collective-permute-start | bytes 589832 | tf_op jit(solution)/shard_map/ppermute | solution.py:385
  10.9 1.7 %collective-permute-done.refs_0_ = bf16[4,96,256]{2,1,0:T(8,128)(2,1)S(1)} collective-permute-done((bf16[4,96,256]{2,1,0:T(8,128)(2,1)S(1)}, bf16[4,96,256]{2,1,0:T(8,128)(2,1)S(1)}, u32[]{:S(2)}, u32[]{:S(2)}) %collective-permute-start) | collective-permute-done | bytes 196640 | tf_op jit(solution)/shard_map/ppermute | solution.py:388
  12.6 0.0 collective-permute-start.7
  12.6 0.0 collective-permute-start.1
  12.7 3.3 %collective-permute-done.2.refs_1_ = bf16[4,96,256]{2,1,0:T(8,128)(2,1)S(1)} collective-permute-done((bf16[4,96,256]{2,1,0:T(8,128)(2,1)S(1)}, bf16[4,96,256]{2,1,0:T(8,128)(2,1)S(1)}, u32[]{:S(2)}, u32[]{:S(2)}) %collective-permute-start.2) | collective-permute-done | bytes 196640 | tf_op jit(solution)/shard_map/ppermute | solution.py:388
  16.0 0.0 collective-permute-start.8
  16.0 0.0 collective-permute-done.4.y1.refs_2_
  16.0 0.0 collective-permute-start.3
  16.0 0.0 collective-permute-done.5.y2.refs_3_
  16.0 0.7 %complete.1.w_ref = bf16[2,2,4,192,256]{4,3,2,1,0:T(8,128)(2,1)S(1)} custom-call(bf16[2,2,4,192,256]{4,3,2,1,0:T(8,128)(2,1)S(1)} %get-tuple-element.31.before_ref, bf16[2,2,256,256]{3,2,1,0:T(8,128)(2,1)S(1)} %get-tuple-element.32.green_ref, bf16[4,96,256]{2,1,0:T(8,128)(2,1)S(1)} %collective-permute-done.4.y1.refs_2_, ...), custom_call_target="tpu_custom_call", output_to_operand_aliasing={{}: (0, {})} | custom-call | flops 1073741824 | bytes 256 | tf_op jit(solution)/shard_map/complete/pallas_call | solution.py:156
  16.7 0.7 %far.1 = bf16[288,128]{1,0:T(8,128)(2,1)S(1)} custom-call(bf16[2,2,4,192,256]{4,3,2,1,0:T(8,128)(2,1)S(1)} %complete.1.w_ref, bf16[4,96,256]{2,1,0:T(8,128)(2,1)S(1)} %collective-permute-done.refs_0_, bf16[4,96,256]{2,1,0:T(8,128)(2,1)S(1)} %collective-permute-done.2.refs_1_), custom_call_target="tpu_custom_call" | custom-call | flops 536870912 | bytes 256 | tf_op jit(solution)/shard_map/far/pallas_call | solution.py:264
  17.4 3.8 %collective-permute-start.6 = (bf16[288,128]{1,0:T(8,128)(2,1)S(1)}, bf16[288,128]{1,0:T(8,128)(2,1)S(1)}, u32[]{:S(2)}, u32[]{:S(2)}) collective-permute-start(bf16[288,128]{1,0:T(8,128)(2,1)S(1)} %far.1), channel_id=1, source_target_pairs={{0,6},{1,7},{2,0},{3,1},{4,2},{5,3},{6,4},{7,5},{8,14},{9,15},{10,... | collective-permute-start | bytes 221192 | tf_op jit(solution)/shard_map/ppermute | solution.py:405
  21.3 0.7 %mirror.1.sibling_ref = bf16[2,4,192,256]{3,2,1,0:T(8,128)(2,1)S(1)} custom-call(bf16[2,2,256,256]{3,2,1,0:T(8,128)(2,1)S(1)} %get-tuple-element.32.green_ref, bf16[4,96,256]{2,1,0:T(8,128)(2,1)S(1)} %collective-permute-done.4.y1.refs_2_, bf16[4,96,256]{2,1,0:T(8,128)(2,1)S(1)} %collective-permute-done.5.y2.refs_3_), custom_call_target="tpu_custom_call" | custom-call | flops 536870912 | bytes 256 | tf_op jit(solution)/shard_map/mirror/pallas_call | solution.py:176
  21.9 0.4 near.3.refs_0_
  22.4 0.0 collective-permute-done.7.refs_2_
  22.4 0.0 collective-permute-done.8.refs_3_
  22.4 0.4 near.2.refs_1_
  22.8 0.0 copy-start
  22.8 4.7 %collective-permute-done.6.refs_4_ = bf16[288,128]{1,0:T(8,128)(2,1)S(1)} collective-permute-done((bf16[288,128]{1,0:T(8,128)(2,1)S(1)}, bf16[288,128]{1,0:T(8,128)(2,1)S(1)}, u32[]{:S(2)}, u32[]{:S(2)}) %collective-permute-start.6) | collective-permute-done | bytes 73760 | tf_op jit(solution)/shard_map/ppermute | solution.py:405
  27.5 0.0 collective-permute-done.1.y1
  27.5 0.0 collective-permute-done.3.y2
  27.5 0.5 %both.1 = (f32[192,96]{1,0:T(8,128)S(1)}, f32[192,96]{1,0:T(8,128)S(1)}) custom-call(bf16[2,4,192,256]{3,2,1,0:T(8,128)(2,1)S(1)} %get-tuple-element.35.z_ref, bf16[2,4,192,256]{3,2,1,0:T(8,128)(2,1)S(1)} %mirror.1.sibling_ref, bf16[4,96,256]{2,1,0:T(8,128)(2,1)S(1)} %collective-permute-done.1.y1, bf16[4,96,256]{2,1,0:T(8,128)(2,1)S(1)} %collective-permute-done.3.y2), custom_call_target="tpu_custom_call" | custom-call | flops 536870912 | bytes 256 | tf_op jit(solution)/shard_map/both/pallas_call | solution.py:197
  28.1 0.1 collective-permute-start.9
  28.2 1.2 %collective-permute-done.9.refs_3_ = f32[192,96]{1,0:T(8,128)S(1)} collective-permute-done((f32[192,96]{1,0:T(8,128)S(1)}, f32[192,96]{1,0:T(8,128)S(1)}, u32[]{:S(2)}, u32[]{:S(2)}) %collective-permute-start.9) | collective-permute-done | bytes 73760 | tf_op jit(solution)/shard_map/ppermute | solution.py:385
  29.4 0.2 pack.1
  29.6 2.8 %collective-permute-start.10 = (bf16[288,128]{1,0:T(8,128)(2,1)S(1)}, bf16[288,128]{1,0:T(8,128)(2,1)S(1)}, u32[]{:S(2)}, u32[]{:S(2)}) collective-permute-start(bf16[288,128]{1,0:T(8,128)(2,1)S(1)} %get-tuple-element.47), channel_id=1, source_target_pairs={{0,24},{8,16},{16,8},{24,0},{1,25},{9,17},{17,9},{25,1},{2,26},{10... | collective-permute-start | bytes 221192 | tf_op jit(solution)/shard_map/ppermute | solution.py:420
  32.4 0.5 %collective-permute-start.11 = (bf16[288,128]{1,0:T(8,128)(2,1)S(1)}, bf16[288,128]{1,0:T(8,128)(2,1)S(1)}, u32[]{:S(2)}, u32[]{:S(2)}) collective-permute-start(bf16[288,128]{1,0:T(8,128)(2,1)S(1)} %get-tuple-element.48), channel_id=1, source_target_pairs={{0,16},{8,24},{16,0},{24,8},{1,17},{9,25},{17,1},{25,9},{2,18},{10... | collective-permute-start | bytes 221192 | tf_op jit(solution)/shard_map/ppermute | solution.py:420
  32.9 0.3 collective-permute-start.12
  33.2 1.8 %collective-permute-done.10.refs_1_ = bf16[288,128]{1,0:T(8,128)(2,1)S(1)} collective-permute-done((bf16[288,128]{1,0:T(8,128)(2,1)S(1)}, bf16[288,128]{1,0:T(8,128)(2,1)S(1)}, u32[]{:S(2)}, u32[]{:S(2)}) %collective-permute-start.10) | collective-permute-done | bytes 73760 | tf_op jit(solution)/shard_map/ppermute | solution.py:420
  35.0 1.7 %collective-permute-done.11.refs_2_ = bf16[288,128]{1,0:T(8,128)(2,1)S(1)} collective-permute-done((bf16[288,128]{1,0:T(8,128)(2,1)S(1)}, bf16[288,128]{1,0:T(8,128)(2,1)S(1)}, u32[]{:S(2)}, u32[]{:S(2)}) %collective-permute-start.11) | collective-permute-done | bytes 73760 | tf_op jit(solution)/shard_map/ppermute | solution.py:420
  36.8 0.5 %collective-permute-done.12.refs_3_ = bf16[288,128]{1,0:T(8,128)(2,1)S(1)} collective-permute-done((bf16[288,128]{1,0:T(8,128)(2,1)S(1)}, bf16[288,128]{1,0:T(8,128)(2,1)S(1)}, u32[]{:S(2)}, u32[]{:S(2)}) %collective-permute-start.12) | collective-permute-done | bytes 73760 | tf_op jit(solution)/shard_map/ppermute | solution.py:420
  37.3 0.0 copy-done
  37.3 0.4 combine.1
  37.6 8.9 %all_to_all.11 = f32[32,1,128]{2,1,0:T(1,128)S(1)} all-to-all(f32[32,1,128]{2,1,0:T(1,128)S(1)} %bitcast.6), channel_id=1, replica_groups=mesh['pair'=4,'aux'=8] {'pair','aux'}, dimensions={0} | all-to-all | bytes 32768 | tf_op jit(solution)/shard_map/all_to_all | solution.py:427
  46.5 1.2 %close.1 = (f32[2,96,192]{2,1,0:T(8,128)}, f32[1,1]{1,0:T(1,128)}) custom-call(f32[2,96,192]{2,1,0:T(8,128)S(1)} %get-tuple-element.50.tile_ref, f32[32,128]{1,0:T(8,128)S(1)} %bitcast.7), custom_call_target="tpu_custom_call" | custom-call | flops 268435456 | bytes 256 | tf_op jit(solution)/shard_map/close/pallas_call | solution.py:358
Async XLA Ops:
  1.8 10.8 %collective-permute-start = (bf16[4,96,256]{2,1,0:T(8,128)(2,1)S(1)}, bf16[4,96,256]{2,1,0:T(8,128)(2,1)S(1)}, u32[]{:S(2)}, u32[]{:S(2)}) collective-permute-start(bf16[4,96,256]{2,1,0:T(8,128)(2,1)S(1)} %arrange.2.y1.refs_0_), channel_id=1, source_target_pairs={{0,2},{1,3},{2,4},{3,5},{4,6},{5,7},{6,0},{7,1},{8,10},{9,11},{10,... | collective-permute-start | bytes 589832 | tf_op jit(solution)/shard_map/ppermute | solution.py:388
  6.0 10.0 %collective-permute-start.2 = (bf16[4,96,256]{2,1,0:T(8,128)(2,1)S(1)}, bf16[4,96,256]{2,1,0:T(8,128)(2,1)S(1)}, u32[]{:S(2)}, u32[]{:S(2)}) collective-permute-start(bf16[4,96,256]{2,1,0:T(8,128)(2,1)S(1)} %arrange.3.y2.refs_1_), channel_id=1, source_target_pairs={{0,2},{1,3},{2,4},{3,5},{4,6},{5,7},{6,0},{7,1},{8,10},{9,11},{10,... | collective-permute-start | bytes 589832 | tf_op jit(solution)/shard_map/ppermute | solution.py:388
  10.3 5.7 %collective-permute-start.4 = (bf16[4,96,256]{2,1,0:T(8,128)(2,1)S(1)}, bf16[4,96,256]{2,1,0:T(8,128)(2,1)S(1)}, u32[]{:S(2)}, u32[]{:S(2)}) collective-permute-start(bf16[4,96,256]{2,1,0:T(8,128)(2,1)S(1)} %arrange.2.y1.refs_0_), channel_id=1, source_target_pairs={{0,1},{1,0},{2,3},{3,2},{4,5},{5,4},{6,7},{7,6},{8,9},{9,8},{10,11... | collective-permute-start | bytes 589832 | tf_op jit(solution)/shard_map/ppermute | solution.py:385
  10.4 5.6 %collective-permute-start.5 = (bf16[4,96,256]{2,1,0:T(8,128)(2,1)S(1)}, bf16[4,96,256]{2,1,0:T(8,128)(2,1)S(1)}, u32[]{:S(2)}, u32[]{:S(2)}) collective-permute-start(bf16[4,96,256]{2,1,0:T(8,128)(2,1)S(1)} %arrange.3.y2.refs_1_), channel_id=1, source_target_pairs={{0,1},{1,0},{2,3},{3,2},{4,5},{5,4},{6,7},{7,6},{8,9},{9,8},{10,11... | collective-permute-start | bytes 589832 | tf_op jit(solution)/shard_map/ppermute | solution.py:385
  12.6 9.7 %collective-permute-start.7 = (bf16[4,96,256]{2,1,0:T(8,128)(2,1)S(1)}, bf16[4,96,256]{2,1,0:T(8,128)(2,1)S(1)}, u32[]{:S(2)}, u32[]{:S(2)}) collective-permute-start(bf16[4,96,256]{2,1,0:T(8,128)(2,1)S(1)} %collective-permute-done.refs_0_), channel_id=1, source_target_pairs={{0,1},{1,0},{2,3},{3,2},{4,5},{5,4},{6,7},{7,6},{8,9},{9,8},{10,11... | collective-permute-start | bytes 589832 | tf_op jit(solution)/shard_map/ppermute | solution.py:385
  12.6 14.9 %collective-permute-start.1 = (bf16[4,96,256]{2,1,0:T(8,128)(2,1)S(1)}, bf16[4,96,256]{2,1,0:T(8,128)(2,1)S(1)}, u32[]{:S(2)}, u32[]{:S(2)}) collective-permute-start(bf16[4,96,256]{2,1,0:T(8,128)(2,1)S(1)} %collective-permute-done.refs_0_), channel_id=1, source_target_pairs={{0,2},{1,3},{2,4},{3,5},{4,6},{5,7},{6,0},{7,1},{8,10},{9,11},{10,... | collective-permute-start | bytes 589832 | tf_op jit(solution)/shard_map/ppermute | solution.py:398
  16.0 6.4 %collective-permute-start.8 = (bf16[4,96,256]{2,1,0:T(8,128)(2,1)S(1)}, bf16[4,96,256]{2,1,0:T(8,128)(2,1)S(1)}, u32[]{:S(2)}, u32[]{:S(2)}) collective-permute-start(bf16[4,96,256]{2,1,0:T(8,128)(2,1)S(1)} %collective-permute-done.2.refs_1_), channel_id=1, source_target_pairs={{0,1},{1,0},{2,3},{3,2},{4,5},{5,4},{6,7},{7,6},{8,9},{9,8},{10,11... | collective-permute-start | bytes 589832 | tf_op jit(solution)/shard_map/ppermute | solution.py:385
  16.0 11.5 %collective-permute-start.3 = (bf16[4,96,256]{2,1,0:T(8,128)(2,1)S(1)}, bf16[4,96,256]{2,1,0:T(8,128)(2,1)S(1)}, u32[]{:S(2)}, u32[]{:S(2)}) collective-permute-start(bf16[4,96,256]{2,1,0:T(8,128)(2,1)S(1)} %collective-permute-done.2.refs_1_), channel_id=1, source_target_pairs={{0,2},{1,3},{2,4},{3,5},{4,6},{5,7},{6,0},{7,1},{8,10},{9,11},{10,... | collective-permute-start | bytes 589832 | tf_op jit(solution)/shard_map/ppermute | solution.py:398
  17.4 10.1 %collective-permute-start.6 = (bf16[288,128]{1,0:T(8,128)(2,1)S(1)}, bf16[288,128]{1,0:T(8,128)(2,1)S(1)}, u32[]{:S(2)}, u32[]{:S(2)}) collective-permute-start(bf16[288,128]{1,0:T(8,128)(2,1)S(1)} %far.1), channel_id=1, source_target_pairs={{0,6},{1,7},{2,0},{3,1},{4,2},{5,3},{6,4},{7,5},{8,14},{9,15},{10,... | collective-permute-start | bytes 221192 | tf_op jit(solution)/shard_map/ppermute | solution.py:405
  22.8 14.5 %copy-start = (f32[2]{0:T(128)S(1)}, f32[2]{0:T(128)}, u32[]{:S(2)}) copy-start(f32[2]{0:T(128)} %param.11) | copy-start | bytes 28
  28.1 1.4 %collective-permute-start.9 = (f32[192,96]{1,0:T(8,128)S(1)}, f32[192,96]{1,0:T(8,128)S(1)}, u32[]{:S(2)}, u32[]{:S(2)}) collective-permute-start(f32[192,96]{1,0:T(8,128)S(1)} %get-tuple-element.44), channel_id=1, source_target_pairs={{0,1},{1,0},{2,3},{3,2},{4,5},{5,4},{6,7},{7,6},{8,9},{9,8},{10,11... | collective-permute-start | bytes 221192 | tf_op jit(solution)/shard_map/ppermute | solution.py:385
  29.6 5.4 %collective-permute-start.10 = (bf16[288,128]{1,0:T(8,128)(2,1)S(1)}, bf16[288,128]{1,0:T(8,128)(2,1)S(1)}, u32[]{:S(2)}, u32[]{:S(2)}) collective-permute-start(bf16[288,128]{1,0:T(8,128)(2,1)S(1)} %get-tuple-element.47), channel_id=1, source_target_pairs={{0,24},{8,16},{16,8},{24,0},{1,25},{9,17},{17,9},{25,1},{2,26},{10... | collective-permute-start | bytes 221192 | tf_op jit(solution)/shard_map/ppermute | solution.py:420
  32.4 4.4 %collective-permute-start.11 = (bf16[288,128]{1,0:T(8,128)(2,1)S(1)}, bf16[288,128]{1,0:T(8,128)(2,1)S(1)}, u32[]{:S(2)}, u32[]{:S(2)}) collective-permute-start(bf16[288,128]{1,0:T(8,128)(2,1)S(1)} %get-tuple-element.48), channel_id=1, source_target_pairs={{0,16},{8,24},{16,0},{24,8},{1,17},{9,25},{17,1},{25,9},{2,18},{10... | collective-permute-start | bytes 221192 | tf_op jit(solution)/shard_map/ppermute | solution.py:420
  32.9 4.4 %collective-permute-start.12 = (bf16[288,128]{1,0:T(8,128)(2,1)S(1)}, bf16[288,128]{1,0:T(8,128)(2,1)S(1)}, u32[]{:S(2)}, u32[]{:S(2)}) collective-permute-start(bf16[288,128]{1,0:T(8,128)(2,1)S(1)} %get-tuple-element.49), channel_id=1, source_target_pairs={{0,8},{8,0},{16,24},{24,16},{1,9},{9,1},{17,25},{25,17},{2,10},{10... | collective-permute-start | bytes 221192 | tf_op jit(solution)/shard_map/ppermute | solution.py:420

commit v13 on v12

--- a/solution.py
+++ b/solution.py
@@ -346,12 +346,15 @@
     )(time_weights[None], *parts)
 
 
-def close_kernel(norm, tile_ref, sums_ref, chi_hbm, energy_ref, leaving):
-    copy = pltpu.make_async_copy(tile_ref, chi_hbm, leaving)
-    copy.start()
+def close_kernel(norm, tile_ref, sums_ref, chi_hbm, energy_hbm, energy_ref, leaving):
+    tile = pltpu.make_async_copy(tile_ref, chi_hbm, leaving.at[0])
+    tile.start()
     total = jnp.sum(sums_ref[...], axis=0, keepdims=True)
     energy_ref[...] = -total[:, :1] / norm
-    copy.wait()
+    energy = pltpu.make_async_copy(energy_ref, energy_hbm, leaving.at[1])
+    energy.start()
+    tile.wait()
+    energy.wait()
 
 
 def close(norm, tile, sums):
@@ -364,8 +367,8 @@
             jax.ShapeDtypeStruct((1, 1), jnp.float32),
         ),
         in_specs=[VMEM, VMEM],
-        out_specs=(HBM, VMEM),
-        scratch_shapes=[pltpu.SemaphoreType.DMA],
+        out_specs=(HBM, HBM),
+        scratch_shapes=[pltpu.VMEM((1, 1), jnp.float32), pltpu.SemaphoreType.DMA((2,))],
     )(tile, sums)
 
 

time: 47.9 us -> 47.5 us (level)
  Pallas kernels: 10.1 us -> 9.61 us
    pallas_call x1, Pallas kernels: 1.19 us -> 0.7 us  [close(): call(functools.partial(close_kernel, norm), 'close', 1 << 28, out_shape=(...]
where the time goes in v13:
time: 47.5 us; the launch traced here: 47.2 us
  waiting for transfers between devices  15.1 us (32%)
  starting transfers between devices  12.9 us (27%)
  Pallas kernels  9.61 us (20%)
  blocking collectives  8.86 us (19%)
  between operations  0.76 us (2%)
    all_to_all x1, blocking collectives, per_device(): everyone = lax.all_to_all(sums, ('pair', 'aux'), 0, 0, tiled=True)  8.86 us
    ppermute x2, waiting for transfers between devices, per_device(): arriving = [lax.ppermute(a, 'aux', along(1)) for a in own]  5.07 us
    ppermute x1, waiting for transfers between devices, per_device(): ahead = lax.ppermute(share, 'aux', along(-step))  4.73 us
    ppermute x2, starting transfers between devices, per_device(): arriving = [lax.ppermute(a, 'aux', along(1)) for a in own]  4.71 us
    ppermute x3, waiting for transfers between devices, per_device(): lax.ppermute(sends[j - 1], 'pair', [(i, i ^ j) for i in range(pairs)])  4.08 us
    ppermute x1, starting transfers between devices, per_device(): ahead = lax.ppermute(share, 'aux', along(-step))  3.85 us
    ppermute x3, starting transfers between devices, per_device(): lax.ppermute(sends[j - 1], 'pair', [(i, i ^ j) for i in range(pairs)])  3.55 us
    pallas_call x1, Pallas kernels, transform(): call(functools.partial(transform_kernel, nt, rows), 'transform', 2 << 30,...  2.67 us
  transfers between devices with their start and end apart: 13, of which 7 were waited for; matrix products, arithmetic and copies ran while one was open for 0% of the time, Pallas kernels for 14%

profile of v13, /device:TPU:0, one launch (start us, length us, event | category | flops | bytes accessed | tf_op | source)
XLA Modules:
  0.0 47.2 jit_solution(17636237696594896374)
XLA Ops:
  0.6 1.1 %arrange.2.y1.refs_0_ = bf16[4,96,256]{2,1,0:T(8,128)(2,1)S(1)} custom-call(bf16[32,6144]{1,0:T(8,128)(2,1)} %x_hbm.3, s32[2,96]{1,0:T(2,128)} %mask_hbm.3), custom_call_target="tpu_custom_call" | custom-call | flops 268435456 | bytes 256 | tf_op jit(solution)/shard_map/arrange/pallas_call | solution.py:62
  1.8 3.1 %collective-permute-start = (bf16[4,96,256]{2,1,0:T(8,128)(2,1)S(1)}, bf16[4,96,256]{2,1,0:T(8,128)(2,1)S(1)}, u32[]{:S(2)}, u32[]{:S(2)}) collective-permute-start(bf16[4,96,256]{2,1,0:T(8,128)(2,1)S(1)} %arrange.2.y1.refs_0_), channel_id=1, source_target_pairs={{0,2},{1,3},{2,4},{3,5},{4,6},{5,7},{6,0},{7,1},{8,10},{9,11},{10,... | collective-permute-start | bytes 589832 | tf_op jit(solution)/shard_map/ppermute | solution.py:391
  4.9 1.1 %arrange.3.y2.refs_1_ = bf16[4,96,256]{2,1,0:T(8,128)(2,1)S(1)} custom-call(bf16[32,6144]{1,0:T(8,128)(2,1)} %x_hbm.3, s32[2,96]{1,0:T(2,128)} %mask_hbm.3), custom_call_target="tpu_custom_call" | custom-call | flops 268435456 | bytes 256 | tf_op jit(solution)/shard_map/arrange/pallas_call | solution.py:62
  6.0 1.6 %collective-permute-start.2 = (bf16[4,96,256]{2,1,0:T(8,128)(2,1)S(1)}, bf16[4,96,256]{2,1,0:T(8,128)(2,1)S(1)}, u32[]{:S(2)}, u32[]{:S(2)}) collective-permute-start(bf16[4,96,256]{2,1,0:T(8,128)(2,1)S(1)} %arrange.3.y2.refs_1_), channel_id=1, source_target_pairs={{0,2},{1,3},{2,4},{3,5},{4,6},{5,7},{6,0},{7,1},{8,10},{9,11},{10,... | collective-permute-start | bytes 589832 | tf_op jit(solution)/shard_map/ppermute | solution.py:391
  7.6 2.7 %transform.1 = (bf16[2,4,192,256]{3,2,1,0:T(8,128)(2,1)S(1)}, bf16[2,2,4,192,256]{4,3,2,1,0:T(8,128)(2,1)S(1)}, bf16[2,2,256,256]{3,2,1,0:T(8,128)(2,1)S(1)}) custom-call(s32[2]{0:T(128)} %atom_hbm.1, bf16[2,16,64,64]{3,2,1,0:T(8,128)(2,1)} %occ_hbm.1, bf16[2,16,64,64]{3,2,1,0:T(8,128)(2,1)} %virt_hbm.1, bf16[4,96,256]{2,1,0:T(8,128)(2,1)S(1)} %arrange.2.y1.refs_0_, ...), custom_call_target="tpu_custom_call" | custom-call | flops 2147483648 | bytes 256 | tf_op jit(solution)/shard_map/transform/pallas_call | solution.py:128
  10.3 0.1 collective-permute-start.4
  10.4 0.5 %collective-permute-start.5 = (bf16[4,96,256]{2,1,0:T(8,128)(2,1)S(1)}, bf16[4,96,256]{2,1,0:T(8,128)(2,1)S(1)}, u32[]{:S(2)}, u32[]{:S(2)}) collective-permute-start(bf16[4,96,256]{2,1,0:T(8,128)(2,1)S(1)} %arrange.3.y2.refs_1_), channel_id=1, source_target_pairs={{0,1},{1,0},{2,3},{3,2},{4,5},{5,4},{6,7},{7,6},{8,9},{9,8},{10,11... | collective-permute-start | bytes 589832 | tf_op jit(solution)/shard_map/ppermute | solution.py:388
  10.9 1.7 %collective-permute-done.refs_0_ = bf16[4,96,256]{2,1,0:T(8,128)(2,1)S(1)} collective-permute-done((bf16[4,96,256]{2,1,0:T(8,128)(2,1)S(1)}, bf16[4,96,256]{2,1,0:T(8,128)(2,1)S(1)}, u32[]{:S(2)}, u32[]{:S(2)}) %collective-permute-start) | collective-permute-done | bytes 196640 | tf_op jit(solution)/shard_map/ppermute | solution.py:391
  12.6 0.0 collective-permute-start.7
  12.6 0.0 collective-permute-start.1
  12.7 3.3 %collective-permute-done.2.refs_1_ = bf16[4,96,256]{2,1,0:T(8,128)(2,1)S(1)} collective-permute-done((bf16[4,96,256]{2,1,0:T(8,128)(2,1)S(1)}, bf16[4,96,256]{2,1,0:T(8,128)(2,1)S(1)}, u32[]{:S(2)}, u32[]{:S(2)}) %collective-permute-start.2) | collective-permute-done | bytes 196640 | tf_op jit(solution)/shard_map/ppermute | solution.py:391
  16.0 0.0 collective-permute-start.8
  16.0 0.0 collective-permute-done.4.y1.refs_2_
  16.0 0.0 collective-permute-start.3
  16.0 0.0 collective-permute-done.5.y2.refs_3_
  16.0 0.7 %complete.1.w_ref = bf16[2,2,4,192,256]{4,3,2,1,0:T(8,128)(2,1)S(1)} custom-call(bf16[2,2,4,192,256]{4,3,2,1,0:T(8,128)(2,1)S(1)} %get-tuple-element.31.before_ref, bf16[2,2,256,256]{3,2,1,0:T(8,128)(2,1)S(1)} %get-tuple-element.32.green_ref, bf16[4,96,256]{2,1,0:T(8,128)(2,1)S(1)} %collective-permute-done.4.y1.refs_2_, ...), custom_call_target="tpu_custom_call", output_to_operand_aliasing={{}: (0, {})} | custom-call | flops 1073741824 | bytes 256 | tf_op jit(solution)/shard_map/complete/pallas_call | solution.py:156
  16.7 0.7 %far.1 = bf16[288,128]{1,0:T(8,128)(2,1)S(1)} custom-call(bf16[2,2,4,192,256]{4,3,2,1,0:T(8,128)(2,1)S(1)} %complete.1.w_ref, bf16[4,96,256]{2,1,0:T(8,128)(2,1)S(1)} %collective-permute-done.refs_0_, bf16[4,96,256]{2,1,0:T(8,128)(2,1)S(1)} %collective-permute-done.2.refs_1_), custom_call_target="tpu_custom_call" | custom-call | flops 536870912 | bytes 256 | tf_op jit(solution)/shard_map/far/pallas_call | solution.py:264
  17.4 3.8 %collective-permute-start.6 = (bf16[288,128]{1,0:T(8,128)(2,1)S(1)}, bf16[288,128]{1,0:T(8,128)(2,1)S(1)}, u32[]{:S(2)}, u32[]{:S(2)}) collective-permute-start(bf16[288,128]{1,0:T(8,128)(2,1)S(1)} %far.1), channel_id=1, source_target_pairs={{0,6},{1,7},{2,0},{3,1},{4,2},{5,3},{6,4},{7,5},{8,14},{9,15},{10,... | collective-permute-start | bytes 221192 | tf_op jit(solution)/shard_map/ppermute | solution.py:408
  21.3 0.7 %mirror.1.sibling_ref = bf16[2,4,192,256]{3,2,1,0:T(8,128)(2,1)S(1)} custom-call(bf16[2,2,256,256]{3,2,1,0:T(8,128)(2,1)S(1)} %get-tuple-element.32.green_ref, bf16[4,96,256]{2,1,0:T(8,128)(2,1)S(1)} %collective-permute-done.4.y1.refs_2_, bf16[4,96,256]{2,1,0:T(8,128)(2,1)S(1)} %collective-permute-done.5.y2.refs_3_), custom_call_target="tpu_custom_call" | custom-call | flops 536870912 | bytes 256 | tf_op jit(solution)/shard_map/mirror/pallas_call | solution.py:176
  21.9 0.4 near.3.refs_0_
  22.4 0.0 collective-permute-done.7.refs_2_
  22.4 0.0 collective-permute-done.8.refs_3_
  22.4 0.4 near.2.refs_1_
  22.8 0.0 copy-start
  22.8 4.7 %collective-permute-done.6.refs_4_ = bf16[288,128]{1,0:T(8,128)(2,1)S(1)} collective-permute-done((bf16[288,128]{1,0:T(8,128)(2,1)S(1)}, bf16[288,128]{1,0:T(8,128)(2,1)S(1)}, u32[]{:S(2)}, u32[]{:S(2)}) %collective-permute-start.6) | collective-permute-done | bytes 73760 | tf_op jit(solution)/shard_map/ppermute | solution.py:408
  27.5 0.0 collective-permute-done.1.y1
  27.5 0.0 collective-permute-done.3.y2
  27.5 0.5 %both.1 = (f32[192,96]{1,0:T(8,128)S(1)}, f32[192,96]{1,0:T(8,128)S(1)}) custom-call(bf16[2,4,192,256]{3,2,1,0:T(8,128)(2,1)S(1)} %get-tuple-element.35.z_ref, bf16[2,4,192,256]{3,2,1,0:T(8,128)(2,1)S(1)} %mirror.1.sibling_ref, bf16[4,96,256]{2,1,0:T(8,128)(2,1)S(1)} %collective-permute-done.1.y1, bf16[4,96,256]{2,1,0:T(8,128)(2,1)S(1)} %collective-permute-done.3.y2), custom_call_target="tpu_custom_call" | custom-call | flops 536870912 | bytes 256 | tf_op jit(solution)/shard_map/both/pallas_call | solution.py:197
  28.1 0.1 collective-permute-start.9
  28.2 1.2 %collective-permute-done.9.refs_3_ = f32[192,96]{1,0:T(8,128)S(1)} collective-permute-done((f32[192,96]{1,0:T(8,128)S(1)}, f32[192,96]{1,0:T(8,128)S(1)}, u32[]{:S(2)}, u32[]{:S(2)}) %collective-permute-start.9) | collective-permute-done | bytes 73760 | tf_op jit(solution)/shard_map/ppermute | solution.py:388
  29.4 0.2 pack.1
  29.6 2.8 %collective-permute-start.10 = (bf16[288,128]{1,0:T(8,128)(2,1)S(1)}, bf16[288,128]{1,0:T(8,128)(2,1)S(1)}, u32[]{:S(2)}, u32[]{:S(2)}) collective-permute-start(bf16[288,128]{1,0:T(8,128)(2,1)S(1)} %get-tuple-element.47), channel_id=1, source_target_pairs={{0,24},{8,16},{16,8},{24,0},{1,25},{9,17},{17,9},{25,1},{2,26},{10... | collective-permute-start | bytes 221192 | tf_op jit(solution)/shard_map/ppermute | solution.py:423
  32.4 0.5 %collective-permute-start.11 = (bf16[288,128]{1,0:T(8,128)(2,1)S(1)}, bf16[288,128]{1,0:T(8,128)(2,1)S(1)}, u32[]{:S(2)}, u32[]{:S(2)}) collective-permute-start(bf16[288,128]{1,0:T(8,128)(2,1)S(1)} %get-tuple-element.48), channel_id=1, source_target_pairs={{0,16},{8,24},{16,0},{24,8},{1,17},{9,25},{17,1},{25,9},{2,18},{10... | collective-permute-start | bytes 221192 | tf_op jit(solution)/shard_map/ppermute | solution.py:423
  32.9 0.3 collective-permute-start.12
  33.2 1.8 %collective-permute-done.10.refs_1_ = bf16[288,128]{1,0:T(8,128)(2,1)S(1)} collective-permute-done((bf16[288,128]{1,0:T(8,128)(2,1)S(1)}, bf16[288,128]{1,0:T(8,128)(2,1)S(1)}, u32[]{:S(2)}, u32[]{:S(2)}) %collective-permute-start.10) | collective-permute-done | bytes 73760 | tf_op jit(solution)/shard_map/ppermute | solution.py:423
  35.0 1.7 %collective-permute-done.11.refs_2_ = bf16[288,128]{1,0:T(8,128)(2,1)S(1)} collective-permute-done((bf16[288,128]{1,0:T(8,128)(2,1)S(1)}, bf16[288,128]{1,0:T(8,128)(2,1)S(1)}, u32[]{:S(2)}, u32[]{:S(2)}) %collective-permute-start.11) | collective-permute-done | bytes 73760 | tf_op jit(solution)/shard_map/ppermute | solution.py:423
  36.8 0.5 %collective-permute-done.12.refs_3_ = bf16[288,128]{1,0:T(8,128)(2,1)S(1)} collective-permute-done((bf16[288,128]{1,0:T(8,128)(2,1)S(1)}, bf16[288,128]{1,0:T(8,128)(2,1)S(1)}, u32[]{:S(2)}, u32[]{:S(2)}) %collective-permute-start.12) | collective-permute-done | bytes 73760 | tf_op jit(solution)/shard_map/ppermute | solution.py:423
  37.3 0.0 copy-done
  37.3 0.4 combine.1
  37.6 8.9 %all_to_all.11 = f32[32,1,128]{2,1,0:T(1,128)S(1)} all-to-all(f32[32,1,128]{2,1,0:T(1,128)S(1)} %bitcast.6), channel_id=1, replica_groups=mesh['pair'=4,'aux'=8] {'pair','aux'}, dimensions={0} | all-to-all | bytes 32768 | tf_op jit(solution)/shard_map/all_to_all | solution.py:430
  46.5 0.7 %close.1 = (f32[2,96,192]{2,1,0:T(8,128)}, f32[1,1]{1,0:T(1,128)}) custom-call(f32[2,96,192]{2,1,0:T(8,128)S(1)} %get-tuple-element.50.tile_ref, f32[32,128]{1,0:T(8,128)S(1)} %bitcast.7), custom_call_target="tpu_custom_call" | custom-call | flops 268435456 | bytes 256 | tf_op jit(solution)/shard_map/close/pallas_call | solution.py:361
Async XLA Ops:
  1.8 10.8 %collective-permute-start = (bf16[4,96,256]{2,1,0:T(8,128)(2,1)S(1)}, bf16[4,96,256]{2,1,0:T(8,128)(2,1)S(1)}, u32[]{:S(2)}, u32[]{:S(2)}) collective-permute-start(bf16[4,96,256]{2,1,0:T(8,128)(2,1)S(1)} %arrange.2.y1.refs_0_), channel_id=1, source_target_pairs={{0,2},{1,3},{2,4},{3,5},{4,6},{5,7},{6,0},{7,1},{8,10},{9,11},{10,... | collective-permute-start | bytes 589832 | tf_op jit(solution)/shard_map/ppermute | solution.py:391
  6.0 10.0 %collective-permute-start.2 = (bf16[4,96,256]{2,1,0:T(8,128)(2,1)S(1)}, bf16[4,96,256]{2,1,0:T(8,128)(2,1)S(1)}, u32[]{:S(2)}, u32[]{:S(2)}) collective-permute-start(bf16[4,96,256]{2,1,0:T(8,128)(2,1)S(1)} %arrange.3.y2.refs_1_), channel_id=1, source_target_pairs={{0,2},{1,3},{2,4},{3,5},{4,6},{5,7},{6,0},{7,1},{8,10},{9,11},{10,... | collective-permute-start | bytes 589832 | tf_op jit(solution)/shard_map/ppermute | solution.py:391
  10.3 5.7 %collective-permute-start.4 = (bf16[4,96,256]{2,1,0:T(8,128)(2,1)S(1)}, bf16[4,96,256]{2,1,0:T(8,128)(2,1)S(1)}, u32[]{:S(2)}, u32[]{:S(2)}) collective-permute-start(bf16[4,96,256]{2,1,0:T(8,128)(2,1)S(1)} %arrange.2.y1.refs_0_), channel_id=1, source_target_pairs={{0,1},{1,0},{2,3},{3,2},{4,5},{5,4},{6,7},{7,6},{8,9},{9,8},{10,11... | collective-permute-start | bytes 589832 | tf_op jit(solution)/shard_map/ppermute | solution.py:388
  10.4 5.6 %collective-permute-start.5 = (bf16[4,96,256]{2,1,0:T(8,128)(2,1)S(1)}, bf16[4,96,256]{2,1,0:T(8,128)(2,1)S(1)}, u32[]{:S(2)}, u32[]{:S(2)}) collective-permute-start(bf16[4,96,256]{2,1,0:T(8,128)(2,1)S(1)} %arrange.3.y2.refs_1_), channel_id=1, source_target_pairs={{0,1},{1,0},{2,3},{3,2},{4,5},{5,4},{6,7},{7,6},{8,9},{9,8},{10,11... | collective-permute-start | bytes 589832 | tf_op jit(solution)/shard_map/ppermute | solution.py:388
  12.6 9.7 %collective-permute-start.7 = (bf16[4,96,256]{2,1,0:T(8,128)(2,1)S(1)}, bf16[4,96,256]{2,1,0:T(8,128)(2,1)S(1)}, u32[]{:S(2)}, u32[]{:S(2)}) collective-permute-start(bf16[4,96,256]{2,1,0:T(8,128)(2,1)S(1)} %collective-permute-done.refs_0_), channel_id=1, source_target_pairs={{0,1},{1,0},{2,3},{3,2},{4,5},{5,4},{6,7},{7,6},{8,9},{9,8},{10,11... | collective-permute-start | bytes 589832 | tf_op jit(solution)/shard_map/ppermute | solution.py:388
  12.6 14.9 %collective-permute-start.1 = (bf16[4,96,256]{2,1,0:T(8,128)(2,1)S(1)}, bf16[4,96,256]{2,1,0:T(8,128)(2,1)S(1)}, u32[]{:S(2)}, u32[]{:S(2)}) collective-permute-start(bf16[4,96,256]{2,1,0:T(8,128)(2,1)S(1)} %collective-permute-done.refs_0_), channel_id=1, source_target_pairs={{0,2},{1,3},{2,4},{3,5},{4,6},{5,7},{6,0},{7,1},{8,10},{9,11},{10,... | collective-permute-start | bytes 589832 | tf_op jit(solution)/shard_map/ppermute | solution.py:401
  16.0 6.4 %collective-permute-start.8 = (bf16[4,96,256]{2,1,0:T(8,128)(2,1)S(1)}, bf16[4,96,256]{2,1,0:T(8,128)(2,1)S(1)}, u32[]{:S(2)}, u32[]{:S(2)}) collective-permute-start(bf16[4,96,256]{2,1,0:T(8,128)(2,1)S(1)} %collective-permute-done.2.refs_1_), channel_id=1, source_target_pairs={{0,1},{1,0},{2,3},{3,2},{4,5},{5,4},{6,7},{7,6},{8,9},{9,8},{10,11... | collective-permute-start | bytes 589832 | tf_op jit(solution)/shard_map/ppermute | solution.py:388
  16.0 11.5 %collective-permute-start.3 = (bf16[4,96,256]{2,1,0:T(8,128)(2,1)S(1)}, bf16[4,96,256]{2,1,0:T(8,128)(2,1)S(1)}, u32[]{:S(2)}, u32[]{:S(2)}) collective-permute-start(bf16[4,96,256]{2,1,0:T(8,128)(2,1)S(1)} %collective-permute-done.2.refs_1_), channel_id=1, source_target_pairs={{0,2},{1,3},{2,4},{3,5},{4,6},{5,7},{6,0},{7,1},{8,10},{9,11},{10,... | collective-permute-start | bytes 589832 | tf_op jit(solution)/shard_map/ppermute | solution.py:401
  17.4 10.1 %collective-permute-start.6 = (bf16[288,128]{1,0:T(8,128)(2,1)S(1)}, bf16[288,128]{1,0:T(8,128)(2,1)S(1)}, u32[]{:S(2)}, u32[]{:S(2)}) collective-permute-start(bf16[288,128]{1,0:T(8,128)(2,1)S(1)} %far.1), channel_id=1, source_target_pairs={{0,6},{1,7},{2,0},{3,1},{4,2},{5,3},{6,4},{7,5},{8,14},{9,15},{10,... | collective-permute-start | bytes 221192 | tf_op jit(solution)/shard_map/ppermute | solution.py:408
  22.8 14.5 %copy-start = (f32[2]{0:T(128)S(1)}, f32[2]{0:T(128)}, u32[]{:S(2)}) copy-start(f32[2]{0:T(128)} %param.11) | copy-start | bytes 28
  28.1 1.4 %collective-permute-start.9 = (f32[192,96]{1,0:T(8,128)S(1)}, f32[192,96]{1,0:T(8,128)S(1)}, u32[]{:S(2)}, u32[]{:S(2)}) collective-permute-start(f32[192,96]{1,0:T(8,128)S(1)} %get-tuple-element.44), channel_id=1, source_target_pairs={{0,1},{1,0},{2,3},{3,2},{4,5},{5,4},{6,7},{7,6},{8,9},{9,8},{10,11... | collective-permute-start | bytes 221192 | tf_op jit(solution)/shard_map/ppermute | solution.py:388
  29.6 5.4 %collective-permute-start.10 = (bf16[288,128]{1,0:T(8,128)(2,1)S(1)}, bf16[288,128]{1,0:T(8,128)(2,1)S(1)}, u32[]{:S(2)}, u32[]{:S(2)}) collective-permute-start(bf16[288,128]{1,0:T(8,128)(2,1)S(1)} %get-tuple-element.47), channel_id=1, source_target_pairs={{0,24},{8,16},{16,8},{24,0},{1,25},{9,17},{17,9},{25,1},{2,26},{10... | collective-permute-start | bytes 221192 | tf_op jit(solution)/shard_map/ppermute | solution.py:423
  32.4 4.4 %collective-permute-start.11 = (bf16[288,128]{1,0:T(8,128)(2,1)S(1)}, bf16[288,128]{1,0:T(8,128)(2,1)S(1)}, u32[]{:S(2)}, u32[]{:S(2)}) collective-permute-start(bf16[288,128]{1,0:T(8,128)(2,1)S(1)} %get-tuple-element.48), channel_id=1, source_target_pairs={{0,16},{8,24},{16,0},{24,8},{1,17},{9,25},{17,1},{25,9},{2,18},{10... | collective-permute-start | bytes 221192 | tf_op jit(solution)/shard_map/ppermute | solution.py:423
  32.9 4.4 %collective-permute-start.12 = (bf16[288,128]{1,0:T(8,128)(2,1)S(1)}, bf16[288,128]{1,0:T(8,128)(2,1)S(1)}, u32[]{:S(2)}, u32[]{:S(2)}) collective-permute-start(bf16[288,128]{1,0:T(8,128)(2,1)S(1)} %get-tuple-element.49), channel_id=1, source_target_pairs={{0,8},{8,0},{16,24},{24,16},{1,9},{9,1},{17,25},{25,17},{2,10},{10... | collective-permute-start | bytes 221192 | tf_op jit(solution)/shard_map/ppermute | solution.py:423

commit v14 on v13

--- a/solution.py
+++ b/solution.py
@@ -183,25 +183,23 @@
     )(greens, *sibling)
 
 
-def both_kernel(z_ref, sibling_ref, y1, y2, mine_ref, theirs_ref):
-    for operand, out_ref in ((sibling_ref, theirs_ref), (z_ref, mine_ref)):
-        total = jnp.zeros(out_ref.shape, jnp.float32)
-        for half, y in enumerate((y1, y2)):
-            for j in range(y.shape[0]):
-                total += lax.dot_general(operand[half, j], y[j], NT_DIMS, preferred_element_type=jnp.float32)
-        out_ref[...] = total
-
-
-def both(z, z_sibling, pieces):
-    share = jax.ShapeDtypeStruct((z.shape[2], pieces[0].shape[1]), jnp.float32)
-    return call(
-        both_kernel,
-        "both",
+def last_kernel(z_ref, y1, y2, out_ref):
+    total = jnp.zeros(out_ref.shape, jnp.float32)
+    for half, y in enumerate((y1, y2)):
+        for j in range(y.shape[0]):
+            total += lax.dot_general(z_ref[half, j], y[j], NT_DIMS, preferred_element_type=jnp.float32)
+    out_ref[...] = total
+
+
+def last_share(z, pieces):
+    return call(
+        last_kernel,
+        "last_share",
         1 << 29,
-        out_shape=(share, share),
-        in_specs=[VMEM] * 4,
-        out_specs=(VMEM, VMEM),
-    )(z, z_sibling, *pieces)
+        out_shape=jax.ShapeDtypeStruct((z.shape[2], pieces[0].shape[1]), jnp.float32),
+        in_specs=[VMEM] * 3,
+        out_specs=VMEM,
+    )(z, *pieces)
 
 
 def near_kernel(count, z_ref, *refs):
@@ -400,8 +398,9 @@
         if not last:
             arriving = [lax.ppermute(a, "aux", along(1)) for a in held]
         if last:
-            mine, theirs = both(z, z_sibling, held)
-            backs += [mine, to_sibling(theirs)]
+            theirs = last_share(z_sibling, held)
+            *pieces, theirs = lax.optimization_barrier((*held, theirs))
+            backs += [last_share(z, pieces), to_sibling(theirs)]
             continue
         other = [to_sibling(a) for a in held]
         share = far(w, held)

time: 47.5 us -> 47.3 us (level)
  transfers between devices with their start and end apart: 13 -> 13, of which waited for: 7 -> 7; matrix products, arithmetic and copies ran while one was open for 0% -> 0% of each run, Pallas kernels for 14% -> 15%
where the time goes in v14:
time: 47.3 us; the launch traced here: 47 us
  waiting for transfers between devices  14.8 us (31%)
  starting transfers between devices  12.9 us (27%)
  Pallas kernels  9.78 us (21%)
  blocking collectives  8.87 us (19%)
  between operations  0.76 us (2%)
    all_to_all x1, blocking collectives, per_device(): everyone = lax.all_to_all(sums, ('pair', 'aux'), 0, 0, tiled=True)  8.87 us
    ppermute x2, waiting for transfers between devices, per_device(): arriving = [lax.ppermute(a, 'aux', along(1)) for a in own]  5.07 us
    ppermute x1, waiting for transfers between devices, per_device(): ahead = lax.ppermute(share, 'aux', along(-step))  4.73 us
    ppermute x2, starting transfers between devices, per_device(): arriving = [lax.ppermute(a, 'aux', along(1)) for a in own]  4.71 us
    ppermute x3, waiting for transfers between devices, per_device(): lax.ppermute(sends[j - 1], 'pair', [(i, i ^ j) for i in range(pairs)])  4.07 us
    ppermute x1, starting transfers between devices, per_device(): ahead = lax.ppermute(share, 'aux', along(-step))  3.85 us
    ppermute x3, starting transfers between devices, per_device(): lax.ppermute(sends[j - 1], 'pair', [(i, i ^ j) for i in range(pairs)])  3.55 us
    pallas_call x1, Pallas kernels, transform(): call(functools.partial(transform_kernel, nt, rows), 'transform', 2 << 30,...  2.67 us
  transfers between devices with their start and end apart: 13, of which 7 were waited for; matrix products, arithmetic and copies ran while one was open for 0% of the time, Pallas kernels for 15%

profile of v14, /device:TPU:0, one launch (start us, length us, event | category | flops | bytes accessed | tf_op | source)
XLA Modules:
  0.0 47.0 jit_solution(1503297680223183299)
XLA Ops:
  0.6 1.1 %arrange.2.y1.refs_0_ = bf16[4,96,256]{2,1,0:T(8,128)(2,1)S(1)} custom-call(bf16[32,6144]{1,0:T(8,128)(2,1)} %x_hbm.3, s32[2,96]{1,0:T(2,128)} %mask_hbm.3), custom_call_target="tpu_custom_call" | custom-call | flops 268435456 | bytes 256 | tf_op jit(solution)/shard_map/arrange/pallas_call | solution.py:62
  1.8 3.1 %collective-permute-start = (bf16[4,96,256]{2,1,0:T(8,128)(2,1)S(1)}, bf16[4,96,256]{2,1,0:T(8,128)(2,1)S(1)}, u32[]{:S(2)}, u32[]{:S(2)}) collective-permute-start(bf16[4,96,256]{2,1,0:T(8,128)(2,1)S(1)} %arrange.2.y1.refs_0_), channel_id=1, source_target_pairs={{0,2},{1,3},{2,4},{3,5},{4,6},{5,7},{6,0},{7,1},{8,10},{9,11},{10,... | collective-permute-start | bytes 589832 | tf_op jit(solution)/shard_map/ppermute | solution.py:389
  4.9 1.1 %arrange.3.y2.refs_1_ = bf16[4,96,256]{2,1,0:T(8,128)(2,1)S(1)} custom-call(bf16[32,6144]{1,0:T(8,128)(2,1)} %x_hbm.3, s32[2,96]{1,0:T(2,128)} %mask_hbm.3), custom_call_target="tpu_custom_call" | custom-call | flops 268435456 | bytes 256 | tf_op jit(solution)/shard_map/arrange/pallas_call | solution.py:62
  6.0 1.6 %collective-permute-start.2 = (bf16[4,96,256]{2,1,0:T(8,128)(2,1)S(1)}, bf16[4,96,256]{2,1,0:T(8,128)(2,1)S(1)}, u32[]{:S(2)}, u32[]{:S(2)}) collective-permute-start(bf16[4,96,256]{2,1,0:T(8,128)(2,1)S(1)} %arrange.3.y2.refs_1_), channel_id=1, source_target_pairs={{0,2},{1,3},{2,4},{3,5},{4,6},{5,7},{6,0},{7,1},{8,10},{9,11},{10,... | collective-permute-start | bytes 589832 | tf_op jit(solution)/shard_map/ppermute | solution.py:389
  7.6 2.7 %transform.1 = (bf16[2,4,192,256]{3,2,1,0:T(8,128)(2,1)S(1)}, bf16[2,2,4,192,256]{4,3,2,1,0:T(8,128)(2,1)S(1)}, bf16[2,2,256,256]{3,2,1,0:T(8,128)(2,1)S(1)}) custom-call(s32[2]{0:T(128)} %atom_hbm.1, bf16[2,16,64,64]{3,2,1,0:T(8,128)(2,1)} %occ_hbm.1, bf16[2,16,64,64]{3,2,1,0:T(8,128)(2,1)} %virt_hbm.1, bf16[4,96,256]{2,1,0:T(8,128)(2,1)S(1)} %arrange.2.y1.refs_0_, ...), custom_call_target="tpu_custom_call" | custom-call | flops 2147483648 | bytes 256 | tf_op jit(solution)/shard_map/transform/pallas_call | solution.py:128
  10.3 0.1 collective-permute-start.4
  10.4 0.5 %collective-permute-start.5 = (bf16[4,96,256]{2,1,0:T(8,128)(2,1)S(1)}, bf16[4,96,256]{2,1,0:T(8,128)(2,1)S(1)}, u32[]{:S(2)}, u32[]{:S(2)}) collective-permute-start(bf16[4,96,256]{2,1,0:T(8,128)(2,1)S(1)} %arrange.3.y2.refs_1_), channel_id=1, source_target_pairs={{0,1},{1,0},{2,3},{3,2},{4,5},{5,4},{6,7},{7,6},{8,9},{9,8},{10,11... | collective-permute-start | bytes 589832 | tf_op jit(solution)/shard_map/ppermute | solution.py:386
  10.9 1.7 %collective-permute-done.refs_0_ = bf16[4,96,256]{2,1,0:T(8,128)(2,1)S(1)} collective-permute-done((bf16[4,96,256]{2,1,0:T(8,128)(2,1)S(1)}, bf16[4,96,256]{2,1,0:T(8,128)(2,1)S(1)}, u32[]{:S(2)}, u32[]{:S(2)}) %collective-permute-start) | collective-permute-done | bytes 196640 | tf_op jit(solution)/shard_map/ppermute | solution.py:389
  12.6 0.0 collective-permute-start.7
  12.6 0.0 collective-permute-start.1
  12.7 3.3 %collective-permute-done.2.refs_1_ = bf16[4,96,256]{2,1,0:T(8,128)(2,1)S(1)} collective-permute-done((bf16[4,96,256]{2,1,0:T(8,128)(2,1)S(1)}, bf16[4,96,256]{2,1,0:T(8,128)(2,1)S(1)}, u32[]{:S(2)}, u32[]{:S(2)}) %collective-permute-start.2) | collective-permute-done | bytes 196640 | tf_op jit(solution)/shard_map/ppermute | solution.py:389
  16.0 0.0 collective-permute-start.8
  16.0 0.0 collective-permute-done.4.y1.refs_2_
  16.0 0.0 collective-permute-start.3
  16.0 0.0 collective-permute-done.5.y2.refs_3_
  16.0 0.7 %complete.1.w_ref = bf16[2,2,4,192,256]{4,3,2,1,0:T(8,128)(2,1)S(1)} custom-call(bf16[2,2,4,192,256]{4,3,2,1,0:T(8,128)(2,1)S(1)} %get-tuple-element.32.before_ref, bf16[2,2,256,256]{3,2,1,0:T(8,128)(2,1)S(1)} %get-tuple-element.33.green_ref, bf16[4,96,256]{2,1,0:T(8,128)(2,1)S(1)} %collective-permute-done.4.y1.refs_2_, ...), custom_call_target="tpu_custom_call", output_to_operand_aliasing={{}: (0, {})} | custom-call | flops 1073741824 | bytes 256 | tf_op jit(solution)/shard_map/complete/pallas_call | solution.py:156
  16.7 0.7 %far.1 = bf16[288,128]{1,0:T(8,128)(2,1)S(1)} custom-call(bf16[2,2,4,192,256]{4,3,2,1,0:T(8,128)(2,1)S(1)} %complete.1.w_ref, bf16[4,96,256]{2,1,0:T(8,128)(2,1)S(1)} %collective-permute-done.refs_0_, bf16[4,96,256]{2,1,0:T(8,128)(2,1)S(1)} %collective-permute-done.2.refs_1_), custom_call_target="tpu_custom_call" | custom-call | flops 536870912 | bytes 256 | tf_op jit(solution)/shard_map/far/pallas_call | solution.py:262
  17.4 3.9 %collective-permute-start.6 = (bf16[288,128]{1,0:T(8,128)(2,1)S(1)}, bf16[288,128]{1,0:T(8,128)(2,1)S(1)}, u32[]{:S(2)}, u32[]{:S(2)}) collective-permute-start(bf16[288,128]{1,0:T(8,128)(2,1)S(1)} %far.1), channel_id=1, source_target_pairs={{0,6},{1,7},{2,0},{3,1},{4,2},{5,3},{6,4},{7,5},{8,14},{9,15},{10,... | collective-permute-start | bytes 221192 | tf_op jit(solution)/shard_map/ppermute | solution.py:407
  21.3 0.7 %mirror.1.z_ref = bf16[2,4,192,256]{3,2,1,0:T(8,128)(2,1)S(1)} custom-call(bf16[2,2,256,256]{3,2,1,0:T(8,128)(2,1)S(1)} %get-tuple-element.33.green_ref, bf16[4,96,256]{2,1,0:T(8,128)(2,1)S(1)} %collective-permute-done.4.y1.refs_2_, bf16[4,96,256]{2,1,0:T(8,128)(2,1)S(1)} %collective-permute-done.5.y2.refs_3_), custom_call_target="tpu_custom_call" | custom-call | flops 536870912 | bytes 256 | tf_op jit(solution)/shard_map/mirror/pallas_call | solution.py:176
  21.9 0.4 near.3.refs_0_
  22.4 0.0 collective-permute-done.7.refs_2_
  22.4 0.0 collective-permute-done.8.refs_3_
  22.4 0.4 near.2.refs_1_
  22.8 4.7 %collective-permute-done.6.refs_4_ = bf16[288,128]{1,0:T(8,128)(2,1)S(1)} collective-permute-done((bf16[288,128]{1,0:T(8,128)(2,1)S(1)}, bf16[288,128]{1,0:T(8,128)(2,1)S(1)}, u32[]{:S(2)}, u32[]{:S(2)}) %collective-permute-start.6) | collective-permute-done | bytes 73760 | tf_op jit(solution)/shard_map/ppermute | solution.py:407
  27.5 0.0 collective-permute-done.1.y1
  27.5 0.0 collective-permute-done.3.y2
  27.5 0.4 last_share.2
  27.9 0.0 copy-start
  27.9 0.1 collective-permute-start.9
  28.0 0.4 last_share.3.refs_2_
  28.4 0.9 %collective-permute-done.9.refs_3_ = f32[192,96]{1,0:T(8,128)S(1)} collective-permute-done((f32[192,96]{1,0:T(8,128)S(1)}, f32[192,96]{1,0:T(8,128)S(1)}, u32[]{:S(2)}, u32[]{:S(2)}) %collective-permute-start.9) | collective-permute-done | bytes 73760 | tf_op jit(solution)/shard_map/ppermute | solution.py:386
  29.3 0.2 pack.1
  29.5 2.8 %collective-permute-start.10 = (bf16[288,128]{1,0:T(8,128)(2,1)S(1)}, bf16[288,128]{1,0:T(8,128)(2,1)S(1)}, u32[]{:S(2)}, u32[]{:S(2)}) collective-permute-start(bf16[288,128]{1,0:T(8,128)(2,1)S(1)} %get-tuple-element.49), channel_id=1, source_target_pairs={{0,24},{8,16},{16,8},{24,0},{1,25},{9,17},{17,9},{25,1},{2,26},{10... | collective-permute-start | bytes 221192 | tf_op jit(solution)/shard_map/ppermute | solution.py:422
  32.2 0.5 %collective-permute-start.11 = (bf16[288,128]{1,0:T(8,128)(2,1)S(1)}, bf16[288,128]{1,0:T(8,128)(2,1)S(1)}, u32[]{:S(2)}, u32[]{:S(2)}) collective-permute-start(bf16[288,128]{1,0:T(8,128)(2,1)S(1)} %get-tuple-element.50), channel_id=1, source_target_pairs={{0,16},{8,24},{16,0},{24,8},{1,17},{9,25},{17,1},{25,9},{2,18},{10... | collective-permute-start | bytes 221192 | tf_op jit(solution)/shard_map/ppermute | solution.py:422
  32.8 0.3 collective-permute-start.12
  33.0 1.8 %collective-permute-done.10.refs_1_ = bf16[288,128]{1,0:T(8,128)(2,1)S(1)} collective-permute-done((bf16[288,128]{1,0:T(8,128)(2,1)S(1)}, bf16[288,128]{1,0:T(8,128)(2,1)S(1)}, u32[]{:S(2)}, u32[]{:S(2)}) %collective-permute-start.10) | collective-permute-done | bytes 73760 | tf_op jit(solution)/shard_map/ppermute | solution.py:422
  34.9 1.7 %collective-permute-done.11.refs_2_ = bf16[288,128]{1,0:T(8,128)(2,1)S(1)} collective-permute-done((bf16[288,128]{1,0:T(8,128)(2,1)S(1)}, bf16[288,128]{1,0:T(8,128)(2,1)S(1)}, u32[]{:S(2)}, u32[]{:S(2)}) %collective-permute-start.11) | collective-permute-done | bytes 73760 | tf_op jit(solution)/shard_map/ppermute | solution.py:422
  36.6 0.5 %collective-permute-done.12.refs_3_ = bf16[288,128]{1,0:T(8,128)(2,1)S(1)} collective-permute-done((bf16[288,128]{1,0:T(8,128)(2,1)S(1)}, bf16[288,128]{1,0:T(8,128)(2,1)S(1)}, u32[]{:S(2)}, u32[]{:S(2)}) %collective-permute-start.12) | collective-permute-done | bytes 73760 | tf_op jit(solution)/shard_map/ppermute | solution.py:422
  37.1 0.0 copy-done
  37.1 0.4 combine.1
  37.5 8.9 %all_to_all.11 = f32[32,1,128]{2,1,0:T(1,128)S(1)} all-to-all(f32[32,1,128]{2,1,0:T(1,128)S(1)} %bitcast.6), channel_id=1, replica_groups=mesh['pair'=4,'aux'=8] {'pair','aux'}, dimensions={0} | all-to-all | bytes 32768 | tf_op jit(solution)/shard_map/all_to_all | solution.py:429
  46.3 0.7 %close.1 = (f32[2,96,192]{2,1,0:T(8,128)}, f32[1,1]{1,0:T(1,128)}) custom-call(f32[2,96,192]{2,1,0:T(8,128)S(1)} %get-tuple-element.52.tile_ref, f32[32,128]{1,0:T(8,128)S(1)} %bitcast.7), custom_call_target="tpu_custom_call" | custom-call | flops 268435456 | bytes 256 | tf_op jit(solution)/shard_map/close/pallas_call | solution.py:359
Async XLA Ops:
  1.8 10.8 %collective-permute-start = (bf16[4,96,256]{2,1,0:T(8,128)(2,1)S(1)}, bf16[4,96,256]{2,1,0:T(8,128)(2,1)S(1)}, u32[]{:S(2)}, u32[]{:S(2)}) collective-permute-start(bf16[4,96,256]{2,1,0:T(8,128)(2,1)S(1)} %arrange.2.y1.refs_0_), channel_id=1, source_target_pairs={{0,2},{1,3},{2,4},{3,5},{4,6},{5,7},{6,0},{7,1},{8,10},{9,11},{10,... | collective-permute-start | bytes 589832 | tf_op jit(solution)/shard_map/ppermute | solution.py:389
  6.0 10.0 %collective-permute-start.2 = (bf16[4,96,256]{2,1,0:T(8,128)(2,1)S(1)}, bf16[4,96,256]{2,1,0:T(8,128)(2,1)S(1)}, u32[]{:S(2)}, u32[]{:S(2)}) collective-permute-start(bf16[4,96,256]{2,1,0:T(8,128)(2,1)S(1)} %arrange.3.y2.refs_1_), channel_id=1, source_target_pairs={{0,2},{1,3},{2,4},{3,5},{4,6},{5,7},{6,0},{7,1},{8,10},{9,11},{10,... | collective-permute-start | bytes 589832 | tf_op jit(solution)/shard_map/ppermute | solution.py:389
  10.3 5.7 %collective-permute-start.4 = (bf16[4,96,256]{2,1,0:T(8,128)(2,1)S(1)}, bf16[4,96,256]{2,1,0:T(8,128)(2,1)S(1)}, u32[]{:S(2)}, u32[]{:S(2)}) collective-permute-start(bf16[4,96,256]{2,1,0:T(8,128)(2,1)S(1)} %arrange.2.y1.refs_0_), channel_id=1, source_target_pairs={{0,1},{1,0},{2,3},{3,2},{4,5},{5,4},{6,7},{7,6},{8,9},{9,8},{10,11... | collective-permute-start | bytes 589832 | tf_op jit(solution)/shard_map/ppermute | solution.py:386
  10.4 5.6 %collective-permute-start.5 = (bf16[4,96,256]{2,1,0:T(8,128)(2,1)S(1)}, bf16[4,96,256]{2,1,0:T(8,128)(2,1)S(1)}, u32[]{:S(2)}, u32[]{:S(2)}) collective-permute-start(bf16[4,96,256]{2,1,0:T(8,128)(2,1)S(1)} %arrange.3.y2.refs_1_), channel_id=1, source_target_pairs={{0,1},{1,0},{2,3},{3,2},{4,5},{5,4},{6,7},{7,6},{8,9},{9,8},{10,11... | collective-permute-start | bytes 589832 | tf_op jit(solution)/shard_map/ppermute | solution.py:386
  12.6 9.7 %collective-permute-start.7 = (bf16[4,96,256]{2,1,0:T(8,128)(2,1)S(1)}, bf16[4,96,256]{2,1,0:T(8,128)(2,1)S(1)}, u32[]{:S(2)}, u32[]{:S(2)}) collective-permute-start(bf16[4,96,256]{2,1,0:T(8,128)(2,1)S(1)} %collective-permute-done.refs_0_), channel_id=1, source_target_pairs={{0,1},{1,0},{2,3},{3,2},{4,5},{5,4},{6,7},{7,6},{8,9},{9,8},{10,11... | collective-permute-start | bytes 589832 | tf_op jit(solution)/shard_map/ppermute | solution.py:386
  12.6 14.9 %collective-permute-start.1 = (bf16[4,96,256]{2,1,0:T(8,128)(2,1)S(1)}, bf16[4,96,256]{2,1,0:T(8,128)(2,1)S(1)}, u32[]{:S(2)}, u32[]{:S(2)}) collective-permute-start(bf16[4,96,256]{2,1,0:T(8,128)(2,1)S(1)} %collective-permute-done.refs_0_), channel_id=1, source_target_pairs={{0,2},{1,3},{2,4},{3,5},{4,6},{5,7},{6,0},{7,1},{8,10},{9,11},{10,... | collective-permute-start | bytes 589832 | tf_op jit(solution)/shard_map/ppermute | solution.py:399
  16.0 6.4 %collective-permute-start.8 = (bf16[4,96,256]{2,1,0:T(8,128)(2,1)S(1)}, bf16[4,96,256]{2,1,0:T(8,128)(2,1)S(1)}, u32[]{:S(2)}, u32[]{:S(2)}) collective-permute-start(bf16[4,96,256]{2,1,0:T(8,128)(2,1)S(1)} %collective-permute-done.2.refs_1_), channel_id=1, source_target_pairs={{0,1},{1,0},{2,3},{3,2},{4,5},{5,4},{6,7},{7,6},{8,9},{9,8},{10,11... | collective-permute-start | bytes 589832 | tf_op jit(solution)/shard_map/ppermute | solution.py:386
  16.0 11.5 %collective-permute-start.3 = (bf16[4,96,256]{2,1,0:T(8,128)(2,1)S(1)}, bf16[4,96,256]{2,1,0:T(8,128)(2,1)S(1)}, u32[]{:S(2)}, u32[]{:S(2)}) collective-permute-start(bf16[4,96,256]{2,1,0:T(8,128)(2,1)S(1)} %collective-permute-done.2.refs_1_), channel_id=1, source_target_pairs={{0,2},{1,3},{2,4},{3,5},{4,6},{5,7},{6,0},{7,1},{8,10},{9,11},{10,... | collective-permute-start | bytes 589832 | tf_op jit(solution)/shard_map/ppermute | solution.py:399
  17.4 10.1 %collective-permute-start.6 = (bf16[288,128]{1,0:T(8,128)(2,1)S(1)}, bf16[288,128]{1,0:T(8,128)(2,1)S(1)}, u32[]{:S(2)}, u32[]{:S(2)}) collective-permute-start(bf16[288,128]{1,0:T(8,128)(2,1)S(1)} %far.1), channel_id=1, source_target_pairs={{0,6},{1,7},{2,0},{3,1},{4,2},{5,3},{6,4},{7,5},{8,14},{9,15},{10,... | collective-permute-start | bytes 221192 | tf_op jit(solution)/shard_map/ppermute | solution.py:407
  27.9 9.2 %copy-start = (f32[2]{0:T(128)S(1)}, f32[2]{0:T(128)}, u32[]{:S(2)}) copy-start(f32[2]{0:T(128)} %param.11) | copy-start | bytes 28
  27.9 1.4 %collective-permute-start.9 = (f32[192,96]{1,0:T(8,128)S(1)}, f32[192,96]{1,0:T(8,128)S(1)}, u32[]{:S(2)}, u32[]{:S(2)}) collective-permute-start(f32[192,96]{1,0:T(8,128)S(1)} %last_share.2), channel_id=1, source_target_pairs={{0,1},{1,0},{2,3},{3,2},{4,5},{5,4},{6,7},{7,6},{8,9},{9,8},{10,11... | collective-permute-start | bytes 221192 | tf_op jit(solution)/shard_map/ppermute | solution.py:386
  29.5 5.4 %collective-permute-start.10 = (bf16[288,128]{1,0:T(8,128)(2,1)S(1)}, bf16[288,128]{1,0:T(8,128)(2,1)S(1)}, u32[]{:S(2)}, u32[]{:S(2)}) collective-permute-start(bf16[288,128]{1,0:T(8,128)(2,1)S(1)} %get-tuple-element.49), channel_id=1, source_target_pairs={{0,24},{8,16},{16,8},{24,0},{1,25},{9,17},{17,9},{25,1},{2,26},{10... | collective-permute-start | bytes 221192 | tf_op jit(solution)/shard_map/ppermute | solution.py:422
  32.2 4.4 %collective-permute-start.11 = (bf16[288,128]{1,0:T(8,128)(2,1)S(1)}, bf16[288,128]{1,0:T(8,128)(2,1)S(1)}, u32[]{:S(2)}, u32[]{:S(2)}) collective-permute-start(bf16[288,128]{1,0:T(8,128)(2,1)S(1)} %get-tuple-element.50), channel_id=1, source_target_pairs={{0,16},{8,24},{16,0},{24,8},{1,17},{9,25},{17,1},{25,9},{2,18},{10... | collective-permute-start | bytes 221192 | tf_op jit(solution)/shard_map/ppermute | solution.py:422
  32.8 4.4 %collective-permute-start.12 = (bf16[288,128]{1,0:T(8,128)(2,1)S(1)}, bf16[288,128]{1,0:T(8,128)(2,1)S(1)}, u32[]{:S(2)}, u32[]{:S(2)}) collective-permute-start(bf16[288,128]{1,0:T(8,128)(2,1)S(1)} %get-tuple-element.51), channel_id=1, source_target_pairs={{0,8},{8,0},{16,24},{24,16},{1,9},{9,1},{17,25},{25,17},{2,10},{10... | collective-permute-start | bytes 221192 | tf_op jit(solution)/shard_map/ppermute | solution.py:422

commit v15 on v14

--- a/solution.py
+++ b/solution.py
@@ -418,7 +418,8 @@
     if columns == 2 * aux_here and pairs & (pairs - 1) == 0:
         mine, *sends = pack(chips, pairs, backs, aheads)
         parts = [mine]
-        for j in range(pairs - 1, 0, -1):
+        half = pairs // 2
+        for j in [half, *range(pairs - 1, half, -1), *range(half - 1, 0, -1)]:
             parts.append(lax.ppermute(sends[j - 1], "pair", [(i, i ^ j) for i in range(pairs)]))
     else:
         (shares,) = pack(chips, None, backs, aheads)

time: 47.3 us -> 48 us (1.015)
  blocking collectives: 8.87 us -> 9.43 us
    all_to_all x1, blocking collectives: 8.87 us -> 9.43 us  [per_device(): everyone = lax.all_to_all(sums, ('pair', 'aux'), 0, 0, tiled=True)]
  transfers between devices with their start and end apart: 13 -> 13, of which waited for: 7 -> 6; matrix products, arithmetic and copies ran while one was open for 0% -> 0% of each run, Pallas kernels for 15% -> 15%
where the time goes in v15:
time: 48 us; the launch traced here: 47.7 us
  waiting for transfers between devices  14.9 us (31%)
  starting transfers between devices  12.9 us (27%)
  Pallas kernels  9.78 us (20%)
  blocking collectives  9.43 us (20%)
  between operations  0.76 us (2%)
    all_to_all x1, blocking collectives, per_device(): everyone = lax.all_to_all(sums, ('pair', 'aux'), 0, 0, tiled=True)  9.43 us
    ppermute x2, waiting for transfers between devices, per_device(): arriving = [lax.ppermute(a, 'aux', along(1)) for a in own]  5.07 us
    ppermute x1, waiting for transfers between devices, per_device(): ahead = lax.ppermute(share, 'aux', along(-step))  4.73 us
    ppermute x2, starting transfers between devices, per_device(): arriving = [lax.ppermute(a, 'aux', along(1)) for a in own]  4.71 us
    ppermute x3, waiting for transfers between devices, per_device(): lax.ppermute(sends[j - 1], 'pair', [(i, i ^ j) for i in range(pairs)])  4.22 us
    ppermute x1, starting transfers between devices, per_device(): ahead = lax.ppermute(share, 'aux', along(-step))  3.85 us
    ppermute x3, starting transfers between devices, per_device(): lax.ppermute(sends[j - 1], 'pair', [(i, i ^ j) for i in range(pairs)])  3.55 us
    pallas_call x1, Pallas kernels, transform(): call(functools.partial(transform_kernel, nt, rows), 'transform', 2 << 30,...  2.67 us
  transfers between devices with their start and end apart: 13, of which 6 were waited for; matrix products, arithmetic and copies ran while one was open for 0% of the time, Pallas kernels for 15%

profile of v15, /device:TPU:0, one launch (start us, length us, event | category | flops | bytes accessed | tf_op | source)
XLA Modules:
  0.0 47.7 jit_solution(14159622515744226902)
XLA Ops:
  0.6 1.1 %arrange.2.y1.refs_0_ = bf16[4,96,256]{2,1,0:T(8,128)(2,1)S(1)} custom-call(bf16[32,6144]{1,0:T(8,128)(2,1)} %x_hbm.3, s32[2,96]{1,0:T(2,128)} %mask_hbm.3), custom_call_target="tpu_custom_call" | custom-call | flops 268435456 | bytes 256 | tf_op jit(solution)/shard_map/arrange/pallas_call | solution.py:62
  1.8 3.1 %collective-permute-start = (bf16[4,96,256]{2,1,0:T(8,128)(2,1)S(1)}, bf16[4,96,256]{2,1,0:T(8,128)(2,1)S(1)}, u32[]{:S(2)}, u32[]{:S(2)}) collective-permute-start(bf16[4,96,256]{2,1,0:T(8,128)(2,1)S(1)} %arrange.2.y1.refs_0_), channel_id=1, source_target_pairs={{0,2},{1,3},{2,4},{3,5},{4,6},{5,7},{6,0},{7,1},{8,10},{9,11},{10,... | collective-permute-start | bytes 589832 | tf_op jit(solution)/shard_map/ppermute | solution.py:389
  4.9 1.1 %arrange.3.y2.refs_1_ = bf16[4,96,256]{2,1,0:T(8,128)(2,1)S(1)} custom-call(bf16[32,6144]{1,0:T(8,128)(2,1)} %x_hbm.3, s32[2,96]{1,0:T(2,128)} %mask_hbm.3), custom_call_target="tpu_custom_call" | custom-call | flops 268435456 | bytes 256 | tf_op jit(solution)/shard_map/arrange/pallas_call | solution.py:62
  6.0 1.6 %collective-permute-start.2 = (bf16[4,96,256]{2,1,0:T(8,128)(2,1)S(1)}, bf16[4,96,256]{2,1,0:T(8,128)(2,1)S(1)}, u32[]{:S(2)}, u32[]{:S(2)}) collective-permute-start(bf16[4,96,256]{2,1,0:T(8,128)(2,1)S(1)} %arrange.3.y2.refs_1_), channel_id=1, source_target_pairs={{0,2},{1,3},{2,4},{3,5},{4,6},{5,7},{6,0},{7,1},{8,10},{9,11},{10,... | collective-permute-start | bytes 589832 | tf_op jit(solution)/shard_map/ppermute | solution.py:389
  7.6 2.7 %transform.1 = (bf16[2,4,192,256]{3,2,1,0:T(8,128)(2,1)S(1)}, bf16[2,2,4,192,256]{4,3,2,1,0:T(8,128)(2,1)S(1)}, bf16[2,2,256,256]{3,2,1,0:T(8,128)(2,1)S(1)}) custom-call(s32[2]{0:T(128)} %atom_hbm.1, bf16[2,16,64,64]{3,2,1,0:T(8,128)(2,1)} %occ_hbm.1, bf16[2,16,64,64]{3,2,1,0:T(8,128)(2,1)} %virt_hbm.1, bf16[4,96,256]{2,1,0:T(8,128)(2,1)S(1)} %arrange.2.y1.refs_0_, ...), custom_call_target="tpu_custom_call" | custom-call | flops 2147483648 | bytes 256 | tf_op jit(solution)/shard_map/transform/pallas_call | solution.py:128
  10.3 0.1 collective-permute-start.4
  10.4 0.5 %collective-permute-start.5 = (bf16[4,96,256]{2,1,0:T(8,128)(2,1)S(1)}, bf16[4,96,256]{2,1,0:T(8,128)(2,1)S(1)}, u32[]{:S(2)}, u32[]{:S(2)}) collective-permute-start(bf16[4,96,256]{2,1,0:T(8,128)(2,1)S(1)} %arrange.3.y2.refs_1_), channel_id=1, source_target_pairs={{0,1},{1,0},{2,3},{3,2},{4,5},{5,4},{6,7},{7,6},{8,9},{9,8},{10,11... | collective-permute-start | bytes 589832 | tf_op jit(solution)/shard_map/ppermute | solution.py:386
  10.9 1.7 %collective-permute-done.refs_0_ = bf16[4,96,256]{2,1,0:T(8,128)(2,1)S(1)} collective-permute-done((bf16[4,96,256]{2,1,0:T(8,128)(2,1)S(1)}, bf16[4,96,256]{2,1,0:T(8,128)(2,1)S(1)}, u32[]{:S(2)}, u32[]{:S(2)}) %collective-permute-start) | collective-permute-done | bytes 196640 | tf_op jit(solution)/shard_map/ppermute | solution.py:389
  12.6 0.0 collective-permute-start.7
  12.6 0.0 collective-permute-start.1
  12.7 3.3 %collective-permute-done.2.refs_1_ = bf16[4,96,256]{2,1,0:T(8,128)(2,1)S(1)} collective-permute-done((bf16[4,96,256]{2,1,0:T(8,128)(2,1)S(1)}, bf16[4,96,256]{2,1,0:T(8,128)(2,1)S(1)}, u32[]{:S(2)}, u32[]{:S(2)}) %collective-permute-start.2) | collective-permute-done | bytes 196640 | tf_op jit(solution)/shard_map/ppermute | solution.py:389
  16.0 0.0 collective-permute-start.8
  16.0 0.0 collective-permute-done.4.y1.refs_2_
  16.0 0.0 collective-permute-start.3
  16.0 0.0 collective-permute-done.5.y2.refs_3_
  16.0 0.7 %complete.1.w_ref = bf16[2,2,4,192,256]{4,3,2,1,0:T(8,128)(2,1)S(1)} custom-call(bf16[2,2,4,192,256]{4,3,2,1,0:T(8,128)(2,1)S(1)} %get-tuple-element.32.before_ref, bf16[2,2,256,256]{3,2,1,0:T(8,128)(2,1)S(1)} %get-tuple-element.33.green_ref, bf16[4,96,256]{2,1,0:T(8,128)(2,1)S(1)} %collective-permute-done.4.y1.refs_2_, ...), custom_call_target="tpu_custom_call", output_to_operand_aliasing={{}: (0, {})} | custom-call | flops 1073741824 | bytes 256 | tf_op jit(solution)/shard_map/complete/pallas_call | solution.py:156
  16.7 0.7 %far.1 = bf16[288,128]{1,0:T(8,128)(2,1)S(1)} custom-call(bf16[2,2,4,192,256]{4,3,2,1,0:T(8,128)(2,1)S(1)} %complete.1.w_ref, bf16[4,96,256]{2,1,0:T(8,128)(2,1)S(1)} %collective-permute-done.refs_0_, bf16[4,96,256]{2,1,0:T(8,128)(2,1)S(1)} %collective-permute-done.2.refs_1_), custom_call_target="tpu_custom_call" | custom-call | flops 536870912 | bytes 256 | tf_op jit(solution)/shard_map/far/pallas_call | solution.py:262
  17.4 3.9 %collective-permute-start.6 = (bf16[288,128]{1,0:T(8,128)(2,1)S(1)}, bf16[288,128]{1,0:T(8,128)(2,1)S(1)}, u32[]{:S(2)}, u32[]{:S(2)}) collective-permute-start(bf16[288,128]{1,0:T(8,128)(2,1)S(1)} %far.1), channel_id=1, source_target_pairs={{0,6},{1,7},{2,0},{3,1},{4,2},{5,3},{6,4},{7,5},{8,14},{9,15},{10,... | collective-permute-start | bytes 221192 | tf_op jit(solution)/shard_map/ppermute | solution.py:407
  21.3 0.7 %mirror.1.z_ref = bf16[2,4,192,256]{3,2,1,0:T(8,128)(2,1)S(1)} custom-call(bf16[2,2,256,256]{3,2,1,0:T(8,128)(2,1)S(1)} %get-tuple-element.33.green_ref, bf16[4,96,256]{2,1,0:T(8,128)(2,1)S(1)} %collective-permute-done.4.y1.refs_2_, bf16[4,96,256]{2,1,0:T(8,128)(2,1)S(1)} %collective-permute-done.5.y2.refs_3_), custom_call_target="tpu_custom_call" | custom-call | flops 536870912 | bytes 256 | tf_op jit(solution)/shard_map/mirror/pallas_call | solution.py:176
  21.9 0.4 near.3.refs_0_
  22.4 0.0 collective-permute-done.7.refs_2_
  22.4 0.0 collective-permute-done.8.refs_3_
  22.4 0.4 near.2.refs_1_
  22.8 4.7 %collective-permute-done.6.refs_4_ = bf16[288,128]{1,0:T(8,128)(2,1)S(1)} collective-permute-done((bf16[288,128]{1,0:T(8,128)(2,1)S(1)}, bf16[288,128]{1,0:T(8,128)(2,1)S(1)}, u32[]{:S(2)}, u32[]{:S(2)}) %collective-permute-start.6) | collective-permute-done | bytes 73760 | tf_op jit(solution)/shard_map/ppermute | solution.py:407
  27.5 0.0 collective-permute-done.1.y1
  27.5 0.0 collective-permute-done.3.y2
  27.5 0.4 last_share.2
  27.9 0.0 copy-start
  27.9 0.1 collective-permute-start.9
  28.0 0.4 last_share.3.refs_2_
  28.4 0.9 %collective-permute-done.9.refs_3_ = f32[192,96]{1,0:T(8,128)S(1)} collective-permute-done((f32[192,96]{1,0:T(8,128)S(1)}, f32[192,96]{1,0:T(8,128)S(1)}, u32[]{:S(2)}, u32[]{:S(2)}) %collective-permute-start.9) | collective-permute-done | bytes 73760 | tf_op jit(solution)/shard_map/ppermute | solution.py:386
  29.3 0.2 pack.1
  29.5 1.8 %collective-permute-start.10 = (bf16[288,128]{1,0:T(8,128)(2,1)S(1)}, bf16[288,128]{1,0:T(8,128)(2,1)S(1)}, u32[]{:S(2)}, u32[]{:S(2)}) collective-permute-start(bf16[288,128]{1,0:T(8,128)(2,1)S(1)} %get-tuple-element.49), channel_id=1, source_target_pairs={{0,16},{8,24},{16,0},{24,8},{1,17},{9,25},{17,1},{25,9},{2,18},{10... | collective-permute-start | bytes 221192 | tf_op jit(solution)/shard_map/ppermute | solution.py:423
  31.3 1.4 %collective-permute-start.11 = (bf16[288,128]{1,0:T(8,128)(2,1)S(1)}, bf16[288,128]{1,0:T(8,128)(2,1)S(1)}, u32[]{:S(2)}, u32[]{:S(2)}) collective-permute-start(bf16[288,128]{1,0:T(8,128)(2,1)S(1)} %get-tuple-element.50), channel_id=1, source_target_pairs={{0,24},{8,16},{16,8},{24,0},{1,25},{9,17},{17,9},{25,1},{2,26},{10... | collective-permute-start | bytes 221192 | tf_op jit(solution)/shard_map/ppermute | solution.py:423
  32.8 0.3 collective-permute-start.12
  33.0 1.5 %collective-permute-done.10.refs_1_ = bf16[288,128]{1,0:T(8,128)(2,1)S(1)} collective-permute-done((bf16[288,128]{1,0:T(8,128)(2,1)S(1)}, bf16[288,128]{1,0:T(8,128)(2,1)S(1)}, u32[]{:S(2)}, u32[]{:S(2)}) %collective-permute-start.10) | collective-permute-done | bytes 73760 | tf_op jit(solution)/shard_map/ppermute | solution.py:423
  34.5 2.7 %collective-permute-done.11.refs_2_ = bf16[288,128]{1,0:T(8,128)(2,1)S(1)} collective-permute-done((bf16[288,128]{1,0:T(8,128)(2,1)S(1)}, bf16[288,128]{1,0:T(8,128)(2,1)S(1)}, u32[]{:S(2)}, u32[]{:S(2)}) %collective-permute-start.11) | collective-permute-done | bytes 73760 | tf_op jit(solution)/shard_map/ppermute | solution.py:423
  37.2 0.0 collective-permute-done.12.refs_3_
  37.2 0.0 copy-done
  37.3 0.4 combine.1
  37.6 9.4 %all_to_all.11 = f32[32,1,128]{2,1,0:T(1,128)S(1)} all-to-all(f32[32,1,128]{2,1,0:T(1,128)S(1)} %bitcast.6), channel_id=1, replica_groups=mesh['pair'=4,'aux'=8] {'pair','aux'}, dimensions={0} | all-to-all | bytes 32768 | tf_op jit(solution)/shard_map/all_to_all | solution.py:430
  47.0 0.7 %close.1 = (f32[2,96,192]{2,1,0:T(8,128)}, f32[1,1]{1,0:T(1,128)}) custom-call(f32[2,96,192]{2,1,0:T(8,128)S(1)} %get-tuple-element.52.tile_ref, f32[32,128]{1,0:T(8,128)S(1)} %bitcast.7), custom_call_target="tpu_custom_call" | custom-call | flops 268435456 | bytes 256 | tf_op jit(solution)/shard_map/close/pallas_call | solution.py:359
Async XLA Ops:
  1.8 10.8 %collective-permute-start = (bf16[4,96,256]{2,1,0:T(8,128)(2,1)S(1)}, bf16[4,96,256]{2,1,0:T(8,128)(2,1)S(1)}, u32[]{:S(2)}, u32[]{:S(2)}) collective-permute-start(bf16[4,96,256]{2,1,0:T(8,128)(2,1)S(1)} %arrange.2.y1.refs_0_), channel_id=1, source_target_pairs={{0,2},{1,3},{2,4},{3,5},{4,6},{5,7},{6,0},{7,1},{8,10},{9,11},{10,... | collective-permute-start | bytes 589832 | tf_op jit(solution)/shard_map/ppermute | solution.py:389
  6.0 10.0 %collective-permute-start.2 = (bf16[4,96,256]{2,1,0:T(8,128)(2,1)S(1)}, bf16[4,96,256]{2,1,0:T(8,128)(2,1)S(1)}, u32[]{:S(2)}, u32[]{:S(2)}) collective-permute-start(bf16[4,96,256]{2,1,0:T(8,128)(2,1)S(1)} %arrange.3.y2.refs_1_), channel_id=1, source_target_pairs={{0,2},{1,3},{2,4},{3,5},{4,6},{5,7},{6,0},{7,1},{8,10},{9,11},{10,... | collective-permute-start | bytes 589832 | tf_op jit(solution)/shard_map/ppermute | solution.py:389
  10.3 5.7 %collective-permute-start.4 = (bf16[4,96,256]{2,1,0:T(8,128)(2,1)S(1)}, bf16[4,96,256]{2,1,0:T(8,128)(2,1)S(1)}, u32[]{:S(2)}, u32[]{:S(2)}) collective-permute-start(bf16[4,96,256]{2,1,0:T(8,128)(2,1)S(1)} %arrange.2.y1.refs_0_), channel_id=1, source_target_pairs={{0,1},{1,0},{2,3},{3,2},{4,5},{5,4},{6,7},{7,6},{8,9},{9,8},{10,11... | collective-permute-start | bytes 589832 | tf_op jit(solution)/shard_map/ppermute | solution.py:386
  10.4 5.6 %collective-permute-start.5 = (bf16[4,96,256]{2,1,0:T(8,128)(2,1)S(1)}, bf16[4,96,256]{2,1,0:T(8,128)(2,1)S(1)}, u32[]{:S(2)}, u32[]{:S(2)}) collective-permute-start(bf16[4,96,256]{2,1,0:T(8,128)(2,1)S(1)} %arrange.3.y2.refs_1_), channel_id=1, source_target_pairs={{0,1},{1,0},{2,3},{3,2},{4,5},{5,4},{6,7},{7,6},{8,9},{9,8},{10,11... | collective-permute-start | bytes 589832 | tf_op jit(solution)/shard_map/ppermute | solution.py:386
  12.6 9.7 %collective-permute-start.7 = (bf16[4,96,256]{2,1,0:T(8,128)(2,1)S(1)}, bf16[4,96,256]{2,1,0:T(8,128)(2,1)S(1)}, u32[]{:S(2)}, u32[]{:S(2)}) collective-permute-start(bf16[4,96,256]{2,1,0:T(8,128)(2,1)S(1)} %collective-permute-done.refs_0_), channel_id=1, source_target_pairs={{0,1},{1,0},{2,3},{3,2},{4,5},{5,4},{6,7},{7,6},{8,9},{9,8},{10,11... | collective-permute-start | bytes 589832 | tf_op jit(solution)/shard_map/ppermute | solution.py:386
  12.6 14.9 %collective-permute-start.1 = (bf16[4,96,256]{2,1,0:T(8,128)(2,1)S(1)}, bf16[4,96,256]{2,1,0:T(8,128)(2,1)S(1)}, u32[]{:S(2)}, u32[]{:S(2)}) collective-permute-start(bf16[4,96,256]{2,1,0:T(8,128)(2,1)S(1)} %collective-permute-done.refs_0_), channel_id=1, source_target_pairs={{0,2},{1,3},{2,4},{3,5},{4,6},{5,7},{6,0},{7,1},{8,10},{9,11},{10,... | collective-permute-start | bytes 589832 | tf_op jit(solution)/shard_map/ppermute | solution.py:399
  16.0 6.4 %collective-permute-start.8 = (bf16[4,96,256]{2,1,0:T(8,128)(2,1)S(1)}, bf16[4,96,256]{2,1,0:T(8,128)(2,1)S(1)}, u32[]{:S(2)}, u32[]{:S(2)}) collective-permute-start(bf16[4,96,256]{2,1,0:T(8,128)(2,1)S(1)} %collective-permute-done.2.refs_1_), channel_id=1, source_target_pairs={{0,1},{1,0},{2,3},{3,2},{4,5},{5,4},{6,7},{7,6},{8,9},{9,8},{10,11... | collective-permute-start | bytes 589832 | tf_op jit(solution)/shard_map/ppermute | solution.py:386
  16.0 11.5 %collective-permute-start.3 = (bf16[4,96,256]{2,1,0:T(8,128)(2,1)S(1)}, bf16[4,96,256]{2,1,0:T(8,128)(2,1)S(1)}, u32[]{:S(2)}, u32[]{:S(2)}) collective-permute-start(bf16[4,96,256]{2,1,0:T(8,128)(2,1)S(1)} %collective-permute-done.2.refs_1_), channel_id=1, source_target_pairs={{0,2},{1,3},{2,4},{3,5},{4,6},{5,7},{6,0},{7,1},{8,10},{9,11},{10,... | collective-permute-start | bytes 589832 | tf_op jit(solution)/shard_map/ppermute | solution.py:399
  17.4 10.1 %collective-permute-start.6 = (bf16[288,128]{1,0:T(8,128)(2,1)S(1)}, bf16[288,128]{1,0:T(8,128)(2,1)S(1)}, u32[]{:S(2)}, u32[]{:S(2)}) collective-permute-start(bf16[288,128]{1,0:T(8,128)(2,1)S(1)} %far.1), channel_id=1, source_target_pairs={{0,6},{1,7},{2,0},{3,1},{4,2},{5,3},{6,4},{7,5},{8,14},{9,15},{10,... | collective-permute-start | bytes 221192 | tf_op jit(solution)/shard_map/ppermute | solution.py:407
  27.9 9.4 %copy-start = (f32[2]{0:T(128)S(1)}, f32[2]{0:T(128)}, u32[]{:S(2)}) copy-start(f32[2]{0:T(128)} %param.11) | copy-start | bytes 28
  27.9 1.4 %collective-permute-start.9 = (f32[192,96]{1,0:T(8,128)S(1)}, f32[192,96]{1,0:T(8,128)S(1)}, u32[]{:S(2)}, u32[]{:S(2)}) collective-permute-start(f32[192,96]{1,0:T(8,128)S(1)} %last_share.2), channel_id=1, source_target_pairs={{0,1},{1,0},{2,3},{3,2},{4,5},{5,4},{6,7},{7,6},{8,9},{9,8},{10,11... | collective-permute-start | bytes 221192 | tf_op jit(solution)/shard_map/ppermute | solution.py:386
  29.5 5.1 %collective-permute-start.10 = (bf16[288,128]{1,0:T(8,128)(2,1)S(1)}, bf16[288,128]{1,0:T(8,128)(2,1)S(1)}, u32[]{:S(2)}, u32[]{:S(2)}) collective-permute-start(bf16[288,128]{1,0:T(8,128)(2,1)S(1)} %get-tuple-element.49), channel_id=1, source_target_pairs={{0,16},{8,24},{16,0},{24,8},{1,17},{9,25},{17,1},{25,9},{2,18},{10... | collective-permute-start | bytes 221192 | tf_op jit(solution)/shard_map/ppermute | solution.py:423
  31.3 5.9 %collective-permute-start.11 = (bf16[288,128]{1,0:T(8,128)(2,1)S(1)}, bf16[288,128]{1,0:T(8,128)(2,1)S(1)}, u32[]{:S(2)}, u32[]{:S(2)}) collective-permute-start(bf16[288,128]{1,0:T(8,128)(2,1)S(1)} %get-tuple-element.50), channel_id=1, source_target_pairs={{0,24},{8,16},{16,8},{24,0},{1,25},{9,17},{17,9},{25,1},{2,26},{10... | collective-permute-start | bytes 221192 | tf_op jit(solution)/shard_map/ppermute | solution.py:423
  32.8 4.5 %collective-permute-start.12 = (bf16[288,128]{1,0:T(8,128)(2,1)S(1)}, bf16[288,128]{1,0:T(8,128)(2,1)S(1)}, u32[]{:S(2)}, u32[]{:S(2)}) collective-permute-start(bf16[288,128]{1,0:T(8,128)(2,1)S(1)} %get-tuple-element.51), channel_id=1, source_target_pairs={{0,8},{8,0},{16,24},{24,16},{1,9},{9,1},{17,25},{25,17},{2,10},{10... | collective-permute-start | bytes 221192 | tf_op jit(solution)/shard_map/ppermute | solution.py:423
